TPU v7x, 32 devices: a whole 2x2x4 slice. The times are simulated.
32 devices in a mesh: rep: 8 (over y, x, core), shard: 4 (over z).
Axes of the slice: x: 2, y: 2, z: 4, core: 2. Of those that a mesh axis runs over, the one named last changes fastest.
Arguments:
- hidden_in: bfloat16 [8192, 1024], P(('rep', 'shard')), may hold values from -6 to 6
- valid_mask: int32 [8192], P(('rep', 'shard')), may hold values from 0 to 1
- teacher: bfloat16 [8192, 1024], P(('rep', 'shard')), may hold values from -9 to 9
- routes: int32 [8192, 8], P(('rep', 'shard')), may hold values from 0 to 15, all different within a row; in each aligned block of 256 rows (0 to 255, 256 to 511, ...) at most 160 rows name the same one
- attn_norm: bfloat16 [1024], P('shard'), may hold values from 0.5 to 1.5
- w_query: bfloat16 [1024, 1024], P('shard'), may hold values from -0.75 to 0.75
- w_key: bfloat16 [1024, 512], P('shard'), may hold values from -0.75 to 0.75
- w_value: bfloat16 [1024, 512], P('shard'), may hold values from -0.1875 to 0.1875
- w_output: bfloat16 [1024, 1024], P('shard'), may hold values from -4 to 4
- ffn_norm: bfloat16 [1024], P('shard'), may hold values from 0.5 to 1.5
- router: bfloat16 [1024, 16], P('shard'), may hold values from -0.09375 to 0.09375
- w_in: bfloat16 [16, 1024, 1024], P('shard'), may hold values from -0.1875 to 0.1875
- w_out: bfloat16 [16, 512, 1024], P('shard'), may hold values from -4 to 4
Outputs:
- output: bfloat16 [8192, 1024], P(('rep', 'shard'))
- loss: float32 [], replicated
- input_grad: float32 [8192, 1024], P(('rep', 'shard'))
- grad_attn_norm: float32 [1024], P('shard')
- grad_w_query: float32 [1024, 1024], P('shard')
- grad_w_key: float32 [1024, 512], P('shard')
- grad_w_value: float32 [1024, 512], P('shard')
- grad_w_output: float32 [1024, 1024], P('shard')
- grad_ffn_norm: float32 [1024], P('shard')
- grad_router: float32 [1024, 16], P('shard')
- grad_w_in: float32 [16, 1024, 1024], P('shard')
- grad_w_out: float32 [16, 512, 1024], P('shard')
Inputs may be any that keep to these rules, and one draw needn't show every extreme that they name: `routes`: each row names 8 different experts. Among one device's 256 rows (aligned blocks of the token order) no expert is named by more than 160 rows, a bound that some block reaches.
All inputs are finite; a program needn't handle non-finite values.
Results may differ from a plain program's by a relative error of at most 0.013.
The roundings to bfloat16 on the way count: a program that leaves them out, or rounds other values in their place, can miss the bound.
Values may be sent and summed in bfloat16 or wider, within the bound.
No kernel may reach another device: no remote copies, remote signals or barrier semaphores. Data moves between devices by JAX's collectives and lax.ppermute only.
A program may use at most 512 MiB of HBM per device.

v0:
```python
import jax
import jax.numpy as jnp
from jax import lax
from jax.sharding import PartitionSpec as P

HEADS = 16
KV_HEADS = 8
HEAD_DIM = 64
TOP = 8
BLOCK = 256


norm_eps = 1e-06
resid_mult = 0.22
attn_mult = 0.015625
rope_base = 10000.0
very_low = -1e30


def rope_tables(positions, half_dim):
    frequency = rope_base ** (-jnp.arange(half_dim, dtype=jnp.float32) / half_dim)
    angles = positions.astype(jnp.float32)[:, None] * frequency[None, :]
    return (jnp.cos(angles), jnp.sin(angles))


def rotate(values, cosine, sine_table):
    half_dim = values.shape[-1] // 2
    first_half = values[..., :half_dim]
    second_half = values[..., half_dim:]
    cos_wide = cosine[:, None, :]
    sin_wide = sine_table[:, None, :]
    return jnp.concatenate(
        [
            first_half * cos_wide - second_half * sin_wide,
            second_half * cos_wide + first_half * sin_wide,
        ],
        -1,
    )


def rotate_back(grad_vals, cosine, sine_table):
    half_dim = grad_vals.shape[-1] // 2
    first_half = grad_vals[..., :half_dim]
    second_half = grad_vals[..., half_dim:]
    cos_wide = cosine[:, None, :]
    sin_wide = sine_table[:, None, :]
    return jnp.concatenate(
        [
            first_half * cos_wide + second_half * sin_wide,
            second_half * cos_wide - first_half * sin_wide,
        ],
        -1,
    )


def rms_scale(values):
    return lax.rsqrt(jnp.mean(values * values, axis=-1, keepdims=True) + norm_eps)


def norm_back(d_normed, values, scale_vals, gain_vec):
    scaled_grad = d_normed * gain_vec
    d_gain = jnp.sum(d_normed * values * scale_vals, 0)
    d_values = scale_vals * (
        scaled_grad
        - values * scale_vals * scale_vals * jnp.mean(scaled_grad * values, axis=-1, keepdims=True)
    )
    return (d_values, d_gain)


def run_experts(slot_rows, part_in, part_out):
    hidden_units = part_out.shape[1]
    gate_up = jnp.einsum("ecd,edf->ecf", slot_rows, part_in, preferred_element_type=jnp.float32)
    hidden_vals = (jax.nn.silu(gate_up[..., :hidden_units]) * gate_up[..., hidden_units:]).astype(
        jnp.bfloat16
    )
    return jnp.einsum(
        "ecf,efd->ecd", hidden_vals, part_out, preferred_element_type=jnp.float32
    ).astype(jnp.bfloat16)


def back_experts(slot_rows, slot_grads, part_in, part_out):
    hidden_units = part_out.shape[1]
    gate_up = jnp.einsum("ecd,edf->ecf", slot_rows, part_in, preferred_element_type=jnp.float32)
    gate_vals = gate_up[..., :hidden_units]
    up_vals = gate_up[..., hidden_units:]
    sigmoid_gate = jax.nn.sigmoid(gate_vals)
    silu_gate = jax.nn.silu(gate_vals)
    hidden_vals = (silu_gate * up_vals).astype(jnp.bfloat16)
    d_hidden = jnp.einsum("ecd,efd->ecf", slot_grads, part_out, preferred_element_type=jnp.float32)
    d_gate = d_hidden * up_vals * sigmoid_gate * (1.0 + gate_vals * (1.0 - sigmoid_gate))
    d_up = d_hidden * silu_gate
    d_gate_up = jnp.concatenate([d_gate, d_up], -1).astype(jnp.bfloat16)
    d_rows = jnp.einsum(
        "ecf,edf->ecd", d_gate_up, part_in, preferred_element_type=jnp.float32
    ).astype(jnp.bfloat16)
    return (d_rows, d_gate_up, hidden_vals)


def body(
    hidden_in,
    valid_mask,
    teacher,
    routes,
    attn_norm,
    w_query,
    w_key,
    w_value,
    w_output,
    ffn_norm,
    router,
    w_in,
    w_out,
):
    row_count, model_width = hidden_in.shape
    shard_count = lax.axis_size("shard")
    seq_tokens = row_count * shard_count
    all_tokens = seq_tokens * lax.axis_size("rep")
    group_size = HEADS // KV_HEADS
    positions = lax.axis_index("shard") * row_count + jnp.arange(row_count, dtype=jnp.int32)
    cosine, sine_table = rope_tables(positions, HEAD_DIM // 2)
    gain_attn, gain_ffn, query_full, key_full, value_full, output_full, router_full = (
        lax.all_gather(attn_norm, "shard", axis=0, tiled=True),
        lax.all_gather(ffn_norm, "shard", axis=0, tiled=True),
        lax.all_gather(w_query, "shard", axis=0, tiled=True),
        lax.all_gather(w_key, "shard", axis=0, tiled=True),
        lax.all_gather(w_value, "shard", axis=0, tiled=True),
        lax.all_gather(w_output, "shard", axis=0, tiled=True),
        lax.all_gather(router, "shard", axis=0, tiled=True),
    )
    input_float = hidden_in.astype(jnp.float32)
    scale_attn = rms_scale(input_float)
    normed_attn = (input_float * scale_attn * gain_attn).astype(jnp.bfloat16)
    query_lin = jnp.dot(normed_attn, query_full, preferred_element_type=jnp.float32).reshape(
        row_count, HEADS, HEAD_DIM
    )
    key_lin = jnp.dot(normed_attn, key_full, preferred_element_type=jnp.float32).reshape(
        row_count, KV_HEADS, HEAD_DIM
    )
    value_rows = jnp.dot(normed_attn, value_full, preferred_element_type=jnp.float32).astype(
        jnp.bfloat16
    )
    query_rows = rotate(query_lin, cosine, sine_table).astype(jnp.bfloat16)
    key_rows = (
        rotate(key_lin, cosine, sine_table)
        .astype(jnp.bfloat16)
        .reshape(row_count, KV_HEADS * HEAD_DIM)
    )
    keys_all, values_all = (
        lax.all_gather(key_rows, "shard", axis=0, tiled=True),
        lax.all_gather(value_rows, "shard", axis=0, tiled=True),
    )
    query_groups = query_rows.reshape(row_count, KV_HEADS, group_size, HEAD_DIM).transpose(
        1, 2, 0, 3
    )
    key_groups = keys_all.reshape(seq_tokens, KV_HEADS, HEAD_DIM).transpose(1, 0, 2)
    value_groups = values_all.reshape(seq_tokens, KV_HEADS, HEAD_DIM).transpose(1, 0, 2)
    allowed = (jnp.arange(seq_tokens, dtype=jnp.int32) // BLOCK)[None, :] <= (positions // BLOCK)[
        :, None
    ]

    def scores_of(query_part, key_part):
        score_vals = (
            jnp.einsum("hqd,kd->hqk", query_part, key_part, preferred_element_type=jnp.float32)
            * attn_mult
        )
        return jnp.where(allowed[None], score_vals, very_low)

    def forward_group(inputs):
        query_part, key_part, value_part = inputs
        score_vals = scores_of(query_part, key_part)
        row_max = jnp.max(score_vals, -1, keepdims=True)
        expo_vals = jnp.exp(score_vals - row_max)
        row_total = jnp.sum(expo_vals, -1, keepdims=True)
        prob_vals = (expo_vals / row_total).astype(jnp.bfloat16)
        attended_part = jnp.einsum(
            "hqk,kd->hqd", prob_vals, value_part, preferred_element_type=jnp.float32
        )
        return (attended_part, row_max[..., 0] + jnp.log(row_total[..., 0]))

    attended_groups, log_norm = lax.map(forward_group, (query_groups, key_groups, value_groups))
    attended = (
        attended_groups.transpose(2, 0, 1, 3)
        .reshape(row_count, HEADS * HEAD_DIM)
        .astype(jnp.bfloat16)
    )
    branch = jnp.dot(attended, output_full, preferred_element_type=jnp.float32)
    middle = input_float + resid_mult * branch
    scale_ffn = rms_scale(middle)
    normed_ffn = (middle * scale_ffn * gain_ffn).astype(jnp.bfloat16)
    logits = jnp.dot(normed_ffn, router_full, preferred_element_type=jnp.float32)
    expert_count = router_full.shape[1]
    capacity = row_count * TOP * 5 // (4 * expert_count)
    route_hits = (routes[..., None] == jnp.arange(expert_count, dtype=jnp.int32)).astype(jnp.int32)
    route_float = route_hits.astype(jnp.float32)
    chosen = jnp.sum(route_float * logits[:, None, :], -1)
    gates = jax.nn.softmax(chosen, axis=-1)
    flat_hits = route_hits.reshape(row_count * TOP, expert_count)
    slot_pos = jnp.sum((jnp.cumsum(flat_hits, 0) - flat_hits) * flat_hits, -1)
    slot_ids = routes.reshape(-1) * capacity + slot_pos
    pos_hits = (
        slot_pos.reshape(row_count, TOP)[..., None] == jnp.arange(capacity, dtype=jnp.int32)
    ).astype(jnp.bfloat16)
    dispatch = jnp.einsum(
        "tke,tkc->ect",
        route_hits.astype(jnp.bfloat16),
        pos_hits,
        preferred_element_type=jnp.float32,
    ).astype(jnp.bfloat16)
    slots_in = jnp.einsum(
        "ect,td->ecd", dispatch, normed_ffn, preferred_element_type=jnp.float32
    ).astype(jnp.bfloat16)
    part_in, part_out = lax.all_gather((w_in, w_out), "shard", axis=0, tiled=True)
    slot_rows = slots_in
    slots_out = run_experts(slot_rows, part_in, part_out)
    flat_out = slots_out.reshape(expert_count * capacity, model_width)
    picked = (
        jnp.take(flat_out, slot_ids, axis=0)
        .reshape(row_count, TOP, model_width)
        .astype(jnp.float32)
    )
    mixture = jnp.sum(gates[..., None] * picked, 1)
    result_f = middle + resid_mult * mixture
    valid_float = valid_mask.astype(jnp.float32)
    deviation = result_f - teacher.astype(jnp.float32)
    loss_sum, valid_count = lax.psum(
        (jnp.sum(valid_float[:, None] * deviation * deviation), jnp.sum(valid_float)),
        ("rep", "shard"),
    )
    loss = loss_sum / (model_width * valid_count)
    d_result = valid_float[:, None] * deviation * (all_tokens / (2.0 * valid_count))
    attn_gain_back, ffn_gain_back, query_back, key_back, value_back, output_back, router_back = (
        lax.all_gather(attn_norm, "shard", axis=0, tiled=True),
        lax.all_gather(ffn_norm, "shard", axis=0, tiled=True),
        lax.all_gather(w_query, "shard", axis=0, tiled=True),
        lax.all_gather(w_key, "shard", axis=0, tiled=True),
        lax.all_gather(w_value, "shard", axis=0, tiled=True),
        lax.all_gather(w_output, "shard", axis=0, tiled=True),
        lax.all_gather(router, "shard", axis=0, tiled=True),
    )
    d_mix = resid_mult * d_result
    slot_token = (
        jnp.zeros((expert_count * capacity,), jnp.int32)
        .at[slot_ids]
        .set(jnp.arange(row_count * TOP, dtype=jnp.int32) // TOP)
    )
    slot_gate = (
        jnp.zeros((expert_count * capacity,), jnp.float32).at[slot_ids].set(gates.reshape(-1))
    )
    d_slots_out = (
        (slot_gate[:, None] * jnp.take(d_mix, slot_token, axis=0))
        .astype(jnp.bfloat16)
        .reshape(expert_count, capacity, model_width)
    )
    d_gates = jnp.sum(picked * d_mix[:, None, :], -1)
    d_chosen = gates * (d_gates - jnp.sum(gates * d_gates, -1, keepdims=True))
    d_logits = jnp.sum(d_chosen[..., None] * route_float, 1).astype(jnp.bfloat16)
    part_in, part_out = lax.all_gather((w_in, w_out), "shard", axis=0, tiled=True)
    slot_rows = slots_in
    d_slots_in, d_gate_up, hidden_vals = back_experts(slot_rows, d_slots_out, part_in, part_out)
    slot_rows = slots_in
    term_in = jnp.einsum("ecd,ecf->edf", slot_rows, d_gate_up, preferred_element_type=jnp.float32)
    term_out = jnp.einsum(
        "ecd,ecf->edf", d_slots_out, hidden_vals, preferred_element_type=jnp.float32
    )
    owned = lax.psum_scatter(
        jnp.concatenate([term_in, term_out], -1), "shard", scatter_dimension=0, tiled=True
    )
    hidden_units = w_out.shape[1]
    grad_in_part = owned[..., : 2 * hidden_units]
    grad_out_part = owned[..., 2 * hidden_units :].transpose(0, 2, 1)
    d_normed_ffn = jnp.einsum(
        "ect,ecd->td", dispatch, d_slots_in, preferred_element_type=jnp.float32
    ) + jnp.dot(d_logits, router_back.T, preferred_element_type=jnp.float32)
    grad_router = jnp.dot(normed_ffn.T, d_logits, preferred_element_type=jnp.float32)
    d_norm_mid, grad_gain_ffn = norm_back(d_normed_ffn, middle, scale_ffn, ffn_gain_back)
    d_middle = d_result + d_norm_mid
    d_branch = (resid_mult * d_middle).astype(jnp.bfloat16)
    grad_output = jnp.dot(attended.T, d_branch, preferred_element_type=jnp.float32)
    d_attended = jnp.dot(d_branch, output_back.T, preferred_element_type=jnp.float32).astype(
        jnp.bfloat16
    )
    d_att_groups = d_attended.reshape(row_count, KV_HEADS, group_size, HEAD_DIM).transpose(
        1, 2, 0, 3
    )

    def backward_group(inputs):
        query_part, key_part, value_part, norm_part, grad_part = inputs
        score_vals = scores_of(query_part, key_part)
        prob_vals = jnp.exp(score_vals - norm_part[..., None])
        d_probs = jnp.einsum(
            "hqd,kd->hqk", grad_part, value_part, preferred_element_type=jnp.float32
        )
        d_scores = (prob_vals * (d_probs - jnp.sum(prob_vals * d_probs, -1, keepdims=True))).astype(
            jnp.bfloat16
        )
        query_term = (
            jnp.einsum("hqk,kd->hqd", d_scores, key_part, preferred_element_type=jnp.float32)
            * attn_mult
        )
        key_term = (
            jnp.einsum("hqk,hqd->kd", d_scores, query_part, preferred_element_type=jnp.float32)
            * attn_mult
        )
        value_term = jnp.einsum(
            "hqk,hqd->kd",
            prob_vals.astype(jnp.bfloat16),
            grad_part,
            preferred_element_type=jnp.float32,
        )
        return (query_term, jnp.concatenate([key_term, value_term], -1))

    d_query_groups, key_value_terms = lax.map(
        backward_group, (query_groups, key_groups, value_groups, log_norm, d_att_groups)
    )
    key_value_owned = lax.psum_scatter(key_value_terms, "shard", scatter_dimension=1, tiled=True)
    key_grad_rows = (
        rotate_back(key_value_owned[..., :HEAD_DIM].transpose(1, 0, 2), cosine, sine_table)
        .reshape(row_count, KV_HEADS * HEAD_DIM)
        .astype(jnp.bfloat16)
    )
    value_grad_rows = (
        key_value_owned[..., HEAD_DIM:]
        .transpose(1, 0, 2)
        .reshape(row_count, KV_HEADS * HEAD_DIM)
        .astype(jnp.bfloat16)
    )
    query_grad_rows = (
        rotate_back(
            d_query_groups.transpose(2, 0, 1, 3).reshape(row_count, HEADS, HEAD_DIM),
            cosine,
            sine_table,
        )
        .reshape(row_count, HEADS * HEAD_DIM)
        .astype(jnp.bfloat16)
    )
    grad_query = jnp.dot(normed_attn.T, query_grad_rows, preferred_element_type=jnp.float32)
    grad_key = jnp.dot(normed_attn.T, key_grad_rows, preferred_element_type=jnp.float32)
    grad_value = jnp.dot(normed_attn.T, value_grad_rows, preferred_element_type=jnp.float32)
    d_normed_attn = jnp.dot(query_grad_rows, query_back.T, preferred_element_type=jnp.float32)
    d_normed_attn = d_normed_attn + jnp.dot(
        key_grad_rows, key_back.T, preferred_element_type=jnp.float32
    )
    d_normed_attn = d_normed_attn + jnp.dot(
        value_grad_rows, value_back.T, preferred_element_type=jnp.float32
    )
    d_norm_in, grad_gain_attn = norm_back(d_normed_attn, input_float, scale_attn, attn_gain_back)
    d_input = d_middle + d_norm_in
    own_gain_attn, own_query, own_key, own_value, own_output, own_gain_ffn, own_router = (
        lax.psum_scatter(grad_gain_attn, "shard", scatter_dimension=0, tiled=True),
        lax.psum_scatter(grad_query, "shard", scatter_dimension=0, tiled=True),
        lax.psum_scatter(grad_key, "shard", scatter_dimension=0, tiled=True),
        lax.psum_scatter(grad_value, "shard", scatter_dimension=0, tiled=True),
        lax.psum_scatter(grad_output, "shard", scatter_dimension=0, tiled=True),
        lax.psum_scatter(grad_gain_ffn, "shard", scatter_dimension=0, tiled=True),
        lax.psum_scatter(grad_router, "shard", scatter_dimension=0, tiled=True),
    )
    summed = lax.psum(
        (
            own_gain_attn,
            own_query,
            own_key,
            own_value,
            own_output,
            own_gain_ffn,
            own_router,
            grad_in_part,
            grad_out_part,
        ),
        "rep",
    )
    return (
        result_f.astype(jnp.bfloat16),
        loss,
        d_input,
        summed[0],
        summed[1],
        summed[2],
        summed[3],
        summed[4],
        summed[5],
        summed[6],
        summed[7],
        summed[8],
    )


def solution(mesh):
    in_specs = (
        P(("rep", "shard"), None),
        P(("rep", "shard")),
        P(("rep", "shard"), None),
        P(("rep", "shard"), None),
        P("shard"),
        P("shard", None),
        P("shard", None),
        P("shard", None),
        P("shard", None),
        P("shard"),
        P("shard", None),
        P("shard", None, None),
        P("shard", None, None),
    )
    out_specs = (
        P(("rep", "shard"), None),
        P(),
        P(("rep", "shard"), None),
        P("shard"),
        P("shard", None),
        P("shard", None),
        P("shard", None),
        P("shard", None),
        P("shard"),
        P("shard", None),
        P("shard", None, None),
        P("shard", None, None),
    )
    return jax.shard_map(body, mesh=mesh, in_specs=in_specs, out_specs=out_specs, check_vma=False)
```

profile of v0, /device:TPU:0, one launch (start us, length us, event | category | flops | bytes accessed | tf_op | source)
XLA Modules:
  0.0 3639.5 jit_solution(5873474130301113318)
XLA Ops:
  9.4 12.6 all-gather
  23.2 17.1 all-gather.17.cloned.1.call-done
  40.3 2.6 convolution_convert_fusion.3
  43.8 25.5 all-gather.13.cloned.1.call-done
  74.7 41.4 %psum.78 = f32[]{:T(128)} all-reduce(f32[]{:T(128)} %convert_reduce_fusion), channel_id=1, replica_groups=mesh['rep'=8,'shard'=4] {'rep','shard'}, use_global_device_ids=true, to_apply=%region_16.17 | all-reduce | flops 1 | bytes 8 | tf_op jit(solution)/shard_map/psum | solution.py:225
  117.1 9.3 all-gather.1
  126.4 4.5 reduce-window.6
  133.4 8.1 scatter_custom_fusion.1
  141.6 2.9 convert_bitcast_fusion
  144.5 3.4 copy.62
  148.6 13.5 all_gather.50
  165.6 2.6 fusion.114
  168.5 9.8 all-gather.15.cloned.1.call-done
  178.3 37.3 %while.28 = (s32[]{:T(128)}, bf16[8,2,256,64]{2,3,1,0:T(8,128)(2,1)S(1)}, f32[8,2,256]{2,1,0:T(2,128)}, bf16[8,2,256,64]{2,3,1,0:T(8,128)(2,1)S(1)}, bf16[8,1024...) while((s32[]{:T(128)}, ...), condition=%wide.region_4.5_spmd.clone.clone, body=%wide.region_1.4_spmd.clone.sunk.clone | while | flops 140770816 | bytes 7822433 | solution.py:180
  215.6 7.6 all-gather.21.cloned.1.call-done
  229.0 8.2 scatter_custom_fusion
  237.9 4.0 convolution_convert_fusion.1
  241.9 542.8 %all-gather.23.cloned.1.call-done = bf16[16,1024,1024]{2,1,0:T(8,128)(2,1)} async-done(((bf16[4,1024,1024]{2,1,0:T(8,128)(2,1)}), bf16[16,1024,1024]{2,1,0:T(8,128)(2,1)}) %all-gather.23.cloned.1.call-update) | async-done | bytes 33554448 | tf_op jit(solution)/shard_map/all_gather | solution.py:212
  784.7 22.7 fusion.117
  807.4 4.9 multiply_convert_fusion.4
  812.4 258.9 %all-gather.25.cloned.1.call-done = bf16[16,512,1024]{2,1,0:T(8,128)(2,1)} async-done(((bf16[4,512,1024]{2,1,0:T(8,128)(2,1)}), bf16[16,512,1024]{2,1,0:T(8,128)(2,1)}) %all-gather.25.cloned.1.call-update) | async-done | bytes 16777232 | tf_op jit(solution)/shard_map/all_gather | solution.py:212
  1071.3 11.1 convolution_convert_fusion
  1082.3 14.1 gather_fusion
  1096.5 5.5 multiply_reduce_fusion.1
  1109.6 9.3 gather_fusion.1
  1118.9 20.5 multiply_convert_fusion.3
  1139.5 19.0 fusion.55
  1158.5 2.6 multiply_reduce_fusion.2
  1164.4 70.1 %while.29 = (s32[]{:T(128)}, f32[8,2,256,64]{2,3,1,0:T(8,128)}, f32[8,1024,128]{1,2,0:T(8,128)}, bf16[8,2,256,64]{2,3,1,0:T(8,128)(2,1)}, bf16[8,1024,64]{1,2,0:...) while((s32[]{:T(128)}, f32[8,2,256,64]{2,3,1,0:T(8,128)}, ...), condition=%wide.region_25.26_spmd.clone.clone, body=%wide.region_23.25_spmd.clone.sunk.clone | while | flops 340753920 | bytes 18630780 | solution.py:312
  1236.2 16.2 fusion.53
  1252.4 27.6 fusion.48
  1280.0 66.7 %pad_maximum_fusion = f32[16,1024,1536]{1,2,0:T(8,128)} fusion(f32[16,1024,512]{1,2,0:T(8,128)} %fusion.53, f32[16,1024,1024]{1,2,0:T(8,128)} %fusion.48), kind=kLoop, calls=%fused_computation.61 | loop fusion | flops 25165824 | bytes 201326592 | tf_op jit(solution)/shard_map/concatenate | solution.py:266
  1348.0 2.7 fusion.77
  1352.7 2.8 fusion.109
  1362.9 1616.0 %reduce-scatter.20.cloned.1.call-done = f32[4,1024,1536]{1,2,0:T(8,128)} async-done(((f32[16,1024,1536]{1,2,0:T(8,128)}), f32[4,1024,1536]{1,2,0:T(8,128)}) %reduce-scatter.20.cloned.1.call-update) | async-done | bytes 25165840 | tf_op jit(solution)/shard_map/reduce_scatter | solution.py:265
  2978.9 8.4 slice_bitcast_fusion
  2987.4 12.6 slice.85
  3000.0 60.1 %reduce-scatter.16.cloned.1.call-done = f32[256,1024]{1,0:T(8,128)} async-done(((f32[1024,1024]{1,0:T(8,128)}), f32[256,1024]{1,0:T(8,128)}) %reduce-scatter.16.cloned.1.call-update) | async-done | bytes 1048592 | tf_op jit(solution)/shard_map/reduce_scatter | solution.py:353
  3060.1 79.5 %reduce-scatter.10.cloned.1.call-done = f32[256,1024]{1,0:T(8,128)} async-done(((f32[1024,1024]{1,0:T(8,128)}), f32[256,1024]{1,0:T(8,128)}) %reduce-scatter.10.cloned.1.call-update) | async-done | bytes 1048592 | tf_op jit(solution)/shard_map/reduce_scatter | solution.py:350
  3139.7 46.7 %reduce-scatter.14.cloned.1.call-done = f32[256,512]{1,0:T(8,128)} async-done(((f32[1024,512]{1,0:T(8,128)}), f32[256,512]{1,0:T(8,128)}) %reduce-scatter.14.cloned.1.call-update) | async-done | bytes 524304 | tf_op jit(solution)/shard_map/reduce_scatter | solution.py:352
  3186.3 45.5 %reduce-scatter.12.cloned.1.call-done = f32[256,512]{1,0:T(8,128)} async-done(((f32[1024,512]{1,0:T(8,128)}), f32[256,512]{1,0:T(8,128)}) %reduce-scatter.12.cloned.1.call-update) | async-done | bytes 524304 | tf_op jit(solution)/shard_map/reduce_scatter | solution.py:351
  3233.7 40.4 %psum.77 = f32[]{:T(128)} all-reduce(f32[]{:T(128)} %get-tuple-element.186), channel_id=1, replica_groups=mesh['rep'=8,'shard'=4] {'rep','shard'}, use_global_device_ids=true, to_apply=%region_14.15 | all-reduce | flops 1 | bytes 8 | tf_op jit(solution)/shard_map/psum | solution.py:225
  3274.8 2.5 fusion.118
  3278.5 10.9 all-reduce.4
  3289.6 24.8 all-reduce.2
  3315.7 287.3 %all-reduce.7.cloned.1.call-done = (f32[256,1024]{1,0:T(8,128)}, f32[256,512]{1,0:T(8,128)}, f32[256,512]{1,0:T(8,128)}, f32[256,1024]{1,0:T(8,128)}, f32[4,1024,1024]{1,2,0:T(8,128)}, /*index=5*/f32[4,512,1024]{2,1,0:T(8,128)}) async-done(((f32[256,1024]{1,0:T(8,128)}, f32[256,512]{1,0:T(8,128)}, f32[256,512]{1,0:T(8,128)}, f32[256,1024]{1,0:T(8,128)}, f32[4,1024,1024]{1,2,0:T(8,128)}, ...) | async-done | bytes 28311568 | tf_op jit(solution)/shard_map/psum | solution.py:357
  3603.0 16.5 copy.65
  3623.1 8.4 copy.105
  (337 shorter events, 160.1 us)
Async XLA Ops:
  7.2 62.1 %copy-start.3 = (bf16[256,1024]{1,0:T(8,128)(2,1)S(1)}, bf16[256,1024]{1,0:T(8,128)(2,1)}, u32[]{:S(2)}) copy-start(bf16[256,1024]{1,0:T(8,128)(2,1)} %param.17) | copy-start | bytes 1572868
  7.2 33.1 all-gather.17.cloned.1.call-start
  7.9 61.4 %all-gather.13.cloned.1.call-start = ((), (), s32[]{:S(2)}) async-start(), calls=%async_computation.8 | async-start | bytes 1310720 | tf_op jit(solution)/shard_map/all_gather | solution.py:125
  8.7 154.7 %all-gather.19.cloned.1.call-start = ((), (), s32[]{:S(2)}) async-start(), calls=%async_computation.11 | async-start | bytes 1310720 | tf_op jit(solution)/shard_map/all_gather | solution.py:150
  22.0 143.6 %copy-start.34 = (f32[4,1,256]{2,1,0:T(1,128)}, f32[4,1,256]{2,1,0:T(1,128)S(1)}, u32[]{:S(2)}) copy-start(f32[4,1,256]{2,1,0:T(1,128)S(1)} %convert_element_type.169) | copy-start | bytes 12292
  23.2 142.4 %copy-start.36 = (f32[256]{0:T(256)}, f32[256]{0:T(256)S(1)}, u32[]{:S(2)}) copy-start(f32[256]{0:T(256)S(1)} %add_rsqrt_fusion.1) | copy-start | bytes 3076
  42.9 122.7 %all-gather.11.cloned.1.call-start = ((), (), s32[]{:S(2)}) async-start(), calls=%async_computation.7 | async-start | bytes 2621440 | tf_op jit(solution)/shard_map/all_gather | solution.py:124
  43.5 134.8 %all-gather.15.cloned.1.call-start = ((), (), s32[]{:S(2)}) async-start(), calls=%async_computation.9 | async-start | bytes 1310720 | tf_op jit(solution)/shard_map/all_gather | solution.py:149
  43.8 124.4 %copy-start.21 = (f32[256,32]{0,1:T(8,128)}, f32[256,32]{0,1:T(8,128)S(1)}, u32[]{:S(2)}) copy-start(f32[256,32]{0,1:T(8,128)S(1)} %get-tuple-element.250) | copy-start | bytes 98308
  43.8 124.4 %copy-start.23 = (f32[256,32]{0,1:T(8,128)}, f32[256,32]{0,1:T(8,128)S(1)}, u32[]{:S(2)}) copy-start(f32[256,32]{0,1:T(8,128)S(1)} %get-tuple-element.251) | copy-start | bytes 98308
  71.9 151.3 %all-gather.21.cloned.1.call-start = ((), (), s32[]{:S(2)}) async-start(), calls=%async_computation.12 | async-start | bytes 2621440 | tf_op jit(solution)/shard_map/all_gather | solution.py:127
  72.5 712.2 %all-gather.23.cloned.1.call-start = ((), (), s32[]{:S(2)}) async-start(), calls=%async_computation.13 | async-start | bytes 41943040 | tf_op jit(solution)/shard_map/all_gather | solution.py:212
  73.3 43.4 %copy-start.48 = (s32[256,8]{0,1:T(8,128)S(1)}, s32[256,8]{0,1:T(8,128)}, u32[]{:S(2)}) copy-start(s32[256,8]{0,1:T(8,128)} %param.20) | copy-start | bytes 24580
  73.3 43.8 %copy-start.51 = (bf16[256]{0:T(256)(128)(2,1)S(1)}, bf16[256]{0:T(256)(128)(2,1)}, u32[]{:S(2)}) copy-start(bf16[256]{0:T(256)(128)(2,1)} %param.26) | copy-start | bytes 1540
  73.3 998.0 %all-gather.25.cloned.1.call-start = ((), (), s32[]{:S(2)}) async-start(), calls=%async_computation.14 | async-start | bytes 20971520 | tf_op jit(solution)/shard_map/all_gather | solution.py:212
  74.0 1281.6 %reduce-scatter.8.cloned.1.call-start = ((), (), s32[]{:S(2)}) async-start(), calls=%async_computation.15 | async-start | bytes 5242880 | tf_op jit(solution)/shard_map/reduce_scatter | solution.py:315
  131.7 16.8 copy-start.49
  133.4 32.2 copy-start.39
  147.9 89.9 %copy-start.12 = (bf16[16,160,256]{2,1,0:T(8,128)(2,1)}, bf16[16,160,256]{2,1,0:T(8,128)(2,1)S(1)}, u32[]{:S(2)}) copy-start(bf16[16,160,256]{2,1,0:T(8,128)(2,1)S(1)} %copy.62) | copy-start | bytes 3932164
  162.1 64.8 %copy-start.31 = (bf16[1024,16]{0,1:T(8,128)(2,1)}, bf16[1024,16]{0,1:T(8,128)(2,1)S(1)}, u32[]{:S(2)}) copy-start(bf16[1024,16]{0,1:T(8,128)(2,1)S(1)} %all_gather.50) | copy-start | bytes 98308
  215.6 26.3 copy-start.13
  215.6 26.3 copy-start.16
  226.8 15.1 copy-start.10
  812.3 270.0 %copy-start = (bf16[16,160,512]{2,1,0:T(8,128)(2,1)}, bf16[16,160,512]{2,1,0:T(8,128)(2,1)S(1)}, u32[]{:S(2)}) copy-start(bf16[16,160,512]{2,1,0:T(8,128)(2,1)S(1)} %multiply_convert_fusion.4) | copy-start | bytes 7864324
  812.3 270.0 %copy-start.38 = (s32[2048]{0:T(1024)S(1)}, s32[2048]{0:T(1024)}, u32[]{:S(2)}) copy-start(s32[2048]{0:T(1024)} %broadcast_clamp_fusion) | copy-start | bytes 24580
  1082.3 14.1 copy-start.30
  1096.4 5.5 copy-start.6
  1096.4 5.5 copy-start.43
  1096.4 6.8 copy-start.2
  1096.4 6.8 copy-start.47
  1109.5 48.9 %copy-start.25 = (bf16[256,16]{1,0:T(8,128)(2,1)}, bf16[256,16]{1,0:T(8,128)(2,1)S(1)}, u32[]{:S(2)}) copy-start(bf16[256,16]{1,0:T(8,128)(2,1)S(1)} %fusion.66) | copy-start | bytes 24580
  1109.5 9.4 copy-start.33
  1139.5 19.0 copy-start.15
  1139.5 19.0 copy-start.32
  1139.5 19.0 copy-start.44
  1139.5 19.0 copy-start.46
  1158.5 4.9 copy-start.9
  1234.5 1744.5 %reduce-scatter.20.cloned.1.call-start = ((), (), s32[]{:S(2)}) async-start(), calls=%async_computation.21 | async-start | bytes 125829120 | tf_op jit(solution)/shard_map/reduce_scatter | solution.py:265
  1346.7 4.1 copy-start.22
  1346.7 1713.4 %reduce-scatter.16.cloned.1.call-start = ((), (), s32[]{:S(2)}) async-start(), calls=%async_computation.19 | async-start | bytes 5242880 | tf_op jit(solution)/shard_map/reduce_scatter | solution.py:353
  1350.7 1789.0 %reduce-scatter.10.cloned.1.call-start = ((), (), s32[]{:S(2)}) async-start(), calls=%async_computation.16 | async-start | bytes 5242880 | tf_op jit(solution)/shard_map/reduce_scatter | solution.py:350
  1355.6 1830.8 %reduce-scatter.14.cloned.1.call-start = ((), (), s32[]{:S(2)}) async-start(), calls=%async_computation.18 | async-start | bytes 2621440 | tf_op jit(solution)/shard_map/reduce_scatter | solution.py:352
  1358.7 1873.2 %reduce-scatter.12.cloned.1.call-start = ((), (), s32[]{:S(2)}) async-start(), calls=%async_computation.17 | async-start | bytes 2621440 | tf_op jit(solution)/shard_map/reduce_scatter | solution.py:351
  1361.9 1927.7 %reduce-scatter.18.cloned.1.call-start = ((), (), s32[]{:S(2)}) async-start(), calls=%async_computation.20 | async-start | bytes 81920 | tf_op jit(solution)/shard_map/reduce_scatter | solution.py:355
  1362.8 2240.2 %all-reduce.7.cloned.1.call-start = ((), (), s32[]{:S(2)}) async-start(), calls=%async_computation.22 | async-start | bytes 56623104 | tf_op jit(solution)/shard_map/psum | solution.py:357
  3603.0 16.5 copy-start.20
  3603.0 17.5 copy-start.28
  3603.0 18.3 copy-start.27
  (21 other events, 37.5 us)
Sparse Core Ops, SparseCore 0:
  9.6 30.6 all-gather.16
  41.9 27.3 all-gather.12
  71.4 28.2 all-gather.18
  101.1 45.4 all-gather.10
  148.6 29.6 all-gather.14
  179.7 43.4 all-gather.20
  224.8 559.8 all-gather.22
  786.3 284.9 all-gather.24
  1234.6 74.9 reduce-scatter.7
  1346.8 1632.0 reduce-scatter.19
  2981.2 78.8 reduce-scatter.15
  3062.4 77.2 reduce-scatter.9
  3142.0 44.3 reduce-scatter.13
  3188.6 43.1 reduce-scatter.11
  3234.5 18.2 reduce-scatter.17
  3258.9 344.0 all-reduce.6
where the time goes:
time: 3650 us; the launch traced here: 3640 us
  waiting for transfers between devices  3000 us (82%)
  matrix products  230 us (6%)
  blocking collectives  153 us (4%)
  other arithmetic  122 us (3%)
  local copies, waits for them, and re-layouts  114 us (3%)
    reduce_scatter x1, waiting for transfers between devices, body(): lax.psum_scatter(jnp.concatenate([term_in, term_out], -1), 'shard', scatt...  1620 us
    all_gather x2, waiting for transfers between devices, body(): lax.all_gather((w_in, w_out), 'shard', axis=0, tiled=True)  802 us
    psum x1, waiting for transfers between devices, body(): lax.psum((own_gain_attn, own_query, own_key, own_value, own_output, own_g...  287 us
    psum x2, blocking collectives, body(): lax.psum((jnp.sum(valid_float[:, None] * deviation * deviation), jnp.sum(...  81.8 us
    reduce_scatter x1, waiting for transfers between devices, body(): lax.psum_scatter(grad_query, 'shard', scatter_dimension=0, tiled=True)  79.5 us
  transfers between devices with their start and end apart: 16, of which 12 were waited for; matrix products, arithmetic and copies ran while one was open for 7% of the time, Pallas kernels for 0%

commit v1 on v0

v1 whole, which is shorter than its diff:
```python
import jax
import jax.numpy as jnp
from jax import lax
from jax.experimental import pallas as pl
from jax.experimental.pallas import tpu as pltpu
from jax.sharding import PartitionSpec as P

HEADS = 16
KV_HEADS = 8
HEAD_DIM = 64
TOP = 8
BLOCK = 256


norm_eps = 1e-06
resid_mult = 0.22
attn_mult = 0.015625
rope_base = 10000.0
very_low = -1e30


def rope_tables(positions, half_dim):
    frequency = rope_base ** (-jnp.arange(half_dim, dtype=jnp.float32) / half_dim)
    angles = positions.astype(jnp.float32)[:, None] * frequency[None, :]
    return (jnp.cos(angles), jnp.sin(angles))


def rotate(values, cosine, sine_table):
    half_dim = values.shape[-1] // 2
    first_half = values[..., :half_dim]
    second_half = values[..., half_dim:]
    cos_wide = cosine[:, None, :]
    sin_wide = sine_table[:, None, :]
    return jnp.concatenate(
        [
            first_half * cos_wide - second_half * sin_wide,
            second_half * cos_wide + first_half * sin_wide,
        ],
        -1,
    )


def rotate_back(grad_vals, cosine, sine_table):
    half_dim = grad_vals.shape[-1] // 2
    first_half = grad_vals[..., :half_dim]
    second_half = grad_vals[..., half_dim:]
    cos_wide = cosine[:, None, :]
    sin_wide = sine_table[:, None, :]
    return jnp.concatenate(
        [
            first_half * cos_wide + second_half * sin_wide,
            second_half * cos_wide - first_half * sin_wide,
        ],
        -1,
    )


def rms_scale(values):
    return lax.rsqrt(jnp.mean(values * values, axis=-1, keepdims=True) + norm_eps)


def norm_back(d_normed, values, scale_vals, gain_vec):
    scaled_grad = d_normed * gain_vec
    d_gain = jnp.sum(d_normed * values * scale_vals, 0)
    d_values = scale_vals * (
        scaled_grad
        - values * scale_vals * scale_vals * jnp.mean(scaled_grad * values, axis=-1, keepdims=True)
    )
    return (d_values, d_gain)


LANES = 128
ROW_STEP = 256


def row_chunks(count):
    step = min(count, ROW_STEP)
    return [pl.ds(at, step) for at in range(0, count, step)]


def pick_lane(values, lane):
    lanes = lax.broadcasted_iota(jnp.int32, values.shape, 1)
    return jnp.sum(jnp.where(lanes == lane, values, 0.0), axis=1, keepdims=True)


def dot_nn(left, right):
    return jnp.dot(left, right, preferred_element_type=jnp.float32)


def dot_nt(left, right):
    return lax.dot_general(left, right, (((1,), (1,)), ((), ())), preferred_element_type=jnp.float32)


def dot_tn(left, right):
    return lax.dot_general(left, right, (((0,), (0,)), ((), ())), preferred_element_type=jnp.float32)


def experts_forward_kernel(x_ref, gate_ref, in_ref, out_ref, mix_ref, gate_up_ref, hidden_ref, total):
    expert = pl.program_id(0)
    units = out_ref.shape[1]
    for rows in row_chunks(x_ref.shape[0]):
        gate_up = dot_nn(x_ref[rows, :], in_ref[0])
        gate_up_ref[0, rows, :] = gate_up
        gate_vals = gate_up[:, :units]
        silu_gate = gate_vals / (1.0 + jnp.exp(-gate_vals))
        weight = pick_lane(gate_ref[rows, :], expert)
        hidden = (silu_gate * gate_up[:, units:] * weight).astype(jnp.bfloat16)
        hidden_ref[0, rows, :] = hidden
        part = dot_nn(hidden, out_ref[0])

        @pl.when(expert == 0)
        def _():
            total[rows, :] = part

        @pl.when(expert > 0)
        def _():
            total[rows, :] += part

    @pl.when(expert == pl.num_programs(0) - 1)
    def _():
        mix_ref[...] = total[...].astype(mix_ref.dtype)


def experts_forward(tokens, gates_own, w_in, w_out):
    count, width = tokens.shape
    experts, units = w_out.shape[0], w_out.shape[1]
    return pl.pallas_call(
        experts_forward_kernel,
        grid=(experts,),
        in_specs=[
            pl.BlockSpec((count, width), lambda e: (0, 0)),
            pl.BlockSpec((count, LANES), lambda e: (0, 0)),
            pl.BlockSpec((1, width, 2 * units), lambda e: (e, 0, 0)),
            pl.BlockSpec((1, units, width), lambda e: (e, 0, 0)),
        ],
        out_specs=[
            pl.BlockSpec((count, width), lambda e: (0, 0)),
            pl.BlockSpec((1, count, 2 * units), lambda e: (e, 0, 0)),
            pl.BlockSpec((1, count, units), lambda e: (e, 0, 0)),
        ],
        out_shape=[
            jax.ShapeDtypeStruct((count, width), jnp.bfloat16),
            jax.ShapeDtypeStruct((experts, count, 2 * units), jnp.float32),
            jax.ShapeDtypeStruct((experts, count, units), jnp.bfloat16),
        ],
        scratch_shapes=[pltpu.VMEM((count, width), jnp.float32)],
        compiler_params=pltpu.CompilerParams(vmem_limit_bytes=VMEM_BYTES),
        cost_estimate=pl.CostEstimate(
            flops=6 * count * width * units * experts,
            bytes_accessed=experts * units * (6 * width + 10 * count) + 6 * count * width,
            transcendentals=experts * count * units,
        ),
        name="experts_forward",
    )(tokens, gates_own, w_in, w_out)


def experts_backward_kernel(
    dmix_ref, gate_ref, gate_up_ref, in_ref, out_ref, drows_ref, dgate_up_ref, dgates_ref, total
):
    expert = pl.program_id(0)
    units = out_ref.shape[1]
    lanes = lax.broadcasted_iota(jnp.int32, (1, LANES), 1)
    for rows in row_chunks(dmix_ref.shape[0]):
        pulled = dot_nt(dmix_ref[rows, :], out_ref[0])
        gate_vals = gate_up_ref[0, rows, :units]
        up_vals = gate_up_ref[0, rows, units:]
        sigmoid = 1.0 / (1.0 + jnp.exp(-gate_vals))
        silu_gate = gate_vals * sigmoid
        weight = pick_lane(gate_ref[rows, :], expert)
        own = jnp.sum(pulled * silu_gate * up_vals, axis=1, keepdims=True)
        own = jnp.where(lanes == expert, own, 0.0)
        d_hidden = pulled * weight
        d_gate = d_hidden * up_vals * sigmoid * (1.0 + gate_vals * (1.0 - sigmoid))
        d_up = d_hidden * silu_gate
        dgate_up_ref[0, rows, :units] = d_gate.astype(jnp.bfloat16)
        dgate_up_ref[0, rows, units:] = d_up.astype(jnp.bfloat16)
        part = dot_nt(dgate_up_ref[0, rows, :], in_ref[0])

        @pl.when(expert == 0)
        def _():
            total[rows, :] = part
            dgates_ref[rows, :] = own

        @pl.when(expert > 0)
        def _():
            total[rows, :] += part
            dgates_ref[rows, :] += own

    @pl.when(expert == pl.num_programs(0) - 1)
    def _():
        drows_ref[...] = total[...].astype(drows_ref.dtype)


def experts_backward(d_mix, gates_own, gate_up, w_in, w_out):
    count, width = d_mix.shape
    experts, units = w_out.shape[0], w_out.shape[1]
    return pl.pallas_call(
        experts_backward_kernel,
        grid=(experts,),
        in_specs=[
            pl.BlockSpec((count, width), lambda e: (0, 0)),
            pl.BlockSpec((count, LANES), lambda e: (0, 0)),
            pl.BlockSpec((1, count, 2 * units), lambda e: (e, 0, 0)),
            pl.BlockSpec((1, width, 2 * units), lambda e: (e, 0, 0)),
            pl.BlockSpec((1, units, width), lambda e: (e, 0, 0)),
        ],
        out_specs=[
            pl.BlockSpec((count, width), lambda e: (0, 0)),
            pl.BlockSpec((1, count, 2 * units), lambda e: (e, 0, 0)),
            pl.BlockSpec((count, LANES), lambda e: (0, 0)),
        ],
        out_shape=[
            jax.ShapeDtypeStruct((count, width), jnp.bfloat16),
            jax.ShapeDtypeStruct((experts, count, 2 * units), jnp.bfloat16),
            jax.ShapeDtypeStruct((count, LANES), jnp.float32),
        ],
        scratch_shapes=[pltpu.VMEM((count, width), jnp.float32)],
        compiler_params=pltpu.CompilerParams(vmem_limit_bytes=VMEM_BYTES),
        cost_estimate=pl.CostEstimate(
            flops=6 * count * width * units * experts,
            bytes_accessed=experts * units * (6 * width + 12 * count) + 4 * count * width,
            transcendentals=experts * count * units,
        ),
        name="experts_backward",
    )(d_mix, gates_own, gate_up, w_in, w_out)


def experts_grads_kernel(x_ref, dmix_ref, dgate_up_ref, hidden_ref, gin_ref, gout_ref):
    gin_ref[0] = dot_tn(x_ref[...], dgate_up_ref[0]).astype(gin_ref.dtype)
    gout_ref[0] = dot_tn(hidden_ref[0], dmix_ref[...]).astype(gout_ref.dtype)


def experts_grads(tokens, d_mix, dgate_up, hidden):
    count, width = tokens.shape
    experts, units = hidden.shape[0], hidden.shape[2]
    return pl.pallas_call(
        experts_grads_kernel,
        grid=(experts,),
        in_specs=[
            pl.BlockSpec((count, width), lambda e: (0, 0)),
            pl.BlockSpec((count, width), lambda e: (0, 0)),
            pl.BlockSpec((1, count, 2 * units), lambda e: (e, 0, 0)),
            pl.BlockSpec((1, count, units), lambda e: (e, 0, 0)),
        ],
        out_specs=[
            pl.BlockSpec((1, width, 2 * units), lambda e: (e, 0, 0)),
            pl.BlockSpec((1, units, width), lambda e: (e, 0, 0)),
        ],
        out_shape=[
            jax.ShapeDtypeStruct((experts, width, 2 * units), jnp.bfloat16),
            jax.ShapeDtypeStruct((experts, units, width), jnp.bfloat16),
        ],
        compiler_params=pltpu.CompilerParams(vmem_limit_bytes=VMEM_BYTES),
        cost_estimate=pl.CostEstimate(
            flops=6 * count * width * units * experts,
            bytes_accessed=experts * units * (6 * width + 6 * count) + 4 * count * width,
            transcendentals=0,
        ),
        name="experts_grads",
    )(tokens, d_mix, dgate_up, hidden)


VMEM_BYTES = 60 * 1024 * 1024


def body(
    hidden_in,
    valid_mask,
    teacher,
    routes,
    attn_norm,
    w_query,
    w_key,
    w_value,
    w_output,
    ffn_norm,
    router,
    w_in,
    w_out,
):
    row_count, model_width = hidden_in.shape
    shard_count = lax.axis_size("shard")
    seq_tokens = row_count * shard_count
    all_tokens = seq_tokens * lax.axis_size("rep")
    group_size = HEADS // KV_HEADS
    shard_at = lax.axis_index("shard")
    positions = shard_at * row_count + jnp.arange(row_count, dtype=jnp.int32)
    seq_positions = jnp.arange(seq_tokens, dtype=jnp.int32)
    cosine, sine_table = rope_tables(positions, HEAD_DIM // 2)
    cosine_all, sine_all = rope_tables(seq_positions, HEAD_DIM // 2)

    def gather(block):
        return lax.all_gather(block, "shard", axis=0, tiled=True)

    def scatter(block):
        return lax.psum_scatter(block, "shard", scatter_dimension=0, tiled=True)

    input_all = gather(hidden_in)
    valid_float = valid_mask.astype(jnp.float32)
    valid_count = lax.psum(jnp.sum(valid_float), ("rep", "shard"))
    small_full = gather(jnp.concatenate([attn_norm[:, None], ffn_norm[:, None], router], 1))
    gain_attn, gain_ffn, router_full = small_full[:, 0], small_full[:, 1], small_full[:, 2:]
    routes_all = gather(routes)
    kv_width = w_key.shape[1]
    weights_full = gather(jnp.concatenate([w_query, w_key, w_value], 1))
    query_width = w_query.shape[1]
    query_full = weights_full[:, :query_width]
    kv_full = weights_full[:, query_width:]
    output_full = gather(w_output)
    input_float = hidden_in.astype(jnp.float32)
    scale_attn = rms_scale(input_float)
    normed_attn = (input_float * scale_attn * gain_attn).astype(jnp.bfloat16)
    all_float = input_all.astype(jnp.float32)
    normed_all = (all_float * rms_scale(all_float) * gain_attn).astype(jnp.bfloat16)
    query_lin = dot_nn(normed_attn, query_full).reshape(row_count, HEADS, HEAD_DIM)
    kv_lin = dot_nn(normed_all, kv_full)
    keys_all = rotate(
        kv_lin[:, :kv_width].reshape(seq_tokens, KV_HEADS, HEAD_DIM), cosine_all, sine_all
    ).astype(jnp.bfloat16)
    values_all = kv_lin[:, kv_width:].astype(jnp.bfloat16)
    query_rows = rotate(query_lin, cosine, sine_table).astype(jnp.bfloat16)
    query_groups = query_rows.reshape(row_count, KV_HEADS, group_size, HEAD_DIM).transpose(
        1, 2, 0, 3
    )
    key_groups = keys_all.reshape(seq_tokens, KV_HEADS, HEAD_DIM).transpose(1, 0, 2)
    value_groups = values_all.reshape(seq_tokens, KV_HEADS, HEAD_DIM).transpose(1, 0, 2)
    allowed = (jnp.arange(seq_tokens, dtype=jnp.int32) // BLOCK)[None, :] <= (positions // BLOCK)[
        :, None
    ]

    def scores_of(query_part, key_part):
        score_vals = (
            jnp.einsum("hqd,kd->hqk", query_part, key_part, preferred_element_type=jnp.float32)
            * attn_mult
        )
        return jnp.where(allowed[None], score_vals, very_low)

    def forward_group(inputs):
        query_part, key_part, value_part = inputs
        score_vals = scores_of(query_part, key_part)
        row_max = jnp.max(score_vals, -1, keepdims=True)
        expo_vals = jnp.exp(score_vals - row_max)
        row_total = jnp.sum(expo_vals, -1, keepdims=True)
        prob_vals = (expo_vals / row_total).astype(jnp.bfloat16)
        attended_part = jnp.einsum(
            "hqk,kd->hqd", prob_vals, value_part, preferred_element_type=jnp.float32
        )
        return (attended_part, row_max[..., 0] + jnp.log(row_total[..., 0]))

    attended_groups, log_norm = lax.map(forward_group, (query_groups, key_groups, value_groups))
    attended = (
        attended_groups.transpose(2, 0, 1, 3)
        .reshape(row_count, HEADS * HEAD_DIM)
        .astype(jnp.bfloat16)
    )
    branch = dot_nn(attended, output_full)
    middle = input_float + resid_mult * branch
    scale_ffn = rms_scale(middle)
    normed_ffn = (middle * scale_ffn * gain_ffn).astype(jnp.bfloat16)
    own_experts = w_in.shape[0]
    expert_count = router_full.shape[1]
    expert_ids = jnp.arange(expert_count, dtype=jnp.int32)
    tokens_all = gather(normed_ffn)
    logits_all = dot_nn(tokens_all, router_full)
    chosen_all = jnp.any(routes_all[..., None] == expert_ids, 1)
    masked = jnp.where(chosen_all, logits_all, very_low)
    raised = jnp.where(chosen_all, jnp.exp(masked - jnp.max(masked, -1, keepdims=True)), 0.0)
    gates_all = raised / jnp.sum(raised, -1, keepdims=True)
    gates_own = lax.dynamic_slice_in_dim(gates_all, shard_at * own_experts, own_experts, 1)
    gates_own = jnp.pad(gates_own, ((0, 0), (0, LANES - own_experts)))
    gates = lax.dynamic_slice_in_dim(gates_all, shard_at * row_count, row_count, 0)
    mix_part, gate_up, hidden_gated = experts_forward(tokens_all, gates_own, w_in, w_out)
    mixture = scatter(mix_part).astype(jnp.float32)
    result_f = middle + resid_mult * mixture
    deviation = result_f - teacher.astype(jnp.float32)
    loss_sum = lax.psum(jnp.sum(valid_float[:, None] * deviation * deviation), ("rep", "shard"))
    loss = loss_sum / (model_width * valid_count)
    d_result = valid_float[:, None] * deviation * (all_tokens / (2.0 * valid_count))
    d_mix = (resid_mult * d_result).astype(jnp.bfloat16)
    d_mix_all = gather(d_mix)
    d_rows_part, d_gate_up, d_gates_own = experts_backward(
        d_mix_all, gates_own, gate_up, w_in, w_out
    )
    d_rows = scatter(d_rows_part).astype(jnp.float32)
    d_gates = lax.all_to_all(
        d_gates_own[:, :own_experts], "shard", split_axis=0, concat_axis=1, tiled=True
    )
    grad_in, grad_out = experts_grads(tokens_all, d_mix_all, d_gate_up, hidden_gated)
    d_logits = (gates * (d_gates - jnp.sum(gates * d_gates, -1, keepdims=True))).astype(
        jnp.bfloat16
    )
    d_normed_ffn = d_rows + dot_nt(d_logits, router_full)
    grad_router = dot_tn(normed_ffn, d_logits)
    d_norm_mid, grad_gain_ffn = norm_back(d_normed_ffn, middle, scale_ffn, gain_ffn)
    d_middle = d_result + d_norm_mid
    d_branch = (resid_mult * d_middle).astype(jnp.bfloat16)
    grad_output = jnp.dot(attended.T, d_branch, preferred_element_type=jnp.float32)
    d_attended = dot_nt(d_branch, output_full).astype(
        jnp.bfloat16
    )
    d_att_groups = d_attended.reshape(row_count, KV_HEADS, group_size, HEAD_DIM).transpose(
        1, 2, 0, 3
    )

    def backward_group(inputs):
        query_part, key_part, value_part, norm_part, grad_part = inputs
        score_vals = scores_of(query_part, key_part)
        prob_vals = jnp.exp(score_vals - norm_part[..., None])
        d_probs = jnp.einsum(
            "hqd,kd->hqk", grad_part, value_part, preferred_element_type=jnp.float32
        )
        d_scores = (prob_vals * (d_probs - jnp.sum(prob_vals * d_probs, -1, keepdims=True))).astype(
            jnp.bfloat16
        )
        query_term = (
            jnp.einsum("hqk,kd->hqd", d_scores, key_part, preferred_element_type=jnp.float32)
            * attn_mult
        )
        key_term = (
            jnp.einsum("hqk,hqd->kd", d_scores, query_part, preferred_element_type=jnp.float32)
            * attn_mult
        )
        value_term = jnp.einsum(
            "hqk,hqd->kd",
            prob_vals.astype(jnp.bfloat16),
            grad_part,
            preferred_element_type=jnp.float32,
        )
        return (query_term, jnp.concatenate([key_term, value_term], -1))

    d_query_groups, key_value_terms = lax.map(
        backward_group, (query_groups, key_groups, value_groups, log_norm, d_att_groups)
    )
    kv_terms = key_value_terms.transpose(1, 0, 2).reshape(seq_tokens, KV_HEADS, 2, HEAD_DIM)
    kv_owned = scatter(kv_terms.transpose(0, 2, 1, 3).reshape(seq_tokens, -1).astype(jnp.bfloat16))
    kv_owned = kv_owned.astype(jnp.float32)
    key_grad_rows = (
        rotate_back(
            kv_owned[:, :kv_width].reshape(row_count, KV_HEADS, HEAD_DIM), cosine, sine_table
        )
        .reshape(row_count, kv_width)
        .astype(jnp.bfloat16)
    )
    value_grad_rows = kv_owned[:, kv_width:].astype(jnp.bfloat16)
    query_grad_rows = (
        rotate_back(
            d_query_groups.transpose(2, 0, 1, 3).reshape(row_count, HEADS, HEAD_DIM),
            cosine,
            sine_table,
        )
        .reshape(row_count, HEADS * HEAD_DIM)
        .astype(jnp.bfloat16)
    )
    d_linear = jnp.concatenate([query_grad_rows, key_grad_rows, value_grad_rows], 1)
    grad_linear = dot_tn(normed_attn, d_linear)
    d_normed_attn = dot_nt(d_linear, weights_full)
    d_norm_in, grad_gain_attn = norm_back(d_normed_attn, input_float, scale_attn, gain_attn)
    d_input = d_middle + d_norm_in
    own_weights = scatter(jnp.concatenate([grad_linear, grad_output], 1).astype(jnp.bfloat16))
    own_small = scatter(
        jnp.concatenate([grad_gain_attn[:, None], grad_gain_ffn[:, None], grad_router], 1)
    )
    sum_in, sum_out, sum_weights, sum_small = lax.psum(
        (grad_in, grad_out, own_weights, own_small), "rep"
    )
    sum_weights = sum_weights.astype(jnp.float32)
    return (
        result_f.astype(jnp.bfloat16),
        loss,
        d_input,
        sum_small[:, 0],
        sum_weights[:, :query_width],
        sum_weights[:, query_width : query_width + kv_width],
        sum_weights[:, query_width + kv_width : query_width + 2 * kv_width],
        sum_weights[:, query_width + 2 * kv_width :],
        sum_small[:, 1],
        sum_small[:, 2:],
        sum_in.astype(jnp.float32),
        sum_out.astype(jnp.float32),
    )


def solution(mesh):
    in_specs = (
        P(("rep", "shard"), None),
        P(("rep", "shard")),
        P(("rep", "shard"), None),
        P(("rep", "shard"), None),
        P("shard"),
        P("shard", None),
        P("shard", None),
        P("shard", None),
        P("shard", None),
        P("shard"),
        P("shard", None),
        P("shard", None, None),
        P("shard", None, None),
    )
    out_specs = (
        P(("rep", "shard"), None),
        P(),
        P(("rep", "shard"), None),
        P("shard"),
        P("shard", None),
        P("shard", None),
        P("shard", None),
        P("shard", None),
        P("shard"),
        P("shard", None),
        P("shard", None, None),
        P("shard", None, None),
    )
    return jax.shard_map(body, mesh=mesh, in_specs=in_specs, out_specs=out_specs, check_vma=False)
```

time: 3650 us -> 906 us (0.25)
  waiting for transfers between devices: 3000 us -> 506 us
  matrix products: 230 us -> 84 us
  local copies, waits for them, and re-layouts: 114 us -> 19.7 us
  Pallas kernels: 0 us -> 72.6 us
  other arithmetic: 122 us -> 54.3 us
    reduce_scatter x7 -> x5, waiting for transfers between devices: 1850 us -> 156 us  [scatter(): return lax.psum_scatter(block, 'shard', scatter_dimension=0, tiled=True)]
    all_gather x8 -> x5, waiting for transfers between devices: 862 us -> 197 us  [gather(): return lax.all_gather(block, 'shard', axis=0, tiled=True)]
    psum x1, waiting for transfers between devices: 287 us -> 146 us  [body(): lax.psum((grad_in, grad_out, own_weights, own_small), 'rep')]
    dot_general x22 -> x9, matrix products: 148 us -> 18.8 us  [the longest x4 9.91 us: dot_nn(): return jnp.dot(left, right, preferred_element_type=jnp.float32)]
    pallas_call x0 -> x3, Pallas kernels: none -> 72.6 us  [the longest x1 28.9 us: experts_backward(): pl.pallas_call(experts_backward_kernel, grid=(experts,), in_specs=[pl.Blo...]
    concatenate x2 -> x4, other arithmetic: 67.4 us -> 6.1 us  [the longest x1 3.14 us: body(): jnp.concatenate([grad_linear, grad_output], 1).astype(jnp.bfloat16)]
  transfers between devices with their start and end apart: 16 -> 12, of which waited for: 12 -> 10; matrix products, arithmetic and copies ran while one was open for 7% -> 6% of each run, Pallas kernels for 0% -> 2%
where the time goes in v1:
time: 906 us; the launch traced here: 897 us
  waiting for transfers between devices  506 us (56%)
  blocking collectives  137 us (15%)
  matrix products  84 us (9%)
  Pallas kernels  72.6 us (8%)
  other arithmetic  54.3 us (6%)
  local copies, waits for them, and re-layouts  19.7 us (2%)
  between operations  18 us (2%)
    all_gather x5, waiting for transfers between devices, gather(): return lax.all_gather(block, 'shard', axis=0, tiled=True)  197 us
    reduce_scatter x5, waiting for transfers between devices, scatter(): return lax.psum_scatter(block, 'shard', scatter_dimension=0, tiled=True)  156 us
    psum x1, waiting for transfers between devices, body(): lax.psum((grad_in, grad_out, own_weights, own_small), 'rep')  146 us
    psum x1, blocking collectives, body(): valid_count = lax.psum(jnp.sum(valid_float), ('rep', 'shard'))  42.4 us
    psum x1, blocking collectives, body(): lax.psum(jnp.sum(valid_float[:, None] * deviation * deviation), ('rep', '...  41.3 us
    pallas_call x1, Pallas kernels, experts_backward(): pl.pallas_call(experts_backward_kernel, grid=(experts,), in_specs=[pl.Blo...  28.9 us
    all_gather x2, blocking collectives, gather(): return lax.all_gather(block, 'shard', axis=0, tiled=True)  28.4 us
    dot_general x16, matrix products, scores_of(): jnp.einsum('hqd,kd->hqk', query_part, key_part, preferred_element_type=jn...  26.1 us
  transfers between devices with their start and end apart: 12, of which 10 were waited for; matrix products, arithmetic and copies ran while one was open for 6% of the time, Pallas kernels for 2%

profile of v1, /device:TPU:0, one launch (start us, length us, event | category | flops | bytes accessed | tf_op | source)
XLA Modules:
  0.0 897.0 jit_solution(4189834444004658864)
XLA Ops:
  8.0 2.3 pad_maximum_fusion.1
  11.5 14.9 %all_gather.21 = bf16[1024,18]{0,1:T(8,128)(2,1)S(1)} all-gather(bf16[256,18]{0,1:T(8,128)(2,1)S(1)} %pad_maximum_fusion.8), channel_id=1, replica_groups=mesh['rep'=8,'shard'=4] {'shard'}, dimensions={0}, use_global_device_ids=true | all-gather | bytes 46080 | tf_op jit(solution)/shard_map/all_gather | solution.py:293
  27.7 30.8 %all-gather.8.cloned.1.call-done = bf16[1024,1024]{1,0:T(8,128)(2,1)} async-done(((bf16[256,1024]{1,0:T(8,128)(2,1)}), bf16[1024,1024]{1,0:T(8,128)(2,1)}) %all-gather.8.cloned.1.call-update) | async-done | bytes 2097168 | tf_op jit(solution)/shard_map/all_gather | solution.py:293
  58.4 2.2 fusion.44
  61.3 78.8 %all-gather.6.cloned.1.call-done = bf16[1024,2048]{1,0:T(8,128)(2,1)} async-done(((bf16[256,2048]{1,0:T(8,128)(2,1)}), bf16[1024,2048]{1,0:T(8,128)(2,1)}) %all-gather.6.cloned.1.call-update) | async-done | bytes 4194320 | tf_op jit(solution)/shard_map/all_gather | solution.py:293
  140.1 4.1 fusion.47
  144.4 1.9 copy-done.1
  146.4 1.7 copy-done.23
  151.3 25.1 %while.28 = (s32[]{:T(128)}, bf16[8,2,256,64]{2,3,1,0:T(8,128)(2,1)S(1)}, f32[8,2,256]{2,1,0:T(2,128)S(1)}, bf16[8,2,256,64]{2,3,1,0:T(8,128)(2,1)}, bf16[8,1024...) while((s32[]{:T(128)}, ...), condition=%wide.region_5.6_spmd.clone.clone, body=%wide.region_2.5_spmd.clone.sunk.clone | while | flops 140770816 | bytes 7822425 | solution.py:350
  151.6 1.5 fusion.133
  164.1 1.5 fusion.133
  176.4 9.8 %all-gather.10.cloned.1.call-done = bf16[1024,1024]{1,0:T(8,128)(2,1)} async-done(((bf16[256,1024]{1,0:T(8,128)(2,1)}), bf16[1024,1024]{1,0:T(8,128)(2,1)}) %all-gather.10.cloned.1.call-update) | async-done | bytes 2097168 | tf_op jit(solution)/shard_map/all_gather | solution.py:293
  186.2 2.4 multiply_reduce_fusion.3
  189.7 13.5 %all_gather.26 = s32[1024,8]{0,1:T(8,128)S(1)} all-gather(s32[256,8]{0,1:T(8,128)S(1)} %copy-done.18), channel_id=1, replica_groups=mesh['rep'=8,'shard'=4] {'shard'}, dimensions={0}, use_global_device_ids=true | all-gather | bytes 40960 | tf_op jit(solution)/shard_map/all_gather | solution.py:293
  203.5 31.1 %all-gather.12.cloned.1.call-done.x_ref = bf16[1024,1024]{1,0:T(8,128)(2,1)} async-done(((bf16[256,1024]{1,0:T(8,128)(2,1)}), bf16[1024,1024]{1,0:T(8,128)(2,1)}) %all-gather.12.cloned.1.call-update) | async-done | bytes 2097168 | tf_op jit(solution)/shard_map/all_gather | solution.py:293
  234.6 2.3 fusion.87
  238.7 24.7 %experts_forward.1 = (bf16[1024,1024]{1,0:T(8,128)(2,1)}, f32[4,1024,1024]{2,1,0:T(8,128)}, bf16[4,1024,512]{2,1,0:T(8,128)(2,1)}) custom-call(bf16[1024,1024]{1,0:T(8,128)(2,1)} %all-gather.12.cloned.1.call-done.x_ref, f32[1024,128]{1,0:T(8,128)} %pad.4.gate_ref, bf16[4,1024,1024]{2,1,0:T(8,128)(2,1)} %in_ref.3, bf16[4,512,1024]{2,1,0:T(8,128)(2,1)} %out_ref.3), custom_call_target="tpu_custom_call" | custom-call | flops 12884901888 | bytes 39845888 | tf_op jit(solution)/shard_map/experts_forward/pallas_call | solution.py:127
  264.7 42.4 %psum.43 = f32[]{:T(128)} all-reduce(f32[]{:T(128)} %convert_reduce_fusion), channel_id=1, replica_groups=mesh['rep'=8,'shard'=4] {'rep','shard'}, use_global_device_ids=true, to_apply=%region_14.15 | all-reduce | flops 1 | bytes 8 | tf_op jit(solution)/shard_map/psum | solution.py:300
  307.8 2.1 multiply_convert_fusion.2
  310.2 46.3 %all-gather.14.cloned.1.call-done.dmix_ref = bf16[1024,1024]{1,0:T(8,128)(2,1)} async-done(((bf16[256,1024]{1,0:T(8,128)(2,1)}), bf16[1024,1024]{1,0:T(8,128)(2,1)}) %all-gather.14.cloned.1.call-update) | async-done | bytes 2097168 | tf_op jit(solution)/shard_map/all_gather | solution.py:293
  356.5 28.9 %experts_backward.1 = (bf16[1024,1024]{1,0:T(8,128)(2,1)}, bf16[4,1024,1024]{2,1,0:T(8,128)(2,1)}, f32[1024,128]{1,0:T(8,128)}) custom-call(bf16[1024,1024]{1,0:T(8,128)(2,1)} %all-gather.14.cloned.1.call-done.dmix_ref, f32[1024,128]{1,0:T(8,128)} %pad.4.gate_ref, f32[4,1024,1024]{2,1,0:T(8,128)} %get-tuple-element.108.gate_up_ref, ...), custom_call_target="tpu_custom_call" | custom-call | flops 12884901888 | bytes 41943040 | tf_op jit(solution)/shard_map/experts_backward/pallas_call | solution.py:197
  385.4 1.8 copy.55
  387.2 3.3 all-to-all-start
  390.6 5.5 all-to-all-done
  396.5 31.9 %reduce-scatter.8.cloned.1.call-done = bf16[256,1024]{1,0:T(8,128)(2,1)} async-done(((bf16[1024,1024]{1,0:T(8,128)(2,1)}), bf16[256,1024]{1,0:T(8,128)(2,1)}) %reduce-scatter.8.cloned.1.call-update) | async-done | bytes 524304 | tf_op jit(solution)/shard_map/reduce_scatter | solution.py:296
  428.4 2.5 multiply_reduce_fusion.1
  433.7 55.6 %while.29 = (s32[]{:T(128)}, f32[8,2,256,64]{2,3,1,0:T(8,128)}, bf16[8,1024,128]{1,2,0:T(8,128)(2,1)}, bf16[8,2,256,64]{2,3,1,0:T(8,128)(2,1)}, bf16[8,1024,64]{...) while((s32[]{:T(128)}, f32[8,2,256,64]{2,3,1,0:T(8,128)}, ...), condition=%wide.region_20.21_spmd.clone.clone, body=%wide.region_18.20_spmd.clone.sunk.clone | while | flops 341212672 | bytes 17845356 | solution.py:431
  435.3 1.8 multiply_reduce_fusion.7
  442.2 1.8 multiply_reduce_fusion.7
  449.2 1.8 multiply_reduce_fusion.7
  456.1 1.8 multiply_reduce_fusion.7
  463.1 1.8 multiply_reduce_fusion.7
  470.0 1.8 multiply_reduce_fusion.7
  477.0 1.8 multiply_reduce_fusion.7
  483.9 1.8 multiply_reduce_fusion.7
  489.3 3.1 copy.59
  494.9 1.8 convolution_convert_fusion.1
  496.7 39.1 %reduce-scatter.10.cloned.1.call-done = bf16[256,1024]{0,1:T(8,128)(2,1)} async-done(((bf16[1024,1024]{0,1:T(8,128)(2,1)}), bf16[256,1024]{0,1:T(8,128)(2,1)}) %reduce-scatter.10.cloned.1.call-update) | async-done | bytes 524304 | tf_op jit(solution)/shard_map/reduce_scatter | solution.py:296
  538.6 3.1 pad_maximum_fusion
  543.1 3.9 fusion.65
  547.7 19.0 %experts_grads.1 = (bf16[4,1024,1024]{2,1,0:T(8,128)(2,1)}, bf16[4,512,1024]{2,1,0:T(8,128)(2,1)}) custom-call(bf16[1024,1024]{1,0:T(8,128)(2,1)} %all-gather.12.cloned.1.call-done.x_ref, bf16[1024,1024]{1,0:T(8,128)(2,1)} %all-gather.14.cloned.1.call-done.dmix_ref, bf16[4,1024,1024]{2,1,0:T(8,128)(2,1)} %get-tuple-element.114.dgate_up_ref, ...), custom_call_target="tpu_custom_call" | custom-call | flops 12884901888 | bytes 29360128 | tf_op jit(solution)/shard_map/experts_grads/pallas_call | solution.py:236
  566.8 85.3 %reduce-scatter.14.cloned.1.call-done = bf16[256,3072]{1,0:T(8,128)(2,1)} async-done(((bf16[1024,3072]{1,0:T(8,128)(2,1)}), bf16[256,3072]{1,0:T(8,128)(2,1)}) %reduce-scatter.14.cloned.1.call-update) | async-done | bytes 1572880 | tf_op jit(solution)/shard_map/reduce_scatter | solution.py:296
  652.7 41.3 %psum.42 = f32[]{:T(128)} all-reduce(f32[]{:T(128)} %get-tuple-element.166), channel_id=1, replica_groups=mesh['rep'=8,'shard'=4] {'rep','shard'}, use_global_device_ids=true, to_apply=%region_12.13 | all-reduce | flops 1 | bytes 8 | tf_op jit(solution)/shard_map/psum | solution.py:376
  696.0 25.4 %psum.44 = f32[256,18]{0,1:T(8,128)S(1)} all-reduce(f32[256,18]{0,1:T(8,128)} %reduce-scatter.12.cloned.1.call-done), channel_id=1, replica_groups=mesh['rep'=8,'shard'=4] {'rep'}, use_global_device_ids=true, to_apply=%region_26.27 | all-reduce | flops 4608 | bytes 36864 | tf_op jit(solution)/shard_map/psum | solution.py:463
  722.6 146.1 %all-reduce.4.cloned.1.call-done = (bf16[256,3072]{1,0:T(8,128)(2,1)}, bf16[4,1024,1024]{2,1,0:T(8,128)(2,1)}, bf16[4,512,1024]{2,1,0:T(8,128)(2,1)}) async-done(((bf16[256,3072]{1,0:T(8,128)(2,1)}, bf16[4,1024,1024]{2,1,0:T(8,128)(2,1)}, bf16[4,512,1024]{2,1,0:T(8,128)(2,1)}), (bf16[256,3072]{1,0:T(8,128)(2,1)}, bf16[4,1024,1024]{2,1,0:T(8,128)(2,1)}, ...) | async-done | bytes 14155792 | tf_op jit(solution)/shard_map/psum | solution.py:463
  868.7 2.9 fusion.83
  872.6 11.9 %convert_element_type.175 = f32[4,1024,1024]{2,1,0:T(8,128)} convert(bf16[4,1024,1024]{2,1,0:T(8,128)(2,1)} %get-tuple-element.204) | non-fusion elementwise | flops 4194304 | bytes 25165824 | tf_op jit(solution)/shard_map/convert_element_type | solution.py:478
  884.5 4.4 convert_element_type.176
  (233 shorter events, 88.5 us)
Async XLA Ops:
  7.2 3.9 copy-start.2
  7.2 51.3 %all-gather.8.cloned.1.call-start = ((), (), s32[]{:S(2)}) async-start(), calls=%async_computation.7 | async-start | bytes 2621440 | tf_op jit(solution)/shard_map/all_gather | solution.py:293
  7.9 3.5 copy-start.24
  7.9 3.5 copy-start.25
  7.9 3.5 copy-start.19
  8.0 132.2 %all-gather.6.cloned.1.call-start = ((), (), s32[]{:S(2)}) async-start(), calls=%async_computation.6 | async-start | bytes 5242880 | tf_op jit(solution)/shard_map/all_gather | solution.py:293
  10.3 175.9 %all-gather.10.cloned.1.call-start = ((), (), s32[]{:S(2)}) async-start(), calls=%async_computation.8 | async-start | bytes 2621440 | tf_op jit(solution)/shard_map/all_gather | solution.py:293
  11.0 223.5 %all-gather.12.cloned.1.call-start = ((), (), s32[]{:S(2)}) async-start(), calls=%async_computation.9 | async-start | bytes 2621440 | tf_op jit(solution)/shard_map/all_gather | solution.py:293
  58.4 81.7 %copy-start.10 = (bf16[1024,1024]{1,0:T(8,128)(2,1)S(1)}, bf16[1024,1024]{1,0:T(8,128)(2,1)}, u32[]{:S(2)}) copy-start(bf16[1024,1024]{1,0:T(8,128)(2,1)} %all-gather.8.cloned.1.call-done) | copy-start | bytes 6291460
  144.2 2.1 copy-start.1
  144.2 3.9 copy-start.23
  144.2 3.9 copy-start.20
  149.1 1.8 slice-start
  176.4 9.8 %copy-start.9 = (bf16[8,1024,64]{1,2,0:T(8,128)(2,1)}, bf16[8,1024,64]{1,2,0:T(8,128)(2,1)S(1)}, u32[]{:S(2)}) copy-start(bf16[8,1024,64]{1,2,0:T(8,128)(2,1)S(1)} %get-tuple-element.493) | copy-start | bytes 3145732
  176.4 12.2 %copy-start.6 = (bf16[8,2,256,64]{2,3,1,0:T(8,128)(2,1)}, bf16[8,2,256,64]{2,3,1,0:T(8,128)(2,1)S(1)}, u32[]{:S(2)}) copy-start(bf16[8,2,256,64]{2,3,1,0:T(8,128)(2,1)S(1)} %get-tuple-element.106) | copy-start | bytes 1572868
  188.7 1.1 copy-start.18
  189.7 118.1 %reduce-scatter.6.cloned.1.call-start = ((), (), s32[]{:S(2)}) async-start(), calls=%async_computation.10 | async-start | bytes 2621440 | tf_op jit(solution)/shard_map/reduce_scatter | solution.py:296
  263.4 0.7 copy-start.22
  263.4 44.4 %copy-start.11 = (bf16[256,1024]{1,0:T(8,128)(2,1)S(1)}, bf16[256,1024]{1,0:T(8,128)(2,1)}, u32[]{:S(2)}) copy-start(bf16[256,1024]{1,0:T(8,128)(2,1)} %param.19) | copy-start | bytes 1572868
  263.5 93.0 %all-gather.14.cloned.1.call-start = ((), (), s32[]{:S(2)}) async-start(), calls=%async_computation.11 | async-start | bytes 2621440 | tf_op jit(solution)/shard_map/all_gather | solution.py:293
  310.0 118.4 %reduce-scatter.8.cloned.1.call-start = ((), (), s32[]{:S(2)}) async-start(), calls=%async_computation.12 | async-start | bytes 2621440 | tf_op jit(solution)/shard_map/reduce_scatter | solution.py:296
  387.2 8.9 all-to-all-start
  390.5 145.3 %reduce-scatter.10.cloned.1.call-start = ((), (), s32[]{:S(2)}) async-start(), calls=%async_computation.13 | async-start | bytes 2621440 | tf_op jit(solution)/shard_map/reduce_scatter | solution.py:296
  428.4 2.6 copy-start.12
  428.4 2.6 copy-start.13
  431.0 1.7 copy-start
  492.5 159.6 %reduce-scatter.14.cloned.1.call-start = ((), (), s32[]{:S(2)}) async-start(), calls=%async_computation.15 | async-start | bytes 7864320 | tf_op jit(solution)/shard_map/reduce_scatter | solution.py:296
  496.7 40.4 %copy-start.21 = (f32[256]{0:T(256)S(1)}, f32[256]{0:T(256)}, u32[]{:S(2)}) copy-start(f32[256]{0:T(256)} %add_rsqrt_fusion.2) | copy-start | bytes 3076
  535.8 1.3 copy-start.3
  535.8 1.4 copy-start.14
  536.9 1.7 copy-start.17
  537.1 1.5 copy-start.16
  541.8 1.0 copy-start.7
  541.8 1.3 copy-start.4
  541.8 1.4 copy-start.15
  541.8 154.2 %reduce-scatter.12.cloned.1.call-start = ((), (), s32[]{:S(2)}) async-start(), calls=%async_computation.14 | async-start | bytes 122880 | tf_op jit(solution)/shard_map/reduce_scatter | solution.py:296
  547.7 321.0 %all-reduce.4.cloned.1.call-start = ((), (), s32[]{:S(2)}) async-start(), calls=%async_computation.16 | async-start | bytes 28311552 | tf_op jit(solution)/shard_map/psum | solution.py:463
  868.7 2.9 copy-start.5
  872.6 11.9 %copy-start.8 = (bf16[4,512,1024]{2,1,0:T(8,128)(2,1)S(1)}, bf16[4,512,1024]{2,1,0:T(8,128)(2,1)}, u32[]{:S(2)}) copy-start(bf16[4,512,1024]{2,1,0:T(8,128)(2,1)} %get-tuple-element.205) | copy-start | bytes 12582916
Sparse Core Ops, SparseCore 0:
  9.6 48.8 all-gather.7
  60.6 79.4 all-gather.5
  141.7 44.4 all-gather.9
  189.8 44.7 all-gather.11
  263.6 43.9 reduce-scatter.5
  310.1 46.3 all-gather.13
  385.5 42.8 reduce-scatter.7
  492.6 43.1 reduce-scatter.9
  541.9 110.0 reduce-scatter.13
  654.8 19.6 reduce-scatter.11
  679.1 189.5 all-reduce.3

commit v2 on v1

v2 whole, which is shorter than its diff:
```python
import jax
import jax.numpy as jnp
from jax import lax
from jax.experimental import pallas as pl
from jax.experimental.pallas import tpu as pltpu
from jax.sharding import PartitionSpec as P

HEADS = 16
KV_HEADS = 8
HEAD_DIM = 64
TOP = 8
BLOCK = 256


norm_eps = 1e-06
resid_mult = 0.22
attn_mult = 0.015625
rope_base = 10000.0
very_low = -1e30


def rope_tables(positions):
    half_dim = HEAD_DIM // 2
    frequency = rope_base ** (-jnp.arange(half_dim, dtype=jnp.float32) / half_dim)
    angles = positions.astype(jnp.float32)[:, None] * frequency[None, :]
    cosine, sine = jnp.cos(angles), jnp.sin(angles)
    return (
        jnp.concatenate([cosine] * 4, 1),
        jnp.concatenate([-sine, sine, -sine, sine], 1),
    )


def rms_scale(values):
    return lax.rsqrt(jnp.mean(values * values, axis=-1, keepdims=True) + norm_eps)


def norm_back(d_normed, values, scale_vals, gain_vec):
    scaled_grad = d_normed * gain_vec
    d_gain = jnp.sum(d_normed * values * scale_vals, 0)
    d_values = scale_vals * (
        scaled_grad
        - values * scale_vals * scale_vals * jnp.mean(scaled_grad * values, axis=-1, keepdims=True)
    )
    return (d_values, d_gain)


LANES = 128
ROW_STEP = 256


def row_chunks(count):
    step = min(count, ROW_STEP)
    return [pl.ds(at, step) for at in range(0, count, step)]


def pick_lane(values, lane):
    lanes = lax.broadcasted_iota(jnp.int32, values.shape, 1)
    return jnp.sum(jnp.where(lanes == lane, values, 0.0), axis=1, keepdims=True)


def dot_nn(left, right):
    return jnp.dot(left, right, preferred_element_type=jnp.float32)


def dot_nt(left, right):
    return lax.dot_general(left, right, (((1,), (1,)), ((), ())), preferred_element_type=jnp.float32)


def dot_tn(left, right):
    return lax.dot_general(left, right, (((0,), (0,)), ((), ())), preferred_element_type=jnp.float32)


def experts_forward_kernel(x_ref, gate_ref, in_ref, out_ref, mix_ref, gate_up_ref, hidden_ref, total):
    expert = pl.program_id(0)
    units = out_ref.shape[1]
    for rows in row_chunks(x_ref.shape[0]):
        gate_up = dot_nn(x_ref[rows, :], in_ref[0])
        gate_up_ref[0, rows, :] = gate_up
        gate_vals = gate_up[:, :units]
        silu_gate = gate_vals / (1.0 + jnp.exp(-gate_vals))
        weight = pick_lane(gate_ref[rows, :], expert)
        hidden = (silu_gate * gate_up[:, units:] * weight).astype(jnp.bfloat16)
        hidden_ref[0, rows, :] = hidden
        part = dot_nn(hidden, out_ref[0])

        @pl.when(expert == 0)
        def _():
            total[rows, :] = part

        @pl.when(expert > 0)
        def _():
            total[rows, :] += part

    @pl.when(expert == pl.num_programs(0) - 1)
    def _():
        mix_ref[...] = total[...].astype(mix_ref.dtype)


def experts_forward(tokens, gates_own, w_in, w_out):
    count, width = tokens.shape
    experts, units = w_out.shape[0], w_out.shape[1]
    return pl.pallas_call(
        experts_forward_kernel,
        grid=(experts,),
        in_specs=[
            pl.BlockSpec((count, width), lambda e: (0, 0)),
            pl.BlockSpec((count, LANES), lambda e: (0, 0)),
            pl.BlockSpec((1, width, 2 * units), lambda e: (e, 0, 0)),
            pl.BlockSpec((1, units, width), lambda e: (e, 0, 0)),
        ],
        out_specs=[
            pl.BlockSpec((count, width), lambda e: (0, 0)),
            pl.BlockSpec((1, count, 2 * units), lambda e: (e, 0, 0)),
            pl.BlockSpec((1, count, units), lambda e: (e, 0, 0)),
        ],
        out_shape=[
            jax.ShapeDtypeStruct((count, width), jnp.bfloat16),
            jax.ShapeDtypeStruct((experts, count, 2 * units), jnp.float32),
            jax.ShapeDtypeStruct((experts, count, units), jnp.bfloat16),
        ],
        scratch_shapes=[pltpu.VMEM((count, width), jnp.float32)],
        compiler_params=pltpu.CompilerParams(vmem_limit_bytes=VMEM_BYTES),
        cost_estimate=pl.CostEstimate(
            flops=6 * count * width * units * experts,
            bytes_accessed=experts * units * (6 * width + 10 * count) + 6 * count * width,
            transcendentals=experts * count * units,
        ),
        name="experts_forward",
    )(tokens, gates_own, w_in, w_out)


def experts_backward_kernel(
    dmix_ref, gate_ref, gate_up_ref, in_ref, out_ref, drows_ref, dgate_up_ref, dgates_ref, total
):
    expert = pl.program_id(0)
    units = out_ref.shape[1]
    lanes = lax.broadcasted_iota(jnp.int32, (1, LANES), 1)
    for rows in row_chunks(dmix_ref.shape[0]):
        pulled = dot_nt(dmix_ref[rows, :], out_ref[0])
        gate_vals = gate_up_ref[0, rows, :units]
        up_vals = gate_up_ref[0, rows, units:]
        sigmoid = 1.0 / (1.0 + jnp.exp(-gate_vals))
        silu_gate = gate_vals * sigmoid
        weight = pick_lane(gate_ref[rows, :], expert)
        own = jnp.sum(pulled * silu_gate * up_vals, axis=1, keepdims=True)
        own = jnp.where(lanes == expert, own, 0.0)
        d_hidden = pulled * weight
        d_gate = d_hidden * up_vals * sigmoid * (1.0 + gate_vals * (1.0 - sigmoid))
        d_up = d_hidden * silu_gate
        dgate_up_ref[0, rows, :units] = d_gate.astype(jnp.bfloat16)
        dgate_up_ref[0, rows, units:] = d_up.astype(jnp.bfloat16)
        part = dot_nt(dgate_up_ref[0, rows, :], in_ref[0])

        @pl.when(expert == 0)
        def _():
            total[rows, :] = part
            dgates_ref[rows, :] = own

        @pl.when(expert > 0)
        def _():
            total[rows, :] += part
            dgates_ref[rows, :] += own

    @pl.when(expert == pl.num_programs(0) - 1)
    def _():
        drows_ref[...] = total[...].astype(drows_ref.dtype)


def experts_backward(d_mix, gates_own, gate_up, w_in, w_out):
    count, width = d_mix.shape
    experts, units = w_out.shape[0], w_out.shape[1]
    return pl.pallas_call(
        experts_backward_kernel,
        grid=(experts,),
        in_specs=[
            pl.BlockSpec((count, width), lambda e: (0, 0)),
            pl.BlockSpec((count, LANES), lambda e: (0, 0)),
            pl.BlockSpec((1, count, 2 * units), lambda e: (e, 0, 0)),
            pl.BlockSpec((1, width, 2 * units), lambda e: (e, 0, 0)),
            pl.BlockSpec((1, units, width), lambda e: (e, 0, 0)),
        ],
        out_specs=[
            pl.BlockSpec((count, width), lambda e: (0, 0)),
            pl.BlockSpec((1, count, 2 * units), lambda e: (e, 0, 0)),
            pl.BlockSpec((count, LANES), lambda e: (0, 0)),
        ],
        out_shape=[
            jax.ShapeDtypeStruct((count, width), jnp.bfloat16),
            jax.ShapeDtypeStruct((experts, count, 2 * units), jnp.bfloat16),
            jax.ShapeDtypeStruct((count, LANES), jnp.float32),
        ],
        scratch_shapes=[pltpu.VMEM((count, width), jnp.float32)],
        compiler_params=pltpu.CompilerParams(vmem_limit_bytes=VMEM_BYTES),
        cost_estimate=pl.CostEstimate(
            flops=6 * count * width * units * experts,
            bytes_accessed=experts * units * (6 * width + 12 * count) + 4 * count * width,
            transcendentals=experts * count * units,
        ),
        name="experts_backward",
    )(d_mix, gates_own, gate_up, w_in, w_out)


def experts_grads_kernel(order_ref, x_ref, dmix_ref, dgate_up_ref, hidden_ref, grads_ref):
    width = x_ref.shape[1]
    grads_ref[0, :width, :] = dot_tn(x_ref[...], dgate_up_ref[0]).astype(grads_ref.dtype)
    grads_ref[0, width:, :] = dot_tn(hidden_ref[0], dmix_ref[...]).astype(grads_ref.dtype)


def experts_grads(order, tokens, d_mix, dgate_up, hidden):
    count, width = tokens.shape
    units = hidden.shape[2]
    experts = order.shape[0]
    return pl.pallas_call(
        experts_grads_kernel,
        grid_spec=pltpu.PrefetchScalarGridSpec(
            num_scalar_prefetch=1,
            grid=(experts,),
            in_specs=[
                pl.BlockSpec((count, width), lambda e, order: (0, 0)),
                pl.BlockSpec((count, width), lambda e, order: (0, 0)),
                pl.BlockSpec((1, count, 2 * units), lambda e, order: (order[e], 0, 0)),
                pl.BlockSpec((1, count, units), lambda e, order: (order[e], 0, 0)),
            ],
            out_specs=pl.BlockSpec((1, width + units, 2 * units), lambda e, order: (e, 0, 0)),
        ),
        out_shape=jax.ShapeDtypeStruct((experts, width + units, 2 * units), jnp.bfloat16),
        compiler_params=pltpu.CompilerParams(vmem_limit_bytes=VMEM_BYTES),
        cost_estimate=pl.CostEstimate(
            flops=6 * count * width * units * experts,
            bytes_accessed=experts * units * (6 * width + 6 * count) + 4 * count * width,
            transcendentals=0,
        ),
        name="experts_grads",
    )(order, tokens, d_mix, dgate_up, hidden)


def widen_kernel(base_ref, piece_ref, *refs):
    gin_ref, gout_ref = refs[-2:]
    width = gin_ref.shape[1]
    gin_ref[...] = piece_ref[:, :width, :].astype(jnp.float32)
    gout_ref[...] = piece_ref[:, width:, :].astype(jnp.float32)


def widen(base, piece, width, total, held):
    count, rows, columns = piece.shape
    shapes = [
        jax.ShapeDtypeStruct((total, width, columns), jnp.float32),
        jax.ShapeDtypeStruct((total, rows - width, columns), jnp.float32),
    ]
    return pl.pallas_call(
        widen_kernel,
        grid_spec=pltpu.PrefetchScalarGridSpec(
            num_scalar_prefetch=1,
            grid=(count,),
            in_specs=[pl.BlockSpec((1, rows, columns), lambda e, base: (e, 0, 0))]
            + [pl.BlockSpec(memory_space=pl.ANY)] * len(held),
            out_specs=[
                pl.BlockSpec((1, width, columns), lambda e, base: (base[0] + e, 0, 0)),
                pl.BlockSpec((1, rows - width, columns), lambda e, base: (base[0] + e, 0, 0)),
            ],
        ),
        out_shape=shapes,
        input_output_aliases={2 + at: at for at in range(len(held))},
        compiler_params=pltpu.CompilerParams(vmem_limit_bytes=VMEM_BYTES),
        cost_estimate=pl.CostEstimate(flops=0, bytes_accessed=6 * piece.size, transcendentals=0),
        name="widen",
    )(base, piece, *held)


def attention_grads_kernel(
    normed_ref, dquery_ref, all_ref, dkv_ref, attended_ref, dbranch_ref, small_ref, first_ref, second_ref
):
    query_width = dquery_ref.shape[1]
    half = dbranch_ref.shape[1] // 2
    kv_width = dkv_ref.shape[1]
    low = jnp.bfloat16
    second_ref[:, :kv_width] = dot_tn(all_ref[...], dkv_ref[...]).astype(low)
    first_ref[:, :query_width] = dot_tn(normed_ref[...], dquery_ref[...]).astype(low)
    grad_output = dot_tn(attended_ref[...], dbranch_ref[...]).astype(low)
    first_ref[:, query_width : query_width + half] = grad_output[:, :half]
    second_ref[:, kv_width:] = grad_output[:, half:]
    first_ref[:, query_width + half :] = small_ref[...].astype(low)


def attention_grads(normed, d_query, normed_all, d_kv, attended, d_branch, small):
    width = normed.shape[1]
    half = d_branch.shape[1] // 2
    return pl.pallas_call(
        attention_grads_kernel,
        in_specs=[whole_spec()] * 7,
        out_specs=[whole_spec()] * 2,
        out_shape=[
            jax.ShapeDtypeStruct((width, d_query.shape[1] + half + LANES), jnp.bfloat16),
            jax.ShapeDtypeStruct((width, d_kv.shape[1] + half), jnp.bfloat16),
        ],
        compiler_params=pltpu.CompilerParams(vmem_limit_bytes=VMEM_BYTES),
        cost_estimate=pl.CostEstimate(
            flops=2 * width * width * (normed_all.shape[0] + 2 * normed.shape[0]),
            bytes_accessed=14 * width * width,
            transcendentals=0,
        ),
        name="attention_grads",
    )(normed, d_query, normed_all, d_kv, attended, d_branch, small)


VMEM_BYTES = 60 * 1024 * 1024


def swap_halves(values):
    lanes = lax.broadcasted_iota(jnp.int32, values.shape, 1)
    ahead = pltpu.roll(values, LANES - HEAD_DIM // 2, 1)
    behind = pltpu.roll(values, HEAD_DIM // 2, 1)
    return jnp.where(lanes % HEAD_DIM < HEAD_DIM // 2, ahead, behind)


def stack_heads(block, parity):
    values = block.astype(jnp.float32)
    lanes = lax.broadcasted_iota(jnp.int32, values.shape, 1)
    low = jnp.where(lanes < HEAD_DIM, values, 0.0)
    high = values - low
    if parity == 0:
        high = pltpu.roll(high, HEAD_DIM, 1)
    else:
        low = pltpu.roll(low, HEAD_DIM, 1)
    return jnp.concatenate([low, high], 0).astype(jnp.bfloat16)


def unstack_heads(stacked, parity):
    rows = stacked.shape[0] // 2
    low, high = stacked[:rows], stacked[rows:]
    if parity == 0:
        high = pltpu.roll(high, HEAD_DIM, 1)
    else:
        low = pltpu.roll(low, HEAD_DIM, 1)
    lanes = lax.broadcasted_iota(jnp.int32, low.shape, 1)
    return jnp.where(lanes < HEAD_DIM, low, high)


def lane_block(at):
    return pl.ds(pl.multiple_of(at * LANES, LANES), LANES)


def attention_forward_kernel(
    bias_ref, all_ref, own_ref, gain_ref, wq_ref, wkv_ref, cos_ref, sin_ref, cos_own_ref, sin_own_ref,
    normed_ref, query_ref, key_ref, value_ref, attended_ref, norm_ref, scores
):
    tokens, width = all_ref.shape
    kv_width = key_ref.shape[1]
    key_rows = tokens // bias_ref.shape[0]

    def normed_rows(block):
        values = block.astype(jnp.float32)
        scale = lax.rsqrt(jnp.mean(values * values, axis=-1, keepdims=True) + norm_eps)
        return (values * scale * gain_ref[...]).astype(jnp.bfloat16)

    def project(at, carry):
        rows = pl.ds(pl.multiple_of(at * ROW_STEP, ROW_STEP), ROW_STEP)
        normed = normed_rows(all_ref[rows, :])
        normed_ref[rows, :] = normed
        linear = dot_nn(normed, wkv_ref[...])
        for col in range(0, kv_width, LANES):
            part = linear[:, col : col + LANES]
            turned = part * cos_ref[rows, :] + swap_halves(part) * sin_ref[rows, :]
            key_ref[rows, col : col + LANES] = turned.astype(jnp.bfloat16)
        value_ref[rows, :] = linear[:, kv_width:].astype(jnp.bfloat16)
        return carry

    lax.fori_loop(0, tokens // ROW_STEP, project, 0)
    linear = dot_nn(normed_rows(own_ref[...]), wq_ref[...])
    for col in range(0, wq_ref.shape[1], LANES):
        part = linear[:, col : col + LANES]
        turned = part * cos_own_ref[...] + swap_halves(part) * sin_own_ref[...]
        query_ref[:, col : col + LANES] = (turned.astype(jnp.bfloat16).astype(jnp.float32) * attn_mult).astype(jnp.bfloat16)

    def attend(pair, carry):
        lanes = lane_block(pair)
        turned_values = value_ref[:, lanes].astype(jnp.float32).T.astype(jnp.bfloat16)
        for parity in range(2):
            group = 2 * pair + parity
            stacked = stack_heads(query_ref[:, lane_block(group)], parity)
            top = None
            for at in range(bias_ref.shape[0]):
                rows = pl.ds(at * key_rows, key_rows)
                part = dot_nt(key_ref[rows, lanes], stacked) + bias_ref[at]
                scores[rows, :] = part
                high = jnp.max(part, axis=0, keepdims=True)
                top = high if top is None else jnp.maximum(top, high)
            total, gathered = None, None
            for at in range(bias_ref.shape[0]):
                rows = pl.ds(at * key_rows, key_rows)
                raised = jnp.exp(scores[rows, :] - top)
                part = jnp.sum(raised, axis=0, keepdims=True)
                mixed = dot_nn(
                    turned_values[:, at * key_rows : (at + 1) * key_rows], raised.astype(jnp.bfloat16)
                )
                total = part if total is None else total + part
                gathered = mixed if gathered is None else gathered + mixed
            gathered = (gathered / total).T
            attended_ref[:, lane_block(group)] = unstack_heads(gathered, parity).astype(jnp.bfloat16)
            norm_ref[pl.ds(group, 1), :] = top + jnp.log(total)
        return carry

    lax.fori_loop(0, kv_width // LANES, attend, 0)


def whole_spec():
    return pl.BlockSpec(memory_space=pltpu.VMEM)


def attention_forward(bias, input_all, hidden_in, gain, w_query, w_kv, tables, tables_own):
    tokens, width = input_all.shape
    rows = hidden_in.shape[0]
    kv_width = w_kv.shape[1] // 2
    return pl.pallas_call(
        attention_forward_kernel,
        in_specs=[pl.BlockSpec(memory_space=pltpu.SMEM)] + [whole_spec()] * 9,
        out_specs=[whole_spec()] * 6,
        out_shape=[
            jax.ShapeDtypeStruct((tokens, width), jnp.bfloat16),
            jax.ShapeDtypeStruct((rows, w_query.shape[1]), jnp.bfloat16),
            jax.ShapeDtypeStruct((tokens, kv_width), jnp.bfloat16),
            jax.ShapeDtypeStruct((tokens, kv_width), jnp.bfloat16),
            jax.ShapeDtypeStruct((rows, w_query.shape[1]), jnp.bfloat16),
            jax.ShapeDtypeStruct((KV_HEADS, 2 * rows), jnp.float32),
        ],
        scratch_shapes=[pltpu.VMEM((tokens, 2 * rows), jnp.float32)],
        compiler_params=pltpu.CompilerParams(vmem_limit_bytes=VMEM_BYTES),
        cost_estimate=pl.CostEstimate(
            flops=2 * (tokens * width * 2 * kv_width + rows * width * width + 4 * rows * tokens * width),
            bytes_accessed=16 * tokens * width,
            transcendentals=rows * tokens * HEADS,
        ),
        name="attention_forward",
    )(bias, input_all, hidden_in, gain, w_query, w_kv, *tables, *tables_own)


def attention_backward_kernel(
    bias_ref, query_ref, key_ref, value_ref, norm_ref, grad_ref, cos_ref, sin_ref, cos_own_ref, sin_own_ref,
    dquery_ref, dkv_ref, probs, dprobs, dkeys, dvalues
):
    tokens, kv_width = key_ref.shape
    key_rows = tokens // bias_ref.shape[0]

    def pull(pair, carry):
        lanes = lane_block(pair)
        turned_keys = key_ref[:, lanes].astype(jnp.float32).T.astype(jnp.bfloat16)
        for parity in range(2):
            group = 2 * pair + parity
            stacked = stack_heads(query_ref[:, lane_block(group)], parity)
            stacked_grad = stack_heads(grad_ref[:, lane_block(group)], parity)
            log_norm = norm_ref[pl.ds(group, 1), :]
            total = None
            for at in range(bias_ref.shape[0]):
                rows = pl.ds(at * key_rows, key_rows)
                part = dot_nt(key_ref[rows, lanes], stacked) + bias_ref[at]
                prob = jnp.exp(part - log_norm)
                d_prob = dot_nt(value_ref[rows, lanes], stacked_grad)
                probs[rows, :] = prob
                dprobs[rows, :] = d_prob
                d_value = dot_nn(prob.astype(jnp.bfloat16), stacked_grad)
                dvalues[rows, :] = d_value if parity == 0 else dvalues[rows, :] + d_value
                weighted = jnp.sum(prob * d_prob, axis=0, keepdims=True)
                total = weighted if total is None else total + weighted
            d_query = None
            for at in range(bias_ref.shape[0]):
                rows = pl.ds(at * key_rows, key_rows)
                d_score = (probs[rows, :] * (dprobs[rows, :] - total)).astype(jnp.bfloat16)
                d_key = dot_nn(d_score, stacked)
                dkeys[rows, :] = d_key if parity == 0 else dkeys[rows, :] + d_key
                part = dot_nn(turned_keys[:, at * key_rows : (at + 1) * key_rows], d_score)
                d_query = part if d_query is None else d_query + part
            part = unstack_heads(d_query.T, parity) * attn_mult
            turned = part * cos_own_ref[...] - swap_halves(part) * sin_own_ref[...]
            dquery_ref[:, lane_block(group)] = turned.astype(jnp.bfloat16)
        part = dkeys[...]
        turned = part * cos_ref[...] - swap_halves(part) * sin_ref[...]
        dkv_ref[:, lanes] = turned.astype(jnp.bfloat16)
        dkv_ref[:, lane_block(pair + kv_width // LANES)] = dvalues[...].astype(jnp.bfloat16)
        return carry

    lax.fori_loop(0, kv_width // LANES, pull, 0)


def attention_backward(bias, query, key, value, log_norm, grad, tables, tables_own):
    tokens, kv_width = key.shape
    rows, width = query.shape
    return pl.pallas_call(
        attention_backward_kernel,
        in_specs=[pl.BlockSpec(memory_space=pltpu.SMEM)] + [whole_spec()] * 9,
        out_specs=[whole_spec()] * 2,
        out_shape=[
            jax.ShapeDtypeStruct((rows, width), jnp.bfloat16),
            jax.ShapeDtypeStruct((tokens, 2 * kv_width), jnp.bfloat16),
        ],
        scratch_shapes=[
            pltpu.VMEM((tokens, 2 * rows), jnp.float32),
            pltpu.VMEM((tokens, 2 * rows), jnp.float32),
            pltpu.VMEM((tokens, LANES), jnp.float32),
            pltpu.VMEM((tokens, LANES), jnp.float32),
        ],
        compiler_params=pltpu.CompilerParams(vmem_limit_bytes=VMEM_BYTES),
        cost_estimate=pl.CostEstimate(
            flops=20 * rows * tokens * width,
            bytes_accessed=8 * tokens * width,
            transcendentals=rows * tokens * HEADS,
        ),
        name="attention_backward",
    )(bias, query, key, value, log_norm, grad, *tables, *tables_own)


def exchange(block, bit):
    count = lax.axis_size("rep")
    return lax.ppermute(block, "rep", [(at, at ^ bit) for at in range(count)])


def side_of(bit):
    return (lax.axis_index("rep") // bit) % 2


def add_pair(left, right):
    return (left.astype(jnp.float32) + right.astype(jnp.float32)).astype(jnp.bfloat16)


def after(value, *others):
    return lax.optimization_barrier((value, *others))[0]


def piece_at(parts, start, size, axis):
    pieces = [lax.dynamic_slice_in_dim(part, start, size, axis) for part in parts]
    if len(pieces) == 1:
        return pieces[0]
    return add_pair(*pieces)


def halve(parts, bit, axis, offset=0, length=None):
    length = parts[0].shape[axis] if length is None else length
    half = length // 2
    side = side_of(bit)
    sent = piece_at(parts, offset + (1 - side) * half, half, axis)
    kept = piece_at(parts, offset + side * half, half, axis)
    return sent, [kept, exchange(sent, bit)]


def double(block, bit, axis):
    size = block.shape[axis]
    side = side_of(bit)
    held = lax.concatenate([block, block], axis)
    return lax.dynamic_update_slice_in_dim(held, exchange(block, bit), (1 - side) * size, axis)


def rep_bits():
    count = lax.axis_size("rep")
    return [1 << at for at in range(count.bit_length() - 1)]


def body(
    hidden_in,
    valid_mask,
    teacher,
    routes,
    attn_norm,
    w_query,
    w_key,
    w_value,
    w_output,
    ffn_norm,
    router,
    w_in,
    w_out,
):
    row_count, model_width = hidden_in.shape
    shard_count = lax.axis_size("shard")
    seq_tokens = row_count * shard_count
    all_tokens = seq_tokens * lax.axis_size("rep")
    shard_at = lax.axis_index("shard")
    tables = rope_tables(jnp.arange(seq_tokens, dtype=jnp.int32))
    tables_own = tuple(
        lax.dynamic_slice_in_dim(table, shard_at * row_count, row_count, 0) for table in tables
    )
    key_blocks = jnp.arange(seq_tokens // BLOCK, dtype=jnp.int32)
    bias = jnp.where(key_blocks <= shard_at * row_count // BLOCK, 0.0, very_low)
    bits = rep_bits()
    near, far = bits[0], bits[1:]

    def gather(block):
        return lax.all_gather(block, "shard", axis=0, tiled=True)

    def scatter(block):
        return lax.psum_scatter(block, "shard", scatter_dimension=0, tiled=True)

    def gather_pair(left, right):
        width = left.shape[1]
        flat = gather(jnp.concatenate([left.reshape(1, -1), right.reshape(1, -1)], 1))
        split = left.size
        return flat[:, :split].reshape(-1, width), flat[:, split:].reshape(-1, right.shape[1])

    kv_width = w_key.shape[1]
    query_width = w_query.shape[1]
    half_width = w_output.shape[1] // 2
    own_rows = w_query.shape[0]
    piece_rows = own_rows // lax.axis_size("rep")

    def piece_of(block, order):
        index = 0
        for at, bit in enumerate(order):
            index = index + side_of(bit) * (1 << at)
        return lax.dynamic_slice_in_dim(block, index * piece_rows, piece_rows, 0)

    order_first, order_second = far + [near], far[::-1] + [near]
    w_kv = jnp.concatenate([w_key, w_value], 1)
    input_all = gather(hidden_in)
    pieces = lax.all_gather(
        jnp.concatenate([piece_of(w_query, order_first), piece_of(w_kv, order_second)], 1),
        "shard",
        axis=0,
    )
    query_full = pieces[..., :query_width]
    kv_full = pieces[..., query_width:]
    for bit_first, bit_second in zip(order_first, order_second):
        query_full = double(query_full, bit_first, 1)
        kv_full = double(kv_full, bit_second, 1)
    query_full = query_full.reshape(own_rows * shard_count, query_width)
    kv_full = kv_full.reshape(own_rows * shard_count, 2 * kv_width)
    near_rows = own_rows // 2
    output_half = lax.dynamic_slice_in_dim(w_output, side_of(near) * near_rows, near_rows, 0)
    output_half = lax.all_gather(after(output_half, input_all), "shard", axis=0)
    expert_count = router.shape[1]
    small_parts = [attn_norm[:, None], ffn_norm[:, None], router]
    small_full, routes_all = gather_pair(
        jnp.concatenate(small_parts, 1), routes.astype(jnp.bfloat16)
    )
    gain_attn, gain_ffn = small_full[:, 0], small_full[:, 1]
    router_full = small_full[:, 2:]
    gain_attn = gain_attn.astype(jnp.float32)
    valid_float = valid_mask.astype(jnp.float32)
    input_float = hidden_in.astype(jnp.float32)
    scale_attn = rms_scale(input_float)
    all_float = input_all.astype(jnp.float32)
    normed_all, query_rows, keys_all, values_all, attended, log_norm = attention_forward(
        bias, input_all, hidden_in, gain_attn[None], query_full, kv_full, tables, tables_own
    )
    normed_attn = lax.dynamic_slice_in_dim(normed_all, shard_at * row_count, row_count, 0)
    output_half, attended = lax.optimization_barrier((output_half, attended))
    output_full = double(output_half, near, 1).reshape(own_rows * shard_count, -1)
    branch = dot_nn(attended, output_full)
    middle = input_float + resid_mult * branch
    scale_ffn = rms_scale(middle)
    normed_ffn = (middle * scale_ffn * gain_ffn).astype(jnp.bfloat16)
    own_experts = w_in.shape[0]
    expert_ids = jnp.arange(expert_count, dtype=jnp.bfloat16)
    valid_count = lax.psum(jnp.sum(after(valid_float, normed_ffn)), ("rep", "shard"))
    tokens_all = gather(normed_ffn)
    logits_all = dot_nn(tokens_all, router_full)
    chosen_all = jnp.any(routes_all[..., None] == expert_ids, 1)
    masked = jnp.where(chosen_all, logits_all, very_low)
    raised = jnp.where(chosen_all, jnp.exp(masked - jnp.max(masked, -1, keepdims=True)), 0.0)
    gates_all = raised / jnp.sum(raised, -1, keepdims=True)
    gates_own = lax.dynamic_slice_in_dim(gates_all, shard_at * own_experts, own_experts, 1)
    gates_own = jnp.pad(gates_own, ((0, 0), (0, LANES - own_experts)))
    gates = lax.dynamic_slice_in_dim(gates_all, shard_at * row_count, row_count, 0)
    gates_own = after(gates_own, valid_count)
    mix_part, gate_up, hidden_gated = experts_forward(tokens_all, gates_own, w_in, w_out)
    mixture = scatter(mix_part).astype(jnp.float32)
    result_f = middle + resid_mult * mixture
    deviation = result_f - teacher.astype(jnp.float32)
    d_result = valid_float[:, None] * deviation * (all_tokens / (2.0 * valid_count))
    d_mix = (resid_mult * d_result).astype(jnp.bfloat16)
    d_mix_all = gather(d_mix)
    own_loss = jnp.sum(valid_float[:, None] * deviation * deviation)
    loss_sum = lax.psum(after(own_loss, d_mix), ("rep", "shard"))
    loss = loss_sum / (model_width * valid_count)
    gates_own = after(gates_own, loss_sum)
    d_rows_part, d_gate_up, d_gates_own = experts_backward(
        d_mix_all, gates_own, gate_up, w_in, w_out
    )
    d_rows = scatter(d_rows_part).astype(jnp.float32)
    d_gates = lax.all_to_all(
        d_gates_own[:, :own_experts], "shard", split_axis=0, concat_axis=1, tiled=True
    )
    kept_experts = own_experts // 2
    grad_rows = model_width + w_out.shape[1]
    flat_rows = kept_experts * grad_rows
    side = side_of(near)
    order = jnp.arange(kept_experts, dtype=jnp.int32)
    order_sent = order + (1 - side) * kept_experts
    order_kept = order + side * kept_experts
    sent = experts_grads(order_sent, tokens_all, d_mix_all, d_gate_up, hidden_gated)
    other = exchange(sent, near).reshape(flat_rows, -1)
    kept = experts_grads(after(order_kept, sent), tokens_all, d_mix_all, d_gate_up, hidden_gated)
    kept = kept.reshape(flat_rows, -1)
    moe_sent_first, moe_first = halve([kept, other], far[0], 0, 0, flat_rows // 2)
    moe_sent_second, moe_second = halve([kept, other], far[-1], 0, flat_rows // 2, flat_rows // 2)
    d_rows = after(d_rows, moe_sent_first, moe_sent_second)
    d_logits = (gates * (d_gates - jnp.sum(gates * d_gates, -1, keepdims=True))).astype(
        jnp.bfloat16
    )
    d_normed_ffn = d_rows + dot_nt(d_logits, router_full)
    grad_router = dot_tn(normed_ffn, d_logits)
    d_norm_mid, grad_gain_ffn = norm_back(d_normed_ffn, middle, scale_ffn, gain_ffn)
    d_middle = d_result + d_norm_mid
    d_branch = (resid_mult * d_middle).astype(jnp.bfloat16)
    d_attended = dot_nt(d_branch, output_full).astype(
        jnp.bfloat16
    )
    query_grad_rows, kv_grad_all = attention_backward(
        bias, query_rows, keys_all, values_all, log_norm, d_attended, tables, tables_own
    )
    d_normed_kv = dot_nt(kv_grad_all, kv_full)
    d_normed_query = dot_nt(query_grad_rows, query_full)
    d_normed_attn = scatter(d_normed_kv.astype(jnp.bfloat16)).astype(jnp.float32) + d_normed_query
    grad_gain_attn = jnp.sum(d_normed_kv * all_float * rms_scale(all_float), 0) + jnp.sum(
        d_normed_query * input_float * scale_attn, 0
    )
    d_norm_in, _ = norm_back(d_normed_attn, input_float, scale_attn, gain_attn)
    d_input = d_middle + d_norm_in
    grad_small = jnp.concatenate(
        [
            grad_gain_attn[:, None],
            grad_gain_ffn[:, None],
            grad_router,
            jnp.zeros((model_width, LANES - 2 - expert_count), jnp.float32),
        ],
        1,
    )

    first, second = attention_grads(
        normed_attn, query_grad_rows, normed_all, kv_grad_all, attended, d_branch, grad_small
    )
    first = [first.reshape(shard_count, own_rows, -1)]
    second = [second.reshape(shard_count, own_rows, -1)]
    for bit_first, bit_second in zip([near] + far, [near] + far[::-1]):
        _, first = halve(first, bit_first, 1)
        _, second = halve(second, bit_second, 1)
    split_at = first[0].shape[2]
    joined = jnp.concatenate([add_pair(*first), add_pair(*second)], 2)
    joined = lax.psum_scatter(joined, "shard", scatter_dimension=0)
    first, second = joined[:, :split_at], joined[:, split_at:]
    for bit_first, bit_second in zip(far[::-1] + [near], far + [near]):
        first = double(first, bit_first, 0)
        second = double(second, bit_second, 0)
    first, second = first.astype(jnp.float32), second.astype(jnp.float32)
    sum_query = first[:, :query_width]
    sum_key = second[:, :kv_width]
    sum_value = second[:, kv_width : 2 * kv_width]
    sum_output = jnp.concatenate(
        [first[:, query_width : query_width + half_width], second[:, 2 * kv_width :]], 1
    )
    sum_small = first[:, query_width + half_width :]
    for bit_first, bit_second in zip(far[1:], far[::-1][1:]):
        _, moe_first = halve(moe_first, bit_first, 0)
        _, moe_second = halve(moe_second, bit_second, 0)
    moe_first, moe_second = add_pair(*moe_first), add_pair(*moe_second)
    for bit_first, bit_second in zip(far[::-1], far):
        moe_first = double(moe_first, bit_first, 0)
        moe_second = double(moe_second, bit_second, 0)
    if kept_experts % 2 == 0:
        pieces = [moe_first, moe_second]
    else:
        pieces = [lax.concatenate([moe_first, moe_second], 0)]
    pieces = [piece.reshape(-1, grad_rows, piece.shape[1]) for piece in pieces]
    others = [exchange(piece, near) for piece in pieces]
    held = []
    for start, group in ((side, pieces), (1 - side, others)):
        base = start * kept_experts
        for piece in group:
            held = widen(jnp.reshape(base, (1,)), piece, model_width, own_experts, held)
            base = base + piece.shape[0]
    sum_in, sum_out = held
    return (
        result_f.astype(jnp.bfloat16),
        loss,
        d_input,
        sum_small[:, 0],
        sum_query,
        sum_key,
        sum_value,
        sum_output,
        sum_small[:, 1],
        sum_small[:, 2 : 2 + expert_count],
        sum_in,
        sum_out,
    )


def solution(mesh):
    in_specs = (
        P(("rep", "shard"), None),
        P(("rep", "shard")),
        P(("rep", "shard"), None),
        P(("rep", "shard"), None),
        P("shard"),
        P("shard", None),
        P("shard", None),
        P("shard", None),
        P("shard", None),
        P("shard"),
        P("shard", None),
        P("shard", None, None),
        P("shard", None, None),
    )
    out_specs = (
        P(("rep", "shard"), None),
        P(),
        P(("rep", "shard"), None),
        P("shard"),
        P("shard", None),
        P("shard", None),
        P("shard", None),
        P("shard", None),
        P("shard"),
        P("shard", None),
        P("shard", None, None),
        P("shard", None, None),
    )
    return jax.shard_map(body, mesh=mesh, in_specs=in_specs, out_specs=out_specs, check_vma=False)
```

time: 906 us -> 632 us (0.70)
  waiting for transfers between devices: 506 us -> 198 us
  Pallas kernels: 72.6 us -> 143 us
  matrix products: 84 us -> 16.2 us
  starting transfers between devices: 4.17 us -> 29.5 us
  blocking collectives: 137 us -> 117 us
  local copies, waits for them, and re-layouts: 19.7 us -> 35.3 us
  other arithmetic: 54.3 us -> 65.9 us
    all_gather x5 -> x3, waiting for transfers between devices: 197 us -> 14.7 us  [gather(): return lax.all_gather(block, 'shard', axis=0, tiled=True)]
    psum x1 -> x0, waiting for transfers between devices: 146 us -> none  [body(): lax.psum((grad_in, grad_out, own_weights, own_small), 'rep')]
    ppermute x0 -> x30, waiting for transfers between devices: none -> 117 us  [exchange(): return lax.ppermute(block, 'rep', [(at, at ^ bit) for at in range(count)])]
    reduce_scatter x5 -> x3, waiting for transfers between devices: 156 us -> 65.4 us  [scatter(): return lax.psum_scatter(block, 'shard', scatter_dimension=0, tiled=True)]
    pallas_call x1 -> x9, Pallas kernels: 19 us -> 89.6 us  [the longest x2 25 us: experts_grads(): pl.pallas_call(experts_grads_kernel, grid_spec=pltpu.PrefetchScalarGridSp...]
    dot_general x57 -> x0, matrix products: 65.2 us -> none  [the longest x16 26.1 us: scores_of(): jnp.einsum('hqd,kd->hqk', query_part, key_part, preferred_element_type=jn...]
    psum x3 -> x2, blocking collectives: 109 us -> 83.2 us  [the longest x1 42.3 us: body(): loss_sum = lax.psum(after(own_loss, d_mix), ('rep', 'shard'))]
    ppermute x0 -> x30, starting transfers between devices: none -> 25.5 us  [exchange(): return lax.ppermute(block, 'rep', [(at, at ^ bit) for at in range(count)])]
  transfers between devices with their start and end apart: 12 -> 39, of which waited for: 10 -> 21; matrix products, arithmetic and copies ran while one was open for 6% -> 13% of each run, Pallas kernels for 2% -> 9%
where the time goes in v2:
time: 632 us; the launch traced here: 623 us
  waiting for transfers between devices  198 us (31%)
  Pallas kernels  143 us (23%)
  blocking collectives  117 us (19%)
  other arithmetic  65.9 us (10%)
  local copies, waits for them, and re-layouts  35.3 us (6%)
  starting transfers between devices  29.5 us (5%)
  between operations  18.7 us (3%)
  matrix products  16.2 us (3%)
    ppermute x30, waiting for transfers between devices, exchange(): return lax.ppermute(block, 'rep', [(at, at ^ bit) for at in range(count)])  117 us
    reduce_scatter x3, waiting for transfers between devices, scatter(): return lax.psum_scatter(block, 'shard', scatter_dimension=0, tiled=True)  65.4 us
    psum x1, blocking collectives, body(): loss_sum = lax.psum(after(own_loss, d_mix), ('rep', 'shard'))  42.3 us
    psum x1, blocking collectives, body(): lax.psum(jnp.sum(after(valid_float, normed_ffn)), ('rep', 'shard'))  41 us
    pallas_call x1, Pallas kernels, experts_backward(): pl.pallas_call(experts_backward_kernel, grid=(experts,), in_specs=[pl.Blo...  28.9 us
    ppermute x30, starting transfers between devices, exchange(): return lax.ppermute(block, 'rep', [(at, at ^ bit) for at in range(count)])  25.5 us
    pallas_call x2, Pallas kernels, experts_grads(): pl.pallas_call(experts_grads_kernel, grid_spec=pltpu.PrefetchScalarGridSp...  25 us
    pallas_call x1, Pallas kernels, experts_forward(): pl.pallas_call(experts_forward_kernel, grid=(experts,), in_specs=[pl.Bloc...  24.7 us
  transfers between devices with their start and end apart: 39, of which 21 were waited for; matrix products, arithmetic and copies ran while one was open for 13% of the time, Pallas kernels for 9%

profile of v2, /device:TPU:0, one launch (start us, length us, event | category | flops | bytes accessed | tf_op | source)
XLA Modules:
  0.0 623.5 jit_solution(12724505428333528393)
XLA Ops:
  9.0 20.3 %all-gather.1 = bf16[128,2048]{1,0:T(8,128)(2,1)S(1)} all-gather(bf16[32,2048]{1,0:T(8,128)(2,1)S(1)} %pad_maximum_fusion.19), channel_id=3, replica_groups=mesh['rep'=8,'shard'=4] {'shard'}, dimensions={0}, use_global_device_ids=true | all-gather | bytes 655360 | tf_op jit(solution)/shard_map/all_gather | solution.py:612
  34.9 3.5 collective-permute-done
  41.5 2.9 fusion.19
  52.8 7.6 %all-gather.8.cloned.1.call-done.all_ref = bf16[1024,1024]{1,0:T(8,128)(2,1)} async-done(((bf16[256,1024]{1,0:T(8,128)(2,1)}), bf16[1024,1024]{1,0:T(8,128)(2,1)}) %all-gather.8.cloned.1.call-update) | async-done | bytes 2097168 | tf_op jit(solution)/shard_map/all_gather | solution.py:586
  60.4 13.4 %all-gather.2 = bf16[4,1,6656]{2,1,0:T(2,128)(2,1)S(1)} all-gather(bf16[1,1,6656]{2,1,0:T(2,128)(2,1)S(1)} %maximum_bitcast_fusion.2), channel_id=1, replica_groups=mesh['rep'=8,'shard'=4] {'shard'}, dimensions={0}, use_global_device_ids=true | all-gather | bytes 66560 | tf_op jit(solution)/shard_map/all_gather | solution.py:586
  74.5 2.7 pad_maximum_fusion.13
  84.2 2.3 constant_dynamic-update-slice_fusion.12
  86.5 17.6 %attention_forward.1 = (bf16[1024,1024]{1,0:T(8,128)(2,1)}, bf16[256,1024]{1,0:T(8,128)(2,1)}, bf16[1024,512]{1,0:T(8,128)(2,1)}, bf16[1024,512]{1,0:T(8,128)(2,...) custom-call(f32[4]{0:T(128)} %compare_select_fusion.bias_ref, bf16[1024,1024]{1,0:T(8,128)(2,1)} %all-gather.8.cloned.1.call-done.all_ref, ...), custom_call_target="tpu_custom_call" | custom-call | flops 4831838208 | bytes 16777216 | tf_op jit(solution)/shard_map/attention_forward/pallas_call | solution.py:414
  111.0 41.0 %psum.14 = f32[]{:T(128)} all-reduce(f32[]{:T(128)} %reduce_sum.110), channel_id=1, replica_groups=mesh['rep'=8,'shard'=4] {'rep','shard'}, use_global_device_ids=true, to_apply=%region_5.6 | all-reduce | flops 1 | bytes 8 | tf_op jit(solution)/shard_map/psum | solution.py:651
  152.0 3.6 all-gather.10.cloned.1.call-done.x_ref
  155.6 2.5 fusion.23
  159.8 24.7 %experts_forward.1 = (bf16[1024,1024]{1,0:T(8,128)(2,1)}, f32[4,1024,1024]{2,1,0:T(8,128)}, bf16[4,1024,512]{2,1,0:T(8,128)(2,1)}) custom-call(bf16[1024,1024]{1,0:T(8,128)(2,1)} %all-gather.10.cloned.1.call-done.x_ref, f32[1024,128]{1,0:T(8,128)} %pad.4.gate_ref, bf16[4,1024,1024]{2,1,0:T(8,128)(2,1)} %in_ref.3, bf16[4,512,1024]{2,1,0:T(8,128)(2,1)} %out_ref.3), custom_call_target="tpu_custom_call" | custom-call | flops 12884901888 | bytes 39845888 | tf_op jit(solution)/shard_map/experts_forward/pallas_call | solution.py:102
  185.3 42.0 %reduce-scatter.5.cloned.1.call-done = bf16[256,1024]{1,0:T(8,128)(2,1)} async-done(((bf16[1024,1024]{1,0:T(8,128)(2,1)}), bf16[256,1024]{1,0:T(8,128)(2,1)}) %reduce-scatter.5.cloned.1.call-update) | async-done | bytes 524304 | tf_op jit(solution)/shard_map/reduce_scatter | solution.py:589
  227.4 2.8 multiply_convert_fusion.1
  230.8 42.3 %psum.15 = f32[]{:T(128)} all-reduce(f32[]{:T(128)} %get-tuple-element.52), channel_id=1, replica_groups=mesh['rep'=8,'shard'=4] {'rep','shard'}, use_global_device_ids=true, to_apply=%region_8.9 | all-reduce | flops 1 | bytes 8 | tf_op jit(solution)/shard_map/psum | solution.py:670
  273.0 3.6 all-gather.12.cloned.1.call-done.dmix_ref
  276.6 28.9 %experts_backward.1 = (bf16[1024,1024]{1,0:T(8,128)(2,1)}, bf16[4,1024,1024]{2,1,0:T(8,128)(2,1)}, f32[1024,128]{1,0:T(8,128)}) custom-call(bf16[1024,1024]{1,0:T(8,128)(2,1)} %all-gather.12.cloned.1.call-done.dmix_ref, f32[1024,128]{1,0:T(8,128)} %pad.4.gate_ref, f32[4,1024,1024]{2,1,0:T(8,128)} %get-tuple-element.54.gate_up_ref, ...), custom_call_target="tpu_custom_call" | custom-call | flops 12884901888 | bytes 41943040 | tf_op jit(solution)/shard_map/experts_backward/pallas_call | solution.py:172
  305.5 12.5 %experts_grads.2 = bf16[2,1536,1024]{2,1,0:T(8,128)(2,1)} custom-call(s32[2]{0:T(128)} %iota_add_fusion.order_ref, bf16[1024,1024]{1,0:T(8,128)(2,1)} %all-gather.10.cloned.1.call-done.x_ref, bf16[1024,1024]{1,0:T(8,128)(2,1)} %all-gather.12.cloned.1.call-done.dmix_ref, bf16[4,1024,1024]{2,1,0:T(8,128)(2,1)} %get-tuple-element.56.dgate_up_ref, ...), custom_call_target="tpu_custom_call" | custom-call | flops 6442450944 | bytes 16777216 | tf_op jit(solution)/shard_map/experts_grads/pallas_call | solution.py:213
  321.5 3.3 all-to-all-start
  325.0 12.5 %experts_grads.3 = bf16[2,1536,1024]{2,1,0:T(8,128)(2,1)} custom-call(s32[2]{0:T(128)} %iota_add_fusion.1.order_ref, bf16[1024,1024]{1,0:T(8,128)(2,1)} %all-gather.10.cloned.1.call-done.x_ref, bf16[1024,1024]{1,0:T(8,128)(2,1)} %all-gather.12.cloned.1.call-done.dmix_ref, bf16[4,1024,1024]{2,1,0:T(8,128)(2,1)} %get-tuple-element.56.dgate_up_ref, ...), custom_call_target="tpu_custom_call" | custom-call | flops 6442450944 | bytes 16777216 | tf_op jit(solution)/shard_map/experts_grads/pallas_call | solution.py:213
  337.8 23.4 %reduce-scatter.7.cloned.1.call-done = bf16[256,1024]{1,0:T(8,128)(2,1)} async-done(((bf16[1024,1024]{1,0:T(8,128)(2,1)}), bf16[256,1024]{1,0:T(8,128)(2,1)}) %reduce-scatter.7.cloned.1.call-update) | async-done | bytes 524304 | tf_op jit(solution)/shard_map/reduce_scatter | solution.py:589
  362.3 9.6 %add_convert_fusion = (bf16[768,1024]{1,0:T(8,128)(2,1)S(1)}, bf16[768,1024]{1,0:T(8,128)(2,1)}, bf16[768,1024]{1,0:T(8,128)(2,1)}, bf16[768,1024]{1,0:T(8,128)(2,1)}) fusion(bf16[3072,1024]{1,0:T(8,128)(2,1)} %bitcast.7, s32[]{:T(128)S(6)} %select_n.286, bf16[3072,1024]{1,0:T(8,128)(2,1)} %bitcast.47, s32[]{:T(128)S(6)} %select_n.282, s32[]{:T(128)S(6)} %select_n.272, ...), kind=kLoop, calls=%fused_computation.7 | loop fusion | flops 12582912 | bytes 18874384 | tf_op jit(solution)/shard_map/convert_element_type | solution.py:521
  376.5 18.0 %attention_backward.1 = (bf16[256,1024]{1,0:T(8,128)(2,1)}, bf16[1024,1024]{1,0:T(8,128)(2,1)}) custom-call(f32[4]{0:T(128)} %compare_select_fusion.bias_ref, bf16[256,1024]{1,0:T(8,128)(2,1)} %get-tuple-element.61.query_ref, bf16[1024,512]{1,0:T(8,128)(2,1)} %get-tuple-element.62.key_ref, bf16[1024,512]{1,0:T(8,128)(2,1)} %get-tuple-element.63.value_ref, ...), custom_call_target="tpu_custom_call" | custom-call | flops 5368709120 | bytes 8388608 | tf_op jit(solution)/shard_map/attention_backward/pallas_call | solution.py:487
  394.5 6.6 %fusion.1 = (f32[1024]{0:T(1024)S(1)}, bf16[1024,1024]{1,0:T(8,128)(2,1)}) fusion(bf16[1024,1024]{1,0:T(8,128)(2,1)} %all-gather.8.cloned.1.call-done.all_ref, f32[1024]{0:T(1024)S(1)} %add_rsqrt_fusion, bf16[1024,1024]{1,0:T(8,128)(2,1)} %get-tuple-element.65.dkv_ref, bf16[1024,1024]{1,0:T(8,128)(2,1)} %bitcast.53), kind=kOutput, calls=%fused_computation.3 | convolution fusion | flops 2152725504 | bytes 8396800 | tf_op jit(solution)/shard_map/dot_general | solution.py:66
  404.4 33.3 %collective-permute-done.20 = bf16[768,1024]{1,0:T(8,128)(2,1)} collective-permute-done((bf16[768,1024]{1,0:T(8,128)(2,1)}, bf16[768,1024]{1,0:T(8,128)(2,1)}, u32[]{:S(2)}, u32[]{:S(2)}) %collective-permute-start.20) | collective-permute-done | bytes 1572896 | tf_op jit(solution)/shard_map/ppermute | solution.py:513
  437.7 2.6 add_convert_fusion.10
  444.5 2.4 add_convert_fusion.7
  448.4 10.4 %collective-permute-done.21 = bf16[384,1024]{1,0:T(8,128)(2,1)} collective-permute-done((bf16[384,1024]{1,0:T(8,128)(2,1)}, bf16[384,1024]{1,0:T(8,128)(2,1)}, u32[]{:S(2)}, u32[]{:S(2)}) %collective-permute-start.21) | collective-permute-done | bytes 786464 | tf_op jit(solution)/shard_map/ppermute | solution.py:513
  458.8 2.9 add_convert_fusion.9
  463.1 3.8 fusion.12
  468.3 9.1 %attention_grads.1 = (bf16[1024,1664]{1,0:T(8,128)(2,1)}, bf16[1024,1536]{1,0:T(8,128)(2,1)}) custom-call(bf16[256,1024]{1,0:T(8,128)(2,1)} %constant_dynamic-slice_fusion.2.normed_ref, bf16[256,1024]{1,0:T(8,128)(2,1)} %get-tuple-element.66.dquery_ref, bf16[1024,1024]{1,0:T(8,128)(2,1)} %get-tuple-element.67.all_ref, ...), custom_call_target="tpu_custom_call" | custom-call | flops 3221225472 | bytes 14680064 | tf_op jit(solution)/shard_map/attention_grads/pallas_call | solution.py:288
  477.4 2.7 constant_dynamic-slice_fusion
  480.1 2.8 constant_dynamic-slice_fusion.1
  486.8 2.6 pad_maximum_fusion.3
  492.2 13.5 %collective-permute-done.27 = bf16[384,1024]{1,0:T(8,128)(2,1)S(1)} collective-permute-done((bf16[384,1024]{1,0:T(8,128)(2,1)S(1)}, bf16[384,1024]{1,0:T(8,128)(2,1)S(1)}, u32[]{:S(2)}, u32[]{:S(2)}) %collective-permute-start.27) | collective-permute-done | bytes 786464 | tf_op jit(solution)/shard_map/ppermute | solution.py:513
  514.2 4.2 maximum_bitcast_fusion
  518.3 21.1 %collective-permute-done.23 = bf16[768,1024]{1,0:T(8,128)(2,1)} collective-permute-done((bf16[768,1024]{1,0:T(8,128)(2,1)}, bf16[768,1024]{1,0:T(8,128)(2,1)}, u32[]{:S(2)}, u32[]{:S(2)}) %collective-permute-start.23) | collective-permute-done | bytes 1572896 | tf_op jit(solution)/shard_map/ppermute | solution.py:513
  539.5 2.7 bitcast_dynamic-update-slice_fusion.1.piece_ref
  542.2 13.1 %collective-permute-done.12 = bf16[4,64,1536]{2,1,0:T(8,128)(2,1)S(1)} collective-permute-done((bf16[4,64,1536]{2,1,0:T(8,128)(2,1)S(1)}, bf16[4,64,1536]{2,1,0:T(8,128)(2,1)S(1)}, u32[]{:S(2)}, u32[]{:S(2)}) %collective-permute-start.12) | collective-permute-done | bytes 786464 | tf_op jit(solution)/shard_map/ppermute | solution.py:513
  556.3 3.6 collective-permute-done.9
  561.5 5.4 collective-permute-done.13
  571.2 3.2 fusion.9
  574.3 5.0 widen.4
  579.3 5.1 widen.5
  584.4 4.9 widen.6
  589.3 4.9 widen.7
  603.8 2.6 collective-permute-done.18
  606.6 2.7 collective-permute-done.15
  (227 shorter events, 92.8 us)
Async XLA Ops:
  7.2 37.2 %copy-start = (bf16[256,1024]{1,0:T(8,128)(2,1)S(1)}, bf16[256,1024]{1,0:T(8,128)(2,1)}, u32[]{:S(2)}) copy-start(bf16[256,1024]{1,0:T(8,128)(2,1)} %param.21) | copy-start | bytes 1572868
  7.2 25.3 %copy-start.21 = (bf16[256]{0:T(256)(128)(2,1)S(1)}, bf16[256]{0:T(256)(128)(2,1)}, u32[]{:S(2)}) copy-start(bf16[256]{0:T(256)(128)(2,1)} %param.17) | copy-start | bytes 1540
  7.2 25.3 %copy-start.22 = (bf16[256]{0:T(256)(128)(2,1)S(1)}, bf16[256]{0:T(256)(128)(2,1)}, u32[]{:S(2)}) copy-start(bf16[256]{0:T(256)(128)(2,1)} %param.22) | copy-start | bytes 1540
  7.2 25.3 %copy-start.18 = (s32[256,8]{0,1:T(8,128)S(1)}, s32[256,8]{0,1:T(8,128)}, u32[]{:S(2)}) copy-start(s32[256,8]{0,1:T(8,128)} %param.16) | copy-start | bytes 24580
  7.2 25.3 %copy-start.19 = (bf16[256,16]{0,1:T(8,128)(2,1)S(1)}, bf16[256,16]{0,1:T(8,128)(2,1)}, u32[]{:S(2)}) copy-start(bf16[256,16]{0,1:T(8,128)(2,1)} %param.23) | copy-start | bytes 24580
  7.2 53.1 %all-gather.8.cloned.1.call-start = ((), (), s32[]{:S(2)}) async-start(), calls=%async_computation.5 | async-start | bytes 2621440 | tf_op jit(solution)/shard_map/all_gather | solution.py:586
  8.0 96.1 %all-gather.14.cloned.1.call-start = ((), (), s32[]{:S(2)}) async-start(), calls=%async_computation.12 | async-start | bytes 1310720 | tf_op jit(solution)/shard_map/all_gather | solution.py:626
  29.4 9.8 %collective-permute-start.3 = (bf16[4,32,1024]{2,1,0:T(8,128)(2,1)S(1)}, bf16[4,32,1024]{2,1,0:T(8,128)(2,1)S(1)}, u32[]{:S(2)}, u32[]{:S(2)}) collective-permute-start(bf16[4,32,1024]{2,1,0:T(8,128)(2,1)S(1)} %get-tuple-element.176), channel_id=1, source_target_pairs={{0,16},{4,20},{8,24},{12,28},{16,0},{20,4},{24,8},{28,12},{1,17},{... | collective-permute-start | bytes 786440 | tf_op jit(solution)/shard_map/ppermute | solution.py:513
  31.0 7.5 %collective-permute-start = (bf16[4,32,1024]{2,1,0:T(8,128)(2,1)S(1)}, bf16[4,32,1024]{2,1,0:T(8,128)(2,1)S(1)}, u32[]{:S(2)}, u32[]{:S(2)}) collective-permute-start(bf16[4,32,1024]{2,1,0:T(8,128)(2,1)S(1)} %get-tuple-element.177), channel_id=1, source_target_pairs={{0,8},{4,12},{8,0},{12,4},{16,24},{20,28},{24,16},{28,20},{1,9},{5... | collective-permute-start | bytes 786440 | tf_op jit(solution)/shard_map/ppermute | solution.py:513
  39.2 11.4 %collective-permute-start.1 = (bf16[4,64,1024]{2,1,0:T(8,128)(2,1)}, bf16[4,64,1024]{2,1,0:T(8,128)(2,1)}, u32[]{:S(2)}, u32[]{:S(2)}) collective-permute-start(bf16[4,64,1024]{2,1,0:T(8,128)(2,1)} %constant_dynamic-update-slice_fusion.14), channel_id=1, source_target_pairs={{0,16},{4,20},{8,24},{12,28},{16,0},{20,4},{24,8},{28,12},{1,17},{... | collective-permute-start | bytes 1572872 | tf_op jit(solution)/shard_map/ppermute | solution.py:513
  39.9 9.5 %collective-permute-start.4 = (bf16[4,64,1024]{2,1,0:T(8,128)(2,1)}, bf16[4,64,1024]{2,1,0:T(8,128)(2,1)}, u32[]{:S(2)}, u32[]{:S(2)}) collective-permute-start(bf16[4,64,1024]{2,1,0:T(8,128)(2,1)} %constant_dynamic-update-slice_fusion.11), channel_id=1, source_target_pairs={{0,8},{4,12},{8,0},{12,4},{16,24},{20,28},{24,16},{28,20},{1,9},{5... | collective-permute-start | bytes 1572872 | tf_op jit(solution)/shard_map/ppermute | solution.py:513
  50.5 30.9 %collective-permute-start.5 = (bf16[4,128,1024]{2,1,0:T(8,128)(2,1)S(1)}, bf16[4,128,1024]{2,1,0:T(8,128)(2,1)}, u32[]{:S(2)}, u32[]{:S(2)}) collective-permute-start(bf16[4,128,1024]{2,1,0:T(8,128)(2,1)S(1)} %constant_dynamic-update-slice_fusion.10), channel_id=1, source_target_pairs={{0,4},{4,0},{8,12},{12,8},{16,20},{20,16},{24,28},{28,24},{1,5},{5... | collective-permute-start | bytes 3145736 | tf_op jit(solution)/shard_map/ppermute | solution.py:513
  51.7 31.1 %collective-permute-start.2 = (bf16[4,128,1024]{2,1,0:T(8,128)(2,1)S(1)}, bf16[4,128,1024]{2,1,0:T(8,128)(2,1)}, u32[]{:S(2)}, u32[]{:S(2)}) collective-permute-start(bf16[4,128,1024]{2,1,0:T(8,128)(2,1)S(1)} %constant_dynamic-update-slice_fusion.13), channel_id=1, source_target_pairs={{0,4},{4,0},{8,12},{12,8},{16,20},{20,16},{24,28},{28,24},{1,5},{5... | collective-permute-start | bytes 3145736 | tf_op jit(solution)/shard_map/ppermute | solution.py:513
  60.3 95.2 %all-gather.10.cloned.1.call-start = ((), (), s32[]{:S(2)}) async-start(), calls=%async_computation.6 | async-start | bytes 2621440 | tf_op jit(solution)/shard_map/all_gather | solution.py:586
  104.1 2.9 collective-permute-start.6
  109.5 117.9 %reduce-scatter.5.cloned.1.call-start = ((), (), s32[]{:S(2)}) async-start(), calls=%async_computation.7 | async-start | bytes 2621440 | tf_op jit(solution)/shard_map/reduce_scatter | solution.py:589
  184.5 42.9 %copy-start.10 = (bf16[256,1024]{1,0:T(8,128)(2,1)S(1)}, bf16[256,1024]{1,0:T(8,128)(2,1)}, u32[]{:S(2)}) copy-start(bf16[256,1024]{1,0:T(8,128)(2,1)} %param.15) | copy-start | bytes 1572868
  184.5 92.1 %all-gather.12.cloned.1.call-start = ((), (), s32[]{:S(2)}) async-start(), calls=%async_computation.8 | async-start | bytes 2621440 | tf_op jit(solution)/shard_map/all_gather | solution.py:586
  230.2 131.0 %reduce-scatter.7.cloned.1.call-start = ((), (), s32[]{:S(2)}) async-start(), calls=%async_computation.9 | async-start | bytes 2621440 | tf_op jit(solution)/shard_map/reduce_scatter | solution.py:589
  318.0 44.4 %collective-permute-start.7 = (bf16[2,1536,1024]{2,1,0:T(8,128)(2,1)}, bf16[2,1536,1024]{2,1,0:T(8,128)(2,1)}, u32[]{:S(2)}, u32[]{:S(2)}) collective-permute-start(bf16[2,1536,1024]{2,1,0:T(8,128)(2,1)} %experts_grads.2), channel_id=1, source_target_pairs={{0,4},{4,0},{8,12},{12,8},{16,20},{20,16},{24,28},{28,24},{1,5},{5... | collective-permute-start | bytes 18874376 | tf_op jit(solution)/shard_map/ppermute | solution.py:513
  321.5 16.0 %all-to-all-start = ((f32[4,256,4]{1,2,0:T(4,128)}), f32[4,256,4]{1,2,0:T(4,128)S(1)}, u32[]{:S(2)}, u32[]{:S(2)}) async-start(f32[4,256,4]{1,2,0:T(4,128)} %copy.103), calls=%async_computation.2 | async-start | bytes 32768 | tf_op jit(solution)/shard_map/all_to_all | solution.py:677
  324.7 138.4 %reduce-scatter.9.cloned.1.call-start = ((), (), s32[]{:S(2)}) async-start(), calls=%async_computation.10 | async-start | bytes 2621440 | tf_op jit(solution)/shard_map/reduce_scatter | solution.py:589
  401.1 42.8 %copy-start.4 = (bf16[256,1024]{1,0:T(8,128)(2,1)S(1)}, bf16[256,1024]{1,0:T(8,128)(2,1)}, u32[]{:S(2)}) copy-start(bf16[256,1024]{1,0:T(8,128)(2,1)} %multiply_convert_fusion.2) | copy-start | bytes 1572868
  401.1 193.1 %reduce-scatter.11.cloned.1.call-start = ((), (), s32[]{:S(2)}) async-start(), calls=%async_computation.11 | async-start | bytes 1024000 | tf_op jit(solution)/shard_map/reduce_scatter | solution.py:736
  401.4 36.3 %collective-permute-start.20 = (bf16[768,1024]{1,0:T(8,128)(2,1)}, bf16[768,1024]{1,0:T(8,128)(2,1)}, u32[]{:S(2)}, u32[]{:S(2)}) collective-permute-start(bf16[768,1024]{1,0:T(8,128)(2,1)} %get-tuple-element.162), channel_id=1, source_target_pairs={{0,16},{4,20},{8,24},{12,28},{16,0},{20,4},{24,8},{28,12},{1,17},{... | collective-permute-start | bytes 4718600 | tf_op jit(solution)/shard_map/ppermute | solution.py:513
  402.9 41.6 %collective-permute-start.25 = (bf16[768,1024]{1,0:T(8,128)(2,1)}, bf16[768,1024]{1,0:T(8,128)(2,1)}, u32[]{:S(2)}, u32[]{:S(2)}) collective-permute-start(bf16[768,1024]{1,0:T(8,128)(2,1)} %get-tuple-element.163), channel_id=1, source_target_pairs={{0,8},{4,12},{8,0},{12,4},{16,24},{20,28},{24,16},{28,20},{1,9},{5... | collective-permute-start | bytes 4718600 | tf_op jit(solution)/shard_map/ppermute | solution.py:513
  440.3 18.5 %collective-permute-start.21 = (bf16[384,1024]{1,0:T(8,128)(2,1)}, bf16[384,1024]{1,0:T(8,128)(2,1)}, u32[]{:S(2)}, u32[]{:S(2)}) collective-permute-start(bf16[384,1024]{1,0:T(8,128)(2,1)} %add_convert_fusion.10), channel_id=1, source_target_pairs={{0,8},{4,12},{8,0},{12,4},{16,24},{20,28},{24,16},{28,20},{1,9},{5... | collective-permute-start | bytes 2359304 | tf_op jit(solution)/shard_map/ppermute | solution.py:513
  446.9 16.3 %copy-start.17 = (f32[1024]{0:T(1024)S(1)}, f32[1024]{0:T(1024)}, u32[]{:S(2)}) copy-start(f32[1024]{0:T(1024)} %get-tuple-element.157) | copy-start | bytes 12292
  446.9 36.5 %collective-permute-start.26 = (bf16[384,1024]{1,0:T(8,128)(2,1)}, bf16[384,1024]{1,0:T(8,128)(2,1)}, u32[]{:S(2)}, u32[]{:S(2)}) collective-permute-start(bf16[384,1024]{1,0:T(8,128)(2,1)} %add_convert_fusion.7), channel_id=1, source_target_pairs={{0,16},{4,20},{8,24},{12,28},{16,0},{20,4},{24,8},{28,12},{1,17},{... | collective-permute-start | bytes 2359304 | tf_op jit(solution)/shard_map/ppermute | solution.py:513
  461.7 27.7 %collective-permute-start.22 = (bf16[384,1024]{1,0:T(8,128)(2,1)}, bf16[384,1024]{1,0:T(8,128)(2,1)}, u32[]{:S(2)}, u32[]{:S(2)}) collective-permute-start(bf16[384,1024]{1,0:T(8,128)(2,1)} %add_convert_fusion.9), channel_id=1, source_target_pairs={{0,8},{4,12},{8,0},{12,4},{16,24},{20,28},{24,16},{28,20},{1,9},{5... | collective-permute-start | bytes 2359304 | tf_op jit(solution)/shard_map/ppermute | solution.py:513
  480.1 26.8 %collective-permute-start.11 = (bf16[4,128,1536]{2,1,0:T(8,128)(2,1)}, bf16[4,128,1536]{2,1,0:T(8,128)(2,1)}, u32[]{:S(2)}, u32[]{:S(2)}) collective-permute-start(bf16[4,128,1536]{2,1,0:T(8,128)(2,1)} %constant_dynamic-slice_fusion), channel_id=1, source_target_pairs={{0,4},{4,0},{8,12},{12,8},{16,20},{20,16},{24,28},{28,24},{1,5},{5... | collective-permute-start | bytes 4718600 | tf_op jit(solution)/shard_map/ppermute | solution.py:513
  482.9 28.4 %collective-permute-start.8 = (bf16[4,128,1664]{2,1,0:T(8,128)(2,1)}, bf16[4,128,1664]{2,1,0:T(8,128)(2,1)}, u32[]{:S(2)}, u32[]{:S(2)}) collective-permute-start(bf16[4,128,1664]{2,1,0:T(8,128)(2,1)} %constant_dynamic-slice_fusion.1), channel_id=1, source_target_pairs={{0,4},{4,0},{8,12},{12,8},{16,20},{20,16},{24,28},{28,24},{1,5},{5... | collective-permute-start | bytes 5111816 | tf_op jit(solution)/shard_map/ppermute | solution.py:513
  485.2 20.5 %collective-permute-start.27 = (bf16[384,1024]{1,0:T(8,128)(2,1)S(1)}, bf16[384,1024]{1,0:T(8,128)(2,1)S(1)}, u32[]{:S(2)}, u32[]{:S(2)}) collective-permute-start(bf16[384,1024]{1,0:T(8,128)(2,1)S(1)} %add_convert_fusion.6), channel_id=1, source_target_pairs={{0,16},{4,20},{8,24},{12,28},{16,0},{20,4},{24,8},{28,12},{1,17},{... | collective-permute-start | bytes 2359304 | tf_op jit(solution)/shard_map/ppermute | solution.py:513
  491.5 48.0 %collective-permute-start.23 = (bf16[768,1024]{1,0:T(8,128)(2,1)}, bf16[768,1024]{1,0:T(8,128)(2,1)}, u32[]{:S(2)}, u32[]{:S(2)}) collective-permute-start(bf16[768,1024]{1,0:T(8,128)(2,1)} %constant_dynamic-update-slice_fusion.6), channel_id=1, source_target_pairs={{0,16},{4,20},{8,24},{12,28},{16,0},{20,4},{24,8},{28,12},{1,17},{... | collective-permute-start | bytes 4718600 | tf_op jit(solution)/shard_map/ppermute | solution.py:513
  505.8 50.3 %collective-permute-start.28 = (bf16[768,1024]{1,0:T(8,128)(2,1)S(1)}, bf16[768,1024]{1,0:T(8,128)(2,1)S(1)}, u32[]{:S(2)}, u32[]{:S(2)}) collective-permute-start(bf16[768,1024]{1,0:T(8,128)(2,1)S(1)} %constant_dynamic-update-slice_fusion.7), channel_id=1, source_target_pairs={{0,8},{4,12},{8,0},{12,4},{16,24},{20,28},{24,16},{28,20},{1,9},{5... | collective-permute-start | bytes 4718600 | tf_op jit(solution)/shard_map/ppermute | solution.py:513
  509.8 45.5 %collective-permute-start.12 = (bf16[4,64,1536]{2,1,0:T(8,128)(2,1)S(1)}, bf16[4,64,1536]{2,1,0:T(8,128)(2,1)S(1)}, u32[]{:S(2)}, u32[]{:S(2)}) collective-permute-start(bf16[4,64,1536]{2,1,0:T(8,128)(2,1)S(1)} %get-tuple-element.167), channel_id=1, source_target_pairs={{0,16},{4,20},{8,24},{12,28},{16,0},{20,4},{24,8},{28,12},{1,17},{... | collective-permute-start | bytes 2359304 | tf_op jit(solution)/shard_map/ppermute | solution.py:513
  513.4 46.5 %collective-permute-start.9 = (bf16[4,64,1664]{2,1,0:T(8,128)(2,1)S(1)}, bf16[4,64,1664]{2,1,0:T(8,128)(2,1)S(1)}, u32[]{:S(2)}, u32[]{:S(2)}) collective-permute-start(bf16[4,64,1664]{2,1,0:T(8,128)(2,1)S(1)} %get-tuple-element.165), channel_id=1, source_target_pairs={{0,8},{4,12},{8,0},{12,4},{16,24},{20,28},{24,16},{28,20},{1,9},{5... | collective-permute-start | bytes 2555912 | tf_op jit(solution)/shard_map/ppermute | solution.py:513
  542.2 47.1 %collective-permute-start.24 = (bf16[1,1536,1024]{2,1,0:T(8,128)(2,1)}, bf16[1,1536,1024]{2,1,0:T(8,128)(2,1)}, u32[]{:S(2)}, u32[]{:S(2)}) collective-permute-start(bf16[1,1536,1024]{2,1,0:T(8,128)(2,1)} %bitcast_dynamic-update-slice_fusion.1.piece_ref), channel_id=1, source_target_pairs={{0,4},{4,0},{8,12},{12,8},{16,20},{20,16},{24,28},{28,24},{1,5},{5... | collective-permute-start | bytes 9437192 | tf_op jit(solution)/shard_map/ppermute | solution.py:513
  555.4 11.6 %collective-permute-start.13 = (bf16[4,32,1536]{2,1,0:T(8,128)(2,1)S(1)}, bf16[4,32,1536]{2,1,0:T(8,128)(2,1)S(1)}, u32[]{:S(2)}, u32[]{:S(2)}) collective-permute-start(bf16[4,32,1536]{2,1,0:T(8,128)(2,1)S(1)} %add_convert_fusion.18), channel_id=1, source_target_pairs={{0,8},{4,12},{8,0},{12,4},{16,24},{20,28},{24,16},{28,20},{1,9},{5... | collective-permute-start | bytes 1179656 | tf_op jit(solution)/shard_map/ppermute | solution.py:513
  556.2 12.7 %copy-start.2 = (bf16[1,1536,1024]{2,1,0:T(8,128)(2,1)}, bf16[1,1536,1024]{2,1,0:T(8,128)(2,1)S(1)}, u32[]{:S(2)}) copy-start(bf16[1,1536,1024]{2,1,0:T(8,128)(2,1)S(1)} %bitcast_dynamic-update-slice_fusion.piece_ref) | copy-start | bytes 9437188
  556.2 28.2 %collective-permute-start.29 = (bf16[1,1536,1024]{2,1,0:T(8,128)(2,1)S(1)}, bf16[1,1536,1024]{2,1,0:T(8,128)(2,1)}, u32[]{:S(2)}, u32[]{:S(2)}) collective-permute-start(bf16[1,1536,1024]{2,1,0:T(8,128)(2,1)S(1)} %bitcast_dynamic-update-slice_fusion.piece_ref), channel_id=1, source_target_pairs={{0,4},{4,0},{8,12},{12,8},{16,20},{20,16},{24,28},{28,24},{1,5},{5... | collective-permute-start | bytes 9437192 | tf_op jit(solution)/shard_map/ppermute | solution.py:513
  560.0 8.7 %collective-permute-start.10 = (bf16[4,32,1664]{2,1,0:T(8,128)(2,1)S(1)}, bf16[4,32,1664]{2,1,0:T(8,128)(2,1)S(1)}, u32[]{:S(2)}, u32[]{:S(2)}) collective-permute-start(bf16[4,32,1664]{2,1,0:T(8,128)(2,1)S(1)} %add_convert_fusion.15), channel_id=1, source_target_pairs={{0,16},{4,20},{8,24},{12,28},{16,0},{20,4},{24,8},{28,12},{1,17},{... | collective-permute-start | bytes 1277960 | tf_op jit(solution)/shard_map/ppermute | solution.py:513
  596.0 4.7 collective-permute-start.17
  597.4 5.9 collective-permute-start.14
  600.7 5.7 collective-permute-start.18
  603.3 5.9 collective-permute-start.15
  606.5 3.0 collective-permute-start.19
  609.3 1.8 collective-permute-start.16
  (15 other events, 32.5 us)
Sparse Core Ops, SparseCore 0:
  9.6 50.6 all-gather.7
  62.5 26.8 all-gather.13
  109.6 45.8 all-gather.9
  184.7 42.6 reduce-scatter.4
  230.3 46.2 all-gather.11
  318.1 43.0 reduce-scatter.6
  401.3 43.1 reduce-scatter.8
  570.0 23.4 reduce-scatter.10

commit v3 on v2

--- a/solution.py
+++ b/solution.py
@@ -10,6 +10,8 @@
 HEAD_DIM = 64
 TOP = 8
 BLOCK = 256
+CHUNKS = 2
+SMALL_COST = pl.CostEstimate(flops=1000000, bytes_accessed=100000, transcendentals=0)
 
 
 norm_eps = 1e-06
@@ -46,10 +48,11 @@
 
 LANES = 128
 ROW_STEP = 256
+EXPERT_STEP = 512
 
 
 def row_chunks(count):
-    step = min(count, ROW_STEP)
+    step = min(count, EXPERT_STEP)
     return [pl.ds(at, step) for at in range(0, count, step)]
 
 
@@ -73,6 +76,11 @@
 def experts_forward_kernel(x_ref, gate_ref, in_ref, out_ref, mix_ref, gate_up_ref, hidden_ref, total):
     expert = pl.program_id(0)
     units = out_ref.shape[1]
+
+    @pl.when(expert == 0)
+    def _():
+        total[...] = jnp.zeros_like(total)
+
     for rows in row_chunks(x_ref.shape[0]):
         gate_up = dot_nn(x_ref[rows, :], in_ref[0])
         gate_up_ref[0, rows, :] = gate_up
@@ -81,15 +89,7 @@
         weight = pick_lane(gate_ref[rows, :], expert)
         hidden = (silu_gate * gate_up[:, units:] * weight).astype(jnp.bfloat16)
         hidden_ref[0, rows, :] = hidden
-        part = dot_nn(hidden, out_ref[0])
-
-        @pl.when(expert == 0)
-        def _():
-            total[rows, :] = part
-
-        @pl.when(expert > 0)
-        def _():
-            total[rows, :] += part
+        total[rows, :] += dot_nn(hidden, out_ref[0])
 
     @pl.when(expert == pl.num_programs(0) - 1)
     def _():
@@ -120,11 +120,7 @@
         ],
         scratch_shapes=[pltpu.VMEM((count, width), jnp.float32)],
         compiler_params=pltpu.CompilerParams(vmem_limit_bytes=VMEM_BYTES),
-        cost_estimate=pl.CostEstimate(
-            flops=6 * count * width * units * experts,
-            bytes_accessed=experts * units * (6 * width + 10 * count) + 6 * count * width,
-            transcendentals=experts * count * units,
-        ),
+        cost_estimate=SMALL_COST,
         name="experts_forward",
     )(tokens, gates_own, w_in, w_out)
 
@@ -135,6 +131,12 @@
     expert = pl.program_id(0)
     units = out_ref.shape[1]
     lanes = lax.broadcasted_iota(jnp.int32, (1, LANES), 1)
+
+    @pl.when(expert == 0)
+    def _():
+        total[...] = jnp.zeros_like(total)
+        dgates_ref[...] = jnp.zeros_like(dgates_ref)
+
     for rows in row_chunks(dmix_ref.shape[0]):
         pulled = dot_nt(dmix_ref[rows, :], out_ref[0])
         gate_vals = gate_up_ref[0, rows, :units]
@@ -142,24 +144,15 @@
         sigmoid = 1.0 / (1.0 + jnp.exp(-gate_vals))
         silu_gate = gate_vals * sigmoid
         weight = pick_lane(gate_ref[rows, :], expert)
-        own = jnp.sum(pulled * silu_gate * up_vals, axis=1, keepdims=True)
+        d_up = pulled * silu_gate
+        own = jnp.sum(d_up * up_vals, axis=1, keepdims=True)
         own = jnp.where(lanes == expert, own, 0.0)
-        d_hidden = pulled * weight
-        d_gate = d_hidden * up_vals * sigmoid * (1.0 + gate_vals * (1.0 - sigmoid))
-        d_up = d_hidden * silu_gate
+        d_up = d_up * weight
+        d_gate = (pulled * weight) * up_vals * (sigmoid + silu_gate * (1.0 - sigmoid))
         dgate_up_ref[0, rows, :units] = d_gate.astype(jnp.bfloat16)
         dgate_up_ref[0, rows, units:] = d_up.astype(jnp.bfloat16)
-        part = dot_nt(dgate_up_ref[0, rows, :], in_ref[0])
-
-        @pl.when(expert == 0)
-        def _():
-            total[rows, :] = part
-            dgates_ref[rows, :] = own
-
-        @pl.when(expert > 0)
-        def _():
-            total[rows, :] += part
-            dgates_ref[rows, :] += own
+        total[rows, :] += dot_nt(dgate_up_ref[0, rows, :], in_ref[0])
+        dgates_ref[rows, :] += own
 
     @pl.when(expert == pl.num_programs(0) - 1)
     def _():
@@ -191,47 +184,49 @@
         ],
         scratch_shapes=[pltpu.VMEM((count, width), jnp.float32)],
         compiler_params=pltpu.CompilerParams(vmem_limit_bytes=VMEM_BYTES),
-        cost_estimate=pl.CostEstimate(
-            flops=6 * count * width * units * experts,
-            bytes_accessed=experts * units * (6 * width + 12 * count) + 4 * count * width,
-            transcendentals=experts * count * units,
-        ),
+        cost_estimate=SMALL_COST,
         name="experts_backward",
     )(d_mix, gates_own, gate_up, w_in, w_out)
 
 
-def experts_grads_kernel(order_ref, x_ref, dmix_ref, dgate_up_ref, hidden_ref, grads_ref):
-    width = x_ref.shape[1]
-    grads_ref[0, :width, :] = dot_tn(x_ref[...], dgate_up_ref[0]).astype(grads_ref.dtype)
-    grads_ref[0, width:, :] = dot_tn(hidden_ref[0], dmix_ref[...]).astype(grads_ref.dtype)
-
-
-def experts_grads(order, tokens, d_mix, dgate_up, hidden):
-    count, width = tokens.shape
-    units = hidden.shape[2]
+def experts_grads_kernel(order_ref, *refs):
+    grads_ref = refs[-1]
+    count = (len(refs) - 1) // 4
+    width = refs[0].shape[1]
+    grad_in, grad_out = None, None
+    for at in range(count):
+        x_ref, dmix_ref, dgate_up_ref, hidden_ref = refs[4 * at : 4 * at + 4]
+        part_in = dot_tn(x_ref[...], dgate_up_ref[0])
+        part_out = dot_tn(hidden_ref[0], dmix_ref[...])
+        grad_in = part_in if grad_in is None else grad_in + part_in
+        grad_out = part_out if grad_out is None else grad_out + part_out
+    grads_ref[0, :width, :] = grad_in.astype(grads_ref.dtype)
+    grads_ref[0, width:, :] = grad_out.astype(grads_ref.dtype)
+
+
+def experts_grads(order, chunks):
+    count, width = chunks[0][0].shape
+    units = chunks[0][3].shape[2]
     experts = order.shape[0]
+    specs = [
+        pl.BlockSpec((count, width), lambda e, order: (0, 0)),
+        pl.BlockSpec((count, width), lambda e, order: (0, 0)),
+        pl.BlockSpec((1, count, 2 * units), lambda e, order: (order[e], 0, 0)),
+        pl.BlockSpec((1, count, units), lambda e, order: (order[e], 0, 0)),
+    ]
     return pl.pallas_call(
         experts_grads_kernel,
         grid_spec=pltpu.PrefetchScalarGridSpec(
             num_scalar_prefetch=1,
             grid=(experts,),
-            in_specs=[
-                pl.BlockSpec((count, width), lambda e, order: (0, 0)),
-                pl.BlockSpec((count, width), lambda e, order: (0, 0)),
-                pl.BlockSpec((1, count, 2 * units), lambda e, order: (order[e], 0, 0)),
-                pl.BlockSpec((1, count, units), lambda e, order: (order[e], 0, 0)),
-            ],
+            in_specs=specs * len(chunks),
             out_specs=pl.BlockSpec((1, width + units, 2 * units), lambda e, order: (e, 0, 0)),
         ),
         out_shape=jax.ShapeDtypeStruct((experts, width + units, 2 * units), jnp.bfloat16),
         compiler_params=pltpu.CompilerParams(vmem_limit_bytes=VMEM_BYTES),
-        cost_estimate=pl.CostEstimate(
-            flops=6 * count * width * units * experts,
-            bytes_accessed=experts * units * (6 * width + 6 * count) + 4 * count * width,
-            transcendentals=0,
-        ),
+        cost_estimate=SMALL_COST,
         name="experts_grads",
-    )(order, tokens, d_mix, dgate_up, hidden)
+    )(order, *[part for chunk in chunks for part in chunk])
 
 
 def widen_kernel(base_ref, piece_ref, *refs):
@@ -262,7 +257,7 @@
         out_shape=shapes,
         input_output_aliases={2 + at: at for at in range(len(held))},
         compiler_params=pltpu.CompilerParams(vmem_limit_bytes=VMEM_BYTES),
-        cost_estimate=pl.CostEstimate(flops=0, bytes_accessed=6 * piece.size, transcendentals=0),
+        cost_estimate=SMALL_COST,
         name="widen",
     )(base, piece, *held)
 
@@ -294,11 +289,7 @@
             jax.ShapeDtypeStruct((width, d_kv.shape[1] + half), jnp.bfloat16),
         ],
         compiler_params=pltpu.CompilerParams(vmem_limit_bytes=VMEM_BYTES),
-        cost_estimate=pl.CostEstimate(
-            flops=2 * width * width * (normed_all.shape[0] + 2 * normed.shape[0]),
-            bytes_accessed=14 * width * width,
-            transcendentals=0,
-        ),
+        cost_estimate=SMALL_COST,
         name="attention_grads",
     )(normed, d_query, normed_all, d_kv, attended, d_branch, small)
 
@@ -425,11 +416,7 @@
         ],
         scratch_shapes=[pltpu.VMEM((tokens, 2 * rows), jnp.float32)],
         compiler_params=pltpu.CompilerParams(vmem_limit_bytes=VMEM_BYTES),
-        cost_estimate=pl.CostEstimate(
-            flops=2 * (tokens * width * 2 * kv_width + rows * width * width + 4 * rows * tokens * width),
-            bytes_accessed=16 * tokens * width,
-            transcendentals=rows * tokens * HEADS,
-        ),
+        cost_estimate=SMALL_COST,
         name="attention_forward",
     )(bias, input_all, hidden_in, gain, w_query, w_kv, *tables, *tables_own)
 
@@ -499,11 +486,7 @@
             pltpu.VMEM((tokens, LANES), jnp.float32),
         ],
         compiler_params=pltpu.CompilerParams(vmem_limit_bytes=VMEM_BYTES),
-        cost_estimate=pl.CostEstimate(
-            flops=20 * rows * tokens * width,
-            bytes_accessed=8 * tokens * width,
-            transcendentals=rows * tokens * HEADS,
-        ),
+        cost_estimate=SMALL_COST,
         name="attention_backward",
     )(bias, query, key, value, log_norm, grad, *tables, *tables_own)
 
@@ -517,28 +500,29 @@
     return (lax.axis_index("rep") // bit) % 2
 
 
-def add_pair(left, right):
-    return (left.astype(jnp.float32) + right.astype(jnp.float32)).astype(jnp.bfloat16)
-
-
 def after(value, *others):
     return lax.optimization_barrier((value, *others))[0]
 
 
-def piece_at(parts, start, size, axis):
-    pieces = [lax.dynamic_slice_in_dim(part, start, size, axis) for part in parts]
-    if len(pieces) == 1:
-        return pieces[0]
-    return add_pair(*pieces)
+def slices_of(parts, start, size, axis):
+    return [lax.dynamic_slice_in_dim(part, start, size, axis) for part in parts]
+
+
+def add_parts(parts):
+    total = parts[0].astype(jnp.float32)
+    for part in parts[1:]:
+        total = total + part.astype(jnp.float32)
+    return total.astype(jnp.bfloat16)
 
 
 def halve(parts, bit, axis, offset=0, length=None):
     length = parts[0].shape[axis] if length is None else length
     half = length // 2
     side = side_of(bit)
-    sent = piece_at(parts, offset + (1 - side) * half, half, axis)
-    kept = piece_at(parts, offset + side * half, half, axis)
-    return sent, [kept, exchange(sent, bit)]
+    sent = slices_of(parts, offset + (1 - side) * half, half, axis)
+    sent = sent[0] if len(sent) == 1 else add_parts(sent)
+    kept = slices_of(parts, offset + side * half, half, axis)
+    return sent, kept + [exchange(sent, bit)]
 
 
 def double(block, bit, axis):
@@ -588,12 +572,6 @@
     def scatter(block):
         return lax.psum_scatter(block, "shard", scatter_dimension=0, tiled=True)
 
-    def gather_pair(left, right):
-        width = left.shape[1]
-        flat = gather(jnp.concatenate([left.reshape(1, -1), right.reshape(1, -1)], 1))
-        split = left.size
-        return flat[:, :split].reshape(-1, width), flat[:, split:].reshape(-1, right.shape[1])
-
     kv_width = w_key.shape[1]
     query_width = w_query.shape[1]
     half_width = w_output.shape[1] // 2
@@ -625,14 +603,23 @@
     output_half = lax.dynamic_slice_in_dim(w_output, side_of(near) * near_rows, near_rows, 0)
     output_half = lax.all_gather(after(output_half, input_all), "shard", axis=0)
     expert_count = router.shape[1]
-    small_parts = [attn_norm[:, None], ffn_norm[:, None], router]
-    small_full, routes_all = gather_pair(
-        jnp.concatenate(small_parts, 1), routes.astype(jnp.bfloat16)
-    )
+    valid_float = valid_mask.astype(jnp.float32)
+    small_parts = [
+        jnp.concatenate([attn_norm[:, None], ffn_norm[:, None], router], 1).reshape(1, -1),
+        routes.astype(jnp.bfloat16).reshape(1, -1),
+        jnp.sum(valid_float).astype(jnp.bfloat16).reshape(1, 1),
+    ]
+    small_all = gather(jnp.concatenate(small_parts, 1))
+    small_size, routes_size = small_parts[0].size, small_parts[1].size
+    small_full = small_all[:, :small_size].reshape(-1, 2 + expert_count)
+    routes_all = small_all[:, small_size : small_size + routes_size]
+    valid_count = jnp.broadcast_to(jnp.sum(small_all[:, -1].astype(jnp.float32)), (8, LANES))
+    for bit in bits:
+        valid_count = valid_count + exchange(valid_count, bit)
+    valid_count = valid_count[0, 0]
     gain_attn, gain_ffn = small_full[:, 0], small_full[:, 1]
     router_full = small_full[:, 2:]
     gain_attn = gain_attn.astype(jnp.float32)
-    valid_float = valid_mask.astype(jnp.float32)
     input_float = hidden_in.astype(jnp.float32)
     scale_attn = rms_scale(input_float)
     all_float = input_all.astype(jnp.float32)
@@ -648,35 +635,51 @@
     normed_ffn = (middle * scale_ffn * gain_ffn).astype(jnp.bfloat16)
     own_experts = w_in.shape[0]
     expert_ids = jnp.arange(expert_count, dtype=jnp.bfloat16)
-    valid_count = lax.psum(jnp.sum(after(valid_float, normed_ffn)), ("rep", "shard"))
-    tokens_all = gather(normed_ffn)
-    logits_all = dot_nn(tokens_all, router_full)
-    chosen_all = jnp.any(routes_all[..., None] == expert_ids, 1)
-    masked = jnp.where(chosen_all, logits_all, very_low)
-    raised = jnp.where(chosen_all, jnp.exp(masked - jnp.max(masked, -1, keepdims=True)), 0.0)
-    gates_all = raised / jnp.sum(raised, -1, keepdims=True)
-    gates_own = lax.dynamic_slice_in_dim(gates_all, shard_at * own_experts, own_experts, 1)
-    gates_own = jnp.pad(gates_own, ((0, 0), (0, LANES - own_experts)))
-    gates = lax.dynamic_slice_in_dim(gates_all, shard_at * row_count, row_count, 0)
-    gates_own = after(gates_own, valid_count)
-    mix_part, gate_up, hidden_gated = experts_forward(tokens_all, gates_own, w_in, w_out)
-    mixture = scatter(mix_part).astype(jnp.float32)
-    result_f = middle + resid_mult * mixture
-    deviation = result_f - teacher.astype(jnp.float32)
-    d_result = valid_float[:, None] * deviation * (all_tokens / (2.0 * valid_count))
-    d_mix = (resid_mult * d_result).astype(jnp.bfloat16)
-    d_mix_all = gather(d_mix)
-    own_loss = jnp.sum(valid_float[:, None] * deviation * deviation)
-    loss_sum = lax.psum(after(own_loss, d_mix), ("rep", "shard"))
-    loss = loss_sum / (model_width * valid_count)
-    gates_own = after(gates_own, loss_sum)
-    d_rows_part, d_gate_up, d_gates_own = experts_backward(
-        d_mix_all, gates_own, gate_up, w_in, w_out
-    )
-    d_rows = scatter(d_rows_part).astype(jnp.float32)
-    d_gates = lax.all_to_all(
-        d_gates_own[:, :own_experts], "shard", split_axis=0, concat_axis=1, tiled=True
-    )
+    chunk_rows = row_count // CHUNKS
+    spans = [slice(at * chunk_rows, (at + 1) * chunk_rows) for at in range(CHUNKS)]
+    tokens_in = [gather(normed_ffn[span]) for span in spans]
+    routes_all = routes_all.reshape(shard_count, row_count, -1)
+    gates, forward = [], []
+    for span, tokens in zip(spans, tokens_in):
+        logits = dot_nn(tokens, router_full)
+        routes_part = routes_all[:, span].reshape(shard_count * chunk_rows, -1)
+        chosen = jnp.any(routes_part[..., None] == expert_ids, 1)
+        masked = jnp.where(chosen, logits, very_low)
+        raised = jnp.where(chosen, jnp.exp(masked - jnp.max(masked, -1, keepdims=True)), 0.0)
+        gates_part = raised / jnp.sum(raised, -1, keepdims=True)
+        gates_own = lax.dynamic_slice_in_dim(gates_part, shard_at * own_experts, own_experts, 1)
+        gates_own = jnp.pad(gates_own, ((0, 0), (0, LANES - own_experts)))
+        gates.append(lax.dynamic_slice_in_dim(gates_part, shard_at * chunk_rows, chunk_rows, 0))
+        forward.append((gates_own, *experts_forward(tokens, gates_own, w_in, w_out)))
+    gates = jnp.concatenate(gates, 0)
+    results, d_results, d_mix_out, d_mix_in, own_loss = [], [], [], [], 0.0
+    for span, (_, mix_part, _, _) in zip(spans, forward):
+        mixture = scatter(mix_part)
+        if d_mix_out:
+            mixture = after(mixture, d_mix_out[-1])
+        mixture = mixture.astype(jnp.float32)
+        result_part = middle[span] + resid_mult * mixture
+        deviation = result_part - teacher[span].astype(jnp.float32)
+        masked = valid_float[span, None] * deviation
+        d_result = masked * (all_tokens / (2.0 * valid_count))
+        results.append(result_part.astype(jnp.bfloat16))
+        d_results.append(d_result)
+        d_mix_out.append((resid_mult * d_result).astype(jnp.bfloat16))
+        d_mix_in.append(gather(d_mix_out[-1]))
+        own_loss = own_loss + jnp.sum(masked * deviation)
+    d_result = jnp.concatenate(d_results, 0)
+    d_rows, d_gates, backward = [], [], []
+    for d_mix, (gates_own, _, gate_up, hidden_gated), tokens in zip(d_mix_in, forward, tokens_in):
+        d_rows_part, d_gate_up, d_gates_part = experts_backward(
+            d_mix, gates_own, gate_up, w_in, w_out
+        )
+        d_rows.append(scatter(d_rows_part))
+        d_gates.append(d_gates_part[:, :own_experts].reshape(shard_count, chunk_rows, own_experts))
+        backward.append((tokens, d_mix, d_gate_up, hidden_gated))
+    d_rows_in = d_rows
+    d_rows = jnp.concatenate(d_rows, 0).astype(jnp.float32)
+    d_gates = jnp.concatenate(d_gates, 1).reshape(shard_count * row_count, own_experts)
+    d_gates = lax.all_to_all(d_gates, "shard", split_axis=0, concat_axis=1, tiled=True)
     kept_experts = own_experts // 2
     grad_rows = model_width + w_out.shape[1]
     flat_rows = kept_experts * grad_rows
@@ -684,12 +687,19 @@
     order = jnp.arange(kept_experts, dtype=jnp.int32)
     order_sent = order + (1 - side) * kept_experts
     order_kept = order + side * kept_experts
-    sent = experts_grads(order_sent, tokens_all, d_mix_all, d_gate_up, hidden_gated)
-    other = exchange(sent, near).reshape(flat_rows, -1)
-    kept = experts_grads(after(order_kept, sent), tokens_all, d_mix_all, d_gate_up, hidden_gated)
-    kept = kept.reshape(flat_rows, -1)
-    moe_sent_first, moe_first = halve([kept, other], far[0], 0, 0, flat_rows // 2)
-    moe_sent_second, moe_second = halve([kept, other], far[-1], 0, flat_rows // 2, flat_rows // 2)
+    flat = (grad_rows, w_in.shape[2])
+    sent = [experts_grads(order_sent[at : at + 1], backward).reshape(flat) for at in range(kept_experts)]
+    other = [exchange(part, near) for part in sent]
+    kept = experts_grads(after(order_kept, *sent, d_rows_in[0]), backward).reshape(flat_rows, -1)
+    if kept_experts > 1:
+        kept_first, kept_second = kept[: flat_rows // 2], kept[flat_rows // 2 :]
+        other_first = jnp.concatenate(other[: kept_experts // 2], 0)
+        other_second = jnp.concatenate(other[kept_experts // 2 :], 0)
+    else:
+        kept_first, kept_second = kept[: flat_rows // 2], kept[flat_rows // 2 :]
+        other_first, other_second = other[0][: flat_rows // 2], other[0][flat_rows // 2 :]
+    moe_sent_first, moe_first = halve([kept_first, other_first], far[0], 0)
+    moe_sent_second, moe_second = halve([kept_second, other_second], far[-1], 0)
     d_rows = after(d_rows, moe_sent_first, moe_sent_second)
     d_logits = (gates * (d_gates - jnp.sum(gates * d_gates, -1, keepdims=True))).astype(
         jnp.bfloat16
@@ -705,14 +715,15 @@
     query_grad_rows, kv_grad_all = attention_backward(
         bias, query_rows, keys_all, values_all, log_norm, d_attended, tables, tables_own
     )
+    query_grad_rows, kv_grad_all = lax.optimization_barrier(
+        (query_grad_rows, kv_grad_all, moe_first[-1], moe_second[-1])
+    )[:2]
     d_normed_kv = dot_nt(kv_grad_all, kv_full)
     d_normed_query = dot_nt(query_grad_rows, query_full)
-    d_normed_attn = scatter(d_normed_kv.astype(jnp.bfloat16)).astype(jnp.float32) + d_normed_query
     grad_gain_attn = jnp.sum(d_normed_kv * all_float * rms_scale(all_float), 0) + jnp.sum(
         d_normed_query * input_float * scale_attn, 0
     )
-    d_norm_in, _ = norm_back(d_normed_attn, input_float, scale_attn, gain_attn)
-    d_input = d_middle + d_norm_in
+    kv_scattered = scatter(d_normed_kv.astype(jnp.bfloat16))
     grad_small = jnp.concatenate(
         [
             grad_gain_attn[:, None],
@@ -726,13 +737,31 @@
     first, second = attention_grads(
         normed_attn, query_grad_rows, normed_all, kv_grad_all, attended, d_branch, grad_small
     )
+    d_normed_query = after(d_normed_query, first, second)
+    d_normed_attn = kv_scattered.astype(jnp.float32) + d_normed_query
+    d_norm_in, _ = norm_back(d_normed_attn, input_float, scale_attn, gain_attn)
+    d_input = d_middle + d_norm_in
+    for bit_first, bit_second in zip(far[1:], far[::-1][1:]):
+        _, moe_first = halve(moe_first, bit_first, 0)
+        _, moe_second = halve(moe_second, bit_second, 0)
+    first, second = lax.optimization_barrier((first, second, moe_first[-1], moe_second[-1]))[:2]
+    moe_first, moe_second = add_parts(moe_first), add_parts(moe_second)
     first = [first.reshape(shard_count, own_rows, -1)]
     second = [second.reshape(shard_count, own_rows, -1)]
-    for bit_first, bit_second in zip([near] + far, [near] + far[::-1]):
+    _, first = halve(first, near, 1)
+    _, second = halve(second, near, 1)
+    for bit_first, bit_second in zip(far[:0:-1], far[:-1]):
+        moe_first = double(moe_first, bit_first, 0)
+        moe_second = double(moe_second, bit_second, 0)
+    for bit_first, bit_second in zip(far, far[::-1]):
         _, first = halve(first, bit_first, 1)
         _, second = halve(second, bit_second, 1)
+    moe_first = after(moe_first, first[-1], second[-1])
+    moe_second = after(moe_second, first[-1], second[-1])
+    moe_first = double(moe_first, far[0], 0)
+    moe_second = double(moe_second, far[-1], 0)
     split_at = first[0].shape[2]
-    joined = jnp.concatenate([add_pair(*first), add_pair(*second)], 2)
+    joined = jnp.concatenate([add_parts(first), add_parts(second)], 2)
     joined = lax.psum_scatter(joined, "shard", scatter_dimension=0)
     first, second = joined[:, :split_at], joined[:, split_at:]
     for bit_first, bit_second in zip(far[::-1] + [near], far + [near]):
@@ -746,13 +775,6 @@
         [first[:, query_width : query_width + half_width], second[:, 2 * kv_width :]], 1
     )
     sum_small = first[:, query_width + half_width :]
-    for bit_first, bit_second in zip(far[1:], far[::-1][1:]):
-        _, moe_first = halve(moe_first, bit_first, 0)
-        _, moe_second = halve(moe_second, bit_second, 0)
-    moe_first, moe_second = add_pair(*moe_first), add_pair(*moe_second)
-    for bit_first, bit_second in zip(far[::-1], far):
-        moe_first = double(moe_first, bit_first, 0)
-        moe_second = double(moe_second, bit_second, 0)
     if kept_experts % 2 == 0:
         pieces = [moe_first, moe_second]
     else:
@@ -766,8 +788,17 @@
             held = widen(jnp.reshape(base, (1,)), piece, model_width, own_experts, held)
             base = base + piece.shape[0]
     sum_in, sum_out = held
+    loss_sum = jnp.broadcast_to(own_loss, (8, LANES))
+    for bit in bits:
+        loss_sum = loss_sum + exchange(loss_sum, bit)
+    step = 1
+    while step < shard_count:
+        pairs = [(at, at ^ step) for at in range(shard_count)]
+        loss_sum = loss_sum + lax.ppermute(loss_sum, "shard", pairs)
+        step = 2 * step
+    loss = loss_sum[0, 0] / (model_width * valid_count)
     return (
-        result_f.astype(jnp.bfloat16),
+        jnp.concatenate(results, 0),
         loss,
         d_input,
         sum_small[:, 0],

time: 632 us -> 572 us (0.905)
  blocking collectives: 117 us -> 34.3 us
  local copies, waits for them, and re-layouts: 35.3 us -> 43.9 us
  Pallas kernels: 143 us -> 151 us
  starting transfers between devices: 29.5 us -> 36.6 us
    psum x2 -> x0, blocking collectives: 83.2 us -> none  [the longest x1 42.3 us: body(): loss_sum = lax.psum(after(own_loss, d_mix), ('rep', 'shard'))]
    all_gather x3 -> x5, waiting for transfers between devices: 14.7 us -> 79.1 us  [gather(): return lax.all_gather(block, 'shard', axis=0, tiled=True)]
    reduce_scatter x3 -> x5, waiting for transfers between devices: 65.4 us -> 26.7 us  [scatter(): return lax.psum_scatter(block, 'shard', scatter_dimension=0, tiled=True)]
    ppermute x30 -> x37, waiting for transfers between devices: 117 us -> 78.6 us  [exchange(): return lax.ppermute(block, 'rep', [(at, at ^ bit) for at in range(count)])]
    ppermute x30 -> x37, starting transfers between devices: 25.5 us -> 31.7 us  [exchange(): return lax.ppermute(block, 'rep', [(at, at ^ bit) for at in range(count)])]
    pallas_call x2 -> x3, Pallas kernels: 25 us -> 30.4 us  [experts_grads(): pl.pallas_call(experts_grads_kernel, grid_spec=pltpu.PrefetchScalarGridSp...]
    convert_element_type x14 -> x16, other arithmetic: 27.9 us -> 30.5 us  [the longest x12 24.2 us: add_parts(): return total.astype(jnp.bfloat16)]
    pallas_call x1 -> x2, Pallas kernels: 24.7 us -> 26.1 us  [experts_forward(): pl.pallas_call(experts_forward_kernel, grid=(experts,), in_specs=[pl.Bloc...]
  transfers between devices with their start and end apart: 39 -> 52, of which waited for: 21 -> 29; matrix products, arithmetic and copies ran while one was open for 13% -> 21% of each run, Pallas kernels for 9% -> 26%
where the time goes in v3:
time: 572 us; the launch traced here: 563 us
  waiting for transfers between devices  195 us (34%)
  Pallas kernels  151 us (26%)
  other arithmetic  68.4 us (12%)
  local copies, waits for them, and re-layouts  43.9 us (8%)
  starting transfers between devices  36.6 us (6%)
  blocking collectives  34.3 us (6%)
  between operations  20.3 us (4%)
  matrix products  13.2 us (2%)
    all_gather x5, waiting for transfers between devices, gather(): return lax.all_gather(block, 'shard', axis=0, tiled=True)  79.1 us
    ppermute x37, waiting for transfers between devices, exchange(): return lax.ppermute(block, 'rep', [(at, at ^ bit) for at in range(count)])  78.6 us
    ppermute x37, starting transfers between devices, exchange(): return lax.ppermute(block, 'rep', [(at, at ^ bit) for at in range(count)])  31.7 us
    pallas_call x3, Pallas kernels, experts_grads(): pl.pallas_call(experts_grads_kernel, grid_spec=pltpu.PrefetchScalarGridSp...  30.4 us
    pallas_call x2, Pallas kernels, experts_backward(): pl.pallas_call(experts_backward_kernel, grid=(experts,), in_specs=[pl.Blo...  30.1 us
    reduce_scatter x5, waiting for transfers between devices, scatter(): return lax.psum_scatter(block, 'shard', scatter_dimension=0, tiled=True)  26.7 us
    pallas_call x2, Pallas kernels, experts_forward(): pl.pallas_call(experts_forward_kernel, grid=(experts,), in_specs=[pl.Bloc...  26.1 us
    convert_element_type x12, other arithmetic, add_parts(): return total.astype(jnp.bfloat16)  24.2 us
  transfers between devices with their start and end apart: 52, of which 29 were waited for; matrix products, arithmetic and copies ran while one was open for 21% of the time, Pallas kernels for 26%

profile of v3, /device:TPU:0, one launch (start us, length us, event | category | flops | bytes accessed | tf_op | source)
XLA Modules:
  0.0 562.5 jit_solution(16516386908852176639)
XLA Ops:
  9.0 20.3 %all-gather.1 = bf16[128,2048]{1,0:T(8,128)(2,1)S(1)} all-gather(bf16[32,2048]{1,0:T(8,128)(2,1)S(1)} %pad_maximum_fusion.20), channel_id=3, replica_groups=mesh['rep'=8,'shard'=4] {'shard'}, dimensions={0}, use_global_device_ids=true | all-gather | bytes 655360 | tf_op jit(solution)/shard_map/all_gather | solution.py:590
  41.7 14.0 %all-gather.2 = bf16[4,1,6657]{2,1,0:T(2,128)(2,1)S(1)} all-gather(bf16[1,1,6657]{2,1,0:T(2,128)(2,1)S(1)} %maximum_bitcast_fusion.2), channel_id=1, replica_groups=mesh['rep'=8,'shard'=4] {'shard'}, dimensions={0}, use_global_device_ids=true | all-gather | bytes 66570 | tf_op jit(solution)/shard_map/all_gather | solution.py:570
  57.1 2.4 pad_maximum_fusion.5
  59.5 2.4 all-gather.10.cloned.1.call-done.all_ref
  74.2 17.6 %attention_forward.1 = (bf16[1024,1024]{1,0:T(8,128)(2,1)}, bf16[256,1024]{1,0:T(8,128)(2,1)}, bf16[1024,512]{1,0:T(8,128)(2,1)}, bf16[1024,512]{1,0:T(8,128)(2,...) custom-call(f32[4]{0:T(128)} %compare_select_fusion.bias_ref, bf16[1024,1024]{1,0:T(8,128)(2,1)} %all-gather.10.cloned.1.call-done.all_ref, ...), custom_call_target="tpu_custom_call" | custom-call | flops 1000000 | bytes 100000 | tf_op jit(solution)/shard_map/attention_forward/pallas_call | solution.py:405
  98.8 25.4 %all-gather.12.cloned.1.call-done.x_ref.refs_0_ = bf16[512,1024]{1,0:T(8,128)(2,1)} async-done(((bf16[128,1024]{1,0:T(8,128)(2,1)}), bf16[512,1024]{1,0:T(8,128)(2,1)}) %all-gather.12.cloned.1.call-update) | async-done | bytes 1048592 | tf_op jit(solution)/shard_map/all_gather | solution.py:570
  127.4 13.1 %experts_forward.2 = (bf16[512,1024]{1,0:T(8,128)(2,1)}, f32[4,512,1024]{2,1,0:T(8,128)}, bf16[4,512,512]{2,1,0:T(8,128)(2,1)}) custom-call(bf16[512,1024]{1,0:T(8,128)(2,1)} %all-gather.12.cloned.1.call-done.x_ref.refs_0_, f32[512,128]{1,0:T(8,128)} %pad.7.gate_ref, bf16[4,1024,1024]{2,1,0:T(8,128)(2,1)} %in_ref.7, bf16[4,512,1024]{2,1,0:T(8,128)(2,1)} %out_ref.7), custom_call_target="tpu_custom_call" | custom-call | flops 1000000 | bytes 100000 | tf_op jit(solution)/shard_map/experts_forward/pallas_call | solution.py:102
  140.9 12.8 %all-gather.14.cloned.1.call-done.x_ref.refs_4_ = bf16[512,1024]{1,0:T(8,128)(2,1)} async-done(((bf16[128,1024]{1,0:T(8,128)(2,1)}), bf16[512,1024]{1,0:T(8,128)(2,1)}) %all-gather.14.cloned.1.call-update) | async-done | bytes 1048592 | tf_op jit(solution)/shard_map/all_gather | solution.py:570
  156.9 13.0 %experts_forward.3 = (bf16[512,1024]{1,0:T(8,128)(2,1)}, f32[4,512,1024]{2,1,0:T(8,128)}, bf16[4,512,512]{2,1,0:T(8,128)(2,1)}) custom-call(bf16[512,1024]{1,0:T(8,128)(2,1)} %all-gather.14.cloned.1.call-done.x_ref.refs_4_, f32[512,128]{1,0:T(8,128)} %pad.8.gate_ref, bf16[4,1024,1024]{2,1,0:T(8,128)(2,1)} %in_ref.7, bf16[4,512,1024]{2,1,0:T(8,128)(2,1)} %out_ref.7), custom_call_target="tpu_custom_call" | custom-call | flops 1000000 | bytes 100000 | tf_op jit(solution)/shard_map/experts_forward/pallas_call | solution.py:102
  184.7 26.4 %reduce-scatter.9.cloned.1.call-done = bf16[128,1024]{1,0:T(8,128)(2,1)} async-done(((bf16[512,1024]{1,0:T(8,128)(2,1)}), bf16[128,1024]{1,0:T(8,128)(2,1)}) %reduce-scatter.9.cloned.1.call-update) | async-done | bytes 262160 | tf_op jit(solution)/shard_map/reduce_scatter | solution.py:573
  211.2 3.2 multiply_convert_fusion.2
  214.4 24.9 %all-gather.16.cloned.1.call-done.dmix_ref.refs_1_ = bf16[512,1024]{1,0:T(8,128)(2,1)} async-done(((bf16[128,1024]{1,0:T(8,128)(2,1)}), bf16[512,1024]{1,0:T(8,128)(2,1)}) %all-gather.16.cloned.1.call-update) | async-done | bytes 1048592 | tf_op jit(solution)/shard_map/all_gather | solution.py:570
  239.3 15.1 %experts_backward.2 = (bf16[512,1024]{1,0:T(8,128)(2,1)}, bf16[4,512,1024]{2,1,0:T(8,128)(2,1)}, f32[512,128]{1,0:T(8,128)}) custom-call(bf16[512,1024]{1,0:T(8,128)(2,1)} %all-gather.16.cloned.1.call-done.dmix_ref.refs_1_, f32[512,128]{1,0:T(8,128)} %pad.7.gate_ref, f32[4,512,1024]{2,1,0:T(8,128)} %get-tuple-element.62.gate_up_ref, ...), custom_call_target="tpu_custom_call" | custom-call | flops 1000000 | bytes 100000 | tf_op jit(solution)/shard_map/experts_backward/pallas_call | solution.py:165
  255.5 13.4 %all-gather.18.cloned.1.call-done.dmix_ref.refs_5_ = bf16[512,1024]{1,0:T(8,128)(2,1)} async-done(((bf16[128,1024]{1,0:T(8,128)(2,1)}), bf16[512,1024]{1,0:T(8,128)(2,1)}) %all-gather.18.cloned.1.call-update) | async-done | bytes 1048592 | tf_op jit(solution)/shard_map/all_gather | solution.py:570
  268.9 15.0 %experts_backward.3 = (bf16[512,1024]{1,0:T(8,128)(2,1)}, bf16[4,512,1024]{2,1,0:T(8,128)(2,1)}, f32[512,128]{1,0:T(8,128)}) custom-call(bf16[512,1024]{1,0:T(8,128)(2,1)} %all-gather.18.cloned.1.call-done.dmix_ref.refs_5_, f32[512,128]{1,0:T(8,128)} %pad.8.gate_ref, f32[4,512,1024]{2,1,0:T(8,128)} %get-tuple-element.64.gate_up_ref, ...), custom_call_target="tpu_custom_call" | custom-call | flops 1000000 | bytes 100000 | tf_op jit(solution)/shard_map/experts_backward/pallas_call | solution.py:165
  283.9 8.9 %experts_grads.3 = bf16[1,1536,1024]{2,1,0:T(8,128)(2,1)} custom-call(s32[1]{0:T(128)} %get-tuple-element.207.order_ref, bf16[512,1024]{1,0:T(8,128)(2,1)} %all-gather.12.cloned.1.call-done.x_ref.refs_0_, bf16[512,1024]{1,0:T(8,128)(2,1)} %all-gather.16.cloned.1.call-done.dmix_ref.refs_1_, bf16[4,512,1024]{2,1,0:T(8,128)(2,1)} %get-tuple-element.66.refs_2_, ...), custom_call_target="tpu_custom_call" | custom-call | flops 1000000 | bytes 100000 | tf_op jit(solution)/shard_map/experts_grads/pallas_call | solution.py:217
  292.8 8.8 %experts_grads.4 = bf16[1,1536,1024]{2,1,0:T(8,128)(2,1)} custom-call(s32[1]{0:T(128)} %get-tuple-element.206.order_ref, bf16[512,1024]{1,0:T(8,128)(2,1)} %all-gather.12.cloned.1.call-done.x_ref.refs_0_, bf16[512,1024]{1,0:T(8,128)(2,1)} %all-gather.16.cloned.1.call-done.dmix_ref.refs_1_, bf16[4,512,1024]{2,1,0:T(8,128)(2,1)} %get-tuple-element.66.refs_2_, ...), custom_call_target="tpu_custom_call" | custom-call | flops 1000000 | bytes 100000 | tf_op jit(solution)/shard_map/experts_grads/pallas_call | solution.py:217
  308.9 3.3 all-to-all-start
  312.5 5.3 all-to-all-done
  317.9 12.7 %experts_grads.5 = bf16[2,1536,1024]{2,1,0:T(8,128)(2,1)} custom-call(s32[2]{0:T(128)} %iota_add_fusion.1.order_ref, bf16[512,1024]{1,0:T(8,128)(2,1)} %all-gather.12.cloned.1.call-done.x_ref.refs_0_, bf16[512,1024]{1,0:T(8,128)(2,1)} %all-gather.16.cloned.1.call-done.dmix_ref.refs_1_, bf16[4,512,1024]{2,1,0:T(8,128)(2,1)} %get-tuple-element.66.refs_2_, ...), custom_call_target="tpu_custom_call" | custom-call | flops 1000000 | bytes 100000 | tf_op jit(solution)/shard_map/experts_grads/pallas_call | solution.py:217
  330.6 3.6 fusion.40
  334.2 4.4 fusion.4
  340.1 3.3 fusion.3
  349.6 3.0 multiply_convert_fusion
  354.1 18.1 %attention_backward.1 = (bf16[256,1024]{1,0:T(8,128)(2,1)}, bf16[1024,1024]{1,0:T(8,128)(2,1)}) custom-call(f32[4]{0:T(128)} %compare_select_fusion.bias_ref, bf16[256,1024]{1,0:T(8,128)(2,1)} %get-tuple-element.74.query_ref, bf16[1024,512]{1,0:T(8,128)(2,1)} %get-tuple-element.75.key_ref, bf16[1024,512]{1,0:T(8,128)(2,1)} %get-tuple-element.76.value_ref, ...), custom_call_target="tpu_custom_call" | custom-call | flops 1000000 | bytes 100000 | tf_op jit(solution)/shard_map/attention_backward/pallas_call | solution.py:474
  374.5 3.2 fusion.14
  379.1 3.0 fusion.12
  384.5 3.8 fusion.41
  389.6 9.1 %attention_grads.1 = (bf16[1024,1664]{1,0:T(8,128)(2,1)}, bf16[1024,1536]{1,0:T(8,128)(2,1)}) custom-call(bf16[256,1024]{1,0:T(8,128)(2,1)} %constant_dynamic-slice_fusion.2.normed_ref, bf16[256,1024]{1,0:T(8,128)(2,1)} %get-tuple-element.81.dquery_ref, bf16[1024,1024]{1,0:T(8,128)(2,1)} %get-tuple-element.82.all_ref, ...), custom_call_target="tpu_custom_call" | custom-call | flops 1000000 | bytes 100000 | tf_op jit(solution)/shard_map/attention_grads/pallas_call | solution.py:283
  399.9 2.7 constant_dynamic-slice_fusion
  402.6 2.8 constant_dynamic-slice_fusion.1
  414.1 2.3 collective-permute-done.12
  417.4 3.7 collective-permute-done.13
  421.0 2.6 fusion.7
  427.3 2.6 fusion.10
  436.0 21.5 %collective-permute-done.25 = bf16[4,64,1536]{2,1,0:T(8,128)(2,1)S(1)} collective-permute-done((bf16[4,64,1536]{2,1,0:T(8,128)(2,1)S(1)}, bf16[4,64,1536]{2,1,0:T(8,128)(2,1)S(1)}, u32[]{:S(2)}, u32[]{:S(2)}) %collective-permute-start.25) | collective-permute-done | bytes 786464 | tf_op jit(solution)/shard_map/ppermute | solution.py:496
  461.3 7.4 %collective-permute-done.22 = bf16[4,64,1664]{2,1,0:T(8,128)(2,1)S(1)} collective-permute-done((bf16[4,64,1664]{2,1,0:T(8,128)(2,1)S(1)}, bf16[4,64,1664]{2,1,0:T(8,128)(2,1)S(1)}, u32[]{:S(2)}, u32[]{:S(2)}) %collective-permute-start.22) | collective-permute-done | bytes 852000 | tf_op jit(solution)/shard_map/ppermute | solution.py:496
  470.1 3.2 collective-permute-done.26
  474.6 6.4 %collective-permute-done.23 = bf16[4,32,1664]{2,1,0:T(8,128)(2,1)S(1)} collective-permute-done((bf16[4,32,1664]{2,1,0:T(8,128)(2,1)S(1)}, bf16[4,32,1664]{2,1,0:T(8,128)(2,1)S(1)}, u32[]{:S(2)}, u32[]{:S(2)}) %collective-permute-start.23) | collective-permute-done | bytes 426016 | tf_op jit(solution)/shard_map/ppermute | solution.py:496
  486.9 3.9 maximum_bitcast_fusion.1
  493.7 15.0 %collective-permute-done.37 = bf16[768,1024]{1,0:T(8,128)(2,1)} collective-permute-done((bf16[768,1024]{1,0:T(8,128)(2,1)}, bf16[768,1024]{1,0:T(8,128)(2,1)}, u32[]{:S(2)}, u32[]{:S(2)}) %collective-permute-start.37) | collective-permute-done | bytes 1572896 | tf_op jit(solution)/shard_map/ppermute | solution.py:496
  508.7 2.8 bitcast_dynamic-update-slice_fusion.piece_ref
  511.4 2.7 bitcast_dynamic-update-slice_fusion.1.piece_ref
  514.6 4.9 widen.4
  519.5 4.9 widen.5
  533.1 3.0 collective-permute-done.31
  544.3 4.9 widen.6
  549.2 4.9 widen.7
  (319 shorter events, 130.6 us)
Async XLA Ops:
  7.2 54.7 %all-gather.10.cloned.1.call-start = ((), (), s32[]{:S(2)}) async-start(), calls=%async_computation.7 | async-start | bytes 2621440 | tf_op jit(solution)/shard_map/all_gather | solution.py:570
  8.0 83.9 %all-gather.20.cloned.1.call-start = ((), (), s32[]{:S(2)}) async-start(), calls=%async_computation.18 | async-start | bytes 1310720 | tf_op jit(solution)/shard_map/all_gather | solution.py:604
  29.4 7.9 %collective-permute-start.3 = (bf16[4,32,1024]{2,1,0:T(8,128)(2,1)S(1)}, bf16[4,32,1024]{2,1,0:T(8,128)(2,1)}, u32[]{:S(2)}, u32[]{:S(2)}) collective-permute-start(bf16[4,32,1024]{2,1,0:T(8,128)(2,1)S(1)} %get-tuple-element.197), channel_id=1, source_target_pairs={{0,16},{4,20},{8,24},{12,28},{16,0},{20,4},{24,8},{28,12},{1,17},{... | collective-permute-start | bytes 786440 | tf_op jit(solution)/shard_map/ppermute | solution.py:496
  31.0 8.1 %collective-permute-start = (bf16[4,32,1024]{2,1,0:T(8,128)(2,1)S(1)}, bf16[4,32,1024]{2,1,0:T(8,128)(2,1)}, u32[]{:S(2)}, u32[]{:S(2)}) collective-permute-start(bf16[4,32,1024]{2,1,0:T(8,128)(2,1)S(1)} %get-tuple-element.198), channel_id=1, source_target_pairs={{0,8},{4,12},{8,0},{12,4},{16,24},{20,28},{24,16},{28,20},{1,9},{5... | collective-permute-start | bytes 786440 | tf_op jit(solution)/shard_map/ppermute | solution.py:496
  38.3 23.8 %collective-permute-start.4 = (bf16[4,64,1024]{2,1,0:T(8,128)(2,1)S(1)}, bf16[4,64,1024]{2,1,0:T(8,128)(2,1)}, u32[]{:S(2)}, u32[]{:S(2)}) collective-permute-start(bf16[4,64,1024]{2,1,0:T(8,128)(2,1)S(1)} %constant_dynamic-update-slice_fusion.10), channel_id=1, source_target_pairs={{0,8},{4,12},{8,0},{12,4},{16,24},{20,28},{24,16},{28,20},{1,9},{5... | collective-permute-start | bytes 1572872 | tf_op jit(solution)/shard_map/ppermute | solution.py:496
  40.8 22.5 %collective-permute-start.1 = (bf16[4,64,1024]{2,1,0:T(8,128)(2,1)}, bf16[4,64,1024]{2,1,0:T(8,128)(2,1)}, u32[]{:S(2)}, u32[]{:S(2)}) collective-permute-start(bf16[4,64,1024]{2,1,0:T(8,128)(2,1)} %constant_dynamic-update-slice_fusion.13), channel_id=1, source_target_pairs={{0,16},{4,20},{8,24},{12,28},{16,0},{20,4},{24,8},{28,12},{1,17},{... | collective-permute-start | bytes 1572872 | tf_op jit(solution)/shard_map/ppermute | solution.py:496
  61.9 62.3 %all-gather.12.cloned.1.call-start = ((), (), s32[]{:S(2)}) async-start(), calls=%async_computation.8 | async-start | bytes 1310720 | tf_op jit(solution)/shard_map/all_gather | solution.py:570
  63.2 8.2 %collective-permute-start.5 = (bf16[4,128,1024]{2,1,0:T(8,128)(2,1)S(1)}, bf16[4,128,1024]{2,1,0:T(8,128)(2,1)S(1)}, u32[]{:S(2)}, u32[]{:S(2)}) collective-permute-start(bf16[4,128,1024]{2,1,0:T(8,128)(2,1)S(1)} %constant_dynamic-update-slice_fusion.9), channel_id=1, source_target_pairs={{0,4},{4,0},{8,12},{12,8},{16,20},{20,16},{24,28},{28,24},{1,5},{5... | collective-permute-start | bytes 3145736 | tf_op jit(solution)/shard_map/ppermute | solution.py:496
  65.2 6.4 %collective-permute-start.2 = (bf16[4,128,1024]{2,1,0:T(8,128)(2,1)}, bf16[4,128,1024]{2,1,0:T(8,128)(2,1)S(1)}, u32[]{:S(2)}, u32[]{:S(2)}) collective-permute-start(bf16[4,128,1024]{2,1,0:T(8,128)(2,1)} %constant_dynamic-update-slice_fusion.12), channel_id=1, source_target_pairs={{0,4},{4,0},{8,12},{12,8},{16,20},{20,16},{24,28},{28,24},{1,5},{5... | collective-permute-start | bytes 3145736 | tf_op jit(solution)/shard_map/ppermute | solution.py:496
  91.9 2.9 collective-permute-start.6
  97.3 56.4 %all-gather.14.cloned.1.call-start = ((), (), s32[]{:S(2)}) async-start(), calls=%async_computation.10 | async-start | bytes 1310720 | tf_op jit(solution)/shard_map/all_gather | solution.py:570
  97.9 84.6 %reduce-scatter.7.cloned.1.call-start = ((), (), s32[]{:S(2)}) async-start(), calls=%async_computation.9 | async-start | bytes 1310720 | tf_op jit(solution)/shard_map/reduce_scatter | solution.py:573
  140.5 70.6 %reduce-scatter.9.cloned.1.call-start = ((), (), s32[]{:S(2)}) async-start(), calls=%async_computation.11 | async-start | bytes 1310720 | tf_op jit(solution)/shard_map/reduce_scatter | solution.py:573
  169.9 69.4 %all-gather.16.cloned.1.call-start = ((), (), s32[]{:S(2)}) async-start(), calls=%async_computation.12 | async-start | bytes 1310720 | tf_op jit(solution)/shard_map/all_gather | solution.py:570
  173.1 3.7 collective-permute-start.8
  177.4 3.7 collective-permute-start.9
  184.7 84.3 %all-gather.18.cloned.1.call-start = ((), (), s32[]{:S(2)}) async-start(), calls=%async_computation.14 | async-start | bytes 1310720 | tf_op jit(solution)/shard_map/all_gather | solution.py:570
  214.4 103.5 %reduce-scatter.11.cloned.1.call-start = ((), (), s32[]{:S(2)}) async-start(), calls=%async_computation.13 | async-start | bytes 1310720 | tf_op jit(solution)/shard_map/reduce_scatter | solution.py:573
  254.5 91.5 %reduce-scatter.13.cloned.1.call-start = ((), (), s32[]{:S(2)}) async-start(), calls=%async_computation.15 | async-start | bytes 1310720 | tf_op jit(solution)/shard_map/reduce_scatter | solution.py:573
  292.8 41.4 %collective-permute-start.15 = (bf16[1536,1024]{1,0:T(8,128)(2,1)}, bf16[1536,1024]{1,0:T(8,128)(2,1)}, u32[]{:S(2)}, u32[]{:S(2)}) collective-permute-start(bf16[1536,1024]{1,0:T(8,128)(2,1)} %bitcast.89), channel_id=1, source_target_pairs={{0,4},{4,0},{8,12},{12,8},{16,20},{20,16},{24,28},{28,24},{1,5},{5... | collective-permute-start | bytes 9437192 | tf_op jit(solution)/shard_map/ppermute | solution.py:496
  301.7 38.4 %collective-permute-start.16 = (bf16[1536,1024]{1,0:T(8,128)(2,1)}, bf16[1536,1024]{1,0:T(8,128)(2,1)}, u32[]{:S(2)}, u32[]{:S(2)}) collective-permute-start(bf16[1536,1024]{1,0:T(8,128)(2,1)} %bitcast.88), channel_id=1, source_target_pairs={{0,4},{4,0},{8,12},{12,8},{16,20},{20,16},{24,28},{28,24},{1,5},{5... | collective-permute-start | bytes 9437192 | tf_op jit(solution)/shard_map/ppermute | solution.py:496
  308.9 8.9 %all-to-all-start = ((f32[4,256,4]{1,2,0:T(4,128)}), f32[4,256,4]{1,2,0:T(4,128)S(1)}, u32[]{:S(2)}, u32[]{:S(2)}) async-start(f32[4,256,4]{1,2,0:T(4,128)} %pad_maximum_fusion.21), calls=%async_computation.4 | async-start | bytes 32768 | tf_op jit(solution)/shard_map/all_to_all | solution.py:682
  312.1 178.7 %reduce-scatter.15.cloned.1.call-start = ((), (), s32[]{:S(2)}) async-start(), calls=%async_computation.16 | async-start | bytes 2621440 | tf_op jit(solution)/shard_map/reduce_scatter | solution.py:573
  338.6 35.8 %collective-permute-start.17 = (bf16[768,1024]{1,0:T(8,128)(2,1)}, bf16[768,1024]{1,0:T(8,128)(2,1)}, u32[]{:S(2)}, u32[]{:S(2)}) collective-permute-start(bf16[768,1024]{1,0:T(8,128)(2,1)} %fusion.4), channel_id=1, source_target_pairs={{0,8},{4,12},{8,0},{12,4},{16,24},{20,28},{24,16},{28,20},{1,9},{5... | collective-permute-start | bytes 4718600 | tf_op jit(solution)/shard_map/ppermute | solution.py:496
  343.4 35.7 %collective-permute-start.18 = (bf16[768,1024]{1,0:T(8,128)(2,1)}, bf16[768,1024]{1,0:T(8,128)(2,1)}, u32[]{:S(2)}, u32[]{:S(2)}) collective-permute-start(bf16[768,1024]{1,0:T(8,128)(2,1)} %fusion.3), channel_id=1, source_target_pairs={{0,16},{4,20},{8,24},{12,28},{16,0},{20,4},{24,8},{28,12},{1,17},{... | collective-permute-start | bytes 4718600 | tf_op jit(solution)/shard_map/ppermute | solution.py:496
  377.6 21.1 %collective-permute-start.19 = (bf16[384,1024]{1,0:T(8,128)(2,1)}, bf16[384,1024]{1,0:T(8,128)(2,1)}, u32[]{:S(2)}, u32[]{:S(2)}) collective-permute-start(bf16[384,1024]{1,0:T(8,128)(2,1)} %fusion.14), channel_id=1, source_target_pairs={{0,16},{4,20},{8,24},{12,28},{16,0},{20,4},{24,8},{28,12},{1,17},{... | collective-permute-start | bytes 2359304 | tf_op jit(solution)/shard_map/ppermute | solution.py:496
  382.1 17.8 %collective-permute-start.20 = (bf16[384,1024]{1,0:T(8,128)(2,1)}, bf16[384,1024]{1,0:T(8,128)(2,1)}, u32[]{:S(2)}, u32[]{:S(2)}) collective-permute-start(bf16[384,1024]{1,0:T(8,128)(2,1)} %fusion.12), channel_id=1, source_target_pairs={{0,8},{4,12},{8,0},{12,4},{16,24},{20,28},{24,16},{28,20},{1,9},{5... | collective-permute-start | bytes 2359304 | tf_op jit(solution)/shard_map/ppermute | solution.py:496
  402.6 22.1 %collective-permute-start.24 = (bf16[4,128,1536]{2,1,0:T(8,128)(2,1)}, bf16[4,128,1536]{2,1,0:T(8,128)(2,1)}, u32[]{:S(2)}, u32[]{:S(2)}) collective-permute-start(bf16[4,128,1536]{2,1,0:T(8,128)(2,1)} %constant_dynamic-slice_fusion), channel_id=1, source_target_pairs={{0,4},{4,0},{8,12},{12,8},{16,20},{20,16},{24,28},{28,24},{1,5},{5... | collective-permute-start | bytes 4718600 | tf_op jit(solution)/shard_map/ppermute | solution.py:496
  405.4 26.0 %collective-permute-start.21 = (bf16[4,128,1664]{2,1,0:T(8,128)(2,1)}, bf16[4,128,1664]{2,1,0:T(8,128)(2,1)S(1)}, u32[]{:S(2)}, u32[]{:S(2)}) collective-permute-start(bf16[4,128,1664]{2,1,0:T(8,128)(2,1)} %constant_dynamic-slice_fusion.1), channel_id=1, source_target_pairs={{0,4},{4,0},{8,12},{12,8},{16,20},{20,16},{24,28},{28,24},{1,5},{5... | collective-permute-start | bytes 5111816 | tf_op jit(solution)/shard_map/ppermute | solution.py:496
  406.0 118.4 %reduce-scatter.17.cloned.1.call-start = ((), (), s32[]{:S(2)}) async-start(), calls=%async_computation.17 | async-start | bytes 1024000 | tf_op jit(solution)/shard_map/reduce_scatter | solution.py:765
  409.2 3.6 collective-permute-start.11
  412.8 3.6 collective-permute-start.12
  416.4 4.6 collective-permute-start.13
  421.0 12.2 %collective-permute-start.14 = (f32[8,128]{1,0:T(8,128)S(1)}, f32[8,128]{1,0:T(8,128)S(1)}, u32[]{:S(2)}, u32[]{:S(2)}) collective-permute-start(f32[8,128]{1,0:T(8,128)S(1)} %add.453), channel_id=1, source_target_pairs={{0,2},{1,3},{2,0},{3,1},{4,6},{5,7},{6,4},{7,5},{8,10},{9,11},{10,... | collective-permute-start | bytes 12296 | tf_op jit(solution)/shard_map/ppermute | solution.py:797
  423.6 36.7 %collective-permute-start.36 = (bf16[384,1024]{1,0:T(8,128)(2,1)S(1)}, bf16[384,1024]{1,0:T(8,128)(2,1)S(1)}, u32[]{:S(2)}, u32[]{:S(2)}) collective-permute-start(bf16[384,1024]{1,0:T(8,128)(2,1)S(1)} %fusion.7), channel_id=1, source_target_pairs={{0,16},{4,20},{8,24},{12,28},{16,0},{20,4},{24,8},{28,12},{1,17},{... | collective-permute-start | bytes 2359304 | tf_op jit(solution)/shard_map/ppermute | solution.py:496
  426.2 31.3 %collective-permute-start.25 = (bf16[4,64,1536]{2,1,0:T(8,128)(2,1)S(1)}, bf16[4,64,1536]{2,1,0:T(8,128)(2,1)S(1)}, u32[]{:S(2)}, u32[]{:S(2)}) collective-permute-start(bf16[4,64,1536]{2,1,0:T(8,128)(2,1)S(1)} %add_convert_fusion.1), channel_id=1, source_target_pairs={{0,16},{4,20},{8,24},{12,28},{16,0},{20,4},{24,8},{28,12},{1,17},{... | collective-permute-start | bytes 2359304 | tf_op jit(solution)/shard_map/ppermute | solution.py:496
  429.9 31.3 %collective-permute-start.33 = (bf16[384,1024]{1,0:T(8,128)(2,1)S(1)}, bf16[384,1024]{1,0:T(8,128)(2,1)S(1)}, u32[]{:S(2)}, u32[]{:S(2)}) collective-permute-start(bf16[384,1024]{1,0:T(8,128)(2,1)S(1)} %fusion.10), channel_id=1, source_target_pairs={{0,8},{4,12},{8,0},{12,4},{16,24},{20,28},{24,16},{28,20},{1,9},{5... | collective-permute-start | bytes 2359304 | tf_op jit(solution)/shard_map/ppermute | solution.py:496
  431.8 36.9 %collective-permute-start.22 = (bf16[4,64,1664]{2,1,0:T(8,128)(2,1)S(1)}, bf16[4,64,1664]{2,1,0:T(8,128)(2,1)S(1)}, u32[]{:S(2)}, u32[]{:S(2)}) collective-permute-start(bf16[4,64,1664]{2,1,0:T(8,128)(2,1)S(1)} %add_convert_fusion), channel_id=1, source_target_pairs={{0,8},{4,12},{8,0},{12,4},{16,24},{20,28},{24,16},{28,20},{1,9},{5... | collective-permute-start | bytes 2555912 | tf_op jit(solution)/shard_map/ppermute | solution.py:496
  458.8 14.5 %collective-permute-start.26 = (bf16[4,32,1536]{2,1,0:T(8,128)(2,1)S(1)}, bf16[4,32,1536]{2,1,0:T(8,128)(2,1)S(1)}, u32[]{:S(2)}, u32[]{:S(2)}) collective-permute-start(bf16[4,32,1536]{2,1,0:T(8,128)(2,1)S(1)} %add_convert_fusion.5), channel_id=1, source_target_pairs={{0,8},{4,12},{8,0},{12,4},{16,24},{20,28},{24,16},{28,20},{1,9},{5... | collective-permute-start | bytes 1179656 | tf_op jit(solution)/shard_map/ppermute | solution.py:496
  469.0 12.0 %collective-permute-start.23 = (bf16[4,32,1664]{2,1,0:T(8,128)(2,1)S(1)}, bf16[4,32,1664]{2,1,0:T(8,128)(2,1)S(1)}, u32[]{:S(2)}, u32[]{:S(2)}) collective-permute-start(bf16[4,32,1664]{2,1,0:T(8,128)(2,1)S(1)} %add_convert_fusion.3), channel_id=1, source_target_pairs={{0,16},{4,20},{8,24},{12,28},{16,0},{20,4},{24,8},{28,12},{1,17},{... | collective-permute-start | bytes 1277960 | tf_op jit(solution)/shard_map/ppermute | solution.py:496
  481.0 30.4 %collective-permute-start.34 = (bf16[768,1024]{1,0:T(8,128)(2,1)S(1)}, bf16[768,1024]{1,0:T(8,128)(2,1)}, u32[]{:S(2)}, u32[]{:S(2)}) collective-permute-start(bf16[768,1024]{1,0:T(8,128)(2,1)S(1)} %constant_dynamic-update-slice_fusion.6), channel_id=1, source_target_pairs={{0,16},{4,20},{8,24},{12,28},{16,0},{20,4},{24,8},{28,12},{1,17},{... | collective-permute-start | bytes 4718600 | tf_op jit(solution)/shard_map/ppermute | solution.py:496
  481.4 27.3 %collective-permute-start.37 = (bf16[768,1024]{1,0:T(8,128)(2,1)}, bf16[768,1024]{1,0:T(8,128)(2,1)}, u32[]{:S(2)}, u32[]{:S(2)}) collective-permute-start(bf16[768,1024]{1,0:T(8,128)(2,1)} %constant_dynamic-update-slice_fusion.4), channel_id=1, source_target_pairs={{0,8},{4,12},{8,0},{12,4},{16,24},{20,28},{24,16},{28,20},{1,9},{5... | collective-permute-start | bytes 4718600 | tf_op jit(solution)/shard_map/ppermute | solution.py:496
  511.4 32.9 %collective-permute-start.38 = (bf16[1,1536,1024]{2,1,0:T(8,128)(2,1)}, bf16[1,1536,1024]{2,1,0:T(8,128)(2,1)}, u32[]{:S(2)}, u32[]{:S(2)}) collective-permute-start(bf16[1,1536,1024]{2,1,0:T(8,128)(2,1)} %bitcast_dynamic-update-slice_fusion.piece_ref), channel_id=1, source_target_pairs={{0,4},{4,0},{8,12},{12,8},{16,20},{20,16},{24,28},{28,24},{1,5},{5... | collective-permute-start | bytes 9437192 | tf_op jit(solution)/shard_map/ppermute | solution.py:496
  514.1 35.1 %collective-permute-start.35 = (bf16[1,1536,1024]{2,1,0:T(8,128)(2,1)}, bf16[1,1536,1024]{2,1,0:T(8,128)(2,1)}, u32[]{:S(2)}, u32[]{:S(2)}) collective-permute-start(bf16[1,1536,1024]{2,1,0:T(8,128)(2,1)} %bitcast_dynamic-update-slice_fusion.1.piece_ref), channel_id=1, source_target_pairs={{0,4},{4,0},{8,12},{12,8},{16,20},{20,16},{24,28},{28,24},{1,5},{5... | collective-permute-start | bytes 9437192 | tf_op jit(solution)/shard_map/ppermute | solution.py:496
  525.2 4.7 collective-permute-start.30
  526.7 5.2 collective-permute-start.27
  530.0 6.1 %collective-permute-start.31 = (bf16[64,1536]{1,0:T(8,128)(2,1)S(1)}, bf16[64,1536]{1,0:T(8,128)(2,1)S(1)}, u32[]{:S(2)}, u32[]{:S(2)}) collective-permute-start(bf16[64,1536]{1,0:T(8,128)(2,1)S(1)} %constant_dynamic-update-slice_fusion.1), channel_id=1, source_target_pairs={{0,16},{4,20},{8,24},{12,28},{16,0},{20,4},{24,8},{28,12},{1,17},{... | collective-permute-start | bytes 589832 | tf_op jit(solution)/shard_map/ppermute | solution.py:496
  532.0 6.6 %collective-permute-start.28 = (bf16[64,1664]{1,0:T(8,128)(2,1)S(1)}, bf16[64,1664]{1,0:T(8,128)(2,1)S(1)}, u32[]{:S(2)}, u32[]{:S(2)}) collective-permute-start(bf16[64,1664]{1,0:T(8,128)(2,1)S(1)} %constant_dynamic-update-slice_fusion.14), channel_id=1, source_target_pairs={{0,8},{4,12},{8,0},{12,4},{16,24},{20,28},{24,16},{28,20},{1,9},{5... | collective-permute-start | bytes 638984 | tf_op jit(solution)/shard_map/ppermute | solution.py:496
  (41 other events, 376.3 us)
Sparse Core Ops, SparseCore 0:
  9.7 52.2 all-gather.9
  64.0 26.8 all-gather.19
  97.4 26.7 all-gather.11
  126.2 27.4 all-gather.13
  155.8 26.6 reduce-scatter.6
  185.3 25.7 reduce-scatter.8
  212.7 26.5 all-gather.15
  241.5 27.4 all-gather.17
  271.2 26.6 reduce-scatter.10
  305.3 26.9 reduce-scatter.12
  406.1 41.8 reduce-scatter.14
  485.0 23.2 reduce-scatter.16

commit v4 on v3

--- a/solution.py
+++ b/solution.py
@@ -1,3 +1,5 @@
+import functools
+
 import jax
 import jax.numpy as jnp
 from jax import lax
@@ -189,9 +191,9 @@
     )(d_mix, gates_own, gate_up, w_in, w_out)
 
 
-def experts_grads_kernel(order_ref, *refs):
-    grads_ref = refs[-1]
-    count = (len(refs) - 1) // 4
+def experts_grads_kernel(outputs, units, order_ref, *refs):
+    grads_refs, refs = refs[-outputs:], refs[:-outputs]
+    count = len(refs) // 4
     width = refs[0].shape[1]
     grad_in, grad_out = None, None
     for at in range(count):
@@ -200,11 +202,23 @@
         part_out = dot_tn(hidden_ref[0], dmix_ref[...])
         grad_in = part_in if grad_in is None else grad_in + part_in
         grad_out = part_out if grad_out is None else grad_out + part_out
-    grads_ref[0, :width, :] = grad_in.astype(grads_ref.dtype)
-    grads_ref[0, width:, :] = grad_out.astype(grads_ref.dtype)
-
-
-def experts_grads(order, chunks):
+    grad_in, grad_out = grad_in.astype(jnp.bfloat16), grad_out.astype(jnp.bfloat16)
+    tall, short = width // units, grad_out.shape[0] // units
+
+    def put(ref):
+        for at in range(units):
+            start = at * (tall + short)
+            ref[start : start + tall, :] = grad_in[at * tall : (at + 1) * tall]
+            ref[start + tall : start + tall + short, :] = grad_out[at * short : (at + 1) * short]
+
+    if outputs == 1:
+        put(grads_refs[0].at[0])
+        return
+    for at in range(outputs):
+        pl.when(pl.program_id(0) == at)(functools.partial(put, grads_refs[at]))
+
+
+def experts_grads(order, chunks, apart, row_units):
     count, width = chunks[0][0].shape
     units = chunks[0][3].shape[2]
     experts = order.shape[0]
@@ -214,84 +228,179 @@
         pl.BlockSpec((1, count, 2 * units), lambda e, order: (order[e], 0, 0)),
         pl.BlockSpec((1, count, units), lambda e, order: (order[e], 0, 0)),
     ]
-    return pl.pallas_call(
-        experts_grads_kernel,
+    rows, columns = width + units, 2 * units
+    if apart and experts > 1:
+        outputs = experts
+        out_specs = [pl.BlockSpec((rows, columns), lambda e, order: (0, 0))] * experts
+        out_shape = [jax.ShapeDtypeStruct((rows, columns), jnp.bfloat16)] * experts
+    else:
+        outputs = 1
+        out_specs = [pl.BlockSpec((1, rows, columns), lambda e, order: (e, 0, 0))]
+        out_shape = [jax.ShapeDtypeStruct((experts, rows, columns), jnp.bfloat16)]
+    grads = pl.pallas_call(
+        functools.partial(experts_grads_kernel, outputs, row_units),
         grid_spec=pltpu.PrefetchScalarGridSpec(
             num_scalar_prefetch=1,
             grid=(experts,),
             in_specs=specs * len(chunks),
-            out_specs=pl.BlockSpec((1, width + units, 2 * units), lambda e, order: (e, 0, 0)),
+            out_specs=out_specs,
         ),
-        out_shape=jax.ShapeDtypeStruct((experts, width + units, 2 * units), jnp.bfloat16),
+        out_shape=out_shape,
         compiler_params=pltpu.CompilerParams(vmem_limit_bytes=VMEM_BYTES),
         cost_estimate=SMALL_COST,
         name="experts_grads",
     )(order, *[part for chunk in chunks for part in chunk])
-
-
-def widen_kernel(base_ref, piece_ref, *refs):
+    return [part.reshape(-1, columns) for part in grads]
+
+
+def widen_kernel(spot_ref, piece_ref, *refs):
     gin_ref, gout_ref = refs[-2:]
-    width = gin_ref.shape[1]
-    gin_ref[...] = piece_ref[:, :width, :].astype(jnp.float32)
-    gout_ref[...] = piece_ref[:, width:, :].astype(jnp.float32)
-
-
-def widen(base, piece, width, total, held):
-    count, rows, columns = piece.shape
-    shapes = [
-        jax.ShapeDtypeStruct((total, width, columns), jnp.float32),
-        jax.ShapeDtypeStruct((total, rows - width, columns), jnp.float32),
-    ]
+    tall = gin_ref.shape[1]
+    gin_ref[0] = piece_ref[:tall, :].astype(jnp.float32)
+    gout_ref[0] = piece_ref[tall:, :].astype(jnp.float32)
+
+
+def widen(spot, piece, shapes, units, held):
+    rows, columns = shapes[0][1] + shapes[1][1], piece.shape[1]
+    unit = rows // units
     return pl.pallas_call(
         widen_kernel,
         grid_spec=pltpu.PrefetchScalarGridSpec(
             num_scalar_prefetch=1,
-            grid=(count,),
-            in_specs=[pl.BlockSpec((1, rows, columns), lambda e, base: (e, 0, 0))]
+            grid=(piece.shape[0] // unit,),
+            in_specs=[pl.BlockSpec((unit, columns), lambda at, spot: (at, 0))]
             + [pl.BlockSpec(memory_space=pl.ANY)] * len(held),
             out_specs=[
-                pl.BlockSpec((1, width, columns), lambda e, base: (base[0] + e, 0, 0)),
-                pl.BlockSpec((1, rows - width, columns), lambda e, base: (base[0] + e, 0, 0)),
+                pl.BlockSpec(
+                    (1, shape[1] // units, columns), lambda at, spot: (spot[0], spot[1] + at, 0)
+                )
+                for shape in shapes
             ],
         ),
-        out_shape=shapes,
+        out_shape=[jax.ShapeDtypeStruct(shape, jnp.float32) for shape in shapes],
         input_output_aliases={2 + at: at for at in range(len(held))},
         compiler_params=pltpu.CompilerParams(vmem_limit_bytes=VMEM_BYTES),
         cost_estimate=SMALL_COST,
         name="widen",
-    )(base, piece, *held)
+    )(spot, piece, *held)
+
+
+def finish_kernel(spots, widths, piece_ref, query_ref, key_ref, value_ref, output_ref, small_ref):
+    query_width, half, kv_width = widths
+    rows = piece_ref.shape[1]
+    for at, (first, second) in enumerate(spots):
+        first_at = slice(first * rows, (first + 1) * rows)
+        second_at = slice(second * rows, (second + 1) * rows)
+        block = piece_ref[at].astype(jnp.float32)
+        query_ref[first_at, :] = block[:, :query_width]
+        start = query_width + half
+        output_ref[first_at, :half] = block[:, query_width:start]
+        small_ref[first_at, :] = block[:, start : start + LANES]
+        start = start + LANES
+        key_ref[second_at, :] = block[:, start : start + kv_width]
+        value_ref[second_at, :] = block[:, start + kv_width : start + 2 * kv_width]
+        output_ref[second_at, half:] = block[:, start + 2 * kv_width :]
+
+
+def finish(pieces, spots, widths):
+    count, rows, _ = pieces.shape
+    query_width, half, kv_width = widths
+    return pl.pallas_call(
+        functools.partial(finish_kernel, spots, widths),
+        in_specs=[whole_spec()],
+        out_specs=[whole_spec()] * 5,
+        out_shape=[
+            jax.ShapeDtypeStruct((count * rows, columns), jnp.float32)
+            for columns in (query_width, kv_width, kv_width, 2 * half, LANES)
+        ],
+        compiler_params=pltpu.CompilerParams(vmem_limit_bytes=VMEM_BYTES),
+        cost_estimate=SMALL_COST,
+        name="finish",
+    )(pieces)
 
 
 def attention_grads_kernel(
-    normed_ref, dquery_ref, all_ref, dkv_ref, attended_ref, dbranch_ref, small_ref, first_ref, second_ref
+    sets,
+    side_ref, digits_ref, normed_ref, dquery_ref, all_ref, dkv_ref, attended_ref, dbranch_ref,
+    gain_ref, router_ref,
+    wq_ref, wkv_ref, input_ref, own_ref,
+    dnormed_kv_ref, dnormed_query_ref, sent_first, kept_first, sent_second, kept_second,
+    first_ref, second_ref
 ):
     query_width = dquery_ref.shape[1]
     half = dbranch_ref.shape[1] // 2
     kv_width = dkv_ref.shape[1]
-    low = jnp.bfloat16
-    second_ref[:, :kv_width] = dot_tn(all_ref[...], dkv_ref[...]).astype(low)
-    first_ref[:, :query_width] = dot_tn(normed_ref[...], dquery_ref[...]).astype(low)
-    grad_output = dot_tn(attended_ref[...], dbranch_ref[...]).astype(low)
-    first_ref[:, query_width : query_width + half] = grad_output[:, :half]
-    second_ref[:, kv_width:] = grad_output[:, half:]
-    first_ref[:, query_width + half :] = small_ref[...].astype(low)
-
-
-def attention_grads(normed, d_query, normed_all, d_kv, attended, d_branch, small):
+    shards, rows = kept_first.shape[0], kept_first.shape[1]
+
+    def gain_of(d_normed, block):
+        values = block.astype(jnp.float32)
+        scale = lax.rsqrt(jnp.mean(values * values, axis=-1, keepdims=True) + norm_eps)
+        return jnp.sum(d_normed * values * scale, axis=0, keepdims=True)
+
+    def put(ref, columns, value):
+        ref[:, :, columns] = value.astype(jnp.bfloat16).reshape(shards, 2 * rows, -1)
+
+    d_normed = dot_nt(dquery_ref[...], wq_ref[...])
+    dnormed_query_ref[...] = d_normed
+    gain = gain_of(d_normed, own_ref[...])
+    for start in range(0, all_ref.shape[0], ROW_STEP):
+        span = pl.ds(start, ROW_STEP)
+        d_normed = dot_nt(dkv_ref[span, :], wkv_ref[...])
+        dnormed_kv_ref[span, :] = d_normed.astype(jnp.bfloat16)
+        gain = gain + gain_of(d_normed, input_ref[span, :])
+    put(second_ref, slice(0, kv_width), dot_tn(all_ref[...], dkv_ref[...]))
+    put(first_ref, slice(0, query_width), dot_tn(normed_ref[...], dquery_ref[...]))
+    grad_output = dot_tn(attended_ref[...], dbranch_ref[...])
+    put(first_ref, slice(query_width, query_width + half), grad_output[:, :half])
+    put(second_ref, slice(kv_width, kv_width + half), grad_output[:, half:])
+    experts, width = router_ref.shape
+    row = lax.broadcasted_iota(jnp.int32, (LANES - experts, width), 0)
+    spot = lax.broadcasted_iota(jnp.int32, row.shape, 1) % (2 * rows)
+    rest = jnp.where(row == 0, gain, jnp.where(row == 1, gain_ref[...], 0.0))
+    for at in range(digits_ref.shape[0]):
+        for turn in range(sets):
+            here = (row == 2 + at * sets + turn) & (spot == side_ref[1] - 2 * rows * turn)
+            rest = jnp.where(here, digits_ref[at], rest)
+    small = jnp.concatenate([router_ref[...], rest], 0).T
+    put(first_ref, slice(query_width + half, first_ref.shape[2]), small)
+    kept_at = pl.ds(pl.multiple_of(side_ref[0] * rows, rows), rows)
+    sent_at = pl.ds(pl.multiple_of((1 - side_ref[0]) * rows, rows), rows)
+    sent_first[...] = first_ref[:, sent_at, :]
+    sent_second[...] = second_ref[:, sent_at, :]
+    kept_first[...] = first_ref[:, kept_at, :]
+    kept_second[...] = second_ref[:, kept_at, :]
+
+
+def attention_grads(
+    side, digits, sets, shards, normed, d_query, normed_all, d_kv, attended, d_branch, gain, router,
+    w_query, w_kv, input_all, hidden_in
+):
     width = normed.shape[1]
     half = d_branch.shape[1] // 2
+    rows = width // shards // 2
+    widths = (d_query.shape[1] + half + LANES, d_kv.shape[1] + half)
     return pl.pallas_call(
-        attention_grads_kernel,
-        in_specs=[whole_spec()] * 7,
-        out_specs=[whole_spec()] * 2,
+        functools.partial(attention_grads_kernel, sets),
+        in_specs=[pl.BlockSpec(memory_space=pltpu.SMEM)] * 2 + [whole_spec()] * 12,
+        out_specs=[whole_spec()] * 6,
         out_shape=[
-            jax.ShapeDtypeStruct((width, d_query.shape[1] + half + LANES), jnp.bfloat16),
-            jax.ShapeDtypeStruct((width, d_kv.shape[1] + half), jnp.bfloat16),
+            jax.ShapeDtypeStruct(input_all.shape, jnp.bfloat16),
+            jax.ShapeDtypeStruct(hidden_in.shape, jnp.float32),
+        ]
+        + [
+            jax.ShapeDtypeStruct((shards, rows, columns), jnp.bfloat16)
+            for columns in (widths[0], widths[0], widths[1], widths[1])
+        ],
+        scratch_shapes=[
+            pltpu.VMEM((shards, 2 * rows, columns), jnp.bfloat16) for columns in widths
         ],
         compiler_params=pltpu.CompilerParams(vmem_limit_bytes=VMEM_BYTES),
         cost_estimate=SMALL_COST,
         name="attention_grads",
-    )(normed, d_query, normed_all, d_kv, attended, d_branch, small)
+    )(
+        side, digits, normed, d_query, normed_all, d_kv, attended, d_branch, gain, router,
+        w_query, w_kv, input_all, hidden_in,
+    )
 
 
 VMEM_BYTES = 60 * 1024 * 1024
@@ -332,12 +441,22 @@
 
 
 def attention_forward_kernel(
-    bias_ref, all_ref, own_ref, gain_ref, wq_ref, wkv_ref, cos_ref, sin_ref, cos_own_ref, sin_own_ref,
-    normed_ref, query_ref, key_ref, value_ref, attended_ref, norm_ref, scores
+    bias_ref, side_ref, all_ref, own_ref, gain_ref, query_held, query_other, kv_held, kv_other,
+    cos_ref, sin_ref, cos_own_ref, sin_own_ref,
+    wq_parts, wkv_parts, normed_ref, normed_own_ref, query_ref, key_ref, value_ref, attended_ref, norm_ref, scores
 ):
     tokens, width = all_ref.shape
     kv_width = key_ref.shape[1]
     key_rows = tokens // bias_ref.shape[0]
+    half_rows = query_held.shape[1]
+    held_at = pl.ds(pl.multiple_of(side_ref[0] * half_rows, half_rows), half_rows)
+    other_at = pl.ds(pl.multiple_of((1 - side_ref[0]) * half_rows, half_rows), half_rows)
+    wq_parts[:, held_at, :] = query_held[...]
+    wq_parts[:, other_at, :] = query_other[...]
+    wkv_parts[:, held_at, :] = kv_held[...]
+    wkv_parts[:, other_at, :] = kv_other[...]
+    wq_ref = wq_parts.reshape(width, wq_parts.shape[2])
+    wkv_ref = wkv_parts.reshape(width, wkv_parts.shape[2])
 
     def normed_rows(block):
         values = block.astype(jnp.float32)
@@ -357,7 +476,9 @@
         return carry
 
     lax.fori_loop(0, tokens // ROW_STEP, project, 0)
-    linear = dot_nn(normed_rows(own_ref[...]), wq_ref[...])
+    normed_own = normed_rows(own_ref[...])
+    normed_own_ref[...] = normed_own
+    linear = dot_nn(normed_own, wq_ref[...])
     for col in range(0, wq_ref.shape[1], LANES):
         part = linear[:, col : col + LANES]
         turned = part * cos_own_ref[...] + swap_halves(part) * sin_own_ref[...]
@@ -398,27 +519,31 @@
     return pl.BlockSpec(memory_space=pltpu.VMEM)
 
 
-def attention_forward(bias, input_all, hidden_in, gain, w_query, w_kv, tables, tables_own):
+def attention_forward(bias, side, input_all, hidden_in, gain, query_pair, kv_pair, tables, tables_own):
     tokens, width = input_all.shape
     rows = hidden_in.shape[0]
-    kv_width = w_kv.shape[1] // 2
+    shards, half_rows, query_width = query_pair[0].shape
+    kv_width = kv_pair[0].shape[2] // 2
     return pl.pallas_call(
         attention_forward_kernel,
-        in_specs=[pl.BlockSpec(memory_space=pltpu.SMEM)] + [whole_spec()] * 9,
-        out_specs=[whole_spec()] * 6,
+        in_specs=[pl.BlockSpec(memory_space=pltpu.SMEM)] * 2 + [whole_spec()] * 11,
+        out_specs=[whole_spec()] * 9,
         out_shape=[
+            jax.ShapeDtypeStruct((shards, 2 * half_rows, query_width), jnp.bfloat16),
+            jax.ShapeDtypeStruct((shards, 2 * half_rows, 2 * kv_width), jnp.bfloat16),
             jax.ShapeDtypeStruct((tokens, width), jnp.bfloat16),
-            jax.ShapeDtypeStruct((rows, w_query.shape[1]), jnp.bfloat16),
+            jax.ShapeDtypeStruct((rows, width), jnp.bfloat16),
+            jax.ShapeDtypeStruct((rows, query_width), jnp.bfloat16),
             jax.ShapeDtypeStruct((tokens, kv_width), jnp.bfloat16),
             jax.ShapeDtypeStruct((tokens, kv_width), jnp.bfloat16),
-            jax.ShapeDtypeStruct((rows, w_query.shape[1]), jnp.bfloat16),
+            jax.ShapeDtypeStruct((rows, query_width), jnp.bfloat16),
             jax.ShapeDtypeStruct((KV_HEADS, 2 * rows), jnp.float32),
         ],
         scratch_shapes=[pltpu.VMEM((tokens, 2 * rows), jnp.float32)],
         compiler_params=pltpu.CompilerParams(vmem_limit_bytes=VMEM_BYTES),
         cost_estimate=SMALL_COST,
         name="attention_forward",
-    )(bias, input_all, hidden_in, gain, w_query, w_kv, *tables, *tables_own)
+    )(bias, side, input_all, hidden_in, gain, *query_pair, *kv_pair, *tables, *tables_own)
 
 
 def attention_backward_kernel(
@@ -505,7 +630,10 @@
 
 
 def slices_of(parts, start, size, axis):
-    return [lax.dynamic_slice_in_dim(part, start, size, axis) for part in parts]
+    return [
+        lax.dynamic_slice_in_dim(part, base + start, size, axis)
+        for part, base in ((part if isinstance(part, tuple) else (part, 0)) for part in parts)
+    ]
 
 
 def add_parts(parts):
@@ -515,13 +643,13 @@
     return total.astype(jnp.bfloat16)
 
 
-def halve(parts, bit, axis, offset=0, length=None):
+def halve(parts, bit, axis, length=None):
     length = parts[0].shape[axis] if length is None else length
     half = length // 2
     side = side_of(bit)
-    sent = slices_of(parts, offset + (1 - side) * half, half, axis)
+    sent = slices_of(parts, (1 - side) * half, half, axis)
     sent = sent[0] if len(sent) == 1 else add_parts(sent)
-    kept = slices_of(parts, offset + side * half, half, axis)
+    kept = slices_of(parts, side * half, half, axis)
     return sent, kept + [exchange(sent, bit)]
 
 
@@ -587,6 +715,14 @@
     order_first, order_second = far + [near], far[::-1] + [near]
     w_kv = jnp.concatenate([w_key, w_value], 1)
     input_all = gather(hidden_in)
+    valid_float = valid_mask.astype(jnp.float32)
+    expert_count = router.shape[1]
+    small_parts = [
+        jnp.concatenate([attn_norm, ffn_norm, router.reshape(-1)]).reshape(1, -1),
+        routes.astype(jnp.bfloat16).reshape(1, -1),
+        jnp.sum(valid_float).astype(jnp.bfloat16).reshape(1, 1),
+    ]
+    small_size, routes_size = small_parts[0].size, small_parts[1].size
     pieces = lax.all_gather(
         jnp.concatenate([piece_of(w_query, order_first), piece_of(w_kv, order_second)], 1),
         "shard",
@@ -594,39 +730,34 @@
     )
     query_full = pieces[..., :query_width]
     kv_full = pieces[..., query_width:]
-    for bit_first, bit_second in zip(order_first, order_second):
+    for bit_first, bit_second in zip(order_first[:-1], order_second[:-1]):
         query_full = double(query_full, bit_first, 1)
         kv_full = double(kv_full, bit_second, 1)
-    query_full = query_full.reshape(own_rows * shard_count, query_width)
-    kv_full = kv_full.reshape(own_rows * shard_count, 2 * kv_width)
+    small_parts = after(jnp.concatenate(small_parts, 1), query_full, kv_full, *tables, *tables_own)
+    small_all = gather(small_parts)
+    query_pair = query_full, exchange(query_full, near)
+    kv_pair = kv_full, exchange(kv_full, near)
     near_rows = own_rows // 2
     output_half = lax.dynamic_slice_in_dim(w_output, side_of(near) * near_rows, near_rows, 0)
-    output_half = lax.all_gather(after(output_half, input_all), "shard", axis=0)
-    expert_count = router.shape[1]
-    valid_float = valid_mask.astype(jnp.float32)
-    small_parts = [
-        jnp.concatenate([attn_norm[:, None], ffn_norm[:, None], router], 1).reshape(1, -1),
-        routes.astype(jnp.bfloat16).reshape(1, -1),
-        jnp.sum(valid_float).astype(jnp.bfloat16).reshape(1, 1),
-    ]
-    small_all = gather(jnp.concatenate(small_parts, 1))
-    small_size, routes_size = small_parts[0].size, small_parts[1].size
-    small_full = small_all[:, :small_size].reshape(-1, 2 + expert_count)
+    output_half = lax.all_gather(after(output_half, query_pair[0], kv_pair[0]), "shard", axis=0)
+    gain_attn = small_all[:, :own_rows].reshape(-1).astype(jnp.float32)
+    gain_ffn = small_all[:, own_rows : 2 * own_rows].reshape(-1)
+    router_full = small_all[:, 2 * own_rows : small_size].reshape(-1, expert_count)
     routes_all = small_all[:, small_size : small_size + routes_size]
-    valid_count = jnp.broadcast_to(jnp.sum(small_all[:, -1].astype(jnp.float32)), (8, LANES))
+    valid_count = jnp.broadcast_to(jnp.sum(small_all[:, small_size + routes_size].astype(jnp.float32)), (8, LANES))
     for bit in bits:
         valid_count = valid_count + exchange(valid_count, bit)
     valid_count = valid_count[0, 0]
-    gain_attn, gain_ffn = small_full[:, 0], small_full[:, 1]
-    router_full = small_full[:, 2:]
-    gain_attn = gain_attn.astype(jnp.float32)
     input_float = hidden_in.astype(jnp.float32)
     scale_attn = rms_scale(input_float)
-    all_float = input_all.astype(jnp.float32)
-    normed_all, query_rows, keys_all, values_all, attended, log_norm = attention_forward(
-        bias, input_all, hidden_in, gain_attn[None], query_full, kv_full, tables, tables_own
-    )
-    normed_attn = lax.dynamic_slice_in_dim(normed_all, shard_at * row_count, row_count, 0)
+    (
+        query_full, kv_full, normed_all, normed_attn, query_rows, keys_all, values_all, attended, log_norm
+    ) = attention_forward(
+        bias, jnp.reshape(side_of(near), (1,)), input_all, hidden_in, gain_attn[None],
+        query_pair, kv_pair, tables, tables_own,
+    )
+    query_full = query_full.reshape(model_width, query_width)
+    kv_full = kv_full.reshape(model_width, 2 * kv_width)
     output_half, attended = lax.optimization_barrier((output_half, attended))
     output_full = double(output_half, near, 1).reshape(own_rows * shard_count, -1)
     branch = dot_nn(attended, output_full)
@@ -650,6 +781,8 @@
         gates_own = lax.dynamic_slice_in_dim(gates_part, shard_at * own_experts, own_experts, 1)
         gates_own = jnp.pad(gates_own, ((0, 0), (0, LANES - own_experts)))
         gates.append(lax.dynamic_slice_in_dim(gates_part, shard_at * chunk_rows, chunk_rows, 0))
+        if not forward:
+            gates_own = after(gates_own, valid_count)
         forward.append((gates_own, *experts_forward(tokens, gates_own, w_in, w_out)))
     gates = jnp.concatenate(gates, 0)
     results, d_results, d_mix_out, d_mix_in, own_loss = [], [], [], [], 0.0
@@ -668,44 +801,70 @@
         d_mix_in.append(gather(d_mix_out[-1]))
         own_loss = own_loss + jnp.sum(masked * deviation)
     d_result = jnp.concatenate(d_results, 0)
+    kept_experts = own_experts // 2
+    grad_rows = model_width + w_out.shape[1]
+    flat_rows = kept_experts * grad_rows
+    row_units = 2 * grad_rows // (flat_rows >> len(far))
+    side = side_of(near)
+    digits, rest = [], own_loss
+    for _ in range(3):
+        digits.append(lax.reduce_precision(rest, 8, 7))
+        rest = rest - digits[-1]
+    device = lax.axis_index("rep") * shard_count + shard_at
+    sets = -(-lax.axis_size("rep") * shard_count // own_rows)
+    place, digits = jnp.stack([side, device]), jnp.stack(digits)
+    columns = w_in.shape[2]
+    shapes = (own_experts, model_width, columns), (own_experts, grad_rows - model_width, columns)
+    half_units = row_units * flat_rows // grad_rows // 4
+    second_at = (1, 0) if kept_experts > 1 else (0, 2 * half_units)
+    targets = {}
+    for path, bit, (expert, unit) in ((0, far[0], (0, 0)), (1, far[-1], second_at)):
+        for across in range(2):
+            half = side_of(bit) if across == 0 else 1 - side_of(bit)
+            for core in range(2):
+                owner = side if core == 0 else 1 - side
+                targets[path, across, core] = jnp.stack(
+                    [owner * kept_experts + expert, unit + half * half_units]
+                )
     d_rows, d_gates, backward = [], [], []
     for d_mix, (gates_own, _, gate_up, hidden_gated), tokens in zip(d_mix_in, forward, tokens_in):
+        if not backward:
+            gates_own = after(gates_own, place, digits, *targets.values())
         d_rows_part, d_gate_up, d_gates_part = experts_backward(
             d_mix, gates_own, gate_up, w_in, w_out
         )
         d_rows.append(scatter(d_rows_part))
-        d_gates.append(d_gates_part[:, :own_experts].reshape(shard_count, chunk_rows, own_experts))
+        d_gates.append(d_gates_part)
         backward.append((tokens, d_mix, d_gate_up, hidden_gated))
-    d_rows_in = d_rows
+    first_rows = d_rows[0]
     d_rows = jnp.concatenate(d_rows, 0).astype(jnp.float32)
-    d_gates = jnp.concatenate(d_gates, 1).reshape(shard_count * row_count, own_experts)
-    d_gates = lax.all_to_all(d_gates, "shard", split_axis=0, concat_axis=1, tiled=True)
-    kept_experts = own_experts // 2
-    grad_rows = model_width + w_out.shape[1]
-    flat_rows = kept_experts * grad_rows
-    side = side_of(near)
     order = jnp.arange(kept_experts, dtype=jnp.int32)
     order_sent = order + (1 - side) * kept_experts
     order_kept = order + side * kept_experts
-    flat = (grad_rows, w_in.shape[2])
-    sent = [experts_grads(order_sent[at : at + 1], backward).reshape(flat) for at in range(kept_experts)]
+    sent = experts_grads(order_sent, backward, True, row_units)
     other = [exchange(part, near) for part in sent]
-    kept = experts_grads(after(order_kept, *sent, d_rows_in[0]), backward).reshape(flat_rows, -1)
+    kept = experts_grads(after(order_kept, *sent, first_rows), backward, False, row_units)[0]
+    half_rows = flat_rows // 2
     if kept_experts > 1:
-        kept_first, kept_second = kept[: flat_rows // 2], kept[flat_rows // 2 :]
         other_first = jnp.concatenate(other[: kept_experts // 2], 0)
         other_second = jnp.concatenate(other[kept_experts // 2 :], 0)
+        spots = ((kept, 0), (other_first, 0)), ((kept, half_rows), (other_second, 0))
     else:
-        kept_first, kept_second = kept[: flat_rows // 2], kept[flat_rows // 2 :]
-        other_first, other_second = other[0][: flat_rows // 2], other[0][flat_rows // 2 :]
-    moe_sent_first, moe_first = halve([kept_first, other_first], far[0], 0)
-    moe_sent_second, moe_second = halve([kept_second, other_second], far[-1], 0)
+        spots = ((kept, 0), (other[0], 0)), ((kept, half_rows), (other[0], half_rows))
+    moe_sent_first, moe_first = halve(spots[0], far[0], 0, half_rows)
+    moe_sent_second, moe_second = halve(spots[1], far[-1], 0, half_rows)
+    d_gates = [after(part, moe_sent_first, moe_sent_second) for part in d_gates]
+    d_gates = [
+        part[:, :own_experts].reshape(shard_count, chunk_rows, own_experts) for part in d_gates
+    ]
+    d_gates = jnp.concatenate(d_gates, 1).reshape(shard_count * row_count, own_experts)
+    d_gates = lax.all_to_all(d_gates, "shard", split_axis=0, concat_axis=1, tiled=True)
     d_rows = after(d_rows, moe_sent_first, moe_sent_second)
     d_logits = (gates * (d_gates - jnp.sum(gates * d_gates, -1, keepdims=True))).astype(
         jnp.bfloat16
     )
     d_normed_ffn = d_rows + dot_nt(d_logits, router_full)
-    grad_router = dot_tn(normed_ffn, d_logits)
+    grad_router = dot_tn(d_logits, normed_ffn)
     d_norm_mid, grad_gain_ffn = norm_back(d_normed_ffn, middle, scale_ffn, gain_ffn)
     d_middle = d_result + d_norm_mid
     d_branch = (resid_mult * d_middle).astype(jnp.bfloat16)
@@ -715,99 +874,88 @@
     query_grad_rows, kv_grad_all = attention_backward(
         bias, query_rows, keys_all, values_all, log_norm, d_attended, tables, tables_own
     )
-    query_grad_rows, kv_grad_all = lax.optimization_barrier(
+    query_grad_rows, kv_grad_all, moe_first[-1], moe_second[-1] = lax.optimization_barrier(
         (query_grad_rows, kv_grad_all, moe_first[-1], moe_second[-1])
-    )[:2]
-    d_normed_kv = dot_nt(kv_grad_all, kv_full)
-    d_normed_query = dot_nt(query_grad_rows, query_full)
-    grad_gain_attn = jnp.sum(d_normed_kv * all_float * rms_scale(all_float), 0) + jnp.sum(
-        d_normed_query * input_float * scale_attn, 0
-    )
-    kv_scattered = scatter(d_normed_kv.astype(jnp.bfloat16))
-    grad_small = jnp.concatenate(
-        [
-            grad_gain_attn[:, None],
-            grad_gain_ffn[:, None],
-            grad_router,
-            jnp.zeros((model_width, LANES - 2 - expert_count), jnp.float32),
-        ],
-        1,
-    )
-
-    first, second = attention_grads(
-        normed_attn, query_grad_rows, normed_all, kv_grad_all, attended, d_branch, grad_small
-    )
-    d_normed_query = after(d_normed_query, first, second)
+    )
+    d_normed_kv, d_normed_query, sent_first, kept_first, sent_second, kept_second = attention_grads(
+        place, digits, sets, shard_count, normed_attn, query_grad_rows,
+        normed_all, kv_grad_all, attended, d_branch, grad_gain_ffn[None], grad_router,
+        query_full, kv_full, input_all, hidden_in
+    )
+    used = expert_count + 2
+    kv_scattered = scatter(d_normed_kv)
+    d_normed_query = after(d_normed_query, sent_first, sent_second)
     d_normed_attn = kv_scattered.astype(jnp.float32) + d_normed_query
     d_norm_in, _ = norm_back(d_normed_attn, input_float, scale_attn, gain_attn)
     d_input = d_middle + d_norm_in
     for bit_first, bit_second in zip(far[1:], far[::-1][1:]):
         _, moe_first = halve(moe_first, bit_first, 0)
         _, moe_second = halve(moe_second, bit_second, 0)
-    first, second = lax.optimization_barrier((first, second, moe_first[-1], moe_second[-1]))[:2]
+    sent_first, sent_second, moe_first[-1], moe_second[-1] = lax.optimization_barrier(
+        (sent_first, sent_second, moe_first[-1], moe_second[-1])
+    )
     moe_first, moe_second = add_parts(moe_first), add_parts(moe_second)
-    first = [first.reshape(shard_count, own_rows, -1)]
-    second = [second.reshape(shard_count, own_rows, -1)]
-    _, first = halve(first, near, 1)
-    _, second = halve(second, near, 1)
+    sent_first, sent_second = lax.optimization_barrier(
+        (sent_first, sent_second, moe_first, moe_second)
+    )[:2]
+    first = [kept_first, exchange(sent_first, near)]
+    second = [kept_second, exchange(sent_second, near)]
     for bit_first, bit_second in zip(far[:0:-1], far[:-1]):
         moe_first = double(moe_first, bit_first, 0)
         moe_second = double(moe_second, bit_second, 0)
     for bit_first, bit_second in zip(far, far[::-1]):
         _, first = halve(first, bit_first, 1)
         _, second = halve(second, bit_second, 1)
+        if bit_first == far[0]:
+            first[-1] = after(first[-1], moe_first, moe_second)
+            second[-1] = after(second[-1], moe_first, moe_second)
+    first[-1] = after(first[-1], kv_scattered)
     moe_first = after(moe_first, first[-1], second[-1])
     moe_second = after(moe_second, first[-1], second[-1])
-    moe_first = double(moe_first, far[0], 0)
-    moe_second = double(moe_second, far[-1], 0)
+    own_first, own_second = moe_first, moe_second
+    far_first, far_second = exchange(own_first, far[0]), exchange(own_second, far[-1])
+    near_own = exchange(own_first, near), exchange(own_second, near)
     split_at = first[0].shape[2]
     joined = jnp.concatenate([add_parts(first), add_parts(second)], 2)
     joined = lax.psum_scatter(joined, "shard", scatter_dimension=0)
-    first, second = joined[:, :split_at], joined[:, split_at:]
-    for bit_first, bit_second in zip(far[::-1] + [near], far + [near]):
-        first = double(first, bit_first, 0)
-        second = double(second, bit_second, 0)
-    first, second = first.astype(jnp.float32), second.astype(jnp.float32)
-    sum_query = first[:, :query_width]
-    sum_key = second[:, :kv_width]
-    sum_value = second[:, kv_width : 2 * kv_width]
-    sum_output = jnp.concatenate(
-        [first[:, query_width : query_width + half_width], second[:, 2 * kv_width :]], 1
-    )
-    sum_small = first[:, query_width + half_width :]
-    if kept_experts % 2 == 0:
-        pieces = [moe_first, moe_second]
-    else:
-        pieces = [lax.concatenate([moe_first, moe_second], 0)]
-    pieces = [piece.reshape(-1, grad_rows, piece.shape[1]) for piece in pieces]
-    others = [exchange(piece, near) for piece in pieces]
+    def put(held, piece, *where):
+        return widen(targets[where], piece, shapes, row_units, held)
+
     held = []
-    for start, group in ((side, pieces), (1 - side, others)):
-        base = start * kept_experts
-        for piece in group:
-            held = widen(jnp.reshape(base, (1,)), piece, model_width, own_experts, held)
-            base = base + piece.shape[0]
+    held = put(held, own_first, 0, 0, 0)
+    held = put(held, own_second, 1, 0, 0)
+    *held, joined, d_input = lax.optimization_barrier((*held, joined, d_input))
+    gathered = lax.all_gather(joined, "rep", axis=0)
+    held = put(held, near_own[0], 0, 0, 1)
+    held = put(held, near_own[1], 1, 0, 1)
+    *held, far_first, far_second = lax.optimization_barrier((*held, far_first, far_second))
+    near_far = exchange(far_first, near), exchange(far_second, near)
+    held = put(held, far_first, 0, 1, 0)
+    held = put(held, far_second, 1, 1, 0)
+    held = put(held, near_far[0], 0, 1, 1)
+    held = put(held, near_far[1], 1, 1, 1)
     sum_in, sum_out = held
-    loss_sum = jnp.broadcast_to(own_loss, (8, LANES))
-    for bit in bits:
-        loss_sum = loss_sum + exchange(loss_sum, bit)
-    step = 1
-    while step < shard_count:
-        pairs = [(at, at ^ step) for at in range(shard_count)]
-        loss_sum = loss_sum + lax.ppermute(loss_sum, "shard", pairs)
-        step = 2 * step
-    loss = loss_sum[0, 0] / (model_width * valid_count)
+    def row_of(at, order):
+        return sum(((at // bit) % 2) << (len(order) - 1 - turn) for turn, bit in enumerate(order))
+
+    pairs = tuple(
+        (row_of(at, [near] + far), row_of(at, [near] + far[::-1])) for at in range(lax.axis_size("rep"))
+    )
+    sum_query, sum_key, sum_value, sum_output, sum_small = finish(
+        gathered, pairs, (query_width, half_width, kv_width)
+    )
+    loss = jnp.sum(sum_small[:, used : used + 3 * sets]) / (model_width * valid_count)
     return (
         jnp.concatenate(results, 0),
         loss,
         d_input,
-        sum_small[:, 0],
+        sum_small[:, expert_count],
         sum_query,
         sum_key,
         sum_value,
         sum_output,
-        sum_small[:, 1],
-        sum_small[:, 2 : 2 + expert_count],
+        sum_small[:, expert_count + 1],
+        sum_small[:, :expert_count],
         sum_in,
         sum_out,
     )

time: 572 us -> 529 us (0.925)
  local copies, waits for them, and re-layouts: 43.9 us -> 21.1 us
  Pallas kernels: 151 us -> 167 us
  waiting for transfers between devices: 195 us -> 180 us
  starting transfers between devices: 36.6 us -> 24.2 us
    all_gather x5, waiting for transfers between devices: 79.1 us -> 57.8 us  [gather(): return lax.all_gather(block, 'shard', axis=0, tiled=True)]
    reduce_scatter x5, waiting for transfers between devices: 26.7 us -> 40.7 us  [scatter(): return lax.psum_scatter(block, 'shard', scatter_dimension=0, tiled=True)]
    ppermute x37 -> x30, starting transfers between devices: 31.7 us -> 19.4 us  [exchange(): return lax.ppermute(block, 'rep', [(at, at ^ bit) for at in range(count)])]
    ppermute x37 -> x30, waiting for transfers between devices: 78.6 us -> 66.7 us  [exchange(): return lax.ppermute(block, 'rep', [(at, at ^ bit) for at in range(count)])]
    reduce_scatter x1, waiting for transfers between devices: 0.01 us -> 10.1 us  [body(): joined = lax.psum_scatter(joined, 'shard', scatter_dimension=0)]
    dynamic_update_slice x17 -> x7, local copies, waits for them, and re-layouts: 12.4 us -> 3.11 us  [double(): lax.dynamic_update_slice_in_dim(held, exchange(block, bit), (1 - side) *...]
    pallas_call x4 -> x8, Pallas kernels: 19.5 us -> 28.7 us  [widen(): pl.pallas_call(widen_kernel, grid_spec=pltpu.PrefetchScalarGridSpec(num_s...]
    slice x11 -> x2, local copies, waits for them, and re-layouts: 9.72 us -> 1.81 us  [the longest x1 1.79 us: body(): sum_small[:, expert_count + 1]]
  transfers between devices with their start and end apart: 52 -> 44, of which waited for: 29 -> 29; matrix products, arithmetic and copies ran while one was open for 21% -> 14% of each run, Pallas kernels for 26% -> 31%
where the time goes in v4:
time: 529 us; the launch traced here: 521 us
  waiting for transfers between devices  180 us (34%)
  Pallas kernels  167 us (32%)
  other arithmetic  65.1 us (12%)
  blocking collectives  33.6 us (6%)
  starting transfers between devices  24.2 us (5%)
  between operations  22.4 us (4%)
  local copies, waits for them, and re-layouts  21.1 us (4%)
  matrix products  7.86 us (1%)
    ppermute x30, waiting for transfers between devices, exchange(): return lax.ppermute(block, 'rep', [(at, at ^ bit) for at in range(count)])  66.7 us
    all_gather x5, waiting for transfers between devices, gather(): return lax.all_gather(block, 'shard', axis=0, tiled=True)  57.8 us
    reduce_scatter x5, waiting for transfers between devices, scatter(): return lax.psum_scatter(block, 'shard', scatter_dimension=0, tiled=True)  40.7 us
    pallas_call x2, Pallas kernels, experts_backward(): pl.pallas_call(experts_backward_kernel, grid=(experts,), in_specs=[pl.Blo...  30 us
    pallas_call x8, Pallas kernels, widen(): pl.pallas_call(widen_kernel, grid_spec=pltpu.PrefetchScalarGridSpec(num_s...  28.7 us
    pallas_call x2, Pallas kernels, experts_grads(): pl.pallas_call(functools.partial(experts_grads_kernel, outputs, row_units...  27 us
    convert_element_type x9, other arithmetic, add_parts(): return total.astype(jnp.bfloat16)  26.7 us
    pallas_call x2, Pallas kernels, experts_forward(): pl.pallas_call(experts_forward_kernel, grid=(experts,), in_specs=[pl.Bloc...  26.1 us
  transfers between devices with their start and end apart: 44, of which 29 were waited for; matrix products, arithmetic and copies ran while one was open for 14% of the time, Pallas kernels for 31%

profile of v4, /device:TPU:0, one launch (start us, length us, event | category | flops | bytes accessed | tf_op | source)
XLA Modules:
  0.0 521.1 jit_solution(3569636242812610932)
XLA Ops:
  9.0 20.3 %all-gather = bf16[128,2048]{1,0:T(8,128)(2,1)S(1)} all-gather(bf16[32,2048]{1,0:T(8,128)(2,1)S(1)} %pad_maximum_fusion.11), channel_id=2, replica_groups=mesh['rep'=8,'shard'=4] {'shard'}, dimensions={0}, use_global_device_ids=true | all-gather | bytes 655360 | tf_op jit(solution)/shard_map/all_gather | solution.py:726
  32.5 3.2 fusion.13
  37.7 2.4 collective-permute-done
  43.6 5.0 collective-permute-done.3
  52.3 3.3 pad_maximum_fusion.8
  59.0 13.3 %all-gather.3 = bf16[4,1,6657]{2,1,0:T(2,128)(2,1)S(1)} all-gather(bf16[1,1,6657]{2,1,0:T(2,128)(2,1)S(1)} %bitcast.91), channel_id=1, replica_groups=mesh['rep'=8,'shard'=4] {'shard'}, dimensions={0}, use_global_device_ids=true | all-gather | bytes 66570 | tf_op jit(solution)/shard_map/all_gather | solution.py:698
  73.0 19.9 %attention_forward.1 = (bf16[4,256,1024]{2,1,0:T(8,128)(2,1)}, bf16[4,256,1024]{2,1,0:T(8,128)(2,1)}, bf16[1024,1024]{1,0:T(8,128)(2,1)}, bf16[256,1024]{1,0:T(8...) custom-call(f32[4]{0:T(128)} %compare_select_fusion.bias_ref, ...), custom_call_target="tpu_custom_call" | custom-call | flops 1000000 | bytes 100000 | tf_op jit(solution)/shard_map/attention_forward/pallas_call | solution.py:527
  93.0 1.8 pad_maximum_fusion
  104.2 2.0 collective-permute-done.8
  107.8 2.8 collective-permute-done.9
  111.0 15.2 %all-gather.14.cloned.1.call-done.x_ref.refs_0_ = bf16[512,1024]{1,0:T(8,128)(2,1)} async-done(((bf16[128,1024]{1,0:T(8,128)(2,1)}), bf16[512,1024]{1,0:T(8,128)(2,1)}) %all-gather.14.cloned.1.call-update) | async-done | bytes 1048592 | tf_op jit(solution)/shard_map/all_gather | solution.py:698
  129.3 13.1 %experts_forward.2 = (bf16[512,1024]{1,0:T(8,128)(2,1)}, f32[4,512,1024]{2,1,0:T(8,128)}, bf16[4,512,512]{2,1,0:T(8,128)(2,1)}) custom-call(bf16[512,1024]{1,0:T(8,128)(2,1)} %all-gather.14.cloned.1.call-done.x_ref.refs_0_, f32[512,128]{1,0:T(8,128)} %pad.7.gate_ref, bf16[4,1024,1024]{2,1,0:T(8,128)(2,1)} %in_ref.7, bf16[4,512,1024]{2,1,0:T(8,128)(2,1)} %out_ref.7), custom_call_target="tpu_custom_call" | custom-call | flops 1000000 | bytes 100000 | tf_op jit(solution)/shard_map/experts_forward/pallas_call | solution.py:104
  142.8 12.9 %all-gather.16.cloned.1.call-done.x_ref.refs_4_ = bf16[512,1024]{1,0:T(8,128)(2,1)} async-done(((bf16[128,1024]{1,0:T(8,128)(2,1)}), bf16[512,1024]{1,0:T(8,128)(2,1)}) %all-gather.16.cloned.1.call-update) | async-done | bytes 1048592 | tf_op jit(solution)/shard_map/all_gather | solution.py:698
  158.8 13.0 %experts_forward.3 = (bf16[512,1024]{1,0:T(8,128)(2,1)}, f32[4,512,1024]{2,1,0:T(8,128)}, bf16[4,512,512]{2,1,0:T(8,128)(2,1)}) custom-call(bf16[512,1024]{1,0:T(8,128)(2,1)} %all-gather.16.cloned.1.call-done.x_ref.refs_4_, f32[512,128]{1,0:T(8,128)} %pad.8.gate_ref, bf16[4,1024,1024]{2,1,0:T(8,128)(2,1)} %in_ref.7, bf16[4,512,1024]{2,1,0:T(8,128)(2,1)} %out_ref.7), custom_call_target="tpu_custom_call" | custom-call | flops 1000000 | bytes 100000 | tf_op jit(solution)/shard_map/experts_forward/pallas_call | solution.py:104
  172.6 12.5 %reduce-scatter.7.cloned.1.call-done = bf16[128,1024]{1,0:T(8,128)(2,1)} async-done(((bf16[512,1024]{1,0:T(8,128)(2,1)}), bf16[128,1024]{1,0:T(8,128)(2,1)}) %reduce-scatter.7.cloned.1.call-update) | async-done | bytes 262160 | tf_op jit(solution)/shard_map/reduce_scatter | solution.py:701
  185.1 1.9 multiply_convert_fusion.3
  187.1 26.6 %reduce-scatter.9.cloned.1.call-done = bf16[128,1024]{1,0:T(8,128)(2,1)} async-done(((bf16[512,1024]{1,0:T(8,128)(2,1)}), bf16[128,1024]{1,0:T(8,128)(2,1)}) %reduce-scatter.9.cloned.1.call-update) | async-done | bytes 262160 | tf_op jit(solution)/shard_map/reduce_scatter | solution.py:701
  213.7 3.1 multiply_convert_fusion.2
  224.2 2.5 pad_maximum_fusion.16.digits_ref
  226.7 15.8 %all-gather.18.cloned.1.call-done.dmix_ref.refs_1_ = bf16[512,1024]{1,0:T(8,128)(2,1)} async-done(((bf16[128,1024]{1,0:T(8,128)(2,1)}), bf16[512,1024]{1,0:T(8,128)(2,1)}) %all-gather.18.cloned.1.call-update) | async-done | bytes 1048592 | tf_op jit(solution)/shard_map/all_gather | solution.py:698
  242.5 15.0 %experts_backward.2 = (bf16[512,1024]{1,0:T(8,128)(2,1)}, bf16[4,512,1024]{2,1,0:T(8,128)(2,1)}, f32[512,128]{1,0:T(8,128)}) custom-call(bf16[512,1024]{1,0:T(8,128)(2,1)} %all-gather.18.cloned.1.call-done.dmix_ref.refs_1_, f32[512,128]{1,0:T(8,128)} %pad.7.gate_ref, f32[4,512,1024]{2,1,0:T(8,128)} %get-tuple-element.109.gate_up_ref, ...), custom_call_target="tpu_custom_call" | custom-call | flops 1000000 | bytes 100000 | tf_op jit(solution)/shard_map/experts_backward/pallas_call | solution.py:167
  258.3 13.8 %all-gather.20.cloned.1.call-done.dmix_ref.refs_5_ = bf16[512,1024]{1,0:T(8,128)(2,1)} async-done(((bf16[128,1024]{1,0:T(8,128)(2,1)}), bf16[512,1024]{1,0:T(8,128)(2,1)}) %all-gather.20.cloned.1.call-update) | async-done | bytes 1048592 | tf_op jit(solution)/shard_map/all_gather | solution.py:698
  272.1 15.0 %experts_backward.3 = (bf16[512,1024]{1,0:T(8,128)(2,1)}, bf16[4,512,1024]{2,1,0:T(8,128)(2,1)}, f32[512,128]{1,0:T(8,128)}) custom-call(bf16[512,1024]{1,0:T(8,128)(2,1)} %all-gather.20.cloned.1.call-done.dmix_ref.refs_5_, f32[512,128]{1,0:T(8,128)} %pad.8.gate_ref, f32[4,512,1024]{2,1,0:T(8,128)} %get-tuple-element.112.gate_up_ref, ...), custom_call_target="tpu_custom_call" | custom-call | flops 1000000 | bytes 100000 | tf_op jit(solution)/shard_map/experts_backward/pallas_call | solution.py:167
  287.1 14.3 %experts_grads.2 = (bf16[1536,1024]{1,0:T(8,128)(2,1)}, bf16[1536,1024]{1,0:T(8,128)(2,1)}) custom-call(s32[2]{0:T(128)} %iota_add_fusion.order_ref, bf16[512,1024]{1,0:T(8,128)(2,1)} %all-gather.14.cloned.1.call-done.x_ref.refs_0_, bf16[512,1024]{1,0:T(8,128)(2,1)} %all-gather.18.cloned.1.call-done.dmix_ref.refs_1_, ...), custom_call_target="tpu_custom_call" | custom-call | flops 1000000 | bytes 100000 | tf_op jit(solution)/shard_map/experts_grads/pallas_call | solution.py:240
  302.6 12.7 %experts_grads.3 = bf16[2,1536,1024]{2,1,0:T(8,128)(2,1)} custom-call(s32[2]{0:T(128)} %iota_add_fusion.1.order_ref, bf16[512,1024]{1,0:T(8,128)(2,1)} %all-gather.14.cloned.1.call-done.x_ref.refs_0_, bf16[512,1024]{1,0:T(8,128)(2,1)} %all-gather.18.cloned.1.call-done.dmix_ref.refs_1_, bf16[4,512,1024]{2,1,0:T(8,128)(2,1)} %get-tuple-element.110.refs_2_, ...), custom_call_target="tpu_custom_call" | custom-call | flops 1000000 | bytes 100000 | tf_op jit(solution)/shard_map/experts_grads/pallas_call | solution.py:240
  315.3 6.2 %add_convert_fusion = (bf16[768,1024]{1,0:T(8,128)(2,1)}, bf16[768,1024]{1,0:T(8,128)(2,1)}) fusion(bf16[1536,1024]{1,0:T(8,128)(2,1)} %collective-permute-done.10, s32[]{:T(128)S(6)} %select_n.286, bf16[3072,1024]{1,0:T(8,128)(2,1)} %bitcast.65, s32[]{:T(128)S(6)} %select_n.285, bf16[1536,1024]{1,0:T(8,128)(2,1)} %collective-permute-done.11, ...), kind=kLoop, calls=%fused_computation | loop fusion | flops 6291456 | bytes 9437200 | tf_op jit(solution)/shard_map/convert_element_type | solution.py:643
  325.3 3.3 all-to-all-start
  331.4 2.9 all-to-all-done
  339.0 18.2 %attention_backward.1 = (bf16[256,1024]{1,0:T(8,128)(2,1)}, bf16[1024,1024]{1,0:T(8,128)(2,1)}) custom-call(f32[4]{0:T(128)} %compare_select_fusion.bias_ref, bf16[256,1024]{1,0:T(8,128)(2,1)} %get-tuple-element.119.query_ref, bf16[1024,512]{1,0:T(8,128)(2,1)} %get-tuple-element.120.key_ref, bf16[1024,512]{1,0:T(8,128)(2,1)} %get-tuple-element.121.value_ref, ...), custom_call_target="tpu_custom_call" | custom-call | flops 1000000 | bytes 100000 | tf_op jit(solution)/shard_map/attention_backward/pallas_call | solution.py:599
  359.4 4.4 add_convert_fusion.6
  366.7 14.0 %attention_grads.1 = (bf16[1024,1024]{1,0:T(8,128)(2,1)}, f32[256,1024]{1,0:T(8,128)}, bf16[4,128,1664]{2,1,0:T(8,128)(2,1)}, bf16[4,128,1664]{2,1,0:T(8,128)(2,...) custom-call(s32[2]{0:T(128)} %pad_add_fusion.side_ref, f32[3]{0:T(128)} %pad_maximum_fusion.16.digits_ref, ...), custom_call_target="tpu_custom_call" | custom-call | flops 1000000 | bytes 100000 | tf_op jit(solution)/shard_map/attention_grads/pallas_call | solution.py:382
  384.2 5.8 %add_convert_fusion.4 = (bf16[384,1024]{1,0:T(8,128)(2,1)}, bf16[384,1024]{1,0:T(8,128)(2,1)S(1)}) fusion(bf16[384,1024]{1,0:T(8,128)(2,1)} %copy-done.22, bf16[768,1024]{1,0:T(8,128)(2,1)} %collective-permute-done.12, s32[]{:T(128)S(6)} %select_n.299, bf16[1536,1024]{1,0:T(8,128)(2,1)} %collective-permute-done.11, s32[]{:T(128)S(6)} %dynamic_slice.203, ...), kind=kLoop, calls=%fused_computation.11 | loop fusion | flops 6291456 | bytes 7864344 | tf_op jit(solution)/shard_map/convert_element_type | solution.py:643
  391.4 2.3 collective-permute-done.21
  396.2 2.5 add_convert_fusion.2
  400.9 10.2 %collective-permute-done.19 = bf16[384,1024]{1,0:T(8,128)(2,1)S(1)} collective-permute-done((bf16[384,1024]{1,0:T(8,128)(2,1)}, bf16[384,1024]{1,0:T(8,128)(2,1)S(1)}, u32[]{:S(2)}, u32[]{:S(2)}) %collective-permute-start.19) | collective-permute-done | bytes 786464 | tf_op jit(solution)/shard_map/ppermute | solution.py:621
  412.3 14.7 %collective-permute-done.22 = bf16[4,64,1536]{2,1,0:T(8,128)(2,1)S(1)} collective-permute-done((bf16[4,64,1536]{2,1,0:T(8,128)(2,1)S(1)}, bf16[4,64,1536]{2,1,0:T(8,128)(2,1)S(1)}, u32[]{:S(2)}, u32[]{:S(2)}) %collective-permute-start.22) | collective-permute-done | bytes 786464 | tf_op jit(solution)/shard_map/ppermute | solution.py:621
  432.1 7.8 %collective-permute-done.23 = bf16[4,32,1536]{2,1,0:T(8,128)(2,1)} collective-permute-done((bf16[4,32,1536]{2,1,0:T(8,128)(2,1)S(1)}, bf16[4,32,1536]{2,1,0:T(8,128)(2,1)}, u32[]{:S(2)}, u32[]{:S(2)}) %collective-permute-start.23) | collective-permute-done | bytes 393248 | tf_op jit(solution)/shard_map/ppermute | solution.py:621
  448.3 3.5 widen.8
  451.9 3.7 widen.9
  458.1 10.1 %reduce-scatter.17.cloned.1.call-done = bf16[1,32,3200]{2,1,0:T(8,128)(2,1)} async-done(((bf16[4,32,3200]{2,1,0:T(8,128)(2,1)}), bf16[1,32,3200]{2,1,0:T(8,128)(2,1)}) %reduce-scatter.17.cloned.1.call-update) | async-done | bytes 204816 | tf_op jit(solution)/shard_map/reduce_scatter | solution.py:920
  468.2 3.5 widen.10
  471.8 3.7 widen.11
  475.5 9.9 %collective-permute-done.26.piece_ref = bf16[768,1024]{1,0:T(8,128)(2,1)} collective-permute-done((bf16[768,1024]{1,0:T(8,128)(2,1)}, bf16[768,1024]{1,0:T(8,128)(2,1)}, u32[]{:S(2)}, u32[]{:S(2)}) %collective-permute-start.26) | collective-permute-done | bytes 1572896 | tf_op jit(solution)/shard_map/ppermute | solution.py:621
  488.6 3.5 widen.12
  492.2 3.5 widen.13
  495.7 3.6 widen.14
  500.4 3.7 widen.15
  504.1 3.2 finish.1
  (260 shorter events, 93.1 us)
Async XLA Ops:
  7.2 34.2 %copy-start = (bf16[256,1024]{1,0:T(8,128)(2,1)S(1)}, bf16[256,1024]{1,0:T(8,128)(2,1)}, u32[]{:S(2)}) copy-start(bf16[256,1024]{1,0:T(8,128)(2,1)} %param.21) | copy-start | bytes 1572868
  7.2 65.8 %all-gather.12.cloned.1.call-start = ((), (), s32[]{:S(2)}) async-start(), calls=%async_computation.7 | async-start | bytes 2621440 | tf_op jit(solution)/shard_map/all_gather | solution.py:698
  7.9 85.0 %all-gather.22.cloned.1.call-start = ((), (), s32[]{:S(2)}) async-start(), calls=%async_computation.18 | async-start | bytes 1310720 | tf_op jit(solution)/shard_map/all_gather | solution.py:742
  29.3 7.5 %collective-permute-start.2 = (bf16[4,32,1024]{2,1,0:T(8,128)(2,1)S(1)}, bf16[4,32,1024]{2,1,0:T(8,128)(2,1)S(1)}, u32[]{:S(2)}, u32[]{:S(2)}) collective-permute-start(bf16[4,32,1024]{2,1,0:T(8,128)(2,1)S(1)} %get-tuple-element.284), channel_id=1, source_target_pairs={{0,16},{4,20},{8,24},{12,28},{16,0},{20,4},{24,8},{28,12},{1,17},{... | collective-permute-start | bytes 786440 | tf_op jit(solution)/shard_map/ppermute | solution.py:621
  31.0 9.2 %collective-permute-start = (bf16[4,32,1024]{2,1,0:T(8,128)(2,1)S(1)}, bf16[4,32,1024]{2,1,0:T(8,128)(2,1)S(1)}, u32[]{:S(2)}, u32[]{:S(2)}) collective-permute-start(bf16[4,32,1024]{2,1,0:T(8,128)(2,1)S(1)} %get-tuple-element.285), channel_id=1, source_target_pairs={{0,8},{4,12},{8,0},{12,4},{16,24},{20,28},{24,16},{28,20},{1,9},{5... | collective-permute-start | bytes 786440 | tf_op jit(solution)/shard_map/ppermute | solution.py:621
  36.9 11.6 %collective-permute-start.3 = (bf16[4,64,1024]{2,1,0:T(8,128)(2,1)S(1)}, bf16[4,64,1024]{2,1,0:T(8,128)(2,1)}, u32[]{:S(2)}, u32[]{:S(2)}) collective-permute-start(bf16[4,64,1024]{2,1,0:T(8,128)(2,1)S(1)} %constant_dynamic-update-slice_fusion.4), channel_id=1, source_target_pairs={{0,8},{4,12},{8,0},{12,4},{16,24},{20,28},{24,16},{28,20},{1,9},{5... | collective-permute-start | bytes 1572872 | tf_op jit(solution)/shard_map/ppermute | solution.py:621
  40.9 9.5 %collective-permute-start.1 = (bf16[4,64,1024]{2,1,0:T(8,128)(2,1)}, bf16[4,64,1024]{2,1,0:T(8,128)(2,1)}, u32[]{:S(2)}, u32[]{:S(2)}) collective-permute-start(bf16[4,64,1024]{2,1,0:T(8,128)(2,1)} %constant_dynamic-update-slice_fusion.6), channel_id=1, source_target_pairs={{0,16},{4,20},{8,24},{12,28},{16,0},{20,4},{24,8},{28,12},{1,17},{... | collective-permute-start | bytes 1572872 | tf_op jit(solution)/shard_map/ppermute | solution.py:621
  51.5 74.7 %all-gather.14.cloned.1.call-start = ((), (), s32[]{:S(2)}) async-start(), calls=%async_computation.8 | async-start | bytes 1310720 | tf_op jit(solution)/shard_map/all_gather | solution.py:698
  55.6 17.4 %copy-start.6 = (f32[1024,128]{1,0:T(8,128)}, f32[1024,128]{1,0:T(8,128)S(1)}, u32[]{:S(2)}) copy-start(f32[1024,128]{1,0:T(8,128)S(1)} %get-tuple-element.313.cos_ref) | copy-start | bytes 1572868
  57.0 16.0 %collective-permute-start.5 = (bf16[4,128,1024]{2,1,0:T(8,128)(2,1)S(1)}, bf16[4,128,1024]{2,1,0:T(8,128)(2,1)}, u32[]{:S(2)}, u32[]{:S(2)}) collective-permute-start(bf16[4,128,1024]{2,1,0:T(8,128)(2,1)S(1)} %constant_dynamic-update-slice_fusion.3.kv_held), channel_id=1, source_target_pairs={{0,4},{4,0},{8,12},{12,8},{16,20},{20,16},{24,28},{28,24},{1,5},{5... | collective-permute-start | bytes 3145736 | tf_op jit(solution)/shard_map/ppermute | solution.py:621
  57.0 16.0 %collective-permute-start.4 = (bf16[4,128,1024]{2,1,0:T(8,128)(2,1)S(1)}, bf16[4,128,1024]{2,1,0:T(8,128)(2,1)}, u32[]{:S(2)}, u32[]{:S(2)}) collective-permute-start(bf16[4,128,1024]{2,1,0:T(8,128)(2,1)S(1)} %constant_dynamic-update-slice_fusion.5.query_held), channel_id=1, source_target_pairs={{0,4},{4,0},{8,12},{12,8},{16,20},{20,16},{24,28},{28,24},{1,5},{5... | collective-permute-start | bytes 3145736 | tf_op jit(solution)/shard_map/ppermute | solution.py:621
  92.9 2.9 collective-permute-start.6
  98.3 57.4 %all-gather.16.cloned.1.call-start = ((), (), s32[]{:S(2)}) async-start(), calls=%async_computation.10 | async-start | bytes 1310720 | tf_op jit(solution)/shard_map/all_gather | solution.py:698
  98.9 86.2 %reduce-scatter.7.cloned.1.call-start = ((), (), s32[]{:S(2)}) async-start(), calls=%async_computation.9 | async-start | bytes 1310720 | tf_op jit(solution)/shard_map/reduce_scatter | solution.py:701
  100.6 1.2 collective-permute-start.7
  102.5 3.7 collective-permute-start.8
  106.8 3.7 collective-permute-start.9
  142.4 71.3 %reduce-scatter.9.cloned.1.call-start = ((), (), s32[]{:S(2)}) async-start(), calls=%async_computation.11 | async-start | bytes 1310720 | tf_op jit(solution)/shard_map/reduce_scatter | solution.py:701
  171.9 70.6 %all-gather.18.cloned.1.call-start = ((), (), s32[]{:S(2)}) async-start(), calls=%async_computation.12 | async-start | bytes 1310720 | tf_op jit(solution)/shard_map/all_gather | solution.py:698
  185.1 28.6 %copy-start.19 = (bf16[128,1024]{1,0:T(8,128)(2,1)S(1)}, bf16[128,1024]{1,0:T(8,128)(2,1)}, u32[]{:S(2)}) copy-start(bf16[128,1024]{1,0:T(8,128)(2,1)} %reduce-scatter.7.cloned.1.call-done) | copy-start | bytes 786436
  187.1 85.0 %all-gather.20.cloned.1.call-start = ((), (), s32[]{:S(2)}) async-start(), calls=%async_computation.13 | async-start | bytes 1310720 | tf_op jit(solution)/shard_map/all_gather | solution.py:698
  216.9 85.7 %reduce-scatter.11.cloned.1.call-start = ((), (), s32[]{:S(2)}) async-start(), calls=%async_computation.14 | async-start | bytes 1310720 | tf_op jit(solution)/shard_map/reduce_scatter | solution.py:701
  257.5 72.7 %reduce-scatter.13.cloned.1.call-start = ((), (), s32[]{:S(2)}) async-start(), calls=%async_computation.15 | async-start | bytes 1310720 | tf_op jit(solution)/shard_map/reduce_scatter | solution.py:701
  301.3 13.9 %collective-permute-start.10 = (bf16[1536,1024]{1,0:T(8,128)(2,1)}, bf16[1536,1024]{1,0:T(8,128)(2,1)}, u32[]{:S(2)}, u32[]{:S(2)}) collective-permute-start(bf16[1536,1024]{1,0:T(8,128)(2,1)} %get-tuple-element.116), channel_id=1, source_target_pairs={{0,4},{4,0},{8,12},{12,8},{16,20},{20,16},{24,28},{28,24},{1,5},{5... | collective-permute-start | bytes 9437192 | tf_op jit(solution)/shard_map/ppermute | solution.py:621
  301.4 13.9 %collective-permute-start.11 = (bf16[1536,1024]{1,0:T(8,128)(2,1)}, bf16[1536,1024]{1,0:T(8,128)(2,1)}, u32[]{:S(2)}, u32[]{:S(2)}) collective-permute-start(bf16[1536,1024]{1,0:T(8,128)(2,1)} %get-tuple-element.115), channel_id=1, source_target_pairs={{0,4},{4,0},{8,12},{12,8},{16,20},{20,16},{24,28},{28,24},{1,5},{5... | collective-permute-start | bytes 9437192 | tf_op jit(solution)/shard_map/ppermute | solution.py:621
  321.6 36.7 %collective-permute-start.12 = (bf16[768,1024]{1,0:T(8,128)(2,1)}, bf16[768,1024]{1,0:T(8,128)(2,1)}, u32[]{:S(2)}, u32[]{:S(2)}) collective-permute-start(bf16[768,1024]{1,0:T(8,128)(2,1)} %get-tuple-element.277), channel_id=1, source_target_pairs={{0,8},{4,12},{8,0},{12,4},{16,24},{20,28},{24,16},{28,20},{1,9},{5... | collective-permute-start | bytes 4718600 | tf_op jit(solution)/shard_map/ppermute | solution.py:621
  323.0 36.4 %collective-permute-start.13 = (bf16[768,1024]{1,0:T(8,128)(2,1)}, bf16[768,1024]{1,0:T(8,128)(2,1)}, u32[]{:S(2)}, u32[]{:S(2)}) collective-permute-start(bf16[768,1024]{1,0:T(8,128)(2,1)} %get-tuple-element.276), channel_id=1, source_target_pairs={{0,16},{4,20},{8,24},{12,28},{16,0},{20,4},{24,8},{28,12},{1,17},{... | collective-permute-start | bytes 4718600 | tf_op jit(solution)/shard_map/ppermute | solution.py:621
  325.3 8.9 %all-to-all-start = ((f32[4,256,4]{1,2,0:T(4,128)}), f32[4,256,4]{1,2,0:T(4,128)S(1)}, u32[]{:S(2)}, u32[]{:S(2)}) async-start(f32[4,256,4]{1,2,0:T(4,128)} %pad_maximum_fusion.14), calls=%async_computation.4 | async-start | bytes 32768 | tf_op jit(solution)/shard_map/all_to_all | solution.py:861
  328.7 114.4 %reduce-scatter.15.cloned.1.call-start = ((), (), s32[]{:S(2)}) async-start(), calls=%async_computation.16 | async-start | bytes 2621440 | tf_op jit(solution)/shard_map/reduce_scatter | solution.py:701
  363.8 18.6 %collective-permute-start.14 = (bf16[384,1024]{1,0:T(8,128)(2,1)}, bf16[384,1024]{1,0:T(8,128)(2,1)S(1)}, u32[]{:S(2)}, u32[]{:S(2)}) collective-permute-start(bf16[384,1024]{1,0:T(8,128)(2,1)} %get-tuple-element.275), channel_id=1, source_target_pairs={{0,16},{4,20},{8,24},{12,28},{16,0},{20,4},{24,8},{28,12},{1,17},{... | collective-permute-start | bytes 2359304 | tf_op jit(solution)/shard_map/ppermute | solution.py:621
  365.3 18.1 %collective-permute-start.15 = (bf16[384,1024]{1,0:T(8,128)(2,1)S(1)}, bf16[384,1024]{1,0:T(8,128)(2,1)S(1)}, u32[]{:S(2)}, u32[]{:S(2)}) collective-permute-start(bf16[384,1024]{1,0:T(8,128)(2,1)S(1)} %get-tuple-element.274), channel_id=1, source_target_pairs={{0,8},{4,12},{8,0},{12,4},{16,24},{20,28},{24,16},{28,20},{1,9},{5... | collective-permute-start | bytes 2359304 | tf_op jit(solution)/shard_map/ppermute | solution.py:621
  380.7 87.5 %reduce-scatter.17.cloned.1.call-start = ((), (), s32[]{:S(2)}) async-start(), calls=%async_computation.17 | async-start | bytes 1024000 | tf_op jit(solution)/shard_map/reduce_scatter | solution.py:920
  390.0 3.8 collective-permute-start.21
  390.0 6.2 %collective-permute-start.17 = (bf16[4,128,1664]{2,1,0:T(8,128)(2,1)}, bf16[4,128,1664]{2,1,0:T(8,128)(2,1)}, u32[]{:S(2)}, u32[]{:S(2)}) collective-permute-start(bf16[4,128,1664]{2,1,0:T(8,128)(2,1)} %get-tuple-element.146), channel_id=1, source_target_pairs={{0,4},{4,0},{8,12},{12,8},{16,20},{20,16},{24,28},{28,24},{1,5},{5... | collective-permute-start | bytes 5111816 | tf_op jit(solution)/shard_map/ppermute | solution.py:621
  390.5 20.6 %collective-permute-start.19 = (bf16[384,1024]{1,0:T(8,128)(2,1)}, bf16[384,1024]{1,0:T(8,128)(2,1)S(1)}, u32[]{:S(2)}, u32[]{:S(2)}) collective-permute-start(bf16[384,1024]{1,0:T(8,128)(2,1)} %get-tuple-element.272), channel_id=1, source_target_pairs={{0,16},{4,20},{8,24},{12,28},{16,0},{20,4},{24,8},{28,12},{1,17},{... | collective-permute-start | bytes 2359304 | tf_op jit(solution)/shard_map/ppermute | solution.py:621
  391.2 20.4 %collective-permute-start.16 = (bf16[384,1024]{1,0:T(8,128)(2,1)S(1)}, bf16[384,1024]{1,0:T(8,128)(2,1)S(1)}, u32[]{:S(2)}, u32[]{:S(2)}) collective-permute-start(bf16[384,1024]{1,0:T(8,128)(2,1)S(1)} %get-tuple-element.273), channel_id=1, source_target_pairs={{0,8},{4,12},{8,0},{12,4},{16,24},{20,28},{24,16},{28,20},{1,9},{5... | collective-permute-start | bytes 2359304 | tf_op jit(solution)/shard_map/ppermute | solution.py:621
  395.1 31.9 %collective-permute-start.22 = (bf16[4,64,1536]{2,1,0:T(8,128)(2,1)S(1)}, bf16[4,64,1536]{2,1,0:T(8,128)(2,1)S(1)}, u32[]{:S(2)}, u32[]{:S(2)}) collective-permute-start(bf16[4,64,1536]{2,1,0:T(8,128)(2,1)S(1)} %add_convert_fusion.3), channel_id=1, source_target_pairs={{0,16},{4,20},{8,24},{12,28},{16,0},{20,4},{24,8},{28,12},{1,17},{... | collective-permute-start | bytes 2359304 | tf_op jit(solution)/shard_map/ppermute | solution.py:621
  398.7 31.3 %collective-permute-start.18 = (bf16[4,64,1664]{2,1,0:T(8,128)(2,1)}, bf16[4,64,1664]{2,1,0:T(8,128)(2,1)}, u32[]{:S(2)}, u32[]{:S(2)}) collective-permute-start(bf16[4,64,1664]{2,1,0:T(8,128)(2,1)} %add_convert_fusion.2), channel_id=1, source_target_pairs={{0,8},{4,12},{8,0},{12,4},{16,24},{20,28},{24,16},{28,20},{1,9},{5... | collective-permute-start | bytes 2555912 | tf_op jit(solution)/shard_map/ppermute | solution.py:621
  412.3 35.4 %copy-start.4 = (bf16[768,1024]{1,0:T(8,128)(2,1)}, bf16[768,1024]{1,0:T(8,128)(2,1)S(1)}, u32[]{:S(2)}) copy-start(bf16[768,1024]{1,0:T(8,128)(2,1)S(1)} %constant_dynamic-update-slice_fusion.1.piece_ref) | copy-start | bytes 4718596
  429.4 10.4 %collective-permute-start.23 = (bf16[4,32,1536]{2,1,0:T(8,128)(2,1)S(1)}, bf16[4,32,1536]{2,1,0:T(8,128)(2,1)}, u32[]{:S(2)}, u32[]{:S(2)}) collective-permute-start(bf16[4,32,1536]{2,1,0:T(8,128)(2,1)S(1)} %add_convert_fusion.11), channel_id=1, source_target_pairs={{0,8},{4,12},{8,0},{12,4},{16,24},{20,28},{24,16},{28,20},{1,9},{5... | collective-permute-start | bytes 1179656 | tf_op jit(solution)/shard_map/ppermute | solution.py:621
  431.6 10.8 %collective-permute-start.20 = (bf16[4,32,1664]{2,1,0:T(8,128)(2,1)S(1)}, bf16[4,32,1664]{2,1,0:T(8,128)(2,1)S(1)}, u32[]{:S(2)}, u32[]{:S(2)}) collective-permute-start(bf16[4,32,1664]{2,1,0:T(8,128)(2,1)S(1)} %add_convert_fusion.9), channel_id=1, source_target_pairs={{0,16},{4,20},{8,24},{12,28},{16,0},{20,4},{24,8},{28,12},{1,17},{... | collective-permute-start | bytes 1277960 | tf_op jit(solution)/shard_map/ppermute | solution.py:621
  445.9 58.2 %all-gather.24.cloned.1.call-start = ((), (), s32[]{:S(2)}) async-start(), calls=%async_computation.19 | async-start | bytes 1843200 | tf_op jit(solution)/shard_map/all_gather | solution.py:928
  445.9 22.3 %collective-permute-start.25 = (bf16[768,1024]{1,0:T(8,128)(2,1)}, bf16[768,1024]{1,0:T(8,128)(2,1)}, u32[]{:S(2)}, u32[]{:S(2)}) collective-permute-start(bf16[768,1024]{1,0:T(8,128)(2,1)} %copy-done.5), channel_id=1, source_target_pairs={{0,4},{4,0},{8,12},{12,8},{16,20},{20,16},{24,28},{28,24},{1,5},{5... | collective-permute-start | bytes 4718600 | tf_op jit(solution)/shard_map/ppermute | solution.py:621
  446.0 39.3 %collective-permute-start.26 = (bf16[768,1024]{1,0:T(8,128)(2,1)}, bf16[768,1024]{1,0:T(8,128)(2,1)}, u32[]{:S(2)}, u32[]{:S(2)}) collective-permute-start(bf16[768,1024]{1,0:T(8,128)(2,1)} %copy-done.5), channel_id=1, source_target_pairs={{0,8},{4,12},{8,0},{12,4},{16,24},{20,28},{24,16},{28,20},{1,9},{5... | collective-permute-start | bytes 4718600 | tf_op jit(solution)/shard_map/ppermute | solution.py:621
  447.5 24.3 %collective-permute-start.24 = (bf16[768,1024]{1,0:T(8,128)(2,1)S(1)}, bf16[768,1024]{1,0:T(8,128)(2,1)}, u32[]{:S(2)}, u32[]{:S(2)}) collective-permute-start(bf16[768,1024]{1,0:T(8,128)(2,1)S(1)} %constant_dynamic-update-slice_fusion.1.piece_ref), channel_id=1, source_target_pairs={{0,4},{4,0},{8,12},{12,8},{16,20},{20,16},{24,28},{28,24},{1,5},{5... | collective-permute-start | bytes 4718600 | tf_op jit(solution)/shard_map/ppermute | solution.py:621
  447.7 38.9 %collective-permute-start.27 = (bf16[768,1024]{1,0:T(8,128)(2,1)S(1)}, bf16[768,1024]{1,0:T(8,128)(2,1)}, u32[]{:S(2)}, u32[]{:S(2)}) collective-permute-start(bf16[768,1024]{1,0:T(8,128)(2,1)S(1)} %constant_dynamic-update-slice_fusion.1.piece_ref), channel_id=1, source_target_pairs={{0,16},{4,20},{8,24},{12,28},{16,0},{20,4},{24,8},{28,12},{1,17},{... | collective-permute-start | bytes 4718600 | tf_op jit(solution)/shard_map/ppermute | solution.py:621
  486.6 9.1 %collective-permute-start.29 = (bf16[768,1024]{1,0:T(8,128)(2,1)}, bf16[768,1024]{1,0:T(8,128)(2,1)}, u32[]{:S(2)}, u32[]{:S(2)}) collective-permute-start(bf16[768,1024]{1,0:T(8,128)(2,1)} %collective-permute-done.26.piece_ref), channel_id=1, source_target_pairs={{0,4},{4,0},{8,12},{12,8},{16,20},{20,16},{24,28},{28,24},{1,5},{5... | collective-permute-start | bytes 4718600 | tf_op jit(solution)/shard_map/ppermute | solution.py:621
  486.6 12.7 %collective-permute-start.28 = (bf16[768,1024]{1,0:T(8,128)(2,1)}, bf16[768,1024]{1,0:T(8,128)(2,1)S(1)}, u32[]{:S(2)}, u32[]{:S(2)}) collective-permute-start(bf16[768,1024]{1,0:T(8,128)(2,1)} %collective-permute-done.27.piece_ref), channel_id=1, source_target_pairs={{0,4},{4,0},{8,12},{12,8},{16,20},{20,16},{24,28},{28,24},{1,5},{5... | collective-permute-start | bytes 4718600 | tf_op jit(solution)/shard_map/ppermute | solution.py:621
  (31 other events, 173.9 us)
Sparse Core Ops, SparseCore 0:
  9.6 50.6 all-gather.11
  62.4 26.8 all-gather.21
  98.4 27.8 all-gather.13
  128.3 27.4 all-gather.15
  158.4 26.6 reduce-scatter.6
  187.9 25.7 reduce-scatter.8
  215.9 26.5 all-gather.17
  244.6 27.4 all-gather.19
  275.0 26.6 reduce-scatter.10
  304.5 25.7 reduce-scatter.12
  380.8 42.5 reduce-scatter.14
  446.0 22.1 reduce-scatter.16
  470.2 27.2 all-gather.23

commit v5 on v4

--- a/solution.py
+++ b/solution.py
@@ -191,8 +191,9 @@
     )(d_mix, gates_own, gate_up, w_in, w_out)
 
 
-def experts_grads_kernel(outputs, units, order_ref, *refs):
+def experts_grads_kernel(outputs, units, based, order_ref, *refs):
     grads_refs, refs = refs[-outputs:], refs[:-outputs]
+    base_ref, refs = (refs[0], refs[1:]) if based else (None, refs)
     count = len(refs) // 4
     width = refs[0].shape[1]
     grad_in, grad_out = None, None
@@ -202,14 +203,19 @@
         part_out = dot_tn(hidden_ref[0], dmix_ref[...])
         grad_in = part_in if grad_in is None else grad_in + part_in
         grad_out = part_out if grad_out is None else grad_out + part_out
-    grad_in, grad_out = grad_in.astype(jnp.bfloat16), grad_out.astype(jnp.bfloat16)
     tall, short = width // units, grad_out.shape[0] // units
 
     def put(ref):
         for at in range(units):
             start = at * (tall + short)
-            ref[start : start + tall, :] = grad_in[at * tall : (at + 1) * tall]
-            ref[start + tall : start + tall + short, :] = grad_out[at * short : (at + 1) * short]
+            for first, size, value in (
+                (start, tall, grad_in[at * tall : (at + 1) * tall]),
+                (start + tall, short, grad_out[at * short : (at + 1) * short]),
+            ):
+                span = slice(first, first + size)
+                if based:
+                    value = value + base_ref[0, span, :].astype(jnp.float32)
+                ref[span, :] = value.astype(jnp.bfloat16)
 
     if outputs == 1:
         put(grads_refs[0].at[0])
@@ -218,7 +224,7 @@
         pl.when(pl.program_id(0) == at)(functools.partial(put, grads_refs[at]))
 
 
-def experts_grads(order, chunks, apart, row_units):
+def experts_grads(order, chunks, apart, row_units, base=None, base_at=0):
     count, width = chunks[0][0].shape
     units = chunks[0][3].shape[2]
     experts = order.shape[0]
@@ -229,6 +235,9 @@
         pl.BlockSpec((1, count, units), lambda e, order: (order[e], 0, 0)),
     ]
     rows, columns = width + units, 2 * units
+    base_specs = []
+    if base is not None:
+        base_specs = [pl.BlockSpec((1, rows, columns), lambda e, order: (base_at + e, 0, 0))]
     if apart and experts > 1:
         outputs = experts
         out_specs = [pl.BlockSpec((rows, columns), lambda e, order: (0, 0))] * experts
@@ -238,55 +247,72 @@
         out_specs = [pl.BlockSpec((1, rows, columns), lambda e, order: (e, 0, 0))]
         out_shape = [jax.ShapeDtypeStruct((experts, rows, columns), jnp.bfloat16)]
     grads = pl.pallas_call(
-        functools.partial(experts_grads_kernel, outputs, row_units),
+        functools.partial(experts_grads_kernel, outputs, row_units, base is not None),
         grid_spec=pltpu.PrefetchScalarGridSpec(
             num_scalar_prefetch=1,
             grid=(experts,),
-            in_specs=specs * len(chunks),
+            in_specs=base_specs + specs * len(chunks),
             out_specs=out_specs,
         ),
         out_shape=out_shape,
         compiler_params=pltpu.CompilerParams(vmem_limit_bytes=VMEM_BYTES),
         cost_estimate=SMALL_COST,
         name="experts_grads",
-    )(order, *[part for chunk in chunks for part in chunk])
-    return [part.reshape(-1, columns) for part in grads]
-
-
-def widen_kernel(spot_ref, piece_ref, *refs):
+    )(order, *([] if base is None else [base]), *[part for chunk in chunks for part in chunk])
+    return grads
+
+
+def widen_kernel(steps, spot_ref, first_ref, second_ref, *refs):
     gin_ref, gout_ref = refs[-2:]
     tall = gin_ref.shape[1]
-    gin_ref[0] = piece_ref[:tall, :].astype(jnp.float32)
-    gout_ref[0] = piece_ref[tall:, :].astype(jnp.float32)
-
-
-def widen(spot, piece, shapes, units, held):
-    rows, columns = shapes[0][1] + shapes[1][1], piece.shape[1]
+
+    def put(piece_ref):
+        gin_ref[0] = piece_ref[:tall, :].astype(jnp.float32)
+        gout_ref[0] = piece_ref[tall:, :].astype(jnp.float32)
+
+    at = pl.program_id(0)
+    pl.when(at < steps)(functools.partial(put, first_ref))
+    pl.when(at >= steps)(functools.partial(put, second_ref))
+
+
+def widen(spot, first, second, shapes, units, held):
+    rows, columns = shapes[0][1] + shapes[1][1], first.shape[1]
     unit = rows // units
+    steps = first.shape[0] // unit
+
+    def place(at, spot):
+        late = at >= steps
+        expert = jnp.where(late, spot[2], spot[0])
+        return (expert, jnp.where(late, spot[3] + at - steps, spot[1] + at), 0)
+
     return pl.pallas_call(
-        widen_kernel,
+        functools.partial(widen_kernel, steps),
         grid_spec=pltpu.PrefetchScalarGridSpec(
             num_scalar_prefetch=1,
-            grid=(piece.shape[0] // unit,),
-            in_specs=[pl.BlockSpec((unit, columns), lambda at, spot: (at, 0))]
+            grid=(2 * steps,),
+            in_specs=[
+                pl.BlockSpec((unit, columns), lambda at, spot: (jnp.minimum(at, steps - 1), 0)),
+                pl.BlockSpec((unit, columns), lambda at, spot: (jnp.maximum(at - steps, 0), 0)),
+            ]
             + [pl.BlockSpec(memory_space=pl.ANY)] * len(held),
             out_specs=[
-                pl.BlockSpec(
-                    (1, shape[1] // units, columns), lambda at, spot: (spot[0], spot[1] + at, 0)
-                )
-                for shape in shapes
+                pl.BlockSpec((1, shape[1] // units, columns), place) for shape in shapes
             ],
         ),
         out_shape=[jax.ShapeDtypeStruct(shape, jnp.float32) for shape in shapes],
-        input_output_aliases={2 + at: at for at in range(len(held))},
-        compiler_params=pltpu.CompilerParams(vmem_limit_bytes=VMEM_BYTES),
+        input_output_aliases={3 + at: at for at in range(len(held))},
+        compiler_params=pltpu.CompilerParams(vmem_limit_bytes=20 * MIB),
         cost_estimate=SMALL_COST,
         name="widen",
-    )(spot, piece, *held)
-
-
-def finish_kernel(spots, widths, piece_ref, query_ref, key_ref, value_ref, output_ref, small_ref):
+    )(spot, first, second, *held)
+
+
+def finish_kernel(
+    spots, widths, digits, piece_ref, query_ref, key_ref, value_ref, output_ref, router_ref, gain_ref,
+    loss_ref, small_ref
+):
     query_width, half, kv_width = widths
+    experts = router_ref.shape[1]
     rows = piece_ref.shape[1]
     for at, (first, second) in enumerate(spots):
         first_at = slice(first * rows, (first + 1) * rows)
@@ -300,20 +326,28 @@
         key_ref[second_at, :] = block[:, start : start + kv_width]
         value_ref[second_at, :] = block[:, start + kv_width : start + 2 * kv_width]
         output_ref[second_at, half:] = block[:, start + 2 * kv_width :]
-
-
-def finish(pieces, spots, widths):
+    router_ref[...] = small_ref[:, :experts]
+    turned = small_ref[...].T
+    gain_ref[...] = turned[experts : experts + 8]
+    row = lax.broadcasted_iota(jnp.int32, turned.shape, 0) - experts - 2
+    loss = jnp.sum(jnp.where((row >= 0) & (row < digits), turned, 0.0))
+    loss_ref[...] = jnp.full(loss_ref.shape, loss, jnp.float32)
+
+
+def finish(pieces, spots, widths, digits, experts):
     count, rows, _ = pieces.shape
     query_width, half, kv_width = widths
     return pl.pallas_call(
-        functools.partial(finish_kernel, spots, widths),
+        functools.partial(finish_kernel, spots, widths, digits),
         in_specs=[whole_spec()],
-        out_specs=[whole_spec()] * 5,
+        out_specs=[whole_spec()] * 7,
         out_shape=[
             jax.ShapeDtypeStruct((count * rows, columns), jnp.float32)
-            for columns in (query_width, kv_width, kv_width, 2 * half, LANES)
-        ],
-        compiler_params=pltpu.CompilerParams(vmem_limit_bytes=VMEM_BYTES),
+            for columns in (query_width, kv_width, kv_width, 2 * half, experts)
+        ]
+        + [jax.ShapeDtypeStruct((8, columns), jnp.float32) for columns in (count * rows, LANES)],
+        scratch_shapes=[pltpu.VMEM((count * rows, LANES), jnp.float32)],
+        compiler_params=pltpu.CompilerParams(vmem_limit_bytes=20 * MIB),
         cost_estimate=SMALL_COST,
         name="finish",
     )(pieces)
@@ -394,7 +428,7 @@
         scratch_shapes=[
             pltpu.VMEM((shards, 2 * rows, columns), jnp.bfloat16) for columns in widths
         ],
-        compiler_params=pltpu.CompilerParams(vmem_limit_bytes=VMEM_BYTES),
+        compiler_params=pltpu.CompilerParams(vmem_limit_bytes=46 * MIB),
         cost_estimate=SMALL_COST,
         name="attention_grads",
     )(
@@ -403,7 +437,8 @@
     )
 
 
-VMEM_BYTES = 60 * 1024 * 1024
+MIB = 1024 * 1024
+VMEM_BYTES = 60 * MIB
 
 
 def swap_halves(values):
@@ -610,7 +645,7 @@
             pltpu.VMEM((tokens, LANES), jnp.float32),
             pltpu.VMEM((tokens, LANES), jnp.float32),
         ],
-        compiler_params=pltpu.CompilerParams(vmem_limit_bytes=VMEM_BYTES),
+        compiler_params=pltpu.CompilerParams(vmem_limit_bytes=22 * MIB),
         cost_estimate=SMALL_COST,
         name="attention_backward",
     )(bias, query, key, value, log_norm, grad, *tables, *tables_own)
@@ -818,18 +853,25 @@
     half_units = row_units * flat_rows // grad_rows // 4
     second_at = (1, 0) if kept_experts > 1 else (0, 2 * half_units)
     targets = {}
-    for path, bit, (expert, unit) in ((0, far[0], (0, 0)), (1, far[-1], second_at)):
-        for across in range(2):
-            half = side_of(bit) if across == 0 else 1 - side_of(bit)
-            for core in range(2):
+    for across in range(2):
+        for core in range(2):
+            spot = []
+            for bit, (expert, unit) in ((far[0], (0, 0)), (far[-1], second_at)):
+                half = side_of(bit) if across == 0 else 1 - side_of(bit)
                 owner = side if core == 0 else 1 - side
-                targets[path, across, core] = jnp.stack(
-                    [owner * kept_experts + expert, unit + half * half_units]
-                )
+                spot += [owner * kept_experts + expert, unit + half * half_units]
+            targets[across, core] = jnp.stack(spot)
+    order = jnp.arange(kept_experts, dtype=jnp.int32)
+    order_sent = order + (1 - side) * kept_experts
+    order_kept = order + side * kept_experts
     d_rows, d_gates, backward = [], [], []
     for d_mix, (gates_own, _, gate_up, hidden_gated), tokens in zip(d_mix_in, forward, tokens_in):
         if not backward:
             gates_own = after(gates_own, place, digits, *targets.values())
+        if len(backward) == CHUNKS - 1:
+            order_all = jnp.concatenate([order_sent, order_kept])
+            partial_grads = experts_grads(order_all, backward, False, row_units)[0]
+            gates_own = after(gates_own, partial_grads)
         d_rows_part, d_gate_up, d_gates_part = experts_backward(
             d_mix, gates_own, gate_up, w_in, w_out
         )
@@ -838,12 +880,13 @@
         backward.append((tokens, d_mix, d_gate_up, hidden_gated))
     first_rows = d_rows[0]
     d_rows = jnp.concatenate(d_rows, 0).astype(jnp.float32)
-    order = jnp.arange(kept_experts, dtype=jnp.int32)
-    order_sent = order + (1 - side) * kept_experts
-    order_kept = order + side * kept_experts
-    sent = experts_grads(order_sent, backward, True, row_units)
+    sent = experts_grads(order_sent, backward[-1:], True, row_units, partial_grads, 0)
+    sent = [part.reshape(-1, columns) for part in sent]
     other = [exchange(part, near) for part in sent]
-    kept = experts_grads(after(order_kept, *sent, first_rows), backward, False, row_units)[0]
+    kept = experts_grads(
+        after(order_kept, *sent), backward[-1:], False, row_units, partial_grads, kept_experts
+    )
+    kept = after(kept[0].reshape(-1, columns), first_rows)
     half_rows = flat_rows // 2
     if kept_experts > 1:
         other_first = jnp.concatenate(other[: kept_experts // 2], 0)
@@ -882,7 +925,6 @@
         normed_all, kv_grad_all, attended, d_branch, grad_gain_ffn[None], grad_router,
         query_full, kv_full, input_all, hidden_in
     )
-    used = expert_count + 2
     kv_scattered = scatter(d_normed_kv)
     d_normed_query = after(d_normed_query, sent_first, sent_second)
     d_normed_attn = kv_scattered.astype(jnp.float32) + d_normed_query
@@ -918,44 +960,40 @@
     split_at = first[0].shape[2]
     joined = jnp.concatenate([add_parts(first), add_parts(second)], 2)
     joined = lax.psum_scatter(joined, "shard", scatter_dimension=0)
-    def put(held, piece, *where):
-        return widen(targets[where], piece, shapes, row_units, held)
-
-    held = []
-    held = put(held, own_first, 0, 0, 0)
-    held = put(held, own_second, 1, 0, 0)
+    def put(held, pieces, *where):
+        return widen(targets[where], *pieces, shapes, row_units, held)
+
+    held = put([], (own_first, own_second), 0, 0)
+    held = put(held, near_own, 0, 1)
     *held, joined, d_input = lax.optimization_barrier((*held, joined, d_input))
     gathered = lax.all_gather(joined, "rep", axis=0)
-    held = put(held, near_own[0], 0, 0, 1)
-    held = put(held, near_own[1], 1, 0, 1)
     *held, far_first, far_second = lax.optimization_barrier((*held, far_first, far_second))
     near_far = exchange(far_first, near), exchange(far_second, near)
-    held = put(held, far_first, 0, 1, 0)
-    held = put(held, far_second, 1, 1, 0)
-    held = put(held, near_far[0], 0, 1, 1)
-    held = put(held, near_far[1], 1, 1, 1)
+    held = put(held, (far_first, far_second), 1, 0)
+    held = put(held, near_far, 1, 1)
     sum_in, sum_out = held
+
     def row_of(at, order):
         return sum(((at // bit) % 2) << (len(order) - 1 - turn) for turn, bit in enumerate(order))
 
     pairs = tuple(
         (row_of(at, [near] + far), row_of(at, [near] + far[::-1])) for at in range(lax.axis_size("rep"))
     )
-    sum_query, sum_key, sum_value, sum_output, sum_small = finish(
-        gathered, pairs, (query_width, half_width, kv_width)
-    )
-    loss = jnp.sum(sum_small[:, used : used + 3 * sets]) / (model_width * valid_count)
+    sum_query, sum_key, sum_value, sum_output, sum_router, sum_gains, loss = finish(
+        gathered, pairs, (query_width, half_width, kv_width), 3 * sets, expert_count
+    )
+    loss = loss[0, 0] / (model_width * valid_count)
     return (
         jnp.concatenate(results, 0),
         loss,
         d_input,
-        sum_small[:, expert_count],
+        sum_gains[0],
         sum_query,
         sum_key,
         sum_value,
         sum_output,
-        sum_small[:, expert_count + 1],
-        sum_small[:, :expert_count],
+        sum_gains[1],
+        sum_router,
         sum_in,
         sum_out,
     )

time: 529 us -> 519 us (0.981)
  Pallas kernels: 167 us -> 158 us
  other arithmetic: 65.1 us -> 58.7 us
    pallas_call x9 -> x5, Pallas kernels: 32 us -> 20.6 us  [the longest x4 18.6 us: widen(): pl.pallas_call(functools.partial(widen_kernel, steps), grid_spec=pltpu.Pr...]
    all_gather x5, waiting for transfers between devices: 57.8 us -> 48.5 us  [gather(): return lax.all_gather(block, 'shard', axis=0, tiled=True)]
    reduce_scatter x5, waiting for transfers between devices: 40.7 us -> 47.2 us  [scatter(): return lax.psum_scatter(block, 'shard', scatter_dimension=0, tiled=True)]
    pallas_call x2 -> x3, Pallas kernels: 27 us -> 33.3 us  [experts_grads(): pl.pallas_call(functools.partial(experts_grads_kernel, outputs, row_units...]
    unnamed x76 -> x114, local copies, waits for them, and re-layouts: 8.57 us -> 14.8 us
  transfers between devices with their start and end apart: 44 -> 44, of which waited for: 29 -> 25; matrix products, arithmetic and copies ran while one was open for 14% -> 13% of each run, Pallas kernels for 31% -> 31%
where the time goes in v5:
time: 519 us; the launch traced here: 511 us
  waiting for transfers between devices  177 us (34%)
  Pallas kernels  158 us (30%)
  other arithmetic  58.7 us (11%)
  blocking collectives  33.7 us (6%)
  starting transfers between devices  29.4 us (6%)
  local copies, waits for them, and re-layouts  26 us (5%)
  between operations  22.6 us (4%)
  matrix products  5.85 us (1%)
    ppermute x30, waiting for transfers between devices, exchange(): return lax.ppermute(block, 'rep', [(at, at ^ bit) for at in range(count)])  71.7 us
    all_gather x5, waiting for transfers between devices, gather(): return lax.all_gather(block, 'shard', axis=0, tiled=True)  48.5 us
    reduce_scatter x5, waiting for transfers between devices, scatter(): return lax.psum_scatter(block, 'shard', scatter_dimension=0, tiled=True)  47.2 us
    pallas_call x3, Pallas kernels, experts_grads(): pl.pallas_call(functools.partial(experts_grads_kernel, outputs, row_units...  33.3 us
    pallas_call x2, Pallas kernels, experts_backward(): pl.pallas_call(experts_backward_kernel, grid=(experts,), in_specs=[pl.Blo...  30 us
    convert_element_type x9, other arithmetic, add_parts(): return total.astype(jnp.bfloat16)  28.7 us
    pallas_call x2, Pallas kernels, experts_forward(): pl.pallas_call(experts_forward_kernel, grid=(experts,), in_specs=[pl.Bloc...  26.1 us
    ppermute x30, starting transfers between devices, exchange(): return lax.ppermute(block, 'rep', [(at, at ^ bit) for at in range(count)])  24.5 us
  transfers between devices with their start and end apart: 44, of which 25 were waited for; matrix products, arithmetic and copies ran while one was open for 13% of the time, Pallas kernels for 31%

profile of v5, /device:TPU:0, one launch (start us, length us, event | category | flops | bytes accessed | tf_op | source)
XLA Modules:
  0.0 511.0 jit_solution(2810385406373160601)
XLA Ops:
  9.0 20.3 %all-gather = bf16[128,2048]{1,0:T(8,128)(2,1)S(1)} all-gather(bf16[32,2048]{1,0:T(8,128)(2,1)S(1)} %pad_maximum_fusion.11), channel_id=2, replica_groups=mesh['rep'=8,'shard'=4] {'shard'}, dimensions={0}, use_global_device_ids=true | all-gather | bytes 655360 | tf_op jit(solution)/shard_map/all_gather | solution.py:761
  32.5 3.1 fusion.13
  36.0 4.0 collective-permute-done
  42.8 6.6 %collective-permute-done.1 = bf16[4,64,1024]{2,1,0:T(8,128)(2,1)} collective-permute-done((bf16[4,64,1024]{2,1,0:T(8,128)(2,1)S(1)}, bf16[4,64,1024]{2,1,0:T(8,128)(2,1)}, u32[]{:S(2)}, u32[]{:S(2)}) %collective-permute-start.1) | collective-permute-done | bytes 524320 | tf_op jit(solution)/shard_map/ppermute | solution.py:656
  53.4 2.8 pad_maximum_fusion.8
  59.5 13.4 %all-gather.3 = bf16[4,1,6657]{2,1,0:T(2,128)(2,1)S(1)} all-gather(bf16[1,1,6657]{2,1,0:T(2,128)(2,1)S(1)} %bitcast.93), channel_id=1, replica_groups=mesh['rep'=8,'shard'=4] {'shard'}, dimensions={0}, use_global_device_ids=true | all-gather | bytes 66570 | tf_op jit(solution)/shard_map/all_gather | solution.py:733
  73.6 19.8 %attention_forward.1 = (bf16[4,256,1024]{2,1,0:T(8,128)(2,1)}, bf16[4,256,1024]{2,1,0:T(8,128)(2,1)}, bf16[1024,1024]{1,0:T(8,128)(2,1)}, bf16[256,1024]{1,0:T(8...) custom-call(f32[4]{0:T(128)} %compare_select_fusion.bias_ref, ...), custom_call_target="tpu_custom_call" | custom-call | flops 1000000 | bytes 100000 | tf_op jit(solution)/shard_map/attention_forward/pallas_call | solution.py:562
  93.6 1.8 pad_maximum_fusion
  105.6 2.0 collective-permute-done.8
  108.7 3.1 collective-permute-done.9
  112.4 14.8 %all-gather.14.cloned.1.call-done.x_ref.refs_0_ = bf16[512,1024]{1,0:T(8,128)(2,1)} async-done(((bf16[128,1024]{1,0:T(8,128)(2,1)}), bf16[512,1024]{1,0:T(8,128)(2,1)}) %all-gather.14.cloned.1.call-update) | async-done | bytes 1048592 | tf_op jit(solution)/shard_map/all_gather | solution.py:733
  127.2 1.7 fusion.28
  130.3 13.1 %experts_forward.2 = (bf16[512,1024]{1,0:T(8,128)(2,1)}, f32[4,512,1024]{2,1,0:T(8,128)}, bf16[4,512,512]{2,1,0:T(8,128)(2,1)}) custom-call(bf16[512,1024]{1,0:T(8,128)(2,1)} %all-gather.14.cloned.1.call-done.x_ref.refs_0_, f32[512,128]{1,0:T(8,128)} %pad.7.gate_ref, bf16[4,1024,1024]{2,1,0:T(8,128)(2,1)} %in_ref.7, bf16[4,512,1024]{2,1,0:T(8,128)(2,1)} %out_ref.7), custom_call_target="tpu_custom_call" | custom-call | flops 1000000 | bytes 100000 | tf_op jit(solution)/shard_map/experts_forward/pallas_call | solution.py:104
  143.7 13.0 %all-gather.16.cloned.1.call-done.x_ref.refs_1_ = bf16[512,1024]{1,0:T(8,128)(2,1)} async-done(((bf16[128,1024]{1,0:T(8,128)(2,1)}), bf16[512,1024]{1,0:T(8,128)(2,1)}) %all-gather.16.cloned.1.call-update) | async-done | bytes 1048592 | tf_op jit(solution)/shard_map/all_gather | solution.py:733
  159.8 13.1 %experts_forward.3 = (bf16[512,1024]{1,0:T(8,128)(2,1)}, f32[4,512,1024]{2,1,0:T(8,128)}, bf16[4,512,512]{2,1,0:T(8,128)(2,1)}) custom-call(bf16[512,1024]{1,0:T(8,128)(2,1)} %all-gather.16.cloned.1.call-done.x_ref.refs_1_, f32[512,128]{1,0:T(8,128)} %pad.8.gate_ref, bf16[4,1024,1024]{2,1,0:T(8,128)(2,1)} %in_ref.7, bf16[4,512,1024]{2,1,0:T(8,128)(2,1)} %out_ref.7), custom_call_target="tpu_custom_call" | custom-call | flops 1000000 | bytes 100000 | tf_op jit(solution)/shard_map/experts_forward/pallas_call | solution.py:104
  173.6 12.4 %reduce-scatter.7.cloned.1.call-done = bf16[128,1024]{1,0:T(8,128)(2,1)} async-done(((bf16[512,1024]{1,0:T(8,128)(2,1)}), bf16[128,1024]{1,0:T(8,128)(2,1)}) %reduce-scatter.7.cloned.1.call-update) | async-done | bytes 262160 | tf_op jit(solution)/shard_map/reduce_scatter | solution.py:736
  186.1 2.0 multiply_convert_fusion.3
  188.1 26.6 %reduce-scatter.9.cloned.1.call-done = bf16[128,1024]{1,0:T(8,128)(2,1)} async-done(((bf16[512,1024]{1,0:T(8,128)(2,1)}), bf16[128,1024]{1,0:T(8,128)(2,1)}) %reduce-scatter.9.cloned.1.call-update) | async-done | bytes 262160 | tf_op jit(solution)/shard_map/reduce_scatter | solution.py:736
  214.7 3.0 multiply_convert_fusion.2
  222.0 1.9 pad_maximum_fusion.16.digits_ref
  223.9 19.4 %all-gather.18.cloned.1.call-done.dmix_ref.refs_1_ = bf16[512,1024]{1,0:T(8,128)(2,1)} async-done(((bf16[128,1024]{1,0:T(8,128)(2,1)}), bf16[512,1024]{1,0:T(8,128)(2,1)}) %all-gather.18.cloned.1.call-update) | async-done | bytes 1048592 | tf_op jit(solution)/shard_map/all_gather | solution.py:733
  243.3 15.0 %experts_backward.2 = (bf16[512,1024]{1,0:T(8,128)(2,1)}, bf16[4,512,1024]{2,1,0:T(8,128)(2,1)}, f32[512,128]{1,0:T(8,128)}) custom-call(bf16[512,1024]{1,0:T(8,128)(2,1)} %all-gather.18.cloned.1.call-done.dmix_ref.refs_1_, f32[512,128]{1,0:T(8,128)} %pad.7.gate_ref, f32[4,512,1024]{2,1,0:T(8,128)} %get-tuple-element.105.gate_up_ref, ...), custom_call_target="tpu_custom_call" | custom-call | flops 1000000 | bytes 100000 | tf_op jit(solution)/shard_map/experts_backward/pallas_call | solution.py:167
  259.2 12.5 %experts_grads.3.refs_0_ = bf16[4,1536,1024]{2,1,0:T(8,128)(2,1)} custom-call(s32[4]{0:T(128)} %pad_add_fusion.order_ref, bf16[512,1024]{1,0:T(8,128)(2,1)} %all-gather.14.cloned.1.call-done.x_ref.refs_0_, bf16[512,1024]{1,0:T(8,128)(2,1)} %all-gather.18.cloned.1.call-done.dmix_ref.refs_1_, bf16[4,512,1024]{2,1,0:T(8,128)(2,1)} %get-tuple-element.106.refs_2_, ...), custom_call_target="tpu_custom_call" | custom-call | flops 1000000 | bytes 100000 | tf_op jit(solution)/shard_map/experts_grads/pallas_call | solution.py:249
  273.1 15.0 %experts_backward.3 = (bf16[512,1024]{1,0:T(8,128)(2,1)}, bf16[4,512,1024]{2,1,0:T(8,128)(2,1)}, f32[512,128]{1,0:T(8,128)}) custom-call(bf16[512,1024]{1,0:T(8,128)(2,1)} %all-gather.20.cloned.1.call-done.dmix_ref.refs_2_, f32[512,128]{1,0:T(8,128)} %pad.8.gate_ref, f32[4,512,1024]{2,1,0:T(8,128)} %get-tuple-element.109.gate_up_ref, ...), custom_call_target="tpu_custom_call" | custom-call | flops 1000000 | bytes 100000 | tf_op jit(solution)/shard_map/experts_backward/pallas_call | solution.py:167
  288.1 11.4 %experts_grads.4 = (bf16[1536,1024]{1,0:T(8,128)(2,1)}, bf16[1536,1024]{1,0:T(8,128)(2,1)}) custom-call(s32[2]{0:T(128)} %copy-done.50, bf16[4,1536,1024]{2,1,0:T(8,128)(2,1)} %experts_grads.3.refs_0_, bf16[512,1024]{1,0:T(8,128)(2,1)} %all-gather.16.cloned.1.call-done.x_ref.refs_1_, bf16[512,1024]{1,0:T(8,128)(2,1)} %all-gather.20.cloned.1.call-done.dmix_ref.refs_2_, ...), custom_call_target="tpu_custom_call" | custom-call | flops 1000000 | bytes 100000 | tf_op jit(solution)/shard_map/experts_grads/pallas_call | solution.py:249
  300.2 9.4 %experts_grads.5 = bf16[2,1536,1024]{2,1,0:T(8,128)(2,1)} custom-call(s32[2]{0:T(128)} %copy-done.49, bf16[4,1536,1024]{2,1,0:T(8,128)(2,1)} %experts_grads.3.refs_0_, bf16[512,1024]{1,0:T(8,128)(2,1)} %all-gather.16.cloned.1.call-done.x_ref.refs_1_, bf16[512,1024]{1,0:T(8,128)(2,1)} %all-gather.20.cloned.1.call-done.dmix_ref.refs_2_, ...), custom_call_target="tpu_custom_call" | custom-call | flops 1000000 | bytes 100000 | tf_op jit(solution)/shard_map/experts_grads/pallas_call | solution.py:249
  309.9 6.2 %add_convert_fusion = (bf16[768,1024]{1,0:T(8,128)(2,1)}, bf16[768,1024]{1,0:T(8,128)(2,1)}) fusion(bf16[1536,1024]{1,0:T(8,128)(2,1)} %collective-permute-done.11, s32[]{:T(128)S(6)} %select_n.298, bf16[3072,1024]{1,0:T(8,128)(2,1)} %bitcast.69, s32[]{:T(128)S(6)} %select_n.297, bf16[1536,1024]{1,0:T(8,128)(2,1)} %collective-permute-done.10, ...), kind=kLoop, calls=%fused_computation | loop fusion | flops 6291456 | bytes 9437200 | tf_op jit(solution)/shard_map/convert_element_type | solution.py:678
  319.9 3.5 all-to-all-start
  323.4 8.1 %reduce-scatter.13.cloned.1.call-done = bf16[128,1024]{1,0:T(8,128)(2,1)} async-done(((bf16[512,1024]{1,0:T(8,128)(2,1)}), bf16[128,1024]{1,0:T(8,128)(2,1)}) %reduce-scatter.13.cloned.1.call-update) | async-done | bytes 262160 | tf_op jit(solution)/shard_map/reduce_scatter | solution.py:736
  334.3 2.8 multiply_convert_fusion
  339.0 15.1 %attention_backward.1 = (bf16[256,1024]{1,0:T(8,128)(2,1)S(1)}, bf16[1024,1024]{1,0:T(8,128)(2,1)S(1)}) custom-call(f32[4]{0:T(128)S(1)} %copy-done.23, bf16[256,1024]{1,0:T(8,128)(2,1)S(1)} %copy-done.19, bf16[1024,512]{1,0:T(8,128)(2,1)S(1)} %copy-done.15, bf16[1024,512]{1,0:T(8,128)(2,1)S(1)} %copy-done.16, f32[8,512]{1,0:T(8,128)S(1)} %copy-done.22, ...), custom_call_target="tpu_custom_call" | custom-call | flops 1000000 | bytes 100000 | tf_op jit(solution)/shard_map/attention_backward/pallas_call | solution.py:634
  355.5 4.9 add_convert_fusion.6
  364.5 13.1 %attention_grads.1 = (bf16[1024,1024]{1,0:T(8,128)(2,1)}, f32[256,1024]{1,0:T(8,128)S(1)}, bf16[4,128,1664]{2,1,0:T(8,128)(2,1)}, bf16[4,128,1664]{2,1,0:T(8,128...) custom-call(s32[2]{0:T(128)S(1)} %pad_add_fusion.1.side_ref, ...), custom_call_target="tpu_custom_call" | custom-call | flops 1000000 | bytes 100000 | tf_op jit(solution)/shard_map/attention_grads/pallas_call | solution.py:416
  381.0 5.9 %add_convert_fusion.4 = (bf16[384,1024]{1,0:T(8,128)(2,1)}, bf16[384,1024]{1,0:T(8,128)(2,1)}) fusion(bf16[384,1024]{1,0:T(8,128)(2,1)} %collective-permute-done.15, bf16[768,1024]{1,0:T(8,128)(2,1)} %collective-permute-done.13, s32[]{:T(128)S(6)} %select_n.311, bf16[1536,1024]{1,0:T(8,128)(2,1)} %collective-permute-done.11, s32[]{:T(128)S(6)} %dynamic_slice.203, ...), kind=kLoop, calls=%fused_computation.11 | loop fusion | flops 6291456 | bytes 7864344 | tf_op jit(solution)/shard_map/convert_element_type | solution.py:678
  393.6 2.3 add_convert_fusion.2
  397.3 10.7 %collective-permute-done.19 = bf16[384,1024]{1,0:T(8,128)(2,1)S(1)} collective-permute-done((bf16[384,1024]{1,0:T(8,128)(2,1)}, bf16[384,1024]{1,0:T(8,128)(2,1)S(1)}, u32[]{:S(2)}, u32[]{:S(2)}) %collective-permute-start.19) | collective-permute-done | bytes 786464 | tf_op jit(solution)/shard_map/ppermute | solution.py:656
  409.2 15.0 %collective-permute-done.22 = bf16[4,64,1536]{2,1,0:T(8,128)(2,1)S(1)} collective-permute-done((bf16[4,64,1536]{2,1,0:T(8,128)(2,1)S(1)}, bf16[4,64,1536]{2,1,0:T(8,128)(2,1)S(1)}, u32[]{:S(2)}, u32[]{:S(2)}) %collective-permute-start.22) | collective-permute-done | bytes 786464 | tf_op jit(solution)/shard_map/ppermute | solution.py:656
  425.2 2.2 add_convert_fusion.11
  432.1 5.6 %collective-permute-done.23 = bf16[4,32,1536]{2,1,0:T(8,128)(2,1)} collective-permute-done((bf16[4,32,1536]{2,1,0:T(8,128)(2,1)}, bf16[4,32,1536]{2,1,0:T(8,128)(2,1)}, u32[]{:S(2)}, u32[]{:S(2)}) %collective-permute-start.23) | collective-permute-done | bytes 393248 | tf_op jit(solution)/shard_map/ppermute | solution.py:656
  437.6 2.4 add_convert_fusion.10
  441.0 1.9 add_convert_fusion.8
  447.9 3.6 widen.4
  454.1 3.6 widen.5
  457.6 8.0 %reduce-scatter.17.cloned.1.call-done = bf16[1,32,3200]{2,1,0:T(8,128)(2,1)} async-done(((bf16[4,32,3200]{2,1,0:T(8,128)(2,1)}), bf16[1,32,3200]{2,1,0:T(8,128)(2,1)}) %reduce-scatter.17.cloned.1.call-update) | async-done | bytes 204816 | tf_op jit(solution)/shard_map/reduce_scatter | solution.py:962
  465.7 17.4 %collective-permute-done.26.first_ref = bf16[768,1024]{1,0:T(8,128)(2,1)} collective-permute-done((bf16[768,1024]{1,0:T(8,128)(2,1)S(1)}, bf16[768,1024]{1,0:T(8,128)(2,1)}, u32[]{:S(2)}, u32[]{:S(2)}) %collective-permute-start.26) | collective-permute-done | bytes 1572896 | tf_op jit(solution)/shard_map/ppermute | solution.py:656
  485.7 5.8 %widen.6 = (f32[4,1024,1024]{2,1,0:T(8,128)}, f32[4,512,1024]{2,1,0:T(8,128)}) custom-call(s32[4]{0:T(128)S(1)} %get-tuple-element.297.spot_ref, bf16[768,1024]{1,0:T(8,128)(2,1)} %collective-permute-done.26.first_ref, bf16[768,1024]{1,0:T(8,128)(2,1)} %collective-permute-done.27.second_ref, ...), custom_call_target="tpu_custom_call", output_to_operand_aliasing={{0}: (3, {}), {1}: (4, {})} | custom-call | flops 1000000 | bytes 100000 | tf_op jit(solution)/shard_map/widen/pallas_call | solution.py:288
  491.5 5.6 %widen.7 = (f32[4,1024,1024]{2,1,0:T(8,128)}, f32[4,512,1024]{2,1,0:T(8,128)}) custom-call(s32[4]{0:T(128)S(1)} %get-tuple-element.298.spot_ref, bf16[768,1024]{1,0:T(8,128)(2,1)S(1)} %collective-permute-done.28.first_ref, bf16[768,1024]{1,0:T(8,128)(2,1)} %collective-permute-done.29.second_ref, ...), custom_call_target="tpu_custom_call", output_to_operand_aliasing={{0}: (3, {}), {1}: (4, {})} | custom-call | flops 1000000 | bytes 100000 | tf_op jit(solution)/shard_map/widen/pallas_call | solution.py:288
  498.6 1.9 finish.1
  (293 shorter events, 81.7 us)
Async XLA Ops:
  7.2 34.6 %copy-start = (bf16[256,1024]{1,0:T(8,128)(2,1)S(1)}, bf16[256,1024]{1,0:T(8,128)(2,1)}, u32[]{:S(2)}) copy-start(bf16[256,1024]{1,0:T(8,128)(2,1)} %param.21) | copy-start | bytes 1572868
  7.2 66.4 %all-gather.12.cloned.1.call-start = ((), (), s32[]{:S(2)}) async-start(), calls=%async_computation.7 | async-start | bytes 2621440 | tf_op jit(solution)/shard_map/all_gather | solution.py:733
  7.9 85.6 %all-gather.22.cloned.1.call-start = ((), (), s32[]{:S(2)}) async-start(), calls=%async_computation.18 | async-start | bytes 1310720 | tf_op jit(solution)/shard_map/all_gather | solution.py:777
  29.3 10.7 %collective-permute-start.2 = (bf16[4,32,1024]{2,1,0:T(8,128)(2,1)S(1)}, bf16[4,32,1024]{2,1,0:T(8,128)(2,1)S(1)}, u32[]{:S(2)}, u32[]{:S(2)}) collective-permute-start(bf16[4,32,1024]{2,1,0:T(8,128)(2,1)S(1)} %get-tuple-element.274), channel_id=1, source_target_pairs={{0,16},{4,20},{8,24},{12,28},{16,0},{20,4},{24,8},{28,12},{1,17},{... | collective-permute-start | bytes 786440 | tf_op jit(solution)/shard_map/ppermute | solution.py:656
  31.0 9.0 %collective-permute-start = (bf16[4,32,1024]{2,1,0:T(8,128)(2,1)S(1)}, bf16[4,32,1024]{2,1,0:T(8,128)(2,1)S(1)}, u32[]{:S(2)}, u32[]{:S(2)}) collective-permute-start(bf16[4,32,1024]{2,1,0:T(8,128)(2,1)S(1)} %get-tuple-element.275), channel_id=1, source_target_pairs={{0,8},{4,12},{8,0},{12,4},{16,24},{20,28},{24,16},{28,20},{1,9},{5... | collective-permute-start | bytes 786440 | tf_op jit(solution)/shard_map/ppermute | solution.py:656
  40.0 9.4 %collective-permute-start.1 = (bf16[4,64,1024]{2,1,0:T(8,128)(2,1)S(1)}, bf16[4,64,1024]{2,1,0:T(8,128)(2,1)}, u32[]{:S(2)}, u32[]{:S(2)}) collective-permute-start(bf16[4,64,1024]{2,1,0:T(8,128)(2,1)S(1)} %constant_dynamic-update-slice_fusion.6), channel_id=1, source_target_pairs={{0,16},{4,20},{8,24},{12,28},{16,0},{20,4},{24,8},{28,12},{1,17},{... | collective-permute-start | bytes 1572872 | tf_op jit(solution)/shard_map/ppermute | solution.py:656
  40.1 11.3 %collective-permute-start.3 = (bf16[4,64,1024]{2,1,0:T(8,128)(2,1)S(1)}, bf16[4,64,1024]{2,1,0:T(8,128)(2,1)}, u32[]{:S(2)}, u32[]{:S(2)}) collective-permute-start(bf16[4,64,1024]{2,1,0:T(8,128)(2,1)S(1)} %constant_dynamic-update-slice_fusion.4), channel_id=1, source_target_pairs={{0,8},{4,12},{8,0},{12,4},{16,24},{20,28},{24,16},{28,20},{1,9},{5... | collective-permute-start | bytes 1572872 | tf_op jit(solution)/shard_map/ppermute | solution.py:656
  52.6 74.7 %all-gather.14.cloned.1.call-start = ((), (), s32[]{:S(2)}) async-start(), calls=%async_computation.8 | async-start | bytes 1310720 | tf_op jit(solution)/shard_map/all_gather | solution.py:733
  57.6 16.0 %collective-permute-start.5 = (bf16[4,128,1024]{2,1,0:T(8,128)(2,1)S(1)}, bf16[4,128,1024]{2,1,0:T(8,128)(2,1)}, u32[]{:S(2)}, u32[]{:S(2)}) collective-permute-start(bf16[4,128,1024]{2,1,0:T(8,128)(2,1)S(1)} %constant_dynamic-update-slice_fusion.3.kv_held), channel_id=1, source_target_pairs={{0,4},{4,0},{8,12},{12,8},{16,20},{20,16},{24,28},{28,24},{1,5},{5... | collective-permute-start | bytes 3145736 | tf_op jit(solution)/shard_map/ppermute | solution.py:656
  57.6 16.0 %collective-permute-start.4 = (bf16[4,128,1024]{2,1,0:T(8,128)(2,1)}, bf16[4,128,1024]{2,1,0:T(8,128)(2,1)}, u32[]{:S(2)}, u32[]{:S(2)}) collective-permute-start(bf16[4,128,1024]{2,1,0:T(8,128)(2,1)} %copy-done.29), channel_id=1, source_target_pairs={{0,4},{4,0},{8,12},{12,8},{16,20},{20,16},{24,28},{28,24},{1,5},{5... | collective-permute-start | bytes 3145736 | tf_op jit(solution)/shard_map/ppermute | solution.py:656
  93.5 2.9 collective-permute-start.6
  99.7 57.0 %all-gather.16.cloned.1.call-start = ((), (), s32[]{:S(2)}) async-start(), calls=%async_computation.10 | async-start | bytes 1310720 | tf_op jit(solution)/shard_map/all_gather | solution.py:733
  100.2 85.8 %reduce-scatter.7.cloned.1.call-start = ((), (), s32[]{:S(2)}) async-start(), calls=%async_computation.9 | async-start | bytes 1310720 | tf_op jit(solution)/shard_map/reduce_scatter | solution.py:736
  102.0 1.2 collective-permute-start.7
  103.9 3.7 collective-permute-start.8
  108.2 3.7 collective-permute-start.9
  143.4 71.3 %reduce-scatter.9.cloned.1.call-start = ((), (), s32[]{:S(2)}) async-start(), calls=%async_computation.11 | async-start | bytes 1310720 | tf_op jit(solution)/shard_map/reduce_scatter | solution.py:736
  159.8 26.3 %copy-start.40 = (bf16[256,1024]{1,0:T(8,128)(2,1)S(1)}, bf16[256,1024]{1,0:T(8,128)(2,1)}, u32[]{:S(2)}) copy-start(bf16[256,1024]{1,0:T(8,128)(2,1)} %param.15) | copy-start | bytes 1572868
  172.9 70.5 %all-gather.18.cloned.1.call-start = ((), (), s32[]{:S(2)}) async-start(), calls=%async_computation.12 | async-start | bytes 1310720 | tf_op jit(solution)/shard_map/all_gather | solution.py:733
  188.1 85.0 %all-gather.20.cloned.1.call-start = ((), (), s32[]{:S(2)}) async-start(), calls=%async_computation.13 | async-start | bytes 1310720 | tf_op jit(solution)/shard_map/all_gather | solution.py:733
  217.8 91.8 %reduce-scatter.11.cloned.1.call-start = ((), (), s32[]{:S(2)}) async-start(), calls=%async_computation.14 | async-start | bytes 1310720 | tf_op jit(solution)/shard_map/reduce_scatter | solution.py:736
  258.4 73.1 %reduce-scatter.13.cloned.1.call-start = ((), (), s32[]{:S(2)}) async-start(), calls=%async_computation.15 | async-start | bytes 1310720 | tf_op jit(solution)/shard_map/reduce_scatter | solution.py:736
  299.4 10.2 %collective-permute-start.10 = (bf16[1536,1024]{1,0:T(8,128)(2,1)}, bf16[1536,1024]{1,0:T(8,128)(2,1)}, u32[]{:S(2)}, u32[]{:S(2)}) collective-permute-start(bf16[1536,1024]{1,0:T(8,128)(2,1)} %get-tuple-element.112), channel_id=1, source_target_pairs={{0,4},{4,0},{8,12},{12,8},{16,20},{20,16},{24,28},{28,24},{1,5},{5... | collective-permute-start | bytes 9437192 | tf_op jit(solution)/shard_map/ppermute | solution.py:656
  299.4 10.5 %collective-permute-start.11 = (bf16[1536,1024]{1,0:T(8,128)(2,1)}, bf16[1536,1024]{1,0:T(8,128)(2,1)}, u32[]{:S(2)}, u32[]{:S(2)}) collective-permute-start(bf16[1536,1024]{1,0:T(8,128)(2,1)} %get-tuple-element.113), channel_id=1, source_target_pairs={{0,4},{4,0},{8,12},{12,8},{16,20},{20,16},{24,28},{28,24},{1,5},{5... | collective-permute-start | bytes 9437192 | tf_op jit(solution)/shard_map/ppermute | solution.py:656
  316.1 39.4 %collective-permute-start.13 = (bf16[768,1024]{1,0:T(8,128)(2,1)}, bf16[768,1024]{1,0:T(8,128)(2,1)}, u32[]{:S(2)}, u32[]{:S(2)}) collective-permute-start(bf16[768,1024]{1,0:T(8,128)(2,1)} %get-tuple-element.266), channel_id=1, source_target_pairs={{0,16},{4,20},{8,24},{12,28},{16,0},{20,4},{24,8},{28,12},{1,17},{... | collective-permute-start | bytes 4718600 | tf_op jit(solution)/shard_map/ppermute | solution.py:656
  317.6 37.9 %collective-permute-start.12 = (bf16[768,1024]{1,0:T(8,128)(2,1)}, bf16[768,1024]{1,0:T(8,128)(2,1)}, u32[]{:S(2)}, u32[]{:S(2)}) collective-permute-start(bf16[768,1024]{1,0:T(8,128)(2,1)} %get-tuple-element.267), channel_id=1, source_target_pairs={{0,8},{4,12},{8,0},{12,4},{16,24},{20,28},{24,16},{28,20},{1,9},{5... | collective-permute-start | bytes 4718600 | tf_op jit(solution)/shard_map/ppermute | solution.py:656
  319.9 12.8 %all-to-all-start = ((f32[4,256,4]{1,2,0:T(4,128)}), f32[4,256,4]{1,2,0:T(4,128)S(1)}, u32[]{:S(2)}, u32[]{:S(2)}) async-start(f32[4,256,4]{1,2,0:T(4,128)} %pad_maximum_fusion.14), calls=%async_computation.4 | async-start | bytes 32768 | tf_op jit(solution)/shard_map/all_to_all | solution.py:904
  323.4 117.6 %reduce-scatter.15.cloned.1.call-start = ((), (), s32[]{:S(2)}) async-start(), calls=%async_computation.16 | async-start | bytes 2621440 | tf_op jit(solution)/shard_map/reduce_scatter | solution.py:736
  360.3 19.4 %collective-permute-start.15 = (bf16[384,1024]{1,0:T(8,128)(2,1)}, bf16[384,1024]{1,0:T(8,128)(2,1)}, u32[]{:S(2)}, u32[]{:S(2)}) collective-permute-start(bf16[384,1024]{1,0:T(8,128)(2,1)} %get-tuple-element.264), channel_id=1, source_target_pairs={{0,8},{4,12},{8,0},{12,4},{16,24},{20,28},{24,16},{28,20},{1,9},{5... | collective-permute-start | bytes 2359304 | tf_op jit(solution)/shard_map/ppermute | solution.py:656
  361.8 19.1 %collective-permute-start.14 = (bf16[384,1024]{1,0:T(8,128)(2,1)}, bf16[384,1024]{1,0:T(8,128)(2,1)}, u32[]{:S(2)}, u32[]{:S(2)}) collective-permute-start(bf16[384,1024]{1,0:T(8,128)(2,1)} %get-tuple-element.265), channel_id=1, source_target_pairs={{0,16},{4,20},{8,24},{12,28},{16,0},{20,4},{24,8},{28,12},{1,17},{... | collective-permute-start | bytes 2359304 | tf_op jit(solution)/shard_map/ppermute | solution.py:656
  378.8 86.9 %reduce-scatter.17.cloned.1.call-start = ((), (), s32[]{:S(2)}) async-start(), calls=%async_computation.17 | async-start | bytes 1024000 | tf_op jit(solution)/shard_map/reduce_scatter | solution.py:962
  386.9 3.8 collective-permute-start.21
  386.9 6.8 %collective-permute-start.17 = (bf16[4,128,1664]{2,1,0:T(8,128)(2,1)}, bf16[4,128,1664]{2,1,0:T(8,128)(2,1)}, u32[]{:S(2)}, u32[]{:S(2)}) collective-permute-start(bf16[4,128,1664]{2,1,0:T(8,128)(2,1)} %get-tuple-element.144), channel_id=1, source_target_pairs={{0,4},{4,0},{8,12},{12,8},{16,20},{20,16},{24,28},{28,24},{1,5},{5... | collective-permute-start | bytes 5111816 | tf_op jit(solution)/shard_map/ppermute | solution.py:656
  387.4 20.6 %collective-permute-start.19 = (bf16[384,1024]{1,0:T(8,128)(2,1)}, bf16[384,1024]{1,0:T(8,128)(2,1)S(1)}, u32[]{:S(2)}, u32[]{:S(2)}) collective-permute-start(bf16[384,1024]{1,0:T(8,128)(2,1)} %get-tuple-element.262), channel_id=1, source_target_pairs={{0,8},{4,12},{8,0},{12,4},{16,24},{20,28},{24,16},{28,20},{1,9},{5... | collective-permute-start | bytes 2359304 | tf_op jit(solution)/shard_map/ppermute | solution.py:656
  388.1 20.7 %collective-permute-start.16 = (bf16[384,1024]{1,0:T(8,128)(2,1)}, bf16[384,1024]{1,0:T(8,128)(2,1)S(1)}, u32[]{:S(2)}, u32[]{:S(2)}) collective-permute-start(bf16[384,1024]{1,0:T(8,128)(2,1)} %get-tuple-element.263), channel_id=1, source_target_pairs={{0,16},{4,20},{8,24},{12,28},{16,0},{20,4},{24,8},{28,12},{1,17},{... | collective-permute-start | bytes 2359304 | tf_op jit(solution)/shard_map/ppermute | solution.py:656
  392.0 32.3 %collective-permute-start.22 = (bf16[4,64,1536]{2,1,0:T(8,128)(2,1)S(1)}, bf16[4,64,1536]{2,1,0:T(8,128)(2,1)S(1)}, u32[]{:S(2)}, u32[]{:S(2)}) collective-permute-start(bf16[4,64,1536]{2,1,0:T(8,128)(2,1)S(1)} %add_convert_fusion.3), channel_id=1, source_target_pairs={{0,16},{4,20},{8,24},{12,28},{16,0},{20,4},{24,8},{28,12},{1,17},{... | collective-permute-start | bytes 2359304 | tf_op jit(solution)/shard_map/ppermute | solution.py:656
  395.9 32.8 %collective-permute-start.18 = (bf16[4,64,1664]{2,1,0:T(8,128)(2,1)}, bf16[4,64,1664]{2,1,0:T(8,128)(2,1)}, u32[]{:S(2)}, u32[]{:S(2)}) collective-permute-start(bf16[4,64,1664]{2,1,0:T(8,128)(2,1)} %add_convert_fusion.2), channel_id=1, source_target_pairs={{0,8},{4,12},{8,0},{12,4},{16,24},{20,28},{24,16},{28,20},{1,9},{5... | collective-permute-start | bytes 2555912 | tf_op jit(solution)/shard_map/ppermute | solution.py:656
  427.4 10.3 %collective-permute-start.23 = (bf16[4,32,1536]{2,1,0:T(8,128)(2,1)}, bf16[4,32,1536]{2,1,0:T(8,128)(2,1)}, u32[]{:S(2)}, u32[]{:S(2)}) collective-permute-start(bf16[4,32,1536]{2,1,0:T(8,128)(2,1)} %add_convert_fusion.11), channel_id=1, source_target_pairs={{0,8},{4,12},{8,0},{12,4},{16,24},{20,28},{24,16},{28,20},{1,9},{5... | collective-permute-start | bytes 1179656 | tf_op jit(solution)/shard_map/ppermute | solution.py:656
  430.4 10.5 %collective-permute-start.20 = (bf16[4,32,1664]{2,1,0:T(8,128)(2,1)S(1)}, bf16[4,32,1664]{2,1,0:T(8,128)(2,1)}, u32[]{:S(2)}, u32[]{:S(2)}) collective-permute-start(bf16[4,32,1664]{2,1,0:T(8,128)(2,1)S(1)} %add_convert_fusion.9), channel_id=1, source_target_pairs={{0,16},{4,20},{8,24},{12,28},{16,0},{20,4},{24,8},{28,12},{1,17},{... | collective-permute-start | bytes 1277960 | tf_op jit(solution)/shard_map/ppermute | solution.py:656
  443.8 53.3 %all-gather.24.cloned.1.call-start = ((), (), s32[]{:S(2)}) async-start(), calls=%async_computation.19 | async-start | bytes 1843200 | tf_op jit(solution)/shard_map/all_gather | solution.py:969
  443.9 10.2 %collective-permute-start.24 = (bf16[768,1024]{1,0:T(8,128)(2,1)S(1)}, bf16[768,1024]{1,0:T(8,128)(2,1)S(1)}, u32[]{:S(2)}, u32[]{:S(2)}) collective-permute-start(bf16[768,1024]{1,0:T(8,128)(2,1)S(1)} %constant_dynamic-update-slice_fusion.1.first_ref), channel_id=1, source_target_pairs={{0,4},{4,0},{8,12},{12,8},{16,20},{20,16},{24,28},{28,24},{1,5},{5... | collective-permute-start | bytes 4718600 | tf_op jit(solution)/shard_map/ppermute | solution.py:656
  443.9 10.1 %collective-permute-start.25 = (bf16[768,1024]{1,0:T(8,128)(2,1)}, bf16[768,1024]{1,0:T(8,128)(2,1)S(1)}, u32[]{:S(2)}, u32[]{:S(2)}) collective-permute-start(bf16[768,1024]{1,0:T(8,128)(2,1)} %copy-done.3), channel_id=1, source_target_pairs={{0,4},{4,0},{8,12},{12,8},{16,20},{20,16},{24,28},{28,24},{1,5},{5... | collective-permute-start | bytes 4718600 | tf_op jit(solution)/shard_map/ppermute | solution.py:656
  444.4 38.7 %collective-permute-start.26 = (bf16[768,1024]{1,0:T(8,128)(2,1)S(1)}, bf16[768,1024]{1,0:T(8,128)(2,1)}, u32[]{:S(2)}, u32[]{:S(2)}) collective-permute-start(bf16[768,1024]{1,0:T(8,128)(2,1)S(1)} %constant_dynamic-update-slice_fusion.1.first_ref), channel_id=1, source_target_pairs={{0,8},{4,12},{8,0},{12,4},{16,24},{20,28},{24,16},{28,20},{1,9},{5... | collective-permute-start | bytes 4718600 | tf_op jit(solution)/shard_map/ppermute | solution.py:656
  445.0 38.6 %collective-permute-start.27 = (bf16[768,1024]{1,0:T(8,128)(2,1)}, bf16[768,1024]{1,0:T(8,128)(2,1)}, u32[]{:S(2)}, u32[]{:S(2)}) collective-permute-start(bf16[768,1024]{1,0:T(8,128)(2,1)} %copy-done.3), channel_id=1, source_target_pairs={{0,16},{4,20},{8,24},{12,28},{16,0},{20,4},{24,8},{28,12},{1,17},{... | collective-permute-start | bytes 4718600 | tf_op jit(solution)/shard_map/ppermute | solution.py:656
  454.0 30.8 %copy-start.41 = (bf16[128,1024]{1,0:T(8,128)(2,1)S(1)}, bf16[128,1024]{1,0:T(8,128)(2,1)}, u32[]{:S(2)}) copy-start(bf16[128,1024]{1,0:T(8,128)(2,1)} %get-tuple-element.270) | copy-start | bytes 786436
  454.0 30.8 %copy-start.42 = (bf16[128,1024]{1,0:T(8,128)(2,1)S(1)}, bf16[128,1024]{1,0:T(8,128)(2,1)}, u32[]{:S(2)}) copy-start(bf16[128,1024]{1,0:T(8,128)(2,1)} %get-tuple-element.271) | copy-start | bytes 786436
  483.7 7.9 %collective-permute-start.28 = (bf16[768,1024]{1,0:T(8,128)(2,1)}, bf16[768,1024]{1,0:T(8,128)(2,1)S(1)}, u32[]{:S(2)}, u32[]{:S(2)}) collective-permute-start(bf16[768,1024]{1,0:T(8,128)(2,1)} %collective-permute-done.26.first_ref), channel_id=1, source_target_pairs={{0,4},{4,0},{8,12},{12,8},{16,20},{20,16},{24,28},{28,24},{1,5},{5... | collective-permute-start | bytes 4718600 | tf_op jit(solution)/shard_map/ppermute | solution.py:656
  483.7 7.9 %collective-permute-start.29 = (bf16[768,1024]{1,0:T(8,128)(2,1)}, bf16[768,1024]{1,0:T(8,128)(2,1)}, u32[]{:S(2)}, u32[]{:S(2)}) collective-permute-start(bf16[768,1024]{1,0:T(8,128)(2,1)} %collective-permute-done.27.second_ref), channel_id=1, source_target_pairs={{0,4},{4,0},{8,12},{12,8},{16,20},{20,16},{24,28},{28,24},{1,5},{5... | collective-permute-start | bytes 4718600 | tf_op jit(solution)/shard_map/ppermute | solution.py:656
  (50 other events, 236.1 us)
Sparse Core Ops, SparseCore 0:
  9.6 50.6 all-gather.11
  62.4 27.3 all-gather.21
  99.8 27.3 all-gather.13
  129.2 27.4 all-gather.15
  159.4 26.6 reduce-scatter.6
  188.9 25.7 reduce-scatter.8
  216.8 26.4 all-gather.17
  245.5 27.5 all-gather.19
  276.0 26.6 reduce-scatter.10
  305.4 26.0 reduce-scatter.12
  378.9 40.7 reduce-scatter.14
  443.9 21.6 reduce-scatter.16
  467.7 26.9 all-gather.23

commit v6 on v5

--- a/solution.py
+++ b/solution.py
@@ -476,9 +476,10 @@
 
 
 def attention_forward_kernel(
-    bias_ref, side_ref, all_ref, own_ref, gain_ref, query_held, query_other, kv_held, kv_other,
+    bias_ref, side_ref, input_ref, own_ref, gain_ref, query_held, query_other, kv_held, kv_other,
     cos_ref, sin_ref, cos_own_ref, sin_own_ref,
-    wq_parts, wkv_parts, normed_ref, normed_own_ref, query_ref, key_ref, value_ref, attended_ref, norm_ref, scores
+    wq_out, wkv_out, normed_out, key_out, value_out, normed_own_ref, query_ref, attended_ref, norm_ref,
+    all_ref, wq_parts, wkv_parts, normed_ref, key_ref, value_ref, scores, row_sems, in_sems, out_sems
 ):
     tokens, width = all_ref.shape
     kv_width = key_ref.shape[1]
@@ -486,10 +487,24 @@
     half_rows = query_held.shape[1]
     held_at = pl.ds(pl.multiple_of(side_ref[0] * half_rows, half_rows), half_rows)
     other_at = pl.ds(pl.multiple_of((1 - side_ref[0]) * half_rows, half_rows), half_rows)
-    wq_parts[:, held_at, :] = query_held[...]
-    wq_parts[:, other_at, :] = query_other[...]
-    wkv_parts[:, held_at, :] = kv_held[...]
-    wkv_parts[:, other_at, :] = kv_other[...]
+    row_copies = []
+    for at in range(tokens // ROW_STEP):
+        span = pl.ds(at * ROW_STEP, ROW_STEP)
+        copy = pltpu.make_async_copy(input_ref.at[span, :], all_ref.at[span, :], row_sems.at[at])
+        copy.start()
+        row_copies.append(copy)
+    weight_copies = []
+    for at, (source, target) in enumerate(
+        (
+            (kv_held, wkv_parts.at[:, held_at, :]),
+            (kv_other, wkv_parts.at[:, other_at, :]),
+            (query_held, wq_parts.at[:, held_at, :]),
+            (query_other, wq_parts.at[:, other_at, :]),
+        )
+    ):
+        copy = pltpu.make_async_copy(source, target, in_sems.at[at])
+        copy.start()
+        weight_copies.append(copy)
     wq_ref = wq_parts.reshape(width, wq_parts.shape[2])
     wkv_ref = wkv_parts.reshape(width, wkv_parts.shape[2])
 
@@ -498,11 +513,23 @@
         scale = lax.rsqrt(jnp.mean(values * values, axis=-1, keepdims=True) + norm_eps)
         return (values * scale * gain_ref[...]).astype(jnp.bfloat16)
 
+    normed_own = normed_rows(own_ref[...])
+    normed_own_ref[...] = normed_own
+    for at, copy in enumerate(row_copies):
+        copy.wait()
+        span = pl.ds(at * ROW_STEP, ROW_STEP)
+        normed_ref[span, :] = normed_rows(all_ref[span, :])
+    out_copies = [pltpu.make_async_copy(normed_ref, normed_out, out_sems.at[0])]
+    out_copies[0].start()
+    for copy in weight_copies:
+        copy.wait()
+    for at, (source, target) in enumerate(((wq_parts, wq_out), (wkv_parts, wkv_out))):
+        out_copies.append(pltpu.make_async_copy(source, target, out_sems.at[1 + at]))
+        out_copies[-1].start()
+
     def project(at, carry):
         rows = pl.ds(pl.multiple_of(at * ROW_STEP, ROW_STEP), ROW_STEP)
-        normed = normed_rows(all_ref[rows, :])
-        normed_ref[rows, :] = normed
-        linear = dot_nn(normed, wkv_ref[...])
+        linear = dot_nn(normed_ref[rows, :], wkv_ref[...])
         for col in range(0, kv_width, LANES):
             part = linear[:, col : col + LANES]
             turned = part * cos_ref[rows, :] + swap_halves(part) * sin_ref[rows, :]
@@ -511,8 +538,9 @@
         return carry
 
     lax.fori_loop(0, tokens // ROW_STEP, project, 0)
-    normed_own = normed_rows(own_ref[...])
-    normed_own_ref[...] = normed_own
+    for at, (source, target) in enumerate(((key_ref, key_out), (value_ref, value_out))):
+        out_copies.append(pltpu.make_async_copy(source, target, out_sems.at[3 + at]))
+        out_copies[-1].start()
     linear = dot_nn(normed_own, wq_ref[...])
     for col in range(0, wq_ref.shape[1], LANES):
         part = linear[:, col : col + LANES]
@@ -528,14 +556,14 @@
             top = None
             for at in range(bias_ref.shape[0]):
                 rows = pl.ds(at * key_rows, key_rows)
-                part = dot_nt(key_ref[rows, lanes], stacked) + bias_ref[at]
+                part = dot_nt(key_ref[rows, lanes], stacked)
                 scores[rows, :] = part
-                high = jnp.max(part, axis=0, keepdims=True)
+                high = jnp.max(part, axis=0, keepdims=True) + bias_ref[at]
                 top = high if top is None else jnp.maximum(top, high)
             total, gathered = None, None
             for at in range(bias_ref.shape[0]):
                 rows = pl.ds(at * key_rows, key_rows)
-                raised = jnp.exp(scores[rows, :] - top)
+                raised = jnp.exp(scores[rows, :] - (top - bias_ref[at]))
                 part = jnp.sum(raised, axis=0, keepdims=True)
                 mixed = dot_nn(
                     turned_values[:, at * key_rows : (at + 1) * key_rows], raised.astype(jnp.bfloat16)
@@ -548,6 +576,12 @@
         return carry
 
     lax.fori_loop(0, kv_width // LANES, attend, 0)
+    for copy in out_copies:
+        copy.wait()
+
+
+def far_spec():
+    return pl.BlockSpec(memory_space=pl.ANY)
 
 
 def whole_spec():
@@ -561,20 +595,35 @@
     kv_width = kv_pair[0].shape[2] // 2
     return pl.pallas_call(
         attention_forward_kernel,
-        in_specs=[pl.BlockSpec(memory_space=pltpu.SMEM)] * 2 + [whole_spec()] * 11,
-        out_specs=[whole_spec()] * 9,
+        in_specs=[pl.BlockSpec(memory_space=pltpu.SMEM)] * 2
+        + [far_spec()]
+        + [whole_spec()] * 2
+        + [far_spec()] * 4
+        + [whole_spec()] * 4,
+        out_specs=[far_spec()] * 5 + [whole_spec()] * 4,
         out_shape=[
             jax.ShapeDtypeStruct((shards, 2 * half_rows, query_width), jnp.bfloat16),
             jax.ShapeDtypeStruct((shards, 2 * half_rows, 2 * kv_width), jnp.bfloat16),
             jax.ShapeDtypeStruct((tokens, width), jnp.bfloat16),
+            jax.ShapeDtypeStruct((tokens, kv_width), jnp.bfloat16),
+            jax.ShapeDtypeStruct((tokens, kv_width), jnp.bfloat16),
             jax.ShapeDtypeStruct((rows, width), jnp.bfloat16),
             jax.ShapeDtypeStruct((rows, query_width), jnp.bfloat16),
-            jax.ShapeDtypeStruct((tokens, kv_width), jnp.bfloat16),
-            jax.ShapeDtypeStruct((tokens, kv_width), jnp.bfloat16),
             jax.ShapeDtypeStruct((rows, query_width), jnp.bfloat16),
             jax.ShapeDtypeStruct((KV_HEADS, 2 * rows), jnp.float32),
         ],
-        scratch_shapes=[pltpu.VMEM((tokens, 2 * rows), jnp.float32)],
+        scratch_shapes=[
+            pltpu.VMEM((tokens, width), jnp.bfloat16),
+            pltpu.VMEM((shards, 2 * half_rows, query_width), jnp.bfloat16),
+            pltpu.VMEM((shards, 2 * half_rows, 2 * kv_width), jnp.bfloat16),
+            pltpu.VMEM((tokens, width), jnp.bfloat16),
+            pltpu.VMEM((tokens, kv_width), jnp.bfloat16),
+            pltpu.VMEM((tokens, kv_width), jnp.bfloat16),
+            pltpu.VMEM((tokens, 2 * rows), jnp.float32),
+            pltpu.SemaphoreType.DMA((tokens // ROW_STEP,)),
+            pltpu.SemaphoreType.DMA((4,)),
+            pltpu.SemaphoreType.DMA((5,)),
+        ],
         compiler_params=pltpu.CompilerParams(vmem_limit_bytes=VMEM_BYTES),
         cost_estimate=SMALL_COST,
         name="attention_forward",
@@ -599,8 +648,8 @@
             total = None
             for at in range(bias_ref.shape[0]):
                 rows = pl.ds(at * key_rows, key_rows)
-                part = dot_nt(key_ref[rows, lanes], stacked) + bias_ref[at]
-                prob = jnp.exp(part - log_norm)
+                part = dot_nt(key_ref[rows, lanes], stacked)
+                prob = jnp.exp(part - (log_norm - bias_ref[at]))
                 d_prob = dot_nt(value_ref[rows, lanes], stacked_grad)
                 probs[rows, :] = prob
                 dprobs[rows, :] = d_prob
@@ -765,11 +814,14 @@
     )
     query_full = pieces[..., :query_width]
     kv_full = pieces[..., query_width:]
-    for bit_first, bit_second in zip(order_first[:-1], order_second[:-1]):
+    small_parts = jnp.concatenate(small_parts, 1)
+    for at, (bit_first, bit_second) in enumerate(zip(order_first[:-1], order_second[:-1])):
+        if at == len(far) - 1:
+            small_parts = after(small_parts, query_full, kv_full)
         query_full = double(query_full, bit_first, 1)
         kv_full = double(kv_full, bit_second, 1)
-    small_parts = after(jnp.concatenate(small_parts, 1), query_full, kv_full, *tables, *tables_own)
     small_all = gather(small_parts)
+    query_full, kv_full = after(query_full, small_all), after(kv_full, small_all)
     query_pair = query_full, exchange(query_full, near)
     kv_pair = kv_full, exchange(kv_full, near)
     near_rows = own_rows // 2
@@ -786,7 +838,7 @@
     input_float = hidden_in.astype(jnp.float32)
     scale_attn = rms_scale(input_float)
     (
-        query_full, kv_full, normed_all, normed_attn, query_rows, keys_all, values_all, attended, log_norm
+        query_full, kv_full, normed_all, keys_all, values_all, normed_attn, query_rows, attended, log_norm
     ) = attention_forward(
         bias, jnp.reshape(side_of(near), (1,)), input_all, hidden_in, gain_attn[None],
         query_pair, kv_pair, tables, tables_own,
@@ -881,13 +933,14 @@
     first_rows = d_rows[0]
     d_rows = jnp.concatenate(d_rows, 0).astype(jnp.float32)
     sent = experts_grads(order_sent, backward[-1:], True, row_units, partial_grads, 0)
-    sent = [part.reshape(-1, columns) for part in sent]
+    unit_rows = flat_rows // 2 >> len(far)
+    sent = [part.reshape(-1, unit_rows, columns) for part in sent]
     other = [exchange(part, near) for part in sent]
     kept = experts_grads(
         after(order_kept, *sent), backward[-1:], False, row_units, partial_grads, kept_experts
     )
-    kept = after(kept[0].reshape(-1, columns), first_rows)
-    half_rows = flat_rows // 2
+    kept = after(kept[0].reshape(-1, unit_rows, columns), first_rows)
+    half_rows = flat_rows // 2 // unit_rows
     if kept_experts > 1:
         other_first = jnp.concatenate(other[: kept_experts // 2], 0)
         other_second = jnp.concatenate(other[kept_experts // 2 :], 0)
@@ -933,6 +986,9 @@
     for bit_first, bit_second in zip(far[1:], far[::-1][1:]):
         _, moe_first = halve(moe_first, bit_first, 0)
         _, moe_second = halve(moe_second, bit_second, 0)
+    def by_piece(block):
+        return block.reshape(shard_count, -1, piece_rows, block.shape[2])
+
     sent_first, sent_second, moe_first[-1], moe_second[-1] = lax.optimization_barrier(
         (sent_first, sent_second, moe_first[-1], moe_second[-1])
     )
@@ -940,8 +996,8 @@
     sent_first, sent_second = lax.optimization_barrier(
         (sent_first, sent_second, moe_first, moe_second)
     )[:2]
-    first = [kept_first, exchange(sent_first, near)]
-    second = [kept_second, exchange(sent_second, near)]
+    first = [by_piece(kept_first), exchange(by_piece(sent_first), near)]
+    second = [by_piece(kept_second), exchange(by_piece(sent_second), near)]
     for bit_first, bit_second in zip(far[:0:-1], far[:-1]):
         moe_first = double(moe_first, bit_first, 0)
         moe_second = double(moe_second, bit_second, 0)
@@ -957,10 +1013,11 @@
     own_first, own_second = moe_first, moe_second
     far_first, far_second = exchange(own_first, far[0]), exchange(own_second, far[-1])
     near_own = exchange(own_first, near), exchange(own_second, near)
-    split_at = first[0].shape[2]
-    joined = jnp.concatenate([add_parts(first), add_parts(second)], 2)
+    joined = jnp.concatenate([add_parts(first), add_parts(second)], 3)
+    joined = joined.reshape(shard_count, piece_rows, -1)
     joined = lax.psum_scatter(joined, "shard", scatter_dimension=0)
     def put(held, pieces, *where):
+        pieces = [piece.reshape(-1, columns) for piece in pieces]
         return widen(targets[where], *pieces, shapes, row_units, held)
 
     held = put([], (own_first, own_second), 0, 0)

time: 519 us -> 513 us (0.988)
  other arithmetic: 58.7 us -> 46.9 us
    convert_element_type x9, other arithmetic: 28.7 us -> 19.1 us  [add_parts(): return total.astype(jnp.bfloat16)]
    all_gather x1, waiting for transfers between devices: 0.02 us -> 6.15 us  [body(): lax.all_gather(after(output_half, query_pair[0], kv_pair[0]), 'shard', ax...]
  transfers between devices with their start and end apart: 44 -> 44, of which waited for: 25 -> 25; matrix products, arithmetic and copies ran while one was open for 13% -> 11% of each run, Pallas kernels for 31% -> 31%
where the time goes in v6:
time: 513 us; the launch traced here: 505 us
  waiting for transfers between devices  182 us (35%)
  Pallas kernels  156 us (30%)
  other arithmetic  46.9 us (9%)
  blocking collectives  34.5 us (7%)
  starting transfers between devices  29.7 us (6%)
  local copies, waits for them, and re-layouts  26.7 us (5%)
  between operations  22.7 us (4%)
  matrix products  5.85 us (1%)
    ppermute x30, waiting for transfers between devices, exchange(): return lax.ppermute(block, 'rep', [(at, at ^ bit) for at in range(count)])  71.3 us
    all_gather x5, waiting for transfers between devices, gather(): return lax.all_gather(block, 'shard', axis=0, tiled=True)  48.4 us
    reduce_scatter x5, waiting for transfers between devices, scatter(): return lax.psum_scatter(block, 'shard', scatter_dimension=0, tiled=True)  47.2 us
    pallas_call x3, Pallas kernels, experts_grads(): pl.pallas_call(functools.partial(experts_grads_kernel, outputs, row_units...  33.3 us
    pallas_call x2, Pallas kernels, experts_backward(): pl.pallas_call(experts_backward_kernel, grid=(experts,), in_specs=[pl.Blo...  30 us
    pallas_call x2, Pallas kernels, experts_forward(): pl.pallas_call(experts_forward_kernel, grid=(experts,), in_specs=[pl.Bloc...  26.2 us
    ppermute x30, starting transfers between devices, exchange(): return lax.ppermute(block, 'rep', [(at, at ^ bit) for at in range(count)])  24.9 us
    all_gather x1, blocking collectives, body(): lax.all_gather(jnp.concatenate([piece_of(w_query, order_first), piece_of(...  20.3 us
  transfers between devices with their start and end apart: 44, of which 25 were waited for; matrix products, arithmetic and copies ran while one was open for 11% of the time, Pallas kernels for 31%

profile of v6, /device:TPU:0, one launch (start us, length us, event | category | flops | bytes accessed | tf_op | source)
XLA Modules:
  0.0 504.5 jit_solution(9660477774846596614)
XLA Ops:
  9.0 20.3 %all-gather = bf16[128,2048]{1,0:T(8,128)(2,1)S(1)} all-gather(bf16[32,2048]{1,0:T(8,128)(2,1)S(1)} %pad_maximum_fusion.10), channel_id=2, replica_groups=mesh['rep'=8,'shard'=4] {'shard'}, dimensions={0}, use_global_device_ids=true | all-gather | bytes 655360 | tf_op jit(solution)/shard_map/all_gather | solution.py:810
  29.4 1.6 collective-permute-start.2
  34.6 5.5 %collective-permute-done = bf16[4,32,1024]{2,1,0:T(8,128)(2,1)S(1)} collective-permute-done((bf16[4,32,1024]{2,1,0:T(8,128)(2,1)S(1)}, bf16[4,32,1024]{2,1,0:T(8,128)(2,1)S(1)}, u32[]{:S(2)}, u32[]{:S(2)}) %collective-permute-start) | collective-permute-done | bytes 262176 | tf_op jit(solution)/shard_map/ppermute | solution.py:705
  40.2 1.6 collective-permute-start.3
  42.5 14.2 %all-gather.3 = bf16[4,1,6657]{2,1,0:T(2,128)(2,1)S(1)} all-gather(bf16[1,1,6657]{2,1,0:T(2,128)(2,1)S(1)} %bitcast.130), channel_id=1, replica_groups=mesh['rep'=8,'shard'=4] {'shard'}, dimensions={0}, use_global_device_ids=true | all-gather | bytes 66570 | tf_op jit(solution)/shard_map/all_gather | solution.py:782
  61.1 1.9 fusion.13
  66.9 17.9 %attention_forward.1 = (bf16[4,256,1024]{2,1,0:T(8,128)(2,1)}, bf16[4,256,1024]{2,1,0:T(8,128)(2,1)}, bf16[1024,1024]{1,0:T(8,128)(2,1)}, bf16[1024,512]{1,0:T(8...) custom-call(f32[4]{0:T(128)} %compare_select_fusion.bias_ref, ...), custom_call_target="tpu_custom_call" | custom-call | flops 1000000 | bytes 100000 | tf_op jit(solution)/shard_map/attention_forward/pallas_call | solution.py:596
  84.8 6.1 %all-gather.22.cloned.1.call-done = bf16[512,1024]{1,0:T(8,128)(2,1)} async-done(((bf16[128,1024]{1,0:T(8,128)(2,1)}), bf16[512,1024]{1,0:T(8,128)(2,1)}) %all-gather.22.cloned.1.call-update) | async-done | bytes 1048592 | tf_op jit(solution)/shard_map/all_gather | solution.py:829
  91.0 1.8 pad_maximum_fusion
  103.0 2.0 collective-permute-done.8
  107.6 1.7 collective-permute-done.9
  109.9 14.8 %all-gather.14.cloned.1.call-done.x_ref.refs_0_ = bf16[512,1024]{1,0:T(8,128)(2,1)} async-done(((bf16[128,1024]{1,0:T(8,128)(2,1)}), bf16[512,1024]{1,0:T(8,128)(2,1)}) %all-gather.14.cloned.1.call-update) | async-done | bytes 1048592 | tf_op jit(solution)/shard_map/all_gather | solution.py:782
  124.7 1.7 fusion.28
  127.8 13.1 %experts_forward.2 = (bf16[512,1024]{1,0:T(8,128)(2,1)}, f32[4,512,1024]{2,1,0:T(8,128)}, bf16[4,512,512]{2,1,0:T(8,128)(2,1)}) custom-call(bf16[512,1024]{1,0:T(8,128)(2,1)} %all-gather.14.cloned.1.call-done.x_ref.refs_0_, f32[512,128]{1,0:T(8,128)} %pad.7.gate_ref, bf16[4,1024,1024]{2,1,0:T(8,128)(2,1)} %in_ref.7, bf16[4,512,1024]{2,1,0:T(8,128)(2,1)} %out_ref.7), custom_call_target="tpu_custom_call" | custom-call | flops 1000000 | bytes 100000 | tf_op jit(solution)/shard_map/experts_forward/pallas_call | solution.py:104
  141.2 12.9 %all-gather.16.cloned.1.call-done.x_ref.refs_1_ = bf16[512,1024]{1,0:T(8,128)(2,1)} async-done(((bf16[128,1024]{1,0:T(8,128)(2,1)}), bf16[512,1024]{1,0:T(8,128)(2,1)}) %all-gather.16.cloned.1.call-update) | async-done | bytes 1048592 | tf_op jit(solution)/shard_map/all_gather | solution.py:782
  154.1 1.7 fusion.27
  157.2 13.1 %experts_forward.3 = (bf16[512,1024]{1,0:T(8,128)(2,1)}, f32[4,512,1024]{2,1,0:T(8,128)}, bf16[4,512,512]{2,1,0:T(8,128)(2,1)}) custom-call(bf16[512,1024]{1,0:T(8,128)(2,1)} %all-gather.16.cloned.1.call-done.x_ref.refs_1_, f32[512,128]{1,0:T(8,128)} %pad.8.gate_ref, bf16[4,1024,1024]{2,1,0:T(8,128)(2,1)} %in_ref.7, bf16[4,512,1024]{2,1,0:T(8,128)(2,1)} %out_ref.7), custom_call_target="tpu_custom_call" | custom-call | flops 1000000 | bytes 100000 | tf_op jit(solution)/shard_map/experts_forward/pallas_call | solution.py:104
  171.1 12.4 %reduce-scatter.7.cloned.1.call-done = bf16[128,1024]{1,0:T(8,128)(2,1)} async-done(((bf16[512,1024]{1,0:T(8,128)(2,1)}), bf16[128,1024]{1,0:T(8,128)(2,1)}) %reduce-scatter.7.cloned.1.call-update) | async-done | bytes 262160 | tf_op jit(solution)/shard_map/reduce_scatter | solution.py:785
  183.5 2.0 multiply_convert_fusion.3
  185.6 26.6 %reduce-scatter.9.cloned.1.call-done = bf16[128,1024]{1,0:T(8,128)(2,1)} async-done(((bf16[512,1024]{1,0:T(8,128)(2,1)}), bf16[128,1024]{1,0:T(8,128)(2,1)}) %reduce-scatter.9.cloned.1.call-update) | async-done | bytes 262160 | tf_op jit(solution)/shard_map/reduce_scatter | solution.py:785
  212.2 3.0 multiply_convert_fusion.2
  219.5 1.9 pad_maximum_fusion.15.digits_ref
  221.4 19.5 %all-gather.18.cloned.1.call-done.dmix_ref.refs_1_ = bf16[512,1024]{1,0:T(8,128)(2,1)} async-done(((bf16[128,1024]{1,0:T(8,128)(2,1)}), bf16[512,1024]{1,0:T(8,128)(2,1)}) %all-gather.18.cloned.1.call-update) | async-done | bytes 1048592 | tf_op jit(solution)/shard_map/all_gather | solution.py:782
  240.9 15.0 %experts_backward.2 = (bf16[512,1024]{1,0:T(8,128)(2,1)}, bf16[4,512,1024]{2,1,0:T(8,128)(2,1)}, f32[512,128]{1,0:T(8,128)}) custom-call(bf16[512,1024]{1,0:T(8,128)(2,1)} %all-gather.18.cloned.1.call-done.dmix_ref.refs_1_, f32[512,128]{1,0:T(8,128)} %pad.7.gate_ref, f32[4,512,1024]{2,1,0:T(8,128)} %get-tuple-element.109.gate_up_ref, ...), custom_call_target="tpu_custom_call" | custom-call | flops 1000000 | bytes 100000 | tf_op jit(solution)/shard_map/experts_backward/pallas_call | solution.py:167
  256.9 12.5 %experts_grads.3.refs_0_ = bf16[4,1536,1024]{2,1,0:T(8,128)(2,1)} custom-call(s32[4]{0:T(128)} %pad_add_fusion.order_ref, bf16[512,1024]{1,0:T(8,128)(2,1)} %all-gather.14.cloned.1.call-done.x_ref.refs_0_, bf16[512,1024]{1,0:T(8,128)(2,1)} %all-gather.18.cloned.1.call-done.dmix_ref.refs_1_, bf16[4,512,1024]{2,1,0:T(8,128)(2,1)} %get-tuple-element.110.refs_2_, ...), custom_call_target="tpu_custom_call" | custom-call | flops 1000000 | bytes 100000 | tf_op jit(solution)/shard_map/experts_grads/pallas_call | solution.py:249
  270.5 15.0 %experts_backward.3 = (bf16[512,1024]{1,0:T(8,128)(2,1)}, bf16[4,512,1024]{2,1,0:T(8,128)(2,1)}, f32[512,128]{1,0:T(8,128)}) custom-call(bf16[512,1024]{1,0:T(8,128)(2,1)} %all-gather.20.cloned.1.call-done.dmix_ref.refs_2_, f32[512,128]{1,0:T(8,128)} %pad.8.gate_ref, f32[4,512,1024]{2,1,0:T(8,128)} %get-tuple-element.113.gate_up_ref, ...), custom_call_target="tpu_custom_call" | custom-call | flops 1000000 | bytes 100000 | tf_op jit(solution)/shard_map/experts_backward/pallas_call | solution.py:167
  285.5 11.4 %experts_grads.4 = (bf16[1536,1024]{1,0:T(8,128)(2,1)}, bf16[1536,1024]{1,0:T(8,128)(2,1)}) custom-call(s32[2]{0:T(128)} %copy-done.51, bf16[4,1536,1024]{2,1,0:T(8,128)(2,1)} %experts_grads.3.refs_0_, bf16[512,1024]{1,0:T(8,128)(2,1)} %all-gather.16.cloned.1.call-done.x_ref.refs_1_, bf16[512,1024]{1,0:T(8,128)(2,1)} %all-gather.20.cloned.1.call-done.dmix_ref.refs_2_, ...), custom_call_target="tpu_custom_call" | custom-call | flops 1000000 | bytes 100000 | tf_op jit(solution)/shard_map/experts_grads/pallas_call | solution.py:249
  297.7 9.4 %experts_grads.5 = bf16[2,1536,1024]{2,1,0:T(8,128)(2,1)} custom-call(s32[2]{0:T(128)} %copy-done.50, bf16[4,1536,1024]{2,1,0:T(8,128)(2,1)} %experts_grads.3.refs_0_, bf16[512,1024]{1,0:T(8,128)(2,1)} %all-gather.16.cloned.1.call-done.x_ref.refs_1_, bf16[512,1024]{1,0:T(8,128)(2,1)} %all-gather.20.cloned.1.call-done.dmix_ref.refs_2_, ...), custom_call_target="tpu_custom_call" | custom-call | flops 1000000 | bytes 100000 | tf_op jit(solution)/shard_map/experts_grads/pallas_call | solution.py:249
  307.4 6.1 %add_convert_fusion = (bf16[2,384,1024]{2,1,0:T(8,128)(2,1)}, bf16[2,384,1024]{2,1,0:T(8,128)(2,1)}) fusion(bf16[4,384,1024]{2,1,0:T(8,128)(2,1)} %collective-permute-done.11, s32[]{:T(128)S(6)} %select_n.278, bf16[8,384,1024]{2,1,0:T(8,128)(2,1)} %bitcast.102, s32[]{:T(128)S(6)} %select_n.277, bf16[4,384,1024]{2,1,0:T(8,128)(2,1)} %collective-permute-done.10, ...), kind=kLoop, calls=%fused_computation | loop fusion | flops 6291456 | bytes 9437200 | tf_op jit(solution)/shard_map/convert_element_type | solution.py:727
  317.3 3.5 all-to-all-start
  320.8 8.2 %reduce-scatter.13.cloned.1.call-done = bf16[128,1024]{1,0:T(8,128)(2,1)} async-done(((bf16[512,1024]{1,0:T(8,128)(2,1)}), bf16[128,1024]{1,0:T(8,128)(2,1)}) %reduce-scatter.13.cloned.1.call-update) | async-done | bytes 262160 | tf_op jit(solution)/shard_map/reduce_scatter | solution.py:785
  331.7 2.8 multiply_convert_fusion
  336.4 15.2 %attention_backward.1 = (bf16[256,1024]{1,0:T(8,128)(2,1)S(1)}, bf16[1024,1024]{1,0:T(8,128)(2,1)S(1)}) custom-call(f32[4]{0:T(128)S(1)} %copy-done.25, bf16[256,1024]{1,0:T(8,128)(2,1)S(1)} %copy-done.21, bf16[1024,512]{1,0:T(8,128)(2,1)S(1)} %copy-done.17, bf16[1024,512]{1,0:T(8,128)(2,1)S(1)} %copy-done.18, f32[8,512]{1,0:T(8,128)S(1)} %copy-done.24, ...), custom_call_target="tpu_custom_call" | custom-call | flops 1000000 | bytes 100000 | tf_op jit(solution)/shard_map/attention_backward/pallas_call | solution.py:683
  353.0 4.7 add_convert_fusion.6
  362.0 13.0 %attention_grads.1 = (bf16[1024,1024]{1,0:T(8,128)(2,1)}, f32[256,1024]{1,0:T(8,128)S(1)}, bf16[4,128,1664]{2,1,0:T(8,128)(2,1)}, bf16[4,128,1664]{2,1,0:T(8,128...) custom-call(s32[2]{0:T(128)S(1)} %pad_add_fusion.1.side_ref, ...), custom_call_target="tpu_custom_call" | custom-call | flops 1000000 | bytes 100000 | tf_op jit(solution)/shard_map/attention_grads/pallas_call | solution.py:416
  378.4 4.8 add_convert_fusion.4
  390.0 15.3 %collective-permute-done.19 = bf16[1,384,1024]{2,1,0:T(8,128)(2,1)S(1)} collective-permute-done((bf16[1,384,1024]{2,1,0:T(8,128)(2,1)S(1)}, bf16[1,384,1024]{2,1,0:T(8,128)(2,1)S(1)}, u32[]{:S(2)}, u32[]{:S(2)}) %collective-permute-start.19) | collective-permute-done | bytes 786464 | tf_op jit(solution)/shard_map/ppermute | solution.py:705
  405.6 16.1 %collective-permute-done.22 = bf16[4,2,32,1536]{3,2,0,1:T(8,128)(2,1)S(1)} collective-permute-done((bf16[4,2,32,1536]{3,2,0,1:T(8,128)(2,1)S(1)}, bf16[4,2,32,1536]{3,2,0,1:T(8,128)(2,1)S(1)}, u32[]{:S(2)}, u32[]{:S(2)}) %collective-permute-start.22) | collective-permute-done | bytes 786464 | tf_op jit(solution)/shard_map/ppermute | solution.py:705
  421.9 1.8 collective-permute-start.23
  425.4 7.0 %collective-permute-done.23 = bf16[4,1,32,1536]{3,2,0,1:T(8,128)(2,1)S(1)} collective-permute-done((bf16[4,1,32,1536]{3,2,0,1:T(8,128)(2,1)S(1)}, bf16[4,1,32,1536]{3,2,0,1:T(8,128)(2,1)S(1)}, u32[]{:S(2)}, u32[]{:S(2)}) %collective-permute-start.23) | collective-permute-done | bytes 393248 | tf_op jit(solution)/shard_map/ppermute | solution.py:705
  434.9 1.7 add_convert_fusion.8
  441.4 3.6 widen.4
  447.6 3.6 widen.5
  451.2 7.7 %reduce-scatter.17.cloned.1.call-done = bf16[1,32,3200]{2,1,0:T(8,128)(2,1)} async-done(((bf16[4,32,3200]{2,1,0:T(8,128)(2,1)}), bf16[1,32,3200]{2,1,0:T(8,128)(2,1)}) %reduce-scatter.17.cloned.1.call-update) | async-done | bytes 204816 | tf_op jit(solution)/shard_map/reduce_scatter | solution.py:1018
  458.9 17.9 %collective-permute-done.26 = bf16[2,384,1024]{2,1,0:T(8,128)(2,1)} collective-permute-done((bf16[2,384,1024]{2,1,0:T(8,128)(2,1)S(1)}, bf16[2,384,1024]{2,1,0:T(8,128)(2,1)}, u32[]{:S(2)}, u32[]{:S(2)}) %collective-permute-start.26) | collective-permute-done | bytes 1572896 | tf_op jit(solution)/shard_map/ppermute | solution.py:705
  479.2 5.8 %widen.6 = (f32[4,1024,1024]{2,1,0:T(8,128)}, f32[4,512,1024]{2,1,0:T(8,128)}) custom-call(s32[4]{0:T(128)S(1)} %get-tuple-element.301.spot_ref, bf16[768,1024]{1,0:T(8,128)(2,1)} %bitcast.48.first_ref, bf16[768,1024]{1,0:T(8,128)(2,1)} %bitcast.49.second_ref, ...), custom_call_target="tpu_custom_call", output_to_operand_aliasing={{0}: (3, {}), {1}: (4, {})} | custom-call | flops 1000000 | bytes 100000 | tf_op jit(solution)/shard_map/widen/pallas_call | solution.py:288
  485.0 5.6 %widen.7 = (f32[4,1024,1024]{2,1,0:T(8,128)}, f32[4,512,1024]{2,1,0:T(8,128)}) custom-call(s32[4]{0:T(128)S(1)} %get-tuple-element.302.spot_ref, bf16[768,1024]{1,0:T(8,128)(2,1)S(1)} %bitcast.100, bf16[768,1024]{1,0:T(8,128)(2,1)} %bitcast.47.second_ref, f32[4,1024,1024]{2,1,0:T(8,128)} %get-tuple-element.178.refs_0_, ...), custom_call_target="tpu_custom_call", output_to_operand_aliasing={{0}: (3, {}), {1}: (4, {})} | custom-call | flops 1000000 | bytes 100000 | tf_op jit(solution)/shard_map/widen/pallas_call | solution.py:288
  492.1 1.9 finish.1
  (296 shorter events, 74.6 us)
Async XLA Ops:
  7.2 34.6 %copy-start = (bf16[256,1024]{1,0:T(8,128)(2,1)S(1)}, bf16[256,1024]{1,0:T(8,128)(2,1)}, u32[]{:S(2)}) copy-start(bf16[256,1024]{1,0:T(8,128)(2,1)} %param.21) | copy-start | bytes 1572868
  7.2 59.6 %all-gather.12.cloned.1.call-start = ((), (), s32[]{:S(2)}) async-start(), calls=%async_computation.7 | async-start | bytes 2621440 | tf_op jit(solution)/shard_map/all_gather | solution.py:782
  8.0 83.0 %all-gather.22.cloned.1.call-start = ((), (), s32[]{:S(2)}) async-start(), calls=%async_computation.18 | async-start | bytes 1310720 | tf_op jit(solution)/shard_map/all_gather | solution.py:829
  29.4 10.7 %collective-permute-start.2 = (bf16[4,32,1024]{2,1,0:T(8,128)(2,1)S(1)}, bf16[4,32,1024]{2,1,0:T(8,128)(2,1)S(1)}, u32[]{:S(2)}, u32[]{:S(2)}) collective-permute-start(bf16[4,32,1024]{2,1,0:T(8,128)(2,1)S(1)} %get-tuple-element.278), channel_id=1, source_target_pairs={{0,16},{4,20},{8,24},{12,28},{16,0},{20,4},{24,8},{28,12},{1,17},{... | collective-permute-start | bytes 786440 | tf_op jit(solution)/shard_map/ppermute | solution.py:705
  31.0 9.0 %collective-permute-start = (bf16[4,32,1024]{2,1,0:T(8,128)(2,1)S(1)}, bf16[4,32,1024]{2,1,0:T(8,128)(2,1)S(1)}, u32[]{:S(2)}, u32[]{:S(2)}) collective-permute-start(bf16[4,32,1024]{2,1,0:T(8,128)(2,1)S(1)} %get-tuple-element.279), channel_id=1, source_target_pairs={{0,8},{4,12},{8,0},{12,4},{16,24},{20,28},{24,16},{28,20},{1,9},{5... | collective-permute-start | bytes 786440 | tf_op jit(solution)/shard_map/ppermute | solution.py:705
  40.1 17.9 %collective-permute-start.1 = (bf16[4,64,1024]{2,1,0:T(8,128)(2,1)S(1)}, bf16[4,64,1024]{2,1,0:T(8,128)(2,1)S(1)}, u32[]{:S(2)}, u32[]{:S(2)}) collective-permute-start(bf16[4,64,1024]{2,1,0:T(8,128)(2,1)S(1)} %constant_dynamic-update-slice_fusion.6), channel_id=1, source_target_pairs={{0,16},{4,20},{8,24},{12,28},{16,0},{20,4},{24,8},{28,12},{1,17},{... | collective-permute-start | bytes 1572872 | tf_op jit(solution)/shard_map/ppermute | solution.py:705
  40.2 18.6 %collective-permute-start.3 = (bf16[4,64,1024]{2,1,0:T(8,128)(2,1)S(1)}, bf16[4,64,1024]{2,1,0:T(8,128)(2,1)}, u32[]{:S(2)}, u32[]{:S(2)}) collective-permute-start(bf16[4,64,1024]{2,1,0:T(8,128)(2,1)S(1)} %constant_dynamic-update-slice_fusion.4), channel_id=1, source_target_pairs={{0,8},{4,12},{8,0},{12,4},{16,24},{20,28},{24,16},{28,20},{1,9},{5... | collective-permute-start | bytes 1572872 | tf_op jit(solution)/shard_map/ppermute | solution.py:705
  59.9 64.8 %all-gather.14.cloned.1.call-start = ((), (), s32[]{:S(2)}) async-start(), calls=%async_computation.8 | async-start | bytes 1310720 | tf_op jit(solution)/shard_map/all_gather | solution.py:782
  60.0 5.9 %collective-permute-start.5 = (bf16[4,128,1024]{2,1,0:T(8,128)(2,1)S(1)}, bf16[4,128,1024]{2,1,0:T(8,128)(2,1)S(1)}, u32[]{:S(2)}, u32[]{:S(2)}) collective-permute-start(bf16[4,128,1024]{2,1,0:T(8,128)(2,1)S(1)} %constant_dynamic-update-slice_fusion.3.kv_held), channel_id=1, source_target_pairs={{0,4},{4,0},{8,12},{12,8},{16,20},{20,16},{24,28},{28,24},{1,5},{5... | collective-permute-start | bytes 3145736 | tf_op jit(solution)/shard_map/ppermute | solution.py:705
  60.1 6.8 %collective-permute-start.4 = (bf16[4,128,1024]{2,1,0:T(8,128)(2,1)}, bf16[4,128,1024]{2,1,0:T(8,128)(2,1)}, u32[]{:S(2)}, u32[]{:S(2)}) collective-permute-start(bf16[4,128,1024]{2,1,0:T(8,128)(2,1)} %constant_dynamic-update-slice_fusion.5.query_held), channel_id=1, source_target_pairs={{0,4},{4,0},{8,12},{12,8},{16,20},{20,16},{24,28},{28,24},{1,5},{5... | collective-permute-start | bytes 3145736 | tf_op jit(solution)/shard_map/ppermute | solution.py:705
  91.0 2.9 collective-permute-start.6
  97.1 57.0 %all-gather.16.cloned.1.call-start = ((), (), s32[]{:S(2)}) async-start(), calls=%async_computation.10 | async-start | bytes 1310720 | tf_op jit(solution)/shard_map/all_gather | solution.py:782
  97.7 85.8 %reduce-scatter.7.cloned.1.call-start = ((), (), s32[]{:S(2)}) async-start(), calls=%async_computation.9 | async-start | bytes 1310720 | tf_op jit(solution)/shard_map/reduce_scatter | solution.py:785
  99.4 1.2 collective-permute-start.7
  101.3 3.7 collective-permute-start.8
  105.7 3.7 collective-permute-start.9
  140.9 71.3 %reduce-scatter.9.cloned.1.call-start = ((), (), s32[]{:S(2)}) async-start(), calls=%async_computation.11 | async-start | bytes 1310720 | tf_op jit(solution)/shard_map/reduce_scatter | solution.py:785
  170.3 70.6 %all-gather.18.cloned.1.call-start = ((), (), s32[]{:S(2)}) async-start(), calls=%async_computation.12 | async-start | bytes 1310720 | tf_op jit(solution)/shard_map/all_gather | solution.py:782
  185.5 85.0 %all-gather.20.cloned.1.call-start = ((), (), s32[]{:S(2)}) async-start(), calls=%async_computation.13 | async-start | bytes 1310720 | tf_op jit(solution)/shard_map/all_gather | solution.py:782
  215.2 91.9 %reduce-scatter.11.cloned.1.call-start = ((), (), s32[]{:S(2)}) async-start(), calls=%async_computation.14 | async-start | bytes 1310720 | tf_op jit(solution)/shard_map/reduce_scatter | solution.py:785
  256.0 73.0 %reduce-scatter.13.cloned.1.call-start = ((), (), s32[]{:S(2)}) async-start(), calls=%async_computation.15 | async-start | bytes 1310720 | tf_op jit(solution)/shard_map/reduce_scatter | solution.py:785
  296.9 10.2 %collective-permute-start.11 = (bf16[4,384,1024]{2,1,0:T(8,128)(2,1)}, bf16[4,384,1024]{2,1,0:T(8,128)(2,1)}, u32[]{:S(2)}, u32[]{:S(2)}) collective-permute-start(bf16[4,384,1024]{2,1,0:T(8,128)(2,1)} %bitcast.140), channel_id=1, source_target_pairs={{0,4},{4,0},{8,12},{12,8},{16,20},{20,16},{24,28},{28,24},{1,5},{5... | collective-permute-start | bytes 9437192 | tf_op jit(solution)/shard_map/ppermute | solution.py:705
  296.9 10.5 %collective-permute-start.10 = (bf16[4,384,1024]{2,1,0:T(8,128)(2,1)}, bf16[4,384,1024]{2,1,0:T(8,128)(2,1)}, u32[]{:S(2)}, u32[]{:S(2)}) collective-permute-start(bf16[4,384,1024]{2,1,0:T(8,128)(2,1)} %bitcast.139), channel_id=1, source_target_pairs={{0,4},{4,0},{8,12},{12,8},{16,20},{20,16},{24,28},{28,24},{1,5},{5... | collective-permute-start | bytes 9437192 | tf_op jit(solution)/shard_map/ppermute | solution.py:705
  313.5 39.5 %collective-permute-start.13 = (bf16[2,384,1024]{2,1,0:T(8,128)(2,1)}, bf16[2,384,1024]{2,1,0:T(8,128)(2,1)}, u32[]{:S(2)}, u32[]{:S(2)}) collective-permute-start(bf16[2,384,1024]{2,1,0:T(8,128)(2,1)} %get-tuple-element.270), channel_id=1, source_target_pairs={{0,16},{4,20},{8,24},{12,28},{16,0},{20,4},{24,8},{28,12},{1,17},{... | collective-permute-start | bytes 4718600 | tf_op jit(solution)/shard_map/ppermute | solution.py:705
  315.0 38.0 %collective-permute-start.12 = (bf16[2,384,1024]{2,1,0:T(8,128)(2,1)}, bf16[2,384,1024]{2,1,0:T(8,128)(2,1)}, u32[]{:S(2)}, u32[]{:S(2)}) collective-permute-start(bf16[2,384,1024]{2,1,0:T(8,128)(2,1)} %get-tuple-element.271), channel_id=1, source_target_pairs={{0,8},{4,12},{8,0},{12,4},{16,24},{20,28},{24,16},{28,20},{1,9},{5... | collective-permute-start | bytes 4718600 | tf_op jit(solution)/shard_map/ppermute | solution.py:705
  317.3 12.8 %all-to-all-start = ((f32[4,256,4]{1,2,0:T(4,128)}), f32[4,256,4]{1,2,0:T(4,128)S(1)}, u32[]{:S(2)}, u32[]{:S(2)}) async-start(f32[4,256,4]{1,2,0:T(4,128)} %pad_maximum_fusion.13), calls=%async_computation.4 | async-start | bytes 32768 | tf_op jit(solution)/shard_map/all_to_all | solution.py:957
  320.8 114.1 %reduce-scatter.15.cloned.1.call-start = ((), (), s32[]{:S(2)}) async-start(), calls=%async_computation.16 | async-start | bytes 2621440 | tf_op jit(solution)/shard_map/reduce_scatter | solution.py:785
  357.8 19.9 %collective-permute-start.15 = (bf16[1,384,1024]{2,1,0:T(8,128)(2,1)}, bf16[1,384,1024]{2,1,0:T(8,128)(2,1)}, u32[]{:S(2)}, u32[]{:S(2)}) collective-permute-start(bf16[1,384,1024]{2,1,0:T(8,128)(2,1)} %get-tuple-element.268), channel_id=1, source_target_pairs={{0,8},{4,12},{8,0},{12,4},{16,24},{20,28},{24,16},{28,20},{1,9},{5... | collective-permute-start | bytes 2359304 | tf_op jit(solution)/shard_map/ppermute | solution.py:705
  359.3 19.1 %collective-permute-start.14 = (bf16[1,384,1024]{2,1,0:T(8,128)(2,1)}, bf16[1,384,1024]{2,1,0:T(8,128)(2,1)}, u32[]{:S(2)}, u32[]{:S(2)}) collective-permute-start(bf16[1,384,1024]{2,1,0:T(8,128)(2,1)} %get-tuple-element.269), channel_id=1, source_target_pairs={{0,16},{4,20},{8,24},{12,28},{16,0},{20,4},{24,8},{28,12},{1,17},{... | collective-permute-start | bytes 2359304 | tf_op jit(solution)/shard_map/ppermute | solution.py:705
  377.3 81.6 %reduce-scatter.17.cloned.1.call-start = ((), (), s32[]{:S(2)}) async-start(), calls=%async_computation.17 | async-start | bytes 1024000 | tf_op jit(solution)/shard_map/reduce_scatter | solution.py:1018
  383.3 3.5 collective-permute-start.21
  384.8 4.4 collective-permute-start.17
  384.9 20.4 %collective-permute-start.19 = (bf16[1,384,1024]{2,1,0:T(8,128)(2,1)S(1)}, bf16[1,384,1024]{2,1,0:T(8,128)(2,1)S(1)}, u32[]{:S(2)}, u32[]{:S(2)}) collective-permute-start(bf16[1,384,1024]{2,1,0:T(8,128)(2,1)S(1)} %get-tuple-element.266), channel_id=1, source_target_pairs={{0,8},{4,12},{8,0},{12,4},{16,24},{20,28},{24,16},{28,20},{1,9},{5... | collective-permute-start | bytes 2359304 | tf_op jit(solution)/shard_map/ppermute | solution.py:705
  385.1 20.4 %collective-permute-start.16 = (bf16[1,384,1024]{2,1,0:T(8,128)(2,1)S(1)}, bf16[1,384,1024]{2,1,0:T(8,128)(2,1)S(1)}, u32[]{:S(2)}, u32[]{:S(2)}) collective-permute-start(bf16[1,384,1024]{2,1,0:T(8,128)(2,1)S(1)} %get-tuple-element.267), channel_id=1, source_target_pairs={{0,16},{4,20},{8,24},{12,28},{16,0},{20,4},{24,8},{28,12},{1,17},{... | collective-permute-start | bytes 2359304 | tf_op jit(solution)/shard_map/ppermute | solution.py:705
  387.1 34.6 %collective-permute-start.22 = (bf16[4,2,32,1536]{3,2,0,1:T(8,128)(2,1)S(1)}, bf16[4,2,32,1536]{3,2,0,1:T(8,128)(2,1)S(1)}, u32[]{:S(2)}, u32[]{:S(2)}) collective-permute-start(bf16[4,2,32,1536]{3,2,0,1:T(8,128)(2,1)S(1)} %add_convert_fusion.3), channel_id=1, source_target_pairs={{0,16},{4,20},{8,24},{12,28},{16,0},{20,4},{24,8},{28,12},{1,17},{... | collective-permute-start | bytes 2359304 | tf_op jit(solution)/shard_map/ppermute | solution.py:705
  389.3 34.4 %copy-start.37 = (bf16[4,4,32,1664]{3,2,0,1:T(8,128)(2,1)}, bf16[4,4,32,1664]{3,2,0,1:T(8,128)(2,1)S(1)}, u32[]{:S(2)}) copy-start(bf16[4,4,32,1664]{3,2,0,1:T(8,128)(2,1)S(1)} %collective-permute-done.17) | copy-start | bytes 5111812
  389.5 34.2 %collective-permute-start.18 = (bf16[4,2,32,1664]{3,2,0,1:T(8,128)(2,1)S(1)}, bf16[4,2,32,1664]{3,2,0,1:T(8,128)(2,1)S(1)}, u32[]{:S(2)}, u32[]{:S(2)}) collective-permute-start(bf16[4,2,32,1664]{3,2,0,1:T(8,128)(2,1)S(1)} %add_convert_fusion.2), channel_id=1, source_target_pairs={{0,8},{4,12},{8,0},{12,4},{16,24},{20,28},{24,16},{28,20},{1,9},{5... | collective-permute-start | bytes 2555912 | tf_op jit(solution)/shard_map/ppermute | solution.py:705
  421.9 10.5 %collective-permute-start.23 = (bf16[4,1,32,1536]{3,2,0,1:T(8,128)(2,1)S(1)}, bf16[4,1,32,1536]{3,2,0,1:T(8,128)(2,1)S(1)}, u32[]{:S(2)}, u32[]{:S(2)}) collective-permute-start(bf16[4,1,32,1536]{3,2,0,1:T(8,128)(2,1)S(1)} %add_convert_fusion.11), channel_id=1, source_target_pairs={{0,8},{4,12},{8,0},{12,4},{16,24},{20,28},{24,16},{28,20},{1,9},{5... | collective-permute-start | bytes 1179656 | tf_op jit(solution)/shard_map/ppermute | solution.py:705
  423.9 11.0 %collective-permute-start.20 = (bf16[4,1,32,1664]{3,2,0,1:T(8,128)(2,1)S(1)}, bf16[4,1,32,1664]{3,2,0,1:T(8,128)(2,1)}, u32[]{:S(2)}, u32[]{:S(2)}) collective-permute-start(bf16[4,1,32,1664]{3,2,0,1:T(8,128)(2,1)S(1)} %add_convert_fusion.9), channel_id=1, source_target_pairs={{0,16},{4,20},{8,24},{12,28},{16,0},{20,4},{24,8},{28,12},{1,17},{... | collective-permute-start | bytes 1277960 | tf_op jit(solution)/shard_map/ppermute | solution.py:705
  437.5 53.1 %all-gather.24.cloned.1.call-start = ((), (), s32[]{:S(2)}) async-start(), calls=%async_computation.19 | async-start | bytes 1843200 | tf_op jit(solution)/shard_map/all_gather | solution.py:1026
  437.6 10.0 %collective-permute-start.24 = (bf16[2,384,1024]{2,1,0:T(8,128)(2,1)S(1)}, bf16[2,384,1024]{2,1,0:T(8,128)(2,1)S(1)}, u32[]{:S(2)}, u32[]{:S(2)}) collective-permute-start(bf16[2,384,1024]{2,1,0:T(8,128)(2,1)S(1)} %constant_dynamic-update-slice_fusion.1), channel_id=1, source_target_pairs={{0,4},{4,0},{8,12},{12,8},{16,20},{20,16},{24,28},{28,24},{1,5},{5... | collective-permute-start | bytes 4718600 | tf_op jit(solution)/shard_map/ppermute | solution.py:705
  437.6 9.9 %collective-permute-start.25 = (bf16[2,384,1024]{2,1,0:T(8,128)(2,1)}, bf16[2,384,1024]{2,1,0:T(8,128)(2,1)S(1)}, u32[]{:S(2)}, u32[]{:S(2)}) collective-permute-start(bf16[2,384,1024]{2,1,0:T(8,128)(2,1)} %copy-done.3), channel_id=1, source_target_pairs={{0,4},{4,0},{8,12},{12,8},{16,20},{20,16},{24,28},{28,24},{1,5},{5... | collective-permute-start | bytes 4718600 | tf_op jit(solution)/shard_map/ppermute | solution.py:705
  438.1 38.7 %collective-permute-start.26 = (bf16[2,384,1024]{2,1,0:T(8,128)(2,1)S(1)}, bf16[2,384,1024]{2,1,0:T(8,128)(2,1)}, u32[]{:S(2)}, u32[]{:S(2)}) collective-permute-start(bf16[2,384,1024]{2,1,0:T(8,128)(2,1)S(1)} %constant_dynamic-update-slice_fusion.1), channel_id=1, source_target_pairs={{0,8},{4,12},{8,0},{12,4},{16,24},{20,28},{24,16},{28,20},{1,9},{5... | collective-permute-start | bytes 4718600 | tf_op jit(solution)/shard_map/ppermute | solution.py:705
  438.5 38.6 %collective-permute-start.27 = (bf16[2,384,1024]{2,1,0:T(8,128)(2,1)}, bf16[2,384,1024]{2,1,0:T(8,128)(2,1)}, u32[]{:S(2)}, u32[]{:S(2)}) collective-permute-start(bf16[2,384,1024]{2,1,0:T(8,128)(2,1)} %copy-done.3), channel_id=1, source_target_pairs={{0,16},{4,20},{8,24},{12,28},{16,0},{20,4},{24,8},{28,12},{1,17},{... | collective-permute-start | bytes 4718600 | tf_op jit(solution)/shard_map/ppermute | solution.py:705
  447.6 30.7 %copy-start.41 = (bf16[128,1024]{1,0:T(8,128)(2,1)S(1)}, bf16[128,1024]{1,0:T(8,128)(2,1)}, u32[]{:S(2)}) copy-start(bf16[128,1024]{1,0:T(8,128)(2,1)} %get-tuple-element.274) | copy-start | bytes 786436
  447.6 30.7 %copy-start.42 = (bf16[128,1024]{1,0:T(8,128)(2,1)S(1)}, bf16[128,1024]{1,0:T(8,128)(2,1)}, u32[]{:S(2)}) copy-start(bf16[128,1024]{1,0:T(8,128)(2,1)} %get-tuple-element.275) | copy-start | bytes 786436
  477.1 7.9 %collective-permute-start.28 = (bf16[2,384,1024]{2,1,0:T(8,128)(2,1)}, bf16[2,384,1024]{2,1,0:T(8,128)(2,1)S(1)}, u32[]{:S(2)}, u32[]{:S(2)}) collective-permute-start(bf16[2,384,1024]{2,1,0:T(8,128)(2,1)} %collective-permute-done.26), channel_id=1, source_target_pairs={{0,4},{4,0},{8,12},{12,8},{16,20},{20,16},{24,28},{28,24},{1,5},{5... | collective-permute-start | bytes 4718600 | tf_op jit(solution)/shard_map/ppermute | solution.py:705
  477.1 7.9 %collective-permute-start.29 = (bf16[2,384,1024]{2,1,0:T(8,128)(2,1)}, bf16[2,384,1024]{2,1,0:T(8,128)(2,1)}, u32[]{:S(2)}, u32[]{:S(2)}) collective-permute-start(bf16[2,384,1024]{2,1,0:T(8,128)(2,1)} %collective-permute-done.27), channel_id=1, source_target_pairs={{0,4},{4,0},{8,12},{12,8},{16,20},{20,16},{24,28},{28,24},{1,5},{5... | collective-permute-start | bytes 4718600 | tf_op jit(solution)/shard_map/ppermute | solution.py:705
  (50 other events, 324.2 us)
Sparse Core Ops, SparseCore 0:
  9.6 52.1 all-gather.11
  64.0 26.9 all-gather.21
  97.2 27.4 all-gather.13
  126.7 27.4 all-gather.15
  156.9 26.6 reduce-scatter.6
  186.4 25.7 reduce-scatter.8
  214.3 26.5 all-gather.17
  243.1 27.4 all-gather.19
  273.4 26.6 reduce-scatter.10
  302.9 26.0 reduce-scatter.12
  377.4 40.7 reduce-scatter.14
  437.6 21.1 reduce-scatter.16
  460.9 27.1 all-gather.23

commit v7 on v6

--- a/solution.py
+++ b/solution.py
@@ -428,7 +428,7 @@
         scratch_shapes=[
             pltpu.VMEM((shards, 2 * rows, columns), jnp.bfloat16) for columns in widths
         ],
-        compiler_params=pltpu.CompilerParams(vmem_limit_bytes=46 * MIB),
+        compiler_params=pltpu.CompilerParams(vmem_limit_bytes=60 * MIB),
         cost_estimate=SMALL_COST,
         name="attention_grads",
     )(

time: 513 us -> 512 us (level)
  local copies, waits for them, and re-layouts: 26.7 us -> 21.4 us
    unnamed x114 -> x104, local copies, waits for them, and re-layouts: 15.5 us -> 8.9 us
  transfers between devices with their start and end apart: 44 -> 44, of which waited for: 25 -> 27; matrix products, arithmetic and copies ran while one was open for 11% -> 12% of each run, Pallas kernels for 31% -> 31%
where the time goes in v7:
time: 512 us; the launch traced here: 503 us
  waiting for transfers between devices  182 us (36%)
  Pallas kernels  157 us (31%)
  other arithmetic  47.7 us (9%)
  blocking collectives  34.5 us (7%)
  starting transfers between devices  29.7 us (6%)
  between operations  22.7 us (4%)
  local copies, waits for them, and re-layouts  21.4 us (4%)
  matrix products  7.06 us (1%)
    ppermute x30, waiting for transfers between devices, exchange(): return lax.ppermute(block, 'rep', [(at, at ^ bit) for at in range(count)])  73.5 us
    all_gather x5, waiting for transfers between devices, gather(): return lax.all_gather(block, 'shard', axis=0, tiled=True)  47.3 us
    reduce_scatter x5, waiting for transfers between devices, scatter(): return lax.psum_scatter(block, 'shard', scatter_dimension=0, tiled=True)  47.1 us
    pallas_call x3, Pallas kernels, experts_grads(): pl.pallas_call(functools.partial(experts_grads_kernel, outputs, row_units...  33.3 us
    pallas_call x2, Pallas kernels, experts_backward(): pl.pallas_call(experts_backward_kernel, grid=(experts,), in_specs=[pl.Blo...  30 us
    pallas_call x2, Pallas kernels, experts_forward(): pl.pallas_call(experts_forward_kernel, grid=(experts,), in_specs=[pl.Bloc...  26.1 us
    ppermute x30, starting transfers between devices, exchange(): return lax.ppermute(block, 'rep', [(at, at ^ bit) for at in range(count)])  24.9 us
    all_gather x1, blocking collectives, body(): lax.all_gather(jnp.concatenate([piece_of(w_query, order_first), piece_of(...  20.3 us
  transfers between devices with their start and end apart: 44, of which 27 were waited for; matrix products, arithmetic and copies ran while one was open for 12% of the time, Pallas kernels for 31%

profile of v7, /device:TPU:0, one launch (start us, length us, event | category | flops | bytes accessed | tf_op | source)
XLA Modules:
  0.0 502.8 jit_solution(2786097342146356101)
XLA Ops:
  9.0 20.3 %all-gather = bf16[128,2048]{1,0:T(8,128)(2,1)S(1)} all-gather(bf16[32,2048]{1,0:T(8,128)(2,1)S(1)} %pad_maximum_fusion.10), channel_id=2, replica_groups=mesh['rep'=8,'shard'=4] {'shard'}, dimensions={0}, use_global_device_ids=true | all-gather | bytes 655360 | tf_op jit(solution)/shard_map/all_gather | solution.py:810
  29.4 1.6 collective-permute-start.2
  35.4 4.1 collective-permute-done
  42.5 14.2 %all-gather.3 = bf16[4,1,6657]{2,1,0:T(2,128)(2,1)S(1)} all-gather(bf16[1,1,6657]{2,1,0:T(2,128)(2,1)S(1)} %bitcast.129), channel_id=1, replica_groups=mesh['rep'=8,'shard'=4] {'shard'}, dimensions={0}, use_global_device_ids=true | all-gather | bytes 66570 | tf_op jit(solution)/shard_map/all_gather | solution.py:782
  62.0 1.9 fusion.13
  68.5 17.9 %attention_forward.1 = (bf16[4,256,1024]{2,1,0:T(8,128)(2,1)}, bf16[4,256,1024]{2,1,0:T(8,128)(2,1)}, bf16[1024,1024]{1,0:T(8,128)(2,1)}, bf16[1024,512]{1,0:T(8...) custom-call(f32[4]{0:T(128)} %compare_select_fusion.bias_ref, ...), custom_call_target="tpu_custom_call" | custom-call | flops 1000000 | bytes 100000 | tf_op jit(solution)/shard_map/attention_forward/pallas_call | solution.py:596
  86.4 4.6 all-gather.22.cloned.1.call-done
  91.0 1.8 pad_maximum_fusion
  102.2 2.0 collective-permute-done.8
  106.9 1.7 collective-permute-done.9
  109.1 14.8 %all-gather.14.cloned.1.call-done.x_ref.refs_0_ = bf16[512,1024]{1,0:T(8,128)(2,1)} async-done(((bf16[128,1024]{1,0:T(8,128)(2,1)}), bf16[512,1024]{1,0:T(8,128)(2,1)}) %all-gather.14.cloned.1.call-update) | async-done | bytes 1048592 | tf_op jit(solution)/shard_map/all_gather | solution.py:782
  123.9 1.7 fusion.28
  127.0 13.1 %experts_forward.2 = (bf16[512,1024]{1,0:T(8,128)(2,1)}, f32[4,512,1024]{2,1,0:T(8,128)}, bf16[4,512,512]{2,1,0:T(8,128)(2,1)}) custom-call(bf16[512,1024]{1,0:T(8,128)(2,1)} %all-gather.14.cloned.1.call-done.x_ref.refs_0_, f32[512,128]{1,0:T(8,128)} %pad.7.gate_ref, bf16[4,1024,1024]{2,1,0:T(8,128)(2,1)} %in_ref.7, bf16[4,512,1024]{2,1,0:T(8,128)(2,1)} %out_ref.7), custom_call_target="tpu_custom_call" | custom-call | flops 1000000 | bytes 100000 | tf_op jit(solution)/shard_map/experts_forward/pallas_call | solution.py:104
  140.4 13.0 %all-gather.16.cloned.1.call-done.x_ref.refs_1_ = bf16[512,1024]{1,0:T(8,128)(2,1)} async-done(((bf16[128,1024]{1,0:T(8,128)(2,1)}), bf16[512,1024]{1,0:T(8,128)(2,1)}) %all-gather.16.cloned.1.call-update) | async-done | bytes 1048592 | tf_op jit(solution)/shard_map/all_gather | solution.py:782
  153.4 1.7 fusion.27
  156.4 13.1 %experts_forward.3 = (bf16[512,1024]{1,0:T(8,128)(2,1)}, f32[4,512,1024]{2,1,0:T(8,128)}, bf16[4,512,512]{2,1,0:T(8,128)(2,1)}) custom-call(bf16[512,1024]{1,0:T(8,128)(2,1)} %all-gather.16.cloned.1.call-done.x_ref.refs_1_, f32[512,128]{1,0:T(8,128)} %pad.8.gate_ref, bf16[4,1024,1024]{2,1,0:T(8,128)(2,1)} %in_ref.7, bf16[4,512,1024]{2,1,0:T(8,128)(2,1)} %out_ref.7), custom_call_target="tpu_custom_call" | custom-call | flops 1000000 | bytes 100000 | tf_op jit(solution)/shard_map/experts_forward/pallas_call | solution.py:104
  170.3 12.4 %reduce-scatter.7.cloned.1.call-done = bf16[128,1024]{1,0:T(8,128)(2,1)} async-done(((bf16[512,1024]{1,0:T(8,128)(2,1)}), bf16[128,1024]{1,0:T(8,128)(2,1)}) %reduce-scatter.7.cloned.1.call-update) | async-done | bytes 262160 | tf_op jit(solution)/shard_map/reduce_scatter | solution.py:785
  182.7 2.0 multiply_convert_fusion.3
  184.9 26.5 %reduce-scatter.9.cloned.1.call-done = bf16[128,1024]{1,0:T(8,128)(2,1)} async-done(((bf16[512,1024]{1,0:T(8,128)(2,1)}), bf16[128,1024]{1,0:T(8,128)(2,1)}) %reduce-scatter.9.cloned.1.call-update) | async-done | bytes 262160 | tf_op jit(solution)/shard_map/reduce_scatter | solution.py:785
  211.4 2.9 multiply_convert_fusion.2
  219.3 2.5 pad_maximum_fusion.15.digits_ref
  221.8 18.4 %all-gather.18.cloned.1.call-done.dmix_ref.refs_1_ = bf16[512,1024]{1,0:T(8,128)(2,1)} async-done(((bf16[128,1024]{1,0:T(8,128)(2,1)}), bf16[512,1024]{1,0:T(8,128)(2,1)}) %all-gather.18.cloned.1.call-update) | async-done | bytes 1048592 | tf_op jit(solution)/shard_map/all_gather | solution.py:782
  240.1 15.0 %experts_backward.2 = (bf16[512,1024]{1,0:T(8,128)(2,1)}, bf16[4,512,1024]{2,1,0:T(8,128)(2,1)}, f32[512,128]{1,0:T(8,128)}) custom-call(bf16[512,1024]{1,0:T(8,128)(2,1)} %all-gather.18.cloned.1.call-done.dmix_ref.refs_1_, f32[512,128]{1,0:T(8,128)} %pad.7.gate_ref, f32[4,512,1024]{2,1,0:T(8,128)} %get-tuple-element.109.gate_up_ref, ...), custom_call_target="tpu_custom_call" | custom-call | flops 1000000 | bytes 100000 | tf_op jit(solution)/shard_map/experts_backward/pallas_call | solution.py:167
  256.1 12.5 %experts_grads.3.refs_0_ = bf16[4,1536,1024]{2,1,0:T(8,128)(2,1)} custom-call(s32[4]{0:T(128)} %pad_add_fusion.order_ref, bf16[512,1024]{1,0:T(8,128)(2,1)} %all-gather.14.cloned.1.call-done.x_ref.refs_0_, bf16[512,1024]{1,0:T(8,128)(2,1)} %all-gather.18.cloned.1.call-done.dmix_ref.refs_1_, bf16[4,512,1024]{2,1,0:T(8,128)(2,1)} %get-tuple-element.110.refs_2_, ...), custom_call_target="tpu_custom_call" | custom-call | flops 1000000 | bytes 100000 | tf_op jit(solution)/shard_map/experts_grads/pallas_call | solution.py:249
  269.8 15.0 %experts_backward.3 = (bf16[512,1024]{1,0:T(8,128)(2,1)}, bf16[4,512,1024]{2,1,0:T(8,128)(2,1)}, f32[512,128]{1,0:T(8,128)}) custom-call(bf16[512,1024]{1,0:T(8,128)(2,1)} %all-gather.20.cloned.1.call-done.dmix_ref.refs_2_, f32[512,128]{1,0:T(8,128)} %pad.8.gate_ref, f32[4,512,1024]{2,1,0:T(8,128)} %get-tuple-element.113.gate_up_ref, ...), custom_call_target="tpu_custom_call" | custom-call | flops 1000000 | bytes 100000 | tf_op jit(solution)/shard_map/experts_backward/pallas_call | solution.py:167
  284.7 11.4 %experts_grads.4 = (bf16[1536,1024]{1,0:T(8,128)(2,1)}, bf16[1536,1024]{1,0:T(8,128)(2,1)}) custom-call(s32[2]{0:T(128)} %copy-done.46, bf16[4,1536,1024]{2,1,0:T(8,128)(2,1)} %experts_grads.3.refs_0_, bf16[512,1024]{1,0:T(8,128)(2,1)} %all-gather.16.cloned.1.call-done.x_ref.refs_1_, bf16[512,1024]{1,0:T(8,128)(2,1)} %all-gather.20.cloned.1.call-done.dmix_ref.refs_2_, ...), custom_call_target="tpu_custom_call" | custom-call | flops 1000000 | bytes 100000 | tf_op jit(solution)/shard_map/experts_grads/pallas_call | solution.py:249
  296.9 9.4 %experts_grads.5 = bf16[2,1536,1024]{2,1,0:T(8,128)(2,1)} custom-call(s32[2]{0:T(128)} %copy-done.45, bf16[4,1536,1024]{2,1,0:T(8,128)(2,1)} %experts_grads.3.refs_0_, bf16[512,1024]{1,0:T(8,128)(2,1)} %all-gather.16.cloned.1.call-done.x_ref.refs_1_, bf16[512,1024]{1,0:T(8,128)(2,1)} %all-gather.20.cloned.1.call-done.dmix_ref.refs_2_, ...), custom_call_target="tpu_custom_call" | custom-call | flops 1000000 | bytes 100000 | tf_op jit(solution)/shard_map/experts_grads/pallas_call | solution.py:249
  306.6 6.1 %add_convert_fusion = (bf16[2,384,1024]{2,1,0:T(8,128)(2,1)}, bf16[2,384,1024]{2,1,0:T(8,128)(2,1)}) fusion(bf16[4,384,1024]{2,1,0:T(8,128)(2,1)} %collective-permute-done.11, s32[]{:T(128)S(6)} %select_n.278, bf16[8,384,1024]{2,1,0:T(8,128)(2,1)} %bitcast.97, s32[]{:T(128)S(6)} %select_n.277, bf16[4,384,1024]{2,1,0:T(8,128)(2,1)} %collective-permute-done.10, ...), kind=kLoop, calls=%fused_computation | loop fusion | flops 6291456 | bytes 9437200 | tf_op jit(solution)/shard_map/convert_element_type | solution.py:727
  316.6 3.4 all-to-all-start
  320.1 8.1 %reduce-scatter.13.cloned.1.call-done = bf16[128,1024]{1,0:T(8,128)(2,1)} async-done(((bf16[512,1024]{1,0:T(8,128)(2,1)}), bf16[128,1024]{1,0:T(8,128)(2,1)}) %reduce-scatter.13.cloned.1.call-update) | async-done | bytes 262160 | tf_op jit(solution)/shard_map/reduce_scatter | solution.py:785
  334.5 15.3 %attention_backward.1 = (bf16[256,1024]{1,0:T(8,128)(2,1)S(1)}, bf16[1024,1024]{1,0:T(8,128)(2,1)S(1)}) custom-call(f32[4]{0:T(128)S(1)} %copy-done.15, bf16[256,1024]{1,0:T(8,128)(2,1)S(1)} %copy-done.12, bf16[1024,512]{1,0:T(8,128)(2,1)S(1)} %copy-done.10, bf16[1024,512]{1,0:T(8,128)(2,1)S(1)} %copy-done.11, f32[8,512]{1,0:T(8,128)S(1)} %copy-done.14, ...), custom_call_target="tpu_custom_call" | custom-call | flops 1000000 | bytes 100000 | tf_op jit(solution)/shard_map/attention_backward/pallas_call | solution.py:683
  350.8 4.5 add_convert_fusion.6
  359.1 14.1 %attention_grads.1 = (bf16[1024,1024]{1,0:T(8,128)(2,1)}, f32[256,1024]{1,0:T(8,128)}, bf16[4,128,1664]{2,1,0:T(8,128)(2,1)}, bf16[4,128,1664]{2,1,0:T(8,128)(2,...) custom-call(s32[2]{0:T(128)} %pad_add_fusion.1.side_ref, f32[3]{0:T(128)} %pad_maximum_fusion.15.digits_ref, ...), custom_call_target="tpu_custom_call" | custom-call | flops 1000000 | bytes 100000 | tf_op jit(solution)/shard_map/attention_grads/pallas_call | solution.py:416
  375.8 4.3 add_convert_fusion.4
  386.9 15.3 %collective-permute-done.19 = bf16[1,384,1024]{2,1,0:T(8,128)(2,1)S(1)} collective-permute-done((bf16[1,384,1024]{2,1,0:T(8,128)(2,1)S(1)}, bf16[1,384,1024]{2,1,0:T(8,128)(2,1)S(1)}, u32[]{:S(2)}, u32[]{:S(2)}) %collective-permute-start.19) | collective-permute-done | bytes 786464 | tf_op jit(solution)/shard_map/ppermute | solution.py:705
  402.5 16.1 %collective-permute-done.22 = bf16[4,2,32,1536]{3,2,0,1:T(8,128)(2,1)S(1)} collective-permute-done((bf16[4,2,32,1536]{3,2,0,1:T(8,128)(2,1)S(1)}, bf16[4,2,32,1536]{3,2,0,1:T(8,128)(2,1)S(1)}, u32[]{:S(2)}, u32[]{:S(2)}) %collective-permute-start.22) | collective-permute-done | bytes 786464 | tf_op jit(solution)/shard_map/ppermute | solution.py:705
  418.8 1.8 collective-permute-start.23
  422.3 7.0 %collective-permute-done.23 = bf16[4,1,32,1536]{3,2,0,1:T(8,128)(2,1)S(1)} collective-permute-done((bf16[4,1,32,1536]{3,2,0,1:T(8,128)(2,1)S(1)}, bf16[4,1,32,1536]{3,2,0,1:T(8,128)(2,1)S(1)}, u32[]{:S(2)}, u32[]{:S(2)}) %collective-permute-start.23) | collective-permute-done | bytes 393248 | tf_op jit(solution)/shard_map/ppermute | solution.py:705
  429.5 2.3 collective-permute-done.20
  431.8 1.6 add_convert_fusion.8
  437.5 3.6 widen.4
  443.7 3.6 widen.5
  447.3 8.4 %reduce-scatter.17.cloned.1.call-done = bf16[1,32,3200]{2,1,0:T(8,128)(2,1)} async-done(((bf16[4,32,3200]{2,1,0:T(8,128)(2,1)}), bf16[1,32,3200]{2,1,0:T(8,128)(2,1)}) %reduce-scatter.17.cloned.1.call-update) | async-done | bytes 204816 | tf_op jit(solution)/shard_map/reduce_scatter | solution.py:1018
  455.7 18.6 %collective-permute-done.26 = bf16[2,384,1024]{2,1,0:T(8,128)(2,1)} collective-permute-done((bf16[2,384,1024]{2,1,0:T(8,128)(2,1)S(1)}, bf16[2,384,1024]{2,1,0:T(8,128)(2,1)}, u32[]{:S(2)}, u32[]{:S(2)}) %collective-permute-start.26) | collective-permute-done | bytes 1572896 | tf_op jit(solution)/shard_map/ppermute | solution.py:705
  475.7 1.8 pad_maximum_fusion.9
  477.4 5.8 %widen.6 = (f32[4,1024,1024]{2,1,0:T(8,128)}, f32[4,512,1024]{2,1,0:T(8,128)}) custom-call(s32[4]{0:T(128)S(1)} %get-tuple-element.301.spot_ref, bf16[768,1024]{1,0:T(8,128)(2,1)} %bitcast.48.first_ref, bf16[768,1024]{1,0:T(8,128)(2,1)} %bitcast.49.second_ref, ...), custom_call_target="tpu_custom_call", output_to_operand_aliasing={{0}: (3, {}), {1}: (4, {})} | custom-call | flops 1000000 | bytes 100000 | tf_op jit(solution)/shard_map/widen/pallas_call | solution.py:288
  483.3 5.6 %widen.7 = (f32[4,1024,1024]{2,1,0:T(8,128)}, f32[4,512,1024]{2,1,0:T(8,128)}) custom-call(s32[4]{0:T(128)S(1)} %get-tuple-element.302.spot_ref, bf16[768,1024]{1,0:T(8,128)(2,1)S(1)} %bitcast.96, bf16[768,1024]{1,0:T(8,128)(2,1)} %bitcast.47.second_ref, f32[4,1024,1024]{2,1,0:T(8,128)} %get-tuple-element.178.refs_0_, ...), custom_call_target="tpu_custom_call", output_to_operand_aliasing={{0}: (3, {}), {1}: (4, {})} | custom-call | flops 1000000 | bytes 100000 | tf_op jit(solution)/shard_map/widen/pallas_call | solution.py:288
  490.4 1.9 finish.1
  (286 shorter events, 74.8 us)
Async XLA Ops:
  7.2 34.6 %copy-start = (bf16[256,1024]{1,0:T(8,128)(2,1)S(1)}, bf16[256,1024]{1,0:T(8,128)(2,1)}, u32[]{:S(2)}) copy-start(bf16[256,1024]{1,0:T(8,128)(2,1)} %param.21) | copy-start | bytes 1572868
  7.2 61.2 %all-gather.12.cloned.1.call-start = ((), (), s32[]{:S(2)}) async-start(), calls=%async_computation.7 | async-start | bytes 2621440 | tf_op jit(solution)/shard_map/all_gather | solution.py:782
  8.0 83.0 %all-gather.22.cloned.1.call-start = ((), (), s32[]{:S(2)}) async-start(), calls=%async_computation.18 | async-start | bytes 1310720 | tf_op jit(solution)/shard_map/all_gather | solution.py:829
  29.4 10.8 %collective-permute-start.2 = (bf16[4,32,1024]{2,1,0:T(8,128)(2,1)S(1)}, bf16[4,32,1024]{2,1,0:T(8,128)(2,1)S(1)}, u32[]{:S(2)}, u32[]{:S(2)}) collective-permute-start(bf16[4,32,1024]{2,1,0:T(8,128)(2,1)S(1)} %get-tuple-element.278), channel_id=1, source_target_pairs={{0,16},{4,20},{8,24},{12,28},{16,0},{20,4},{24,8},{28,12},{1,17},{... | collective-permute-start | bytes 786440 | tf_op jit(solution)/shard_map/ppermute | solution.py:705
  31.0 8.4 %collective-permute-start = (bf16[4,32,1024]{2,1,0:T(8,128)(2,1)S(1)}, bf16[4,32,1024]{2,1,0:T(8,128)(2,1)S(1)}, u32[]{:S(2)}, u32[]{:S(2)}) collective-permute-start(bf16[4,32,1024]{2,1,0:T(8,128)(2,1)S(1)} %get-tuple-element.279), channel_id=1, source_target_pairs={{0,8},{4,12},{8,0},{12,4},{16,24},{20,28},{24,16},{28,20},{1,9},{5... | collective-permute-start | bytes 786440 | tf_op jit(solution)/shard_map/ppermute | solution.py:705
  40.2 18.1 %collective-permute-start.1 = (bf16[4,64,1024]{2,1,0:T(8,128)(2,1)}, bf16[4,64,1024]{2,1,0:T(8,128)(2,1)}, u32[]{:S(2)}, u32[]{:S(2)}) collective-permute-start(bf16[4,64,1024]{2,1,0:T(8,128)(2,1)} %constant_dynamic-update-slice_fusion.6), channel_id=1, source_target_pairs={{0,16},{4,20},{8,24},{12,28},{16,0},{20,4},{24,8},{28,12},{1,17},{... | collective-permute-start | bytes 1572872 | tf_op jit(solution)/shard_map/ppermute | solution.py:705
  40.2 19.1 %collective-permute-start.3 = (bf16[4,64,1024]{2,1,0:T(8,128)(2,1)S(1)}, bf16[4,64,1024]{2,1,0:T(8,128)(2,1)}, u32[]{:S(2)}, u32[]{:S(2)}) collective-permute-start(bf16[4,64,1024]{2,1,0:T(8,128)(2,1)S(1)} %constant_dynamic-update-slice_fusion.4), channel_id=1, source_target_pairs={{0,8},{4,12},{8,0},{12,4},{16,24},{20,28},{24,16},{28,20},{1,9},{5... | collective-permute-start | bytes 1572872 | tf_op jit(solution)/shard_map/ppermute | solution.py:705
  60.9 63.0 %all-gather.14.cloned.1.call-start = ((), (), s32[]{:S(2)}) async-start(), calls=%async_computation.8 | async-start | bytes 1310720 | tf_op jit(solution)/shard_map/all_gather | solution.py:782
  61.0 6.5 %collective-permute-start.5 = (bf16[4,128,1024]{2,1,0:T(8,128)(2,1)S(1)}, bf16[4,128,1024]{2,1,0:T(8,128)(2,1)S(1)}, u32[]{:S(2)}, u32[]{:S(2)}) collective-permute-start(bf16[4,128,1024]{2,1,0:T(8,128)(2,1)S(1)} %constant_dynamic-update-slice_fusion.3.kv_held), channel_id=1, source_target_pairs={{0,4},{4,0},{8,12},{12,8},{16,20},{20,16},{24,28},{28,24},{1,5},{5... | collective-permute-start | bytes 3145736 | tf_op jit(solution)/shard_map/ppermute | solution.py:705
  61.0 7.4 %collective-permute-start.4 = (bf16[4,128,1024]{2,1,0:T(8,128)(2,1)S(1)}, bf16[4,128,1024]{2,1,0:T(8,128)(2,1)}, u32[]{:S(2)}, u32[]{:S(2)}) collective-permute-start(bf16[4,128,1024]{2,1,0:T(8,128)(2,1)S(1)} %constant_dynamic-update-slice_fusion.5.query_held), channel_id=1, source_target_pairs={{0,4},{4,0},{8,12},{12,8},{16,20},{20,16},{24,28},{28,24},{1,5},{5... | collective-permute-start | bytes 3145736 | tf_op jit(solution)/shard_map/ppermute | solution.py:705
  91.0 2.9 collective-permute-start.6
  96.3 57.0 %all-gather.16.cloned.1.call-start = ((), (), s32[]{:S(2)}) async-start(), calls=%async_computation.10 | async-start | bytes 1310720 | tf_op jit(solution)/shard_map/all_gather | solution.py:782
  96.9 85.8 %reduce-scatter.7.cloned.1.call-start = ((), (), s32[]{:S(2)}) async-start(), calls=%async_computation.9 | async-start | bytes 1310720 | tf_op jit(solution)/shard_map/reduce_scatter | solution.py:785
  98.7 1.2 collective-permute-start.7
  100.6 3.7 collective-permute-start.8
  104.9 3.7 collective-permute-start.9
  140.1 71.3 %reduce-scatter.9.cloned.1.call-start = ((), (), s32[]{:S(2)}) async-start(), calls=%async_computation.11 | async-start | bytes 1310720 | tf_op jit(solution)/shard_map/reduce_scatter | solution.py:785
  169.5 70.6 %all-gather.18.cloned.1.call-start = ((), (), s32[]{:S(2)}) async-start(), calls=%async_computation.12 | async-start | bytes 1310720 | tf_op jit(solution)/shard_map/all_gather | solution.py:782
  182.7 28.7 %copy-start.34 = (bf16[128,1024]{1,0:T(8,128)(2,1)S(1)}, bf16[128,1024]{1,0:T(8,128)(2,1)}, u32[]{:S(2)}) copy-start(bf16[128,1024]{1,0:T(8,128)(2,1)} %reduce-scatter.7.cloned.1.call-done) | copy-start | bytes 786436
  184.8 84.9 %all-gather.20.cloned.1.call-start = ((), (), s32[]{:S(2)}) async-start(), calls=%async_computation.13 | async-start | bytes 1310720 | tf_op jit(solution)/shard_map/all_gather | solution.py:782
  214.3 92.0 %reduce-scatter.11.cloned.1.call-start = ((), (), s32[]{:S(2)}) async-start(), calls=%async_computation.14 | async-start | bytes 1310720 | tf_op jit(solution)/shard_map/reduce_scatter | solution.py:785
  255.2 73.0 %reduce-scatter.13.cloned.1.call-start = ((), (), s32[]{:S(2)}) async-start(), calls=%async_computation.15 | async-start | bytes 1310720 | tf_op jit(solution)/shard_map/reduce_scatter | solution.py:785
  296.1 10.2 %collective-permute-start.11 = (bf16[4,384,1024]{2,1,0:T(8,128)(2,1)}, bf16[4,384,1024]{2,1,0:T(8,128)(2,1)}, u32[]{:S(2)}, u32[]{:S(2)}) collective-permute-start(bf16[4,384,1024]{2,1,0:T(8,128)(2,1)} %bitcast.140), channel_id=1, source_target_pairs={{0,4},{4,0},{8,12},{12,8},{16,20},{20,16},{24,28},{28,24},{1,5},{5... | collective-permute-start | bytes 9437192 | tf_op jit(solution)/shard_map/ppermute | solution.py:705
  296.1 10.5 %collective-permute-start.10 = (bf16[4,384,1024]{2,1,0:T(8,128)(2,1)}, bf16[4,384,1024]{2,1,0:T(8,128)(2,1)}, u32[]{:S(2)}, u32[]{:S(2)}) collective-permute-start(bf16[4,384,1024]{2,1,0:T(8,128)(2,1)} %bitcast.139), channel_id=1, source_target_pairs={{0,4},{4,0},{8,12},{12,8},{16,20},{20,16},{24,28},{28,24},{1,5},{5... | collective-permute-start | bytes 9437192 | tf_op jit(solution)/shard_map/ppermute | solution.py:705
  312.8 37.0 %collective-permute-start.13 = (bf16[2,384,1024]{2,1,0:T(8,128)(2,1)}, bf16[2,384,1024]{2,1,0:T(8,128)(2,1)}, u32[]{:S(2)}, u32[]{:S(2)}) collective-permute-start(bf16[2,384,1024]{2,1,0:T(8,128)(2,1)} %get-tuple-element.270), channel_id=1, source_target_pairs={{0,16},{4,20},{8,24},{12,28},{16,0},{20,4},{24,8},{28,12},{1,17},{... | collective-permute-start | bytes 4718600 | tf_op jit(solution)/shard_map/ppermute | solution.py:705
  314.3 36.5 %collective-permute-start.12 = (bf16[2,384,1024]{2,1,0:T(8,128)(2,1)}, bf16[2,384,1024]{2,1,0:T(8,128)(2,1)}, u32[]{:S(2)}, u32[]{:S(2)}) collective-permute-start(bf16[2,384,1024]{2,1,0:T(8,128)(2,1)} %get-tuple-element.271), channel_id=1, source_target_pairs={{0,8},{4,12},{8,0},{12,4},{16,24},{20,28},{24,16},{28,20},{1,9},{5... | collective-permute-start | bytes 4718600 | tf_op jit(solution)/shard_map/ppermute | solution.py:705
  316.6 12.6 %all-to-all-start = ((f32[4,256,4]{1,2,0:T(4,128)}), f32[4,256,4]{1,2,0:T(4,128)S(1)}, u32[]{:S(2)}, u32[]{:S(2)}) async-start(f32[4,256,4]{1,2,0:T(4,128)} %pad_maximum_fusion.13), calls=%async_computation.4 | async-start | bytes 32768 | tf_op jit(solution)/shard_map/all_to_all | solution.py:957
  320.1 111.7 %reduce-scatter.15.cloned.1.call-start = ((), (), s32[]{:S(2)}) async-start(), calls=%async_computation.16 | async-start | bytes 2621440 | tf_op jit(solution)/shard_map/reduce_scatter | solution.py:785
  355.3 19.3 %collective-permute-start.15 = (bf16[1,384,1024]{2,1,0:T(8,128)(2,1)}, bf16[1,384,1024]{2,1,0:T(8,128)(2,1)S(1)}, u32[]{:S(2)}, u32[]{:S(2)}) collective-permute-start(bf16[1,384,1024]{2,1,0:T(8,128)(2,1)} %get-tuple-element.268), channel_id=1, source_target_pairs={{0,8},{4,12},{8,0},{12,4},{16,24},{20,28},{24,16},{28,20},{1,9},{5... | collective-permute-start | bytes 2359304 | tf_op jit(solution)/shard_map/ppermute | solution.py:705
  356.8 19.0 %collective-permute-start.14 = (bf16[1,384,1024]{2,1,0:T(8,128)(2,1)}, bf16[1,384,1024]{2,1,0:T(8,128)(2,1)S(1)}, u32[]{:S(2)}, u32[]{:S(2)}) collective-permute-start(bf16[1,384,1024]{2,1,0:T(8,128)(2,1)} %get-tuple-element.269), channel_id=1, source_target_pairs={{0,16},{4,20},{8,24},{12,28},{16,0},{20,4},{24,8},{28,12},{1,17},{... | collective-permute-start | bytes 2359304 | tf_op jit(solution)/shard_map/ppermute | solution.py:705
  373.2 82.5 %reduce-scatter.17.cloned.1.call-start = ((), (), s32[]{:S(2)}) async-start(), calls=%async_computation.17 | async-start | bytes 1024000 | tf_op jit(solution)/shard_map/reduce_scatter | solution.py:1018
  380.2 3.5 collective-permute-start.21
  381.7 4.4 collective-permute-start.17
  381.8 20.4 %collective-permute-start.19 = (bf16[1,384,1024]{2,1,0:T(8,128)(2,1)S(1)}, bf16[1,384,1024]{2,1,0:T(8,128)(2,1)S(1)}, u32[]{:S(2)}, u32[]{:S(2)}) collective-permute-start(bf16[1,384,1024]{2,1,0:T(8,128)(2,1)S(1)} %get-tuple-element.266), channel_id=1, source_target_pairs={{0,8},{4,12},{8,0},{12,4},{16,24},{20,28},{24,16},{28,20},{1,9},{5... | collective-permute-start | bytes 2359304 | tf_op jit(solution)/shard_map/ppermute | solution.py:705
  382.0 20.4 %collective-permute-start.16 = (bf16[1,384,1024]{2,1,0:T(8,128)(2,1)S(1)}, bf16[1,384,1024]{2,1,0:T(8,128)(2,1)S(1)}, u32[]{:S(2)}, u32[]{:S(2)}) collective-permute-start(bf16[1,384,1024]{2,1,0:T(8,128)(2,1)S(1)} %get-tuple-element.267), channel_id=1, source_target_pairs={{0,16},{4,20},{8,24},{12,28},{16,0},{20,4},{24,8},{28,12},{1,17},{... | collective-permute-start | bytes 2359304 | tf_op jit(solution)/shard_map/ppermute | solution.py:705
  383.9 34.7 %collective-permute-start.22 = (bf16[4,2,32,1536]{3,2,0,1:T(8,128)(2,1)S(1)}, bf16[4,2,32,1536]{3,2,0,1:T(8,128)(2,1)S(1)}, u32[]{:S(2)}, u32[]{:S(2)}) collective-permute-start(bf16[4,2,32,1536]{3,2,0,1:T(8,128)(2,1)S(1)} %add_convert_fusion.3), channel_id=1, source_target_pairs={{0,16},{4,20},{8,24},{12,28},{16,0},{20,4},{24,8},{28,12},{1,17},{... | collective-permute-start | bytes 2359304 | tf_op jit(solution)/shard_map/ppermute | solution.py:705
  386.1 34.4 %copy-start.29 = (bf16[4,4,32,1664]{3,2,0,1:T(8,128)(2,1)}, bf16[4,4,32,1664]{3,2,0,1:T(8,128)(2,1)S(1)}, u32[]{:S(2)}) copy-start(bf16[4,4,32,1664]{3,2,0,1:T(8,128)(2,1)S(1)} %collective-permute-done.17) | copy-start | bytes 5111812
  386.4 34.2 %collective-permute-start.18 = (bf16[4,2,32,1664]{3,2,0,1:T(8,128)(2,1)S(1)}, bf16[4,2,32,1664]{3,2,0,1:T(8,128)(2,1)S(1)}, u32[]{:S(2)}, u32[]{:S(2)}) collective-permute-start(bf16[4,2,32,1664]{3,2,0,1:T(8,128)(2,1)S(1)} %add_convert_fusion.2), channel_id=1, source_target_pairs={{0,8},{4,12},{8,0},{12,4},{16,24},{20,28},{24,16},{28,20},{1,9},{5... | collective-permute-start | bytes 2555912 | tf_op jit(solution)/shard_map/ppermute | solution.py:705
  418.8 10.5 %collective-permute-start.23 = (bf16[4,1,32,1536]{3,2,0,1:T(8,128)(2,1)S(1)}, bf16[4,1,32,1536]{3,2,0,1:T(8,128)(2,1)S(1)}, u32[]{:S(2)}, u32[]{:S(2)}) collective-permute-start(bf16[4,1,32,1536]{3,2,0,1:T(8,128)(2,1)S(1)} %add_convert_fusion.11), channel_id=1, source_target_pairs={{0,8},{4,12},{8,0},{12,4},{16,24},{20,28},{24,16},{28,20},{1,9},{5... | collective-permute-start | bytes 1179656 | tf_op jit(solution)/shard_map/ppermute | solution.py:705
  420.8 11.0 %collective-permute-start.20 = (bf16[4,1,32,1664]{3,2,0,1:T(8,128)(2,1)S(1)}, bf16[4,1,32,1664]{3,2,0,1:T(8,128)(2,1)}, u32[]{:S(2)}, u32[]{:S(2)}) collective-permute-start(bf16[4,1,32,1664]{3,2,0,1:T(8,128)(2,1)S(1)} %add_convert_fusion.9), channel_id=1, source_target_pairs={{0,16},{4,20},{8,24},{12,28},{16,0},{20,4},{24,8},{28,12},{1,17},{... | collective-permute-start | bytes 1277960 | tf_op jit(solution)/shard_map/ppermute | solution.py:705
  434.4 54.6 %all-gather.24.cloned.1.call-start = ((), (), s32[]{:S(2)}) async-start(), calls=%async_computation.19 | async-start | bytes 1843200 | tf_op jit(solution)/shard_map/all_gather | solution.py:1026
  434.4 9.2 %collective-permute-start.24 = (bf16[2,384,1024]{2,1,0:T(8,128)(2,1)S(1)}, bf16[2,384,1024]{2,1,0:T(8,128)(2,1)S(1)}, u32[]{:S(2)}, u32[]{:S(2)}) collective-permute-start(bf16[2,384,1024]{2,1,0:T(8,128)(2,1)S(1)} %constant_dynamic-update-slice_fusion.1), channel_id=1, source_target_pairs={{0,4},{4,0},{8,12},{12,8},{16,20},{20,16},{24,28},{28,24},{1,5},{5... | collective-permute-start | bytes 4718600 | tf_op jit(solution)/shard_map/ppermute | solution.py:705
  434.5 9.2 %collective-permute-start.25 = (bf16[2,384,1024]{2,1,0:T(8,128)(2,1)S(1)}, bf16[2,384,1024]{2,1,0:T(8,128)(2,1)S(1)}, u32[]{:S(2)}, u32[]{:S(2)}) collective-permute-start(bf16[2,384,1024]{2,1,0:T(8,128)(2,1)S(1)} %constant_dynamic-update-slice_fusion), channel_id=1, source_target_pairs={{0,4},{4,0},{8,12},{12,8},{16,20},{20,16},{24,28},{28,24},{1,5},{5... | collective-permute-start | bytes 4718600 | tf_op jit(solution)/shard_map/ppermute | solution.py:705
  435.7 38.6 %collective-permute-start.26 = (bf16[2,384,1024]{2,1,0:T(8,128)(2,1)S(1)}, bf16[2,384,1024]{2,1,0:T(8,128)(2,1)}, u32[]{:S(2)}, u32[]{:S(2)}) collective-permute-start(bf16[2,384,1024]{2,1,0:T(8,128)(2,1)S(1)} %constant_dynamic-update-slice_fusion.1), channel_id=1, source_target_pairs={{0,8},{4,12},{8,0},{12,4},{16,24},{20,28},{24,16},{28,20},{1,9},{5... | collective-permute-start | bytes 4718600 | tf_op jit(solution)/shard_map/ppermute | solution.py:705
  436.1 38.4 %collective-permute-start.27 = (bf16[2,384,1024]{2,1,0:T(8,128)(2,1)S(1)}, bf16[2,384,1024]{2,1,0:T(8,128)(2,1)}, u32[]{:S(2)}, u32[]{:S(2)}) collective-permute-start(bf16[2,384,1024]{2,1,0:T(8,128)(2,1)S(1)} %constant_dynamic-update-slice_fusion), channel_id=1, source_target_pairs={{0,16},{4,20},{8,24},{12,28},{16,0},{20,4},{24,8},{28,12},{1,17},{... | collective-permute-start | bytes 4718600 | tf_op jit(solution)/shard_map/ppermute | solution.py:705
  443.7 32.0 %copy-start.35 = (bf16[128,1024]{1,0:T(8,128)(2,1)S(1)}, bf16[128,1024]{1,0:T(8,128)(2,1)}, u32[]{:S(2)}) copy-start(bf16[128,1024]{1,0:T(8,128)(2,1)} %get-tuple-element.274) | copy-start | bytes 786436
  474.5 8.8 %collective-permute-start.28 = (bf16[2,384,1024]{2,1,0:T(8,128)(2,1)}, bf16[2,384,1024]{2,1,0:T(8,128)(2,1)S(1)}, u32[]{:S(2)}, u32[]{:S(2)}) collective-permute-start(bf16[2,384,1024]{2,1,0:T(8,128)(2,1)} %collective-permute-done.26), channel_id=1, source_target_pairs={{0,4},{4,0},{8,12},{12,8},{16,20},{20,16},{24,28},{28,24},{1,5},{5... | collective-permute-start | bytes 4718600 | tf_op jit(solution)/shard_map/ppermute | solution.py:705
  474.5 8.8 %collective-permute-start.29 = (bf16[2,384,1024]{2,1,0:T(8,128)(2,1)}, bf16[2,384,1024]{2,1,0:T(8,128)(2,1)}, u32[]{:S(2)}, u32[]{:S(2)}) collective-permute-start(bf16[2,384,1024]{2,1,0:T(8,128)(2,1)} %collective-permute-done.27), channel_id=1, source_target_pairs={{0,4},{4,0},{8,12},{12,8},{16,20},{20,16},{24,28},{28,24},{1,5},{5... | collective-permute-start | bytes 4718600 | tf_op jit(solution)/shard_map/ppermute | solution.py:705
  (45 other events, 329.9 us)
Sparse Core Ops, SparseCore 0:
  9.6 52.1 all-gather.11
  64.0 27.0 all-gather.21
  96.4 27.4 all-gather.13
  125.9 27.4 all-gather.15
  156.1 26.6 reduce-scatter.6
  185.6 25.7 reduce-scatter.8
  213.5 26.5 all-gather.17
  242.3 27.4 all-gather.19
  272.6 26.6 reduce-scatter.10
  302.1 26.0 reduce-scatter.12
  373.3 41.8 reduce-scatter.14
  434.5 21.1 reduce-scatter.16
  457.8 27.4 all-gather.23

commit v8 on v7

--- a/solution.py
+++ b/solution.py
@@ -255,7 +255,7 @@
             out_specs=out_specs,
         ),
         out_shape=out_shape,
-        compiler_params=pltpu.CompilerParams(vmem_limit_bytes=VMEM_BYTES),
+        compiler_params=pltpu.CompilerParams(vmem_limit_bytes=48 * MIB),
         cost_estimate=SMALL_COST,
         name="experts_grads",
     )(order, *([] if base is None else [base]), *[part for chunk in chunks for part in chunk])
@@ -694,7 +694,7 @@
             pltpu.VMEM((tokens, LANES), jnp.float32),
             pltpu.VMEM((tokens, LANES), jnp.float32),
         ],
-        compiler_params=pltpu.CompilerParams(vmem_limit_bytes=22 * MIB),
+        compiler_params=pltpu.CompilerParams(vmem_limit_bytes=28 * MIB),
         cost_estimate=SMALL_COST,
         name="attention_backward",
     )(bias, query, key, value, log_norm, grad, *tables, *tables_own)

time: 512 us -> 511 us (level)
  local copies, waits for them, and re-layouts: 21.4 us -> 28.9 us
    unnamed x104 -> x126, local copies, waits for them, and re-layouts: 8.9 us -> 15.4 us
  transfers between devices with their start and end apart: 44 -> 44, of which waited for: 27 -> 27; matrix products, arithmetic and copies ran while one was open for 12% -> 11% of each run, Pallas kernels for 31% -> 30%
where the time goes in v8:
time: 511 us; the launch traced here: 503 us
  waiting for transfers between devices  182 us (36%)
  Pallas kernels  154 us (30%)
  other arithmetic  46.6 us (9%)
  blocking collectives  34.5 us (7%)
  local copies, waits for them, and re-layouts  28.9 us (6%)
  starting transfers between devices  26.4 us (5%)
  between operations  22.8 us (4%)
  matrix products  7.06 us (1%)
    ppermute x30, waiting for transfers between devices, exchange(): return lax.ppermute(block, 'rep', [(at, at ^ bit) for at in range(count)])  75.5 us
    all_gather x5, waiting for transfers between devices, gather(): return lax.all_gather(block, 'shard', axis=0, tiled=True)  46.8 us
    reduce_scatter x5, waiting for transfers between devices, scatter(): return lax.psum_scatter(block, 'shard', scatter_dimension=0, tiled=True)  45.7 us
    pallas_call x2, Pallas kernels, experts_backward(): pl.pallas_call(experts_backward_kernel, grid=(experts,), in_specs=[pl.Blo...  30.3 us
    pallas_call x3, Pallas kernels, experts_grads(): pl.pallas_call(functools.partial(experts_grads_kernel, outputs, row_units...  29.4 us
    pallas_call x2, Pallas kernels, experts_forward(): pl.pallas_call(experts_forward_kernel, grid=(experts,), in_specs=[pl.Bloc...  26.1 us
    ppermute x30, starting transfers between devices, exchange(): return lax.ppermute(block, 'rep', [(at, at ^ bit) for at in range(count)])  21.7 us
    all_gather x1, blocking collectives, body(): lax.all_gather(jnp.concatenate([piece_of(w_query, order_first), piece_of(...  20.3 us
  transfers between devices with their start and end apart: 44, of which 27 were waited for; matrix products, arithmetic and copies ran while one was open for 11% of the time, Pallas kernels for 30%

profile of v8, /device:TPU:0, one launch (start us, length us, event | category | flops | bytes accessed | tf_op | source)
XLA Modules:
  0.0 502.6 jit_solution(8429440306436186976)
XLA Ops:
  9.0 20.3 %all-gather = bf16[128,2048]{1,0:T(8,128)(2,1)S(1)} all-gather(bf16[32,2048]{1,0:T(8,128)(2,1)S(1)} %pad_maximum_fusion.10), channel_id=2, replica_groups=mesh['rep'=8,'shard'=4] {'shard'}, dimensions={0}, use_global_device_ids=true | all-gather | bytes 655360 | tf_op jit(solution)/shard_map/all_gather | solution.py:810
  29.4 1.6 collective-permute-start.2
  35.4 4.1 collective-permute-done
  42.5 14.2 %all-gather.3 = bf16[4,1,6657]{2,1,0:T(2,128)(2,1)S(1)} all-gather(bf16[1,1,6657]{2,1,0:T(2,128)(2,1)S(1)} %bitcast.129), channel_id=1, replica_groups=mesh['rep'=8,'shard'=4] {'shard'}, dimensions={0}, use_global_device_ids=true | all-gather | bytes 66570 | tf_op jit(solution)/shard_map/all_gather | solution.py:782
  62.0 1.9 fusion.13
  67.9 17.9 %attention_forward.1 = (bf16[4,256,1024]{2,1,0:T(8,128)(2,1)}, bf16[4,256,1024]{2,1,0:T(8,128)(2,1)}, bf16[1024,1024]{1,0:T(8,128)(2,1)}, bf16[1024,512]{1,0:T(8...) custom-call(f32[4]{0:T(128)} %compare_select_fusion.bias_ref, ...), custom_call_target="tpu_custom_call" | custom-call | flops 1000000 | bytes 100000 | tf_op jit(solution)/shard_map/attention_forward/pallas_call | solution.py:596
  85.8 5.2 %all-gather.22.cloned.1.call-done = bf16[512,1024]{1,0:T(8,128)(2,1)} async-done(((bf16[128,1024]{1,0:T(8,128)(2,1)}), bf16[512,1024]{1,0:T(8,128)(2,1)}) %all-gather.22.cloned.1.call-update) | async-done | bytes 1048592 | tf_op jit(solution)/shard_map/all_gather | solution.py:829
  91.0 1.7 pad_maximum_fusion
  102.3 2.0 collective-permute-done.8
  107.0 1.7 collective-permute-done.9
  109.2 14.8 %all-gather.14.cloned.1.call-done.x_ref.refs_0_ = bf16[512,1024]{1,0:T(8,128)(2,1)} async-done(((bf16[128,1024]{1,0:T(8,128)(2,1)}), bf16[512,1024]{1,0:T(8,128)(2,1)}) %all-gather.14.cloned.1.call-update) | async-done | bytes 1048592 | tf_op jit(solution)/shard_map/all_gather | solution.py:782
  124.0 1.7 fusion.28
  127.1 13.0 %experts_forward.2 = (bf16[512,1024]{1,0:T(8,128)(2,1)}, f32[4,512,1024]{2,1,0:T(8,128)}, bf16[4,512,512]{2,1,0:T(8,128)(2,1)}) custom-call(bf16[512,1024]{1,0:T(8,128)(2,1)} %all-gather.14.cloned.1.call-done.x_ref.refs_0_, f32[512,128]{1,0:T(8,128)} %pad.7.gate_ref, bf16[4,1024,1024]{2,1,0:T(8,128)(2,1)} %in_ref.7, bf16[4,512,1024]{2,1,0:T(8,128)(2,1)} %out_ref.7), custom_call_target="tpu_custom_call" | custom-call | flops 1000000 | bytes 100000 | tf_op jit(solution)/shard_map/experts_forward/pallas_call | solution.py:104
  140.5 13.0 %all-gather.16.cloned.1.call-done.x_ref.refs_1_ = bf16[512,1024]{1,0:T(8,128)(2,1)} async-done(((bf16[128,1024]{1,0:T(8,128)(2,1)}), bf16[512,1024]{1,0:T(8,128)(2,1)}) %all-gather.16.cloned.1.call-update) | async-done | bytes 1048592 | tf_op jit(solution)/shard_map/all_gather | solution.py:782
  153.5 1.7 fusion.27
  156.6 13.1 %experts_forward.3 = (bf16[512,1024]{1,0:T(8,128)(2,1)}, f32[4,512,1024]{2,1,0:T(8,128)}, bf16[4,512,512]{2,1,0:T(8,128)(2,1)}) custom-call(bf16[512,1024]{1,0:T(8,128)(2,1)} %all-gather.16.cloned.1.call-done.x_ref.refs_1_, f32[512,128]{1,0:T(8,128)} %pad.8.gate_ref, bf16[4,1024,1024]{2,1,0:T(8,128)(2,1)} %in_ref.7, bf16[4,512,1024]{2,1,0:T(8,128)(2,1)} %out_ref.7), custom_call_target="tpu_custom_call" | custom-call | flops 1000000 | bytes 100000 | tf_op jit(solution)/shard_map/experts_forward/pallas_call | solution.py:104
  170.4 12.4 %reduce-scatter.7.cloned.1.call-done = bf16[128,1024]{1,0:T(8,128)(2,1)} async-done(((bf16[512,1024]{1,0:T(8,128)(2,1)}), bf16[128,1024]{1,0:T(8,128)(2,1)}) %reduce-scatter.7.cloned.1.call-update) | async-done | bytes 262160 | tf_op jit(solution)/shard_map/reduce_scatter | solution.py:785
  182.9 2.0 multiply_convert_fusion.3
  185.0 26.5 %reduce-scatter.9.cloned.1.call-done = bf16[128,1024]{1,0:T(8,128)(2,1)} async-done(((bf16[512,1024]{1,0:T(8,128)(2,1)}), bf16[128,1024]{1,0:T(8,128)(2,1)}) %reduce-scatter.9.cloned.1.call-update) | async-done | bytes 262160 | tf_op jit(solution)/shard_map/reduce_scatter | solution.py:785
  211.5 3.0 multiply_convert_fusion.2
  219.4 2.5 pad_maximum_fusion.15.digits_ref
  221.9 18.4 %all-gather.18.cloned.1.call-done.dmix_ref.refs_1_ = bf16[512,1024]{1,0:T(8,128)(2,1)} async-done(((bf16[128,1024]{1,0:T(8,128)(2,1)}), bf16[512,1024]{1,0:T(8,128)(2,1)}) %all-gather.18.cloned.1.call-update) | async-done | bytes 1048592 | tf_op jit(solution)/shard_map/all_gather | solution.py:782
  240.3 15.1 %experts_backward.2 = (bf16[512,1024]{1,0:T(8,128)(2,1)}, bf16[4,512,1024]{2,1,0:T(8,128)(2,1)}, f32[512,128]{1,0:T(8,128)}) custom-call(bf16[512,1024]{1,0:T(8,128)(2,1)} %all-gather.18.cloned.1.call-done.dmix_ref.refs_1_, f32[512,128]{1,0:T(8,128)} %pad.7.gate_ref, f32[4,512,1024]{2,1,0:T(8,128)} %get-tuple-element.109.gate_up_ref, ...), custom_call_target="tpu_custom_call" | custom-call | flops 1000000 | bytes 100000 | tf_op jit(solution)/shard_map/experts_backward/pallas_call | solution.py:167
  258.3 11.1 %experts_grads.3.refs_0_ = bf16[4,1536,1024]{2,1,0:T(8,128)(2,1)} custom-call(s32[4]{0:T(128)S(1)} %pad_add_fusion.order_ref, bf16[512,1024]{1,0:T(8,128)(2,1)S(1)} %copy-done.4, bf16[512,1024]{1,0:T(8,128)(2,1)S(1)} %copy-done.13, bf16[4,512,1024]{2,1,0:T(8,128)(2,1)} %get-tuple-element.110.refs_2_, bf16[4,512,512]{2,1,0:T(8,128)(2,1)S(1)} %copy-done.14), custom_call_target="tpu_custom_call" | custom-call | flops 1000000 | bytes 100000 | tf_op jit(solution)/shard_map/experts_grads/pallas_call | solution.py:249
  269.9 15.1 %experts_backward.3 = (bf16[512,1024]{1,0:T(8,128)(2,1)}, bf16[4,512,1024]{2,1,0:T(8,128)(2,1)}, f32[512,128]{1,0:T(8,128)}) custom-call(bf16[512,1024]{1,0:T(8,128)(2,1)} %all-gather.20.cloned.1.call-done.dmix_ref.refs_2_, f32[512,128]{1,0:T(8,128)} %pad.8.gate_ref, f32[4,512,1024]{2,1,0:T(8,128)} %get-tuple-element.113.gate_up_ref, ...), custom_call_target="tpu_custom_call" | custom-call | flops 1000000 | bytes 100000 | tf_op jit(solution)/shard_map/experts_backward/pallas_call | solution.py:167
  286.7 10.2 %experts_grads.4 = (bf16[1536,1024]{1,0:T(8,128)(2,1)}, bf16[1536,1024]{1,0:T(8,128)(2,1)}) custom-call(s32[2]{0:T(128)S(1)} %iota_add_fusion.order_ref, bf16[4,1536,1024]{2,1,0:T(8,128)(2,1)} %experts_grads.3.refs_0_, bf16[512,1024]{1,0:T(8,128)(2,1)S(1)} %copy-done.2, bf16[512,1024]{1,0:T(8,128)(2,1)S(1)} %copy-done.3, ...), custom_call_target="tpu_custom_call" | custom-call | flops 1000000 | bytes 100000 | tf_op jit(solution)/shard_map/experts_grads/pallas_call | solution.py:249
  298.4 1.6 copy-done.6
  300.1 8.1 %experts_grads.5 = bf16[2,1536,1024]{2,1,0:T(8,128)(2,1)} custom-call(s32[2]{0:T(128)S(1)} %iota_add_fusion.1.order_ref, bf16[4,1536,1024]{2,1,0:T(8,128)(2,1)} %experts_grads.3.refs_0_, bf16[512,1024]{1,0:T(8,128)(2,1)S(1)} %copy-done.2, bf16[512,1024]{1,0:T(8,128)(2,1)S(1)} %copy-done.3, bf16[4,512,1024]{2,1,0:T(8,128)(2,1)} %get-tuple-element.114.refs_3_, ...), custom_call_target="tpu_custom_call" | custom-call | flops 1000000 | bytes 100000 | tf_op jit(solution)/shard_map/experts_grads/pallas_call | solution.py:249
  308.3 6.1 %add_convert_fusion = (bf16[2,384,1024]{2,1,0:T(8,128)(2,1)}, bf16[2,384,1024]{2,1,0:T(8,128)(2,1)}) fusion(bf16[4,384,1024]{2,1,0:T(8,128)(2,1)} %collective-permute-done.11, s32[]{:T(128)S(6)} %select_n.278, bf16[8,384,1024]{2,1,0:T(8,128)(2,1)} %bitcast.97, s32[]{:T(128)S(6)} %select_n.277, bf16[4,384,1024]{2,1,0:T(8,128)(2,1)} %collective-permute-done.10, ...), kind=kLoop, calls=%fused_computation | loop fusion | flops 6291456 | bytes 9437200 | tf_op jit(solution)/shard_map/convert_element_type | solution.py:727
  318.2 3.3 all-to-all-start
  321.5 6.7 %reduce-scatter.13.cloned.1.call-done = bf16[128,1024]{1,0:T(8,128)(2,1)} async-done(((bf16[512,1024]{1,0:T(8,128)(2,1)}), bf16[128,1024]{1,0:T(8,128)(2,1)}) %reduce-scatter.13.cloned.1.call-update) | async-done | bytes 262160 | tf_op jit(solution)/shard_map/reduce_scatter | solution.py:785
  334.5 15.3 %attention_backward.1 = (bf16[256,1024]{1,0:T(8,128)(2,1)S(1)}, bf16[1024,1024]{1,0:T(8,128)(2,1)S(1)}) custom-call(f32[4]{0:T(128)S(1)} %copy-done.24, bf16[256,1024]{1,0:T(8,128)(2,1)S(1)} %copy-done.21, bf16[1024,512]{1,0:T(8,128)(2,1)S(1)} %copy-done.19, bf16[1024,512]{1,0:T(8,128)(2,1)S(1)} %copy-done.20, f32[8,512]{1,0:T(8,128)S(1)} %copy-done.23, ...), custom_call_target="tpu_custom_call" | custom-call | flops 1000000 | bytes 100000 | tf_op jit(solution)/shard_map/attention_backward/pallas_call | solution.py:683
  352.2 4.5 add_convert_fusion.6
  359.6 14.1 %attention_grads.1 = (bf16[1024,1024]{1,0:T(8,128)(2,1)}, f32[256,1024]{1,0:T(8,128)}, bf16[4,128,1664]{2,1,0:T(8,128)(2,1)}, bf16[4,128,1664]{2,1,0:T(8,128)(2,...) custom-call(s32[2]{0:T(128)} %pad_add_fusion.1.side_ref, f32[3]{0:T(128)} %pad_maximum_fusion.15.digits_ref, ...), custom_call_target="tpu_custom_call" | custom-call | flops 1000000 | bytes 100000 | tf_op jit(solution)/shard_map/attention_grads/pallas_call | solution.py:416
  376.4 4.1 add_convert_fusion.4
  387.5 15.1 %collective-permute-done.19 = bf16[1,384,1024]{2,1,0:T(8,128)(2,1)S(1)} collective-permute-done((bf16[1,384,1024]{2,1,0:T(8,128)(2,1)S(1)}, bf16[1,384,1024]{2,1,0:T(8,128)(2,1)S(1)}, u32[]{:S(2)}, u32[]{:S(2)}) %collective-permute-start.19) | collective-permute-done | bytes 786464 | tf_op jit(solution)/shard_map/ppermute | solution.py:705
  403.1 16.0 %collective-permute-done.22 = bf16[4,2,32,1536]{3,2,0,1:T(8,128)(2,1)S(1)} collective-permute-done((bf16[4,2,32,1536]{3,2,0,1:T(8,128)(2,1)S(1)}, bf16[4,2,32,1536]{3,2,0,1:T(8,128)(2,1)S(1)}, u32[]{:S(2)}, u32[]{:S(2)}) %collective-permute-start.22) | collective-permute-done | bytes 786464 | tf_op jit(solution)/shard_map/ppermute | solution.py:705
  419.3 1.7 collective-permute-start.23
  422.0 7.7 %collective-permute-done.23 = bf16[4,1,32,1536]{3,2,0,1:T(8,128)(2,1)S(1)} collective-permute-done((bf16[4,1,32,1536]{3,2,0,1:T(8,128)(2,1)S(1)}, bf16[4,1,32,1536]{3,2,0,1:T(8,128)(2,1)S(1)}, u32[]{:S(2)}, u32[]{:S(2)}) %collective-permute-start.23) | collective-permute-done | bytes 393248 | tf_op jit(solution)/shard_map/ppermute | solution.py:705
  429.9 2.2 collective-permute-done.20
  438.8 3.6 widen.4
  442.4 1.8 fusion
  445.6 3.6 widen.5
  449.2 8.0 %reduce-scatter.17.cloned.1.call-done = bf16[1,32,3200]{2,1,0:T(8,128)(2,1)} async-done(((bf16[4,32,3200]{2,1,0:T(8,128)(2,1)}), bf16[1,32,3200]{2,1,0:T(8,128)(2,1)}) %reduce-scatter.17.cloned.1.call-update) | async-done | bytes 204816 | tf_op jit(solution)/shard_map/reduce_scatter | solution.py:1018
  457.2 17.5 %collective-permute-done.26 = bf16[2,384,1024]{2,1,0:T(8,128)(2,1)} collective-permute-done((bf16[2,384,1024]{2,1,0:T(8,128)(2,1)S(1)}, bf16[2,384,1024]{2,1,0:T(8,128)(2,1)}, u32[]{:S(2)}, u32[]{:S(2)}) %collective-permute-start.26) | collective-permute-done | bytes 1572896 | tf_op jit(solution)/shard_map/ppermute | solution.py:705
  477.0 6.1 %widen.6 = (f32[4,1024,1024]{2,1,0:T(8,128)}, f32[4,512,1024]{2,1,0:T(8,128)}) custom-call(s32[4]{0:T(128)S(1)} %get-tuple-element.301.spot_ref, bf16[768,1024]{1,0:T(8,128)(2,1)} %bitcast.48.first_ref, bf16[768,1024]{1,0:T(8,128)(2,1)} %bitcast.49.second_ref, ...), custom_call_target="tpu_custom_call", output_to_operand_aliasing={{0}: (3, {}), {1}: (4, {})} | custom-call | flops 1000000 | bytes 100000 | tf_op jit(solution)/shard_map/widen/pallas_call | solution.py:288
  483.1 5.6 %widen.7 = (f32[4,1024,1024]{2,1,0:T(8,128)}, f32[4,512,1024]{2,1,0:T(8,128)}) custom-call(s32[4]{0:T(128)S(1)} %get-tuple-element.302.spot_ref, bf16[768,1024]{1,0:T(8,128)(2,1)S(1)} %bitcast.96, bf16[768,1024]{1,0:T(8,128)(2,1)} %bitcast.47.second_ref, f32[4,1024,1024]{2,1,0:T(8,128)} %get-tuple-element.178.refs_0_, ...), custom_call_target="tpu_custom_call", output_to_operand_aliasing={{0}: (3, {}), {1}: (4, {})} | custom-call | flops 1000000 | bytes 100000 | tf_op jit(solution)/shard_map/widen/pallas_call | solution.py:288
  490.1 1.9 finish.1
  (308 shorter events, 80.5 us)
Async XLA Ops:
  7.2 34.6 %copy-start = (bf16[256,1024]{1,0:T(8,128)(2,1)S(1)}, bf16[256,1024]{1,0:T(8,128)(2,1)}, u32[]{:S(2)}) copy-start(bf16[256,1024]{1,0:T(8,128)(2,1)} %param.21) | copy-start | bytes 1572868
  7.2 60.6 %all-gather.12.cloned.1.call-start = ((), (), s32[]{:S(2)}) async-start(), calls=%async_computation.7 | async-start | bytes 2621440 | tf_op jit(solution)/shard_map/all_gather | solution.py:782
  8.0 83.0 %all-gather.22.cloned.1.call-start = ((), (), s32[]{:S(2)}) async-start(), calls=%async_computation.18 | async-start | bytes 1310720 | tf_op jit(solution)/shard_map/all_gather | solution.py:829
  29.4 10.8 %collective-permute-start.2 = (bf16[4,32,1024]{2,1,0:T(8,128)(2,1)S(1)}, bf16[4,32,1024]{2,1,0:T(8,128)(2,1)S(1)}, u32[]{:S(2)}, u32[]{:S(2)}) collective-permute-start(bf16[4,32,1024]{2,1,0:T(8,128)(2,1)S(1)} %get-tuple-element.278), channel_id=1, source_target_pairs={{0,16},{4,20},{8,24},{12,28},{16,0},{20,4},{24,8},{28,12},{1,17},{... | collective-permute-start | bytes 786440 | tf_op jit(solution)/shard_map/ppermute | solution.py:705
  31.0 8.4 %collective-permute-start = (bf16[4,32,1024]{2,1,0:T(8,128)(2,1)S(1)}, bf16[4,32,1024]{2,1,0:T(8,128)(2,1)S(1)}, u32[]{:S(2)}, u32[]{:S(2)}) collective-permute-start(bf16[4,32,1024]{2,1,0:T(8,128)(2,1)S(1)} %get-tuple-element.279), channel_id=1, source_target_pairs={{0,8},{4,12},{8,0},{12,4},{16,24},{20,28},{24,16},{28,20},{1,9},{5... | collective-permute-start | bytes 786440 | tf_op jit(solution)/shard_map/ppermute | solution.py:705
  40.2 18.1 %collective-permute-start.1 = (bf16[4,64,1024]{2,1,0:T(8,128)(2,1)}, bf16[4,64,1024]{2,1,0:T(8,128)(2,1)}, u32[]{:S(2)}, u32[]{:S(2)}) collective-permute-start(bf16[4,64,1024]{2,1,0:T(8,128)(2,1)} %constant_dynamic-update-slice_fusion.6), channel_id=1, source_target_pairs={{0,16},{4,20},{8,24},{12,28},{16,0},{20,4},{24,8},{28,12},{1,17},{... | collective-permute-start | bytes 1572872 | tf_op jit(solution)/shard_map/ppermute | solution.py:705
  40.2 19.1 %collective-permute-start.3 = (bf16[4,64,1024]{2,1,0:T(8,128)(2,1)S(1)}, bf16[4,64,1024]{2,1,0:T(8,128)(2,1)}, u32[]{:S(2)}, u32[]{:S(2)}) collective-permute-start(bf16[4,64,1024]{2,1,0:T(8,128)(2,1)S(1)} %constant_dynamic-update-slice_fusion.4), channel_id=1, source_target_pairs={{0,8},{4,12},{8,0},{12,4},{16,24},{20,28},{24,16},{28,20},{1,9},{5... | collective-permute-start | bytes 1572872 | tf_op jit(solution)/shard_map/ppermute | solution.py:705
  60.9 63.2 %all-gather.14.cloned.1.call-start = ((), (), s32[]{:S(2)}) async-start(), calls=%async_computation.8 | async-start | bytes 1310720 | tf_op jit(solution)/shard_map/all_gather | solution.py:782
  61.0 5.9 %collective-permute-start.5 = (bf16[4,128,1024]{2,1,0:T(8,128)(2,1)S(1)}, bf16[4,128,1024]{2,1,0:T(8,128)(2,1)S(1)}, u32[]{:S(2)}, u32[]{:S(2)}) collective-permute-start(bf16[4,128,1024]{2,1,0:T(8,128)(2,1)S(1)} %constant_dynamic-update-slice_fusion.3.kv_held), channel_id=1, source_target_pairs={{0,4},{4,0},{8,12},{12,8},{16,20},{20,16},{24,28},{28,24},{1,5},{5... | collective-permute-start | bytes 3145736 | tf_op jit(solution)/shard_map/ppermute | solution.py:705
  61.0 6.8 %collective-permute-start.4 = (bf16[4,128,1024]{2,1,0:T(8,128)(2,1)S(1)}, bf16[4,128,1024]{2,1,0:T(8,128)(2,1)}, u32[]{:S(2)}, u32[]{:S(2)}) collective-permute-start(bf16[4,128,1024]{2,1,0:T(8,128)(2,1)S(1)} %constant_dynamic-update-slice_fusion.5.query_held), channel_id=1, source_target_pairs={{0,4},{4,0},{8,12},{12,8},{16,20},{20,16},{24,28},{28,24},{1,5},{5... | collective-permute-start | bytes 3145736 | tf_op jit(solution)/shard_map/ppermute | solution.py:705
  91.0 2.9 collective-permute-start.6
  95.3 116.2 %copy-start.25 = (f32[256,1024]{1,0:T(8,128)}, f32[256,1024]{1,0:T(8,128)S(1)}, u32[]{:S(2)}) copy-start(f32[256,1024]{1,0:T(8,128)S(1)} %get-tuple-element.293) | copy-start | bytes 3145732
  96.5 57.0 %all-gather.16.cloned.1.call-start = ((), (), s32[]{:S(2)}) async-start(), calls=%async_computation.10 | async-start | bytes 1310720 | tf_op jit(solution)/shard_map/all_gather | solution.py:782
  97.0 85.8 %reduce-scatter.7.cloned.1.call-start = ((), (), s32[]{:S(2)}) async-start(), calls=%async_computation.9 | async-start | bytes 1310720 | tf_op jit(solution)/shard_map/reduce_scatter | solution.py:785
  98.8 1.2 collective-permute-start.7
  100.7 3.7 collective-permute-start.8
  105.0 3.7 collective-permute-start.9
  140.2 71.3 %reduce-scatter.9.cloned.1.call-start = ((), (), s32[]{:S(2)}) async-start(), calls=%async_computation.11 | async-start | bytes 1310720 | tf_op jit(solution)/shard_map/reduce_scatter | solution.py:785
  169.7 70.7 %all-gather.18.cloned.1.call-start = ((), (), s32[]{:S(2)}) async-start(), calls=%async_computation.12 | async-start | bytes 1310720 | tf_op jit(solution)/shard_map/all_gather | solution.py:782
  185.0 84.9 %all-gather.20.cloned.1.call-start = ((), (), s32[]{:S(2)}) async-start(), calls=%async_computation.13 | async-start | bytes 1310720 | tf_op jit(solution)/shard_map/all_gather | solution.py:782
  214.5 93.7 %reduce-scatter.11.cloned.1.call-start = ((), (), s32[]{:S(2)}) async-start(), calls=%async_computation.14 | async-start | bytes 1310720 | tf_op jit(solution)/shard_map/reduce_scatter | solution.py:785
  255.5 72.7 %reduce-scatter.13.cloned.1.call-start = ((), (), s32[]{:S(2)}) async-start(), calls=%async_computation.15 | async-start | bytes 1310720 | tf_op jit(solution)/shard_map/reduce_scatter | solution.py:785
  296.9 11.4 %collective-permute-start.11 = (bf16[4,384,1024]{2,1,0:T(8,128)(2,1)}, bf16[4,384,1024]{2,1,0:T(8,128)(2,1)}, u32[]{:S(2)}, u32[]{:S(2)}) collective-permute-start(bf16[4,384,1024]{2,1,0:T(8,128)(2,1)} %bitcast.140), channel_id=1, source_target_pairs={{0,4},{4,0},{8,12},{12,8},{16,20},{20,16},{24,28},{28,24},{1,5},{5... | collective-permute-start | bytes 9437192 | tf_op jit(solution)/shard_map/ppermute | solution.py:705
  296.9 11.4 %collective-permute-start.10 = (bf16[4,384,1024]{2,1,0:T(8,128)(2,1)}, bf16[4,384,1024]{2,1,0:T(8,128)(2,1)}, u32[]{:S(2)}, u32[]{:S(2)}) collective-permute-start(bf16[4,384,1024]{2,1,0:T(8,128)(2,1)} %bitcast.139), channel_id=1, source_target_pairs={{0,4},{4,0},{8,12},{12,8},{16,20},{20,16},{24,28},{28,24},{1,5},{5... | collective-permute-start | bytes 9437192 | tf_op jit(solution)/shard_map/ppermute | solution.py:705
  314.4 36.6 %collective-permute-start.13 = (bf16[2,384,1024]{2,1,0:T(8,128)(2,1)}, bf16[2,384,1024]{2,1,0:T(8,128)(2,1)}, u32[]{:S(2)}, u32[]{:S(2)}) collective-permute-start(bf16[2,384,1024]{2,1,0:T(8,128)(2,1)} %get-tuple-element.270), channel_id=1, source_target_pairs={{0,16},{4,20},{8,24},{12,28},{16,0},{20,4},{24,8},{28,12},{1,17},{... | collective-permute-start | bytes 4718600 | tf_op jit(solution)/shard_map/ppermute | solution.py:705
  315.8 36.3 %collective-permute-start.12 = (bf16[2,384,1024]{2,1,0:T(8,128)(2,1)}, bf16[2,384,1024]{2,1,0:T(8,128)(2,1)}, u32[]{:S(2)}, u32[]{:S(2)}) collective-permute-start(bf16[2,384,1024]{2,1,0:T(8,128)(2,1)} %get-tuple-element.271), channel_id=1, source_target_pairs={{0,8},{4,12},{8,0},{12,4},{16,24},{20,28},{24,16},{28,20},{1,9},{5... | collective-permute-start | bytes 4718600 | tf_op jit(solution)/shard_map/ppermute | solution.py:705
  318.2 11.1 %all-to-all-start = ((f32[4,256,4]{1,2,0:T(4,128)}), f32[4,256,4]{1,2,0:T(4,128)S(1)}, u32[]{:S(2)}, u32[]{:S(2)}) async-start(f32[4,256,4]{1,2,0:T(4,128)} %pad_maximum_fusion.13), calls=%async_computation.4 | async-start | bytes 32768 | tf_op jit(solution)/shard_map/all_to_all | solution.py:957
  321.5 111.4 %reduce-scatter.15.cloned.1.call-start = ((), (), s32[]{:S(2)}) async-start(), calls=%async_computation.16 | async-start | bytes 2621440 | tf_op jit(solution)/shard_map/reduce_scatter | solution.py:785
  356.7 18.6 %collective-permute-start.15 = (bf16[1,384,1024]{2,1,0:T(8,128)(2,1)}, bf16[1,384,1024]{2,1,0:T(8,128)(2,1)S(1)}, u32[]{:S(2)}, u32[]{:S(2)}) collective-permute-start(bf16[1,384,1024]{2,1,0:T(8,128)(2,1)} %get-tuple-element.268), channel_id=1, source_target_pairs={{0,8},{4,12},{8,0},{12,4},{16,24},{20,28},{24,16},{28,20},{1,9},{5... | collective-permute-start | bytes 2359304 | tf_op jit(solution)/shard_map/ppermute | solution.py:705
  358.2 18.2 %collective-permute-start.14 = (bf16[1,384,1024]{2,1,0:T(8,128)(2,1)}, bf16[1,384,1024]{2,1,0:T(8,128)(2,1)S(1)}, u32[]{:S(2)}, u32[]{:S(2)}) collective-permute-start(bf16[1,384,1024]{2,1,0:T(8,128)(2,1)} %get-tuple-element.269), channel_id=1, source_target_pairs={{0,16},{4,20},{8,24},{12,28},{16,0},{20,4},{24,8},{28,12},{1,17},{... | collective-permute-start | bytes 2359304 | tf_op jit(solution)/shard_map/ppermute | solution.py:705
  373.8 83.4 %reduce-scatter.17.cloned.1.call-start = ((), (), s32[]{:S(2)}) async-start(), calls=%async_computation.17 | async-start | bytes 1024000 | tf_op jit(solution)/shard_map/reduce_scatter | solution.py:1018
  380.7 3.5 collective-permute-start.21
  382.2 4.4 collective-permute-start.17
  382.3 20.4 %collective-permute-start.19 = (bf16[1,384,1024]{2,1,0:T(8,128)(2,1)S(1)}, bf16[1,384,1024]{2,1,0:T(8,128)(2,1)S(1)}, u32[]{:S(2)}, u32[]{:S(2)}) collective-permute-start(bf16[1,384,1024]{2,1,0:T(8,128)(2,1)S(1)} %get-tuple-element.266), channel_id=1, source_target_pairs={{0,8},{4,12},{8,0},{12,4},{16,24},{20,28},{24,16},{28,20},{1,9},{5... | collective-permute-start | bytes 2359304 | tf_op jit(solution)/shard_map/ppermute | solution.py:705
  382.7 20.4 %collective-permute-start.16 = (bf16[1,384,1024]{2,1,0:T(8,128)(2,1)S(1)}, bf16[1,384,1024]{2,1,0:T(8,128)(2,1)S(1)}, u32[]{:S(2)}, u32[]{:S(2)}) collective-permute-start(bf16[1,384,1024]{2,1,0:T(8,128)(2,1)S(1)} %get-tuple-element.267), channel_id=1, source_target_pairs={{0,16},{4,20},{8,24},{12,28},{16,0},{20,4},{24,8},{28,12},{1,17},{... | collective-permute-start | bytes 2359304 | tf_op jit(solution)/shard_map/ppermute | solution.py:705
  384.4 34.8 %collective-permute-start.22 = (bf16[4,2,32,1536]{3,2,0,1:T(8,128)(2,1)S(1)}, bf16[4,2,32,1536]{3,2,0,1:T(8,128)(2,1)S(1)}, u32[]{:S(2)}, u32[]{:S(2)}) collective-permute-start(bf16[4,2,32,1536]{3,2,0,1:T(8,128)(2,1)S(1)} %add_convert_fusion.3), channel_id=1, source_target_pairs={{0,16},{4,20},{8,24},{12,28},{16,0},{20,4},{24,8},{28,12},{1,17},{... | collective-permute-start | bytes 2359304 | tf_op jit(solution)/shard_map/ppermute | solution.py:705
  386.6 34.4 %copy-start.40 = (bf16[4,4,32,1664]{3,2,0,1:T(8,128)(2,1)}, bf16[4,4,32,1664]{3,2,0,1:T(8,128)(2,1)S(1)}, u32[]{:S(2)}) copy-start(bf16[4,4,32,1664]{3,2,0,1:T(8,128)(2,1)S(1)} %collective-permute-done.17) | copy-start | bytes 5111812
  386.9 34.2 %collective-permute-start.18 = (bf16[4,2,32,1664]{3,2,0,1:T(8,128)(2,1)S(1)}, bf16[4,2,32,1664]{3,2,0,1:T(8,128)(2,1)S(1)}, u32[]{:S(2)}, u32[]{:S(2)}) collective-permute-start(bf16[4,2,32,1664]{3,2,0,1:T(8,128)(2,1)S(1)} %add_convert_fusion.2), channel_id=1, source_target_pairs={{0,8},{4,12},{8,0},{12,4},{16,24},{20,28},{24,16},{28,20},{1,9},{5... | collective-permute-start | bytes 2555912 | tf_op jit(solution)/shard_map/ppermute | solution.py:705
  419.3 10.4 %collective-permute-start.23 = (bf16[4,1,32,1536]{3,2,0,1:T(8,128)(2,1)S(1)}, bf16[4,1,32,1536]{3,2,0,1:T(8,128)(2,1)S(1)}, u32[]{:S(2)}, u32[]{:S(2)}) collective-permute-start(bf16[4,1,32,1536]{3,2,0,1:T(8,128)(2,1)S(1)} %add_convert_fusion.11), channel_id=1, source_target_pairs={{0,8},{4,12},{8,0},{12,4},{16,24},{20,28},{24,16},{28,20},{1,9},{5... | collective-permute-start | bytes 1179656 | tf_op jit(solution)/shard_map/ppermute | solution.py:705
  421.2 10.9 %collective-permute-start.20 = (bf16[4,1,32,1664]{3,2,0,1:T(8,128)(2,1)S(1)}, bf16[4,1,32,1664]{3,2,0,1:T(8,128)(2,1)S(1)}, u32[]{:S(2)}, u32[]{:S(2)}) collective-permute-start(bf16[4,1,32,1664]{3,2,0,1:T(8,128)(2,1)S(1)} %add_convert_fusion.9), channel_id=1, source_target_pairs={{0,16},{4,20},{8,24},{12,28},{16,0},{20,4},{24,8},{28,12},{1,17},{... | collective-permute-start | bytes 1277960 | tf_op jit(solution)/shard_map/ppermute | solution.py:705
  435.4 53.3 %all-gather.24.cloned.1.call-start = ((), (), s32[]{:S(2)}) async-start(), calls=%async_computation.19 | async-start | bytes 1843200 | tf_op jit(solution)/shard_map/all_gather | solution.py:1026
  435.4 10.2 %collective-permute-start.24 = (bf16[2,384,1024]{2,1,0:T(8,128)(2,1)S(1)}, bf16[2,384,1024]{2,1,0:T(8,128)(2,1)S(1)}, u32[]{:S(2)}, u32[]{:S(2)}) collective-permute-start(bf16[2,384,1024]{2,1,0:T(8,128)(2,1)S(1)} %constant_dynamic-update-slice_fusion.1), channel_id=1, source_target_pairs={{0,4},{4,0},{8,12},{12,8},{16,20},{20,16},{24,28},{28,24},{1,5},{5... | collective-permute-start | bytes 4718600 | tf_op jit(solution)/shard_map/ppermute | solution.py:705
  435.5 10.1 %collective-permute-start.25 = (bf16[2,384,1024]{2,1,0:T(8,128)(2,1)}, bf16[2,384,1024]{2,1,0:T(8,128)(2,1)S(1)}, u32[]{:S(2)}, u32[]{:S(2)}) collective-permute-start(bf16[2,384,1024]{2,1,0:T(8,128)(2,1)} %copy-done.7), channel_id=1, source_target_pairs={{0,4},{4,0},{8,12},{12,8},{16,20},{20,16},{24,28},{28,24},{1,5},{5... | collective-permute-start | bytes 4718600 | tf_op jit(solution)/shard_map/ppermute | solution.py:705
  436.0 38.7 %collective-permute-start.26 = (bf16[2,384,1024]{2,1,0:T(8,128)(2,1)S(1)}, bf16[2,384,1024]{2,1,0:T(8,128)(2,1)}, u32[]{:S(2)}, u32[]{:S(2)}) collective-permute-start(bf16[2,384,1024]{2,1,0:T(8,128)(2,1)S(1)} %constant_dynamic-update-slice_fusion.1), channel_id=1, source_target_pairs={{0,8},{4,12},{8,0},{12,4},{16,24},{20,28},{24,16},{28,20},{1,9},{5... | collective-permute-start | bytes 4718600 | tf_op jit(solution)/shard_map/ppermute | solution.py:705
  436.3 38.6 %collective-permute-start.27 = (bf16[2,384,1024]{2,1,0:T(8,128)(2,1)}, bf16[2,384,1024]{2,1,0:T(8,128)(2,1)}, u32[]{:S(2)}, u32[]{:S(2)}) collective-permute-start(bf16[2,384,1024]{2,1,0:T(8,128)(2,1)} %copy-done.7), channel_id=1, source_target_pairs={{0,16},{4,20},{8,24},{12,28},{16,0},{20,4},{24,8},{28,12},{1,17},{... | collective-permute-start | bytes 4718600 | tf_op jit(solution)/shard_map/ppermute | solution.py:705
  445.6 30.5 %copy-start.48 = (bf16[128,1024]{1,0:T(8,128)(2,1)S(1)}, bf16[128,1024]{1,0:T(8,128)(2,1)}, u32[]{:S(2)}) copy-start(bf16[128,1024]{1,0:T(8,128)(2,1)} %get-tuple-element.275) | copy-start | bytes 786436
  474.9 8.1 %collective-permute-start.28 = (bf16[2,384,1024]{2,1,0:T(8,128)(2,1)}, bf16[2,384,1024]{2,1,0:T(8,128)(2,1)S(1)}, u32[]{:S(2)}, u32[]{:S(2)}) collective-permute-start(bf16[2,384,1024]{2,1,0:T(8,128)(2,1)} %collective-permute-done.26), channel_id=1, source_target_pairs={{0,4},{4,0},{8,12},{12,8},{16,20},{20,16},{24,28},{28,24},{1,5},{5... | collective-permute-start | bytes 4718600 | tf_op jit(solution)/shard_map/ppermute | solution.py:705
  475.0 8.1 %collective-permute-start.29 = (bf16[2,384,1024]{2,1,0:T(8,128)(2,1)}, bf16[2,384,1024]{2,1,0:T(8,128)(2,1)}, u32[]{:S(2)}, u32[]{:S(2)}) collective-permute-start(bf16[2,384,1024]{2,1,0:T(8,128)(2,1)} %collective-permute-done.27), channel_id=1, source_target_pairs={{0,4},{4,0},{8,12},{12,8},{16,20},{20,16},{24,28},{28,24},{1,5},{5... | collective-permute-start | bytes 4718600 | tf_op jit(solution)/shard_map/ppermute | solution.py:705
  (56 other events, 451.5 us)
Sparse Core Ops, SparseCore 0:
  9.6 52.1 all-gather.11
  64.0 27.0 all-gather.21
  96.6 27.4 all-gather.13
  126.0 27.4 all-gather.15
  156.2 26.6 reduce-scatter.6
  185.7 25.7 reduce-scatter.8
  213.7 26.6 all-gather.17
  242.5 27.3 all-gather.19
  272.8 26.6 reduce-scatter.10
  302.3 25.8 reduce-scatter.12
  373.9 42.6 reduce-scatter.14
  435.5 21.6 reduce-scatter.16
  459.2 27.3 all-gather.23
